TPU v7x, 32 devices: a whole 2x2x4 slice. The times are simulated.
32 devices in a mesh: groups: 2 (over x), docs: 16 (over z, y, core).
Axes of the slice: x: 2, y: 2, z: 4, core: 2. Of those that a mesh axis runs over, the one named last changes fastest.
Arguments:
- sentences: bfloat16 [65536, 1280], P(('groups', 'docs')), parts along dimension 0, may hold values from -10 to 10
- sent_doc: int32 [65536], P('groups'), parts along dimension 0, may hold values from 0 to 2047, never falling along the last dimension, each value on 1 to 32 neighbouring positions
- images: bfloat16 [8192, 1280], P(('groups', 'docs')), parts along dimension 0, may hold values from -30 to 30
- image_owner: int32 [8192, 1], P(('groups', 'docs')), parts along dimension 0, may hold values from 0 to 15, as said below
- anchor: int32 [8192], P(('groups', 'docs')), parts along dimension 0, may hold values from 0 to 2047, as said below
- loader_shard: int32 [8192, 1], P(('groups', 'docs')), parts along dimension 0, may hold values from 0 to 15, as said below
Outputs:
- loaded_images: bfloat16 [16384, 1280], P(('groups', 'docs')), parts along dimension 0
- loaded_text: bfloat16 [16384, 1280], P(('groups', 'docs')), parts along dimension 0
There are 2 independent parts, one for each index of `groups`. A program takes and returns all parts, laid end to end along the dimension named above; each array names one. Nothing has to cross between parts.
Inputs may be any that keep to these rules, and one draw needn't show every extreme that they name: `sent_doc`: documents are runs of 1 to 32 consecutive sentences, ids never falling. `image_owner`: the 256 images of one device name one owner at most 32 times, and some owner exactly 32 times. loader_shard = (a[source device] + b[image_owner]) mod 16 for two permutations a and b of the devices, drawn with the data. So the images of one device name one shard at most 32 times (some exactly 32), and the images that one owner receives from all devices name one shard at most 32 times, all from one source device. `anchor`: the image's document is the document of this sentence of its owner.
All inputs are finite; a program needn't handle non-finite values.
Results may differ from a plain program's by a relative error of at most 0.0048.
Values may be sent and summed in bfloat16 or wider, within the bound.
No kernel may reach another device: no remote copies, remote signals or barrier semaphores. Data moves between devices by JAX's collectives and lax.ppermute only.
A program may use at most 64 MiB of HBM per device.

v0:
```python
import jax
import jax.numpy as jnp
from jax import lax
from jax.sharding import PartitionSpec as P

MOST_SENT = 32


def extended_2(shard, sides, width):
    for axis, dim in sides:
        peers, length = (lax.axis_size(axis), shard.shape[dim])
        up = [(i, (i + 1) % peers) for i in range(peers - 1)]
        down = [(j, i) for i, j in up]
        last = lax.slice_in_dim(shard, length - width, length, axis=dim)
        first = lax.slice_in_dim(shard, 0, width, axis=dim)
        before = lax.ppermute(last, axis, up)
        after = lax.ppermute(first, axis, down)
        shard = jnp.concatenate([before, shard, after], axis=dim)
    return shard


def ranks_of(targets, members):
    labels = jnp.arange(members, dtype=jnp.int32)
    onehot = (targets[:, None] == labels[None, :]).astype(jnp.int32)
    return jnp.sum((jnp.cumsum(onehot, axis=0) - 1) * onehot, axis=1)


def slot_table(targets, members, capacity):
    places = targets * capacity + ranks_of(targets, members)
    slot_ids = jnp.arange(members * capacity, dtype=jnp.int32)
    return slot_ids[:, None] == places[None, :]


def spread_values(table, values):
    return jnp.sum(jnp.where(table, values[None, :] + 1, 0), axis=1) - 1


def shards(sentences, sent_doc, images, image_owner, anchor, loader_shard):
    members = lax.axis_size("docs")
    myself = lax.axis_index("docs")
    own_rows, feature = sentences.shape
    capacity = max(4, 2 * images.shape[0] // members)
    temper = feature ** (-0.5)
    owner_table = slot_table(image_owner[:, 0], members, capacity)
    owner_dispatch = owner_table.astype(jnp.bfloat16)
    extended = extended_2(sentences, (("docs", 0),), MOST_SENT)
    padded_ids = jnp.pad(sent_doc, (MOST_SENT, MOST_SENT), constant_values=-1)
    window_ids = lax.dynamic_slice_in_dim(padded_ids, myself * own_rows, own_rows + 2 * MOST_SENT)
    outgoing = jnp.dot(owner_dispatch, images, preferred_element_type=jnp.float32).astype(
        jnp.bfloat16
    )
    outgoing = outgoing.reshape(members, capacity, feature)
    anchor_slots = spread_values(owner_table, anchor).reshape(members, capacity)
    shard_slots = spread_values(owner_table, loader_shard[:, 0]).reshape(members, capacity)
    out_rows = myself * capacity + ranks_of(loader_shard[:, 0], members)
    row_slots = spread_values(owner_table, out_rows).reshape(members, capacity)
    arrived = lax.all_to_all(outgoing, "docs", split_axis=0, concat_axis=0, tiled=True)
    positions = lax.all_to_all(anchor_slots, "docs", split_axis=0, concat_axis=0, tiled=True)
    shards_in = lax.all_to_all(shard_slots, "docs", split_axis=0, concat_axis=0, tiled=True)
    rows_in = lax.all_to_all(row_slots, "docs", split_axis=0, concat_axis=0, tiled=True)
    items = arrived.shape[1]
    queries = arrived.reshape(members * items, feature)
    spots = positions.reshape(members * items)
    filled = spots >= 0
    docs_of = jnp.where(filled, sent_doc[myself * own_rows + jnp.maximum(spots, 0)], -2)
    scores = (
        lax.dot_general(
            queries, extended, (((1,), (1,)), ((), ())), preferred_element_type=jnp.float32
        )
        * temper
    )
    member = docs_of[:, None] == window_ids[None, :]
    peak = jnp.max(jnp.where(member, scores, -1e30), axis=1, keepdims=True)
    raised = jnp.where(member, jnp.exp(scores - peak), 0.0)
    denominator = jnp.sum(raised, axis=1, keepdims=True)
    weights = (raised / jnp.where(filled[:, None], denominator, 1.0)).astype(jnp.bfloat16)
    aligned = jnp.dot(weights, extended, preferred_element_type=jnp.float32).astype(jnp.bfloat16)
    aligned = aligned.reshape(members, items, feature)
    labels = jnp.arange(members, dtype=jnp.int32)
    route_mask = shards_in[:, None, :] == labels[None, :, None]
    route_weights = route_mask.astype(jnp.bfloat16)
    image_fwd = jnp.einsum(
        "sdj,sje->dje", route_weights, arrived, preferred_element_type=jnp.float32
    ).astype(jnp.bfloat16)
    text_fwd = jnp.einsum(
        "sdj,sje->dje", route_weights, aligned, preferred_element_type=jnp.float32
    ).astype(jnp.bfloat16)
    rows_fwd = (jnp.sum(jnp.where(route_mask, rows_in[:, None, :] + 1, 0), axis=0) - 1).astype(
        jnp.int32
    )
    got_images = lax.all_to_all(image_fwd, "docs", split_axis=0, concat_axis=0, tiled=True)
    got_text = lax.all_to_all(text_fwd, "docs", split_axis=0, concat_axis=0, tiled=True)
    got_rows = lax.all_to_all(rows_fwd, "docs", split_axis=0, concat_axis=0, tiled=True)
    flat_rows = got_rows.reshape(members * capacity)
    block_ids = jnp.arange(members * capacity, dtype=jnp.int32)
    placing = (block_ids[:, None] == flat_rows[None, :]).astype(jnp.bfloat16)
    loaded_images = jnp.dot(
        placing, got_images.reshape(members * capacity, feature), preferred_element_type=jnp.float32
    ).astype(jnp.bfloat16)
    loaded_text = jnp.dot(
        placing, got_text.reshape(members * capacity, feature), preferred_element_type=jnp.float32
    ).astype(jnp.bfloat16)
    return (loaded_images, loaded_text)


def solution(mesh):
    return jax.shard_map(
        shards,
        mesh=mesh,
        in_specs=(
            P(("groups", "docs"), None),
            P("groups"),
            P(("groups", "docs"), None),
            P(("groups", "docs"), None),
            P(("groups", "docs")),
            P(("groups", "docs"), None),
        ),
        out_specs=(P(("groups", "docs"), None), P(("groups", "docs"), None)),
        check_vma=False,
    )
```

profile of v0, /device:TPU:14, one launch (start us, length us, event | category | flops | bytes accessed | tf_op | source)
XLA Modules:
  0.0 172.1 jit_solution(14369713423408936356)
XLA Ops:
  8.3 6.2 %all-to-all-start.5 = ((s32[16,1,32]{2,1,0:T(1,128)}), s32[16,1,32]{2,1,0:T(1,128)S(1)}, u32[]{:S(2)}, u32[]{:S(2)}) async-start(s32[16,1,32]{2,1,0:T(1,128)} %sub.56), calls=%async_computation.5 | async-start | bytes 16384 | tf_op jit(solution)/shard_map/all_to_all | solution.py:58
  15.5 2.1 %collective-permute-start = (bf16[32,1280]{1,0:T(8,128)(2,1)S(1)}, bf16[32,1280]{1,0:T(8,128)(2,1)S(1)}, u32[]{:S(2)}, u32[]{:S(2)}) collective-permute-start(bf16[32,1280]{1,0:T(8,128)(2,1)S(1)} %get-tuple-element.6), channel_id=1, source_target_pairs={{0,1},{1,2},{2,3},{3,4},{4,5},{5,6},{6,7},{7,8},{8,9},{9,10},{10,1... | collective-permute-start | bytes 245768 | tf_op jit(solution)/shard_map/ppermute | solution.py:16
  17.6 3.5 %collective-permute-start.1 = (bf16[32,1280]{1,0:T(8,128)(2,1)S(1)}, bf16[32,1280]{1,0:T(8,128)(2,1)S(1)}, u32[]{:S(2)}, u32[]{:S(2)}) collective-permute-start(bf16[32,1280]{1,0:T(8,128)(2,1)S(1)} %get-tuple-element.5), channel_id=1, source_target_pairs={{1,0},{2,1},{3,2},{4,3},{5,4},{6,5},{7,6},{8,7},{9,8},{10,9},{11,1... | collective-permute-start | bytes 245768 | tf_op jit(solution)/shard_map/ppermute | solution.py:17
  21.8 6.0 %all-to-all-start = ((s32[16,1,32]{2,1,0:T(1,128)}), s32[16,1,32]{2,1,0:T(1,128)S(1)}, u32[]{:S(2)}, u32[]{:S(2)}) async-start(s32[16,1,32]{2,1,0:T(1,128)} %bitcast.4), calls=%async_computation | async-start | bytes 16384 | tf_op jit(solution)/shard_map/all_to_all | solution.py:59
  27.8 1.6 convolution_convert_fusion.5
  30.0 1.8 %all-to-all-done = s32[16,1,32]{2,1,0:T(1,128)S(1)} async-done(((s32[16,1,32]{2,1,0:T(1,128)}), s32[16,1,32]{2,1,0:T(1,128)S(1)}, u32[]{:S(2)}, u32[]{:S(2)}) %all-to-all-start) | async-done | bytes 2080 | tf_op jit(solution)/shard_map/all_to_all | solution.py:59
  31.8 5.7 %all-to-all-start.1 = ((s32[16,1,32]{2,1,0:T(1,128)}), s32[16,1,32]{2,1,0:T(1,128)S(1)}, u32[]{:S(2)}, u32[]{:S(2)}) async-start(s32[16,1,32]{2,1,0:T(1,128)} %bitcast.8), calls=%async_computation.1 | async-start | bytes 16384 | tf_op jit(solution)/shard_map/all_to_all | solution.py:60
  38.3 3.3 %all-to-all-done.1 = s32[16,1,32]{2,1,0:T(1,128)S(1)} async-done(((s32[16,1,32]{2,1,0:T(1,128)}), s32[16,1,32]{2,1,0:T(1,128)S(1)}, u32[]{:S(2)}, u32[]{:S(2)}) %all-to-all-start.1) | async-done | bytes 2080 | tf_op jit(solution)/shard_map/all_to_all | solution.py:60
  41.7 5.9 %all-to-all-start.3 = ((bf16[16,32,1280]{2,1,0:T(8,128)(2,1)}), bf16[16,32,1280]{2,1,0:T(8,128)(2,1)S(1)}, u32[]{:S(2)}, u32[]{:S(2)}) async-start(bf16[16,32,1280]{2,1,0:T(8,128)(2,1)} %bitcast.11), calls=%async_computation.3 | async-start | bytes 2621440 | tf_op jit(solution)/shard_map/all_to_all | solution.py:57
  47.8 3.1 %gather_fusion = s32[512]{0:T(512)S(1)} fusion(s32[32768]{0:T(1024)S(1)} %copy-done.1, s32[1024]{0:T(1024)S(1)} %pad_clamp_fusion), kind=kCustom, calls=%fused_computation | custom fusion | bytes 6144 | tf_op jit(solution)/shard_map/gather | solution.py:65
  53.1 5.1 %constant_dynamic-update-slice_fusion.1 = bf16[2112,1280]{1,0:T(8,128)(2,1)} fusion(bf16[2112,1280]{1,0:T(8,128)(2,1)} %constant_dynamic-update-slice_fusion.2, bf16[2048,1280]{1,0:T(8,128)(2,1)} %param.6), kind=kLoop, calls=%fused_computation.55 | loop fusion | bytes 10485760
  58.9 19.2 %all-to-all-done.3 = bf16[16,32,1280]{2,1,0:T(8,128)(2,1)S(1)} async-done(((bf16[16,32,1280]{2,1,0:T(8,128)(2,1)}), bf16[16,32,1280]{2,1,0:T(8,128)(2,1)S(1)}, u32[]{:S(2)}, u32[]{:S(2)}) %all-to-all-start.3) | async-done | bytes 1310752 | tf_op jit(solution)/shard_map/all_to_all | solution.py:57
  78.1 5.0 %all-to-all-start.2 = ((s32[16,1,32]{2,1,0:T(1,128)}), s32[16,1,32]{2,1,0:T(1,128)S(1)}, u32[]{:S(2)}, u32[]{:S(2)}) async-start(s32[16,1,32]{2,1,0:T(1,128)} %copy.36), calls=%async_computation.2 | async-start | bytes 16384 | tf_op jit(solution)/shard_map/all_to_all | solution.py:93
  83.0 5.4 %fusion = (f32[512]{0:T(512)S(1)}, f32[512,2112]{0,1:T(8,128)S(1)}) fusion(s32[512]{0:T(512)S(1)} %broadcast_select_fusion.1, s32[2112]{0:T(1024)S(1)} %pad_dynamic-slice_fusion, bf16[512,1280]{1,0:T(8,128)(2,1)S(1)} %bitcast.56, bf16[2112,1280]{1,0:T(8,128)(2,1)} %constant_dynamic-update-slice_fusion), kind=kOutput, calls=%fused_computation.4 | convolution fusion | flops 2772565504 | bytes 11055360 | tf_op jit(solution)/shard_map/dot_general | solution.py:67
  88.5 1.3 fusion.1
  89.8 6.1 %convolution_convert_fusion.2 = bf16[512,1280]{1,0:T(8,128)(2,1)S(1)} fusion(bf16[2112,1280]{1,0:T(8,128)(2,1)} %constant_dynamic-update-slice_fusion, f32[512,2112]{0,1:T(8,128)S(1)} %get-tuple-element.8, f32[512]{0:T(512)S(1)} %broadcast_select_fusion, f32[512]{0:T(512)S(1)} %get-tuple-element.7, s32[512]{0:T(512)S(1)} %broadcast_select_fusion.1, ...), kind=kOutput, calls=%fused_computation.9 | convolution fusion | flops 2774302720 | bytes 11057408 | tf_op jit(solution)/shard_map/dot_general | solution.py:77
  96.8 1.4 copy.40
  98.3 6.0 %all-to-all-start.6 = ((bf16[16,32,1280]{2,1,0:T(8,128)(2,1)}), bf16[16,32,1280]{2,1,0:T(8,128)(2,1)S(1)}, u32[]{:S(2)}, u32[]{:S(2)}) async-start(bf16[16,32,1280]{2,1,0:T(8,128)(2,1)} %copy.40), calls=%async_computation.6 | async-start | bytes 2621440 | tf_op jit(solution)/shard_map/all_to_all | solution.py:92
  105.2 1.4 copy.38
  106.7 28.0 %all-to-all-done.6 = bf16[16,32,1280]{2,1,0:T(8,128)(2,1)S(1)} async-done(((bf16[16,32,1280]{2,1,0:T(8,128)(2,1)}), bf16[16,32,1280]{2,1,0:T(8,128)(2,1)S(1)}, u32[]{:S(2)}, u32[]{:S(2)}) %all-to-all-start.6) | async-done | bytes 1310752 | tf_op jit(solution)/shard_map/all_to_all | solution.py:92
  134.7 5.0 %all-to-all-start.4 = ((bf16[16,32,1280]{2,1,0:T(8,128)(2,1)}), bf16[16,32,1280]{2,1,0:T(8,128)(2,1)S(1)}, u32[]{:S(2)}, u32[]{:S(2)}) async-start(bf16[16,32,1280]{2,1,0:T(8,128)(2,1)} %copy.38), calls=%async_computation.4 | async-start | bytes 2621440 | tf_op jit(solution)/shard_map/all_to_all | solution.py:91
  141.0 1.9 %convolution_convert_fusion = bf16[512,1280]{1,0:T(8,128)(2,1)} fusion(bf16[512,1280]{1,0:T(8,128)(2,1)S(1)} %bitcast.58, s32[512]{0:T(512)S(1)} %eq.124), kind=kOutput, calls=%fused_computation.7 | convolution fusion | flops 672006144 | bytes 2623488 | tf_op jit(solution)/shard_map/dot_general | solution.py:100
  142.9 27.2 %all-to-all-done.4 = bf16[16,32,1280]{2,1,0:T(8,128)(2,1)S(1)} async-done(((bf16[16,32,1280]{2,1,0:T(8,128)(2,1)}), bf16[16,32,1280]{2,1,0:T(8,128)(2,1)S(1)}, u32[]{:S(2)}, u32[]{:S(2)}) %all-to-all-start.4) | async-done | bytes 1310752 | tf_op jit(solution)/shard_map/all_to_all | solution.py:91
  170.1 1.9 %convolution_convert_fusion.3 = bf16[512,1280]{1,0:T(8,128)(2,1)} fusion(bf16[512,1280]{1,0:T(8,128)(2,1)S(1)} %bitcast.59, s32[512]{0:T(512)S(1)} %eq.124), kind=kOutput, calls=%fused_computation.10 | convolution fusion | flops 672006144 | bytes 2623488 | tf_op jit(solution)/shard_map/dot_general | solution.py:97
  (53 shorter events, 16.9 us)
Async XLA Ops:
  0.6 27.2 %copy-start = (bf16[256,1280]{1,0:T(8,128)(2,1)S(1)}, bf16[256,1280]{1,0:T(8,128)(2,1)}, u32[]{:S(2)}) copy-start(bf16[256,1280]{1,0:T(8,128)(2,1)} %param.8) | copy-start | bytes 1966084
  0.6 47.1 %copy-start.1 = (s32[32768]{0:T(1024)S(1)}, s32[32768]{0:T(1024)}, u32[]{:S(2)}) copy-start(s32[32768]{0:T(1024)} %param.7) | copy-start | bytes 393220
  8.3 13.5 %all-to-all-start.5 = ((s32[16,1,32]{2,1,0:T(1,128)}), s32[16,1,32]{2,1,0:T(1,128)S(1)}, u32[]{:S(2)}, u32[]{:S(2)}) async-start(s32[16,1,32]{2,1,0:T(1,128)} %sub.56), calls=%async_computation.5 | async-start | bytes 16384 | tf_op jit(solution)/shard_map/all_to_all | solution.py:58
  15.5 37.0 %collective-permute-start = (bf16[32,1280]{1,0:T(8,128)(2,1)S(1)}, bf16[32,1280]{1,0:T(8,128)(2,1)S(1)}, u32[]{:S(2)}, u32[]{:S(2)}) collective-permute-start(bf16[32,1280]{1,0:T(8,128)(2,1)S(1)} %get-tuple-element.6), channel_id=1, source_target_pairs={{0,1},{1,2},{2,3},{3,4},{4,5},{5,6},{6,7},{7,8},{8,9},{9,10},{10,1... | collective-permute-start | bytes 245768 | tf_op jit(solution)/shard_map/ppermute | solution.py:16
  17.6 40.7 %collective-permute-start.1 = (bf16[32,1280]{1,0:T(8,128)(2,1)S(1)}, bf16[32,1280]{1,0:T(8,128)(2,1)S(1)}, u32[]{:S(2)}, u32[]{:S(2)}) collective-permute-start(bf16[32,1280]{1,0:T(8,128)(2,1)S(1)} %get-tuple-element.5), channel_id=1, source_target_pairs={{1,0},{2,1},{3,2},{4,3},{5,4},{6,5},{7,6},{8,7},{9,8},{10,9},{11,1... | collective-permute-start | bytes 245768 | tf_op jit(solution)/shard_map/ppermute | solution.py:17
  21.8 10.0 %all-to-all-start = ((s32[16,1,32]{2,1,0:T(1,128)}), s32[16,1,32]{2,1,0:T(1,128)S(1)}, u32[]{:S(2)}, u32[]{:S(2)}) async-start(s32[16,1,32]{2,1,0:T(1,128)} %bitcast.4), calls=%async_computation | async-start | bytes 16384 | tf_op jit(solution)/shard_map/all_to_all | solution.py:59
  31.8 9.9 %all-to-all-start.1 = ((s32[16,1,32]{2,1,0:T(1,128)}), s32[16,1,32]{2,1,0:T(1,128)S(1)}, u32[]{:S(2)}, u32[]{:S(2)}) async-start(s32[16,1,32]{2,1,0:T(1,128)} %bitcast.8), calls=%async_computation.1 | async-start | bytes 16384 | tf_op jit(solution)/shard_map/all_to_all | solution.py:60
  41.7 36.4 %all-to-all-start.3 = ((bf16[16,32,1280]{2,1,0:T(8,128)(2,1)}), bf16[16,32,1280]{2,1,0:T(8,128)(2,1)S(1)}, u32[]{:S(2)}, u32[]{:S(2)}) async-start(bf16[16,32,1280]{2,1,0:T(8,128)(2,1)} %bitcast.11), calls=%async_computation.3 | async-start | bytes 2621440 | tf_op jit(solution)/shard_map/all_to_all | solution.py:57
  78.1 20.2 %all-to-all-start.2 = ((s32[16,1,32]{2,1,0:T(1,128)}), s32[16,1,32]{2,1,0:T(1,128)S(1)}, u32[]{:S(2)}, u32[]{:S(2)}) async-start(s32[16,1,32]{2,1,0:T(1,128)} %copy.36), calls=%async_computation.2 | async-start | bytes 16384 | tf_op jit(solution)/shard_map/all_to_all | solution.py:93
  98.3 36.4 %all-to-all-start.6 = ((bf16[16,32,1280]{2,1,0:T(8,128)(2,1)}), bf16[16,32,1280]{2,1,0:T(8,128)(2,1)S(1)}, u32[]{:S(2)}, u32[]{:S(2)}) async-start(bf16[16,32,1280]{2,1,0:T(8,128)(2,1)} %copy.40), calls=%async_computation.6 | async-start | bytes 2621440 | tf_op jit(solution)/shard_map/all_to_all | solution.py:92
  134.7 35.4 %all-to-all-start.4 = ((bf16[16,32,1280]{2,1,0:T(8,128)(2,1)}), bf16[16,32,1280]{2,1,0:T(8,128)(2,1)S(1)}, u32[]{:S(2)}, u32[]{:S(2)}) async-start(bf16[16,32,1280]{2,1,0:T(8,128)(2,1)} %copy.38), calls=%async_computation.4 | async-start | bytes 2621440 | tf_op jit(solution)/shard_map/all_to_all | solution.py:91
where the time goes:
time: 173 us; the launch traced here: 172 us
  waiting for transfers between devices  79.5 us (46%)
  starting transfers between devices  45.5 us (26%)
  matrix products  18.8 us (11%)
  local copies, waits for them, and re-layouts  18.1 us (10%)
  other arithmetic  9.28 us (5%)
    all_to_all x1, waiting for transfers between devices, shards(): lax.all_to_all(text_fwd, 'docs', split_axis=0, concat_axis=0, tiled=True)  28 us
    all_to_all x1, waiting for transfers between devices, shards(): lax.all_to_all(image_fwd, 'docs', split_axis=0, concat_axis=0, tiled=True)  27.2 us
    all_to_all x1, waiting for transfers between devices, shards(): lax.all_to_all(outgoing, 'docs', split_axis=0, concat_axis=0, tiled=True)  19.2 us
    all_to_all x1, starting transfers between devices, shards(): lax.all_to_all(anchor_slots, 'docs', split_axis=0, concat_axis=0, tiled=T...  6.24 us
    dot_general x1, matrix products, shards(): jnp.dot(weights, extended, preferred_element_type=jnp.float32)  6.08 us
    all_to_all x1, starting transfers between devices, shards(): lax.all_to_all(text_fwd, 'docs', split_axis=0, concat_axis=0, tiled=True)  6.02 us
    all_to_all x1, starting transfers between devices, shards(): lax.all_to_all(shard_slots, 'docs', split_axis=0, concat_axis=0, tiled=True)  6.02 us
    all_to_all x1, starting transfers between devices, shards(): lax.all_to_all(outgoing, 'docs', split_axis=0, concat_axis=0, tiled=True)  5.94 us
  transfers between devices with their start and end apart: 9, of which 5 were waited for; matrix products, arithmetic and copies ran while one was open for 21% of the time, Pallas kernels for 0%

commit v1 on v0

v1 whole, which is shorter than its diff:
```python
import functools

import jax
import jax.numpy as jnp
from jax import lax
from jax.experimental import pallas as pl
from jax.experimental.pallas import tpu as pltpu
from jax.sharding import PartitionSpec as P

MOST_SENT = 32


def halo_of(sentences):
    peers = lax.axis_size("docs")
    up = [(i, i + 1) for i in range(peers - 1)]
    down = [(j, i) for i, j in up]
    before = lax.ppermute(sentences[-MOST_SENT:], "docs", up)
    after = lax.ppermute(sentences[:MOST_SENT], "docs", down)
    return before, after


def attend_kernel(temper, q_ref, doc_ref, k_ref, before_ref, after_ref, id_ref, id_before_ref, id_after_ref, o_ref):
    q = q_ref[...]
    doc = doc_ref[...]
    parts = ((k_ref, id_ref), (before_ref, id_before_ref), (after_ref, id_after_ref))
    scores = []
    for rows, ids in parts:
        s = lax.dot_general(q, rows[...], (((1,), (1,)), ((), ())), preferred_element_type=jnp.float32) * temper
        scores.append(jnp.where(doc == ids[...], s, -1e30))
    peak = functools.reduce(jnp.maximum, [jnp.max(s, axis=1, keepdims=True) for s in scores])
    raised = [jnp.where(doc == ids[...], jnp.exp(s - peak), 0.0) for s, (_, ids) in zip(scores, parts)]
    total = sum(jnp.sum(r, axis=1, keepdims=True) for r in raised)
    total = jnp.where(total > 0.0, total, 1.0)
    o_ref[...] = sum(
        jnp.dot((r / total).astype(jnp.bfloat16), rows[...], preferred_element_type=jnp.float32)
        for r, (rows, _) in zip(raised, parts)
    ).astype(jnp.bfloat16)


def attend(queries, docs, sentences, before, after, ids, id_before, id_after):
    rows, feature = queries.shape
    own = sentences.shape[0]
    block = min(128, rows)
    whole = lambda a: pl.BlockSpec(a.shape, lambda i: (0, 0))
    fixed = (sentences, before, after, ids, id_before, id_after)
    return pl.pallas_call(
        functools.partial(attend_kernel, feature**-0.5),
        grid=(rows // block,),
        in_specs=[
            pl.BlockSpec((block, feature), lambda i: (i, 0)),
            pl.BlockSpec((block, 1), lambda i: (i, 0)),
            *[whole(a) for a in fixed],
        ],
        out_specs=pl.BlockSpec((block, feature), lambda i: (i, 0)),
        out_shape=jax.ShapeDtypeStruct((rows, feature), jnp.bfloat16),
        compiler_params=pltpu.CompilerParams(vmem_limit_bytes=40 * 1024 * 1024),
        cost_estimate=pl.CostEstimate(
            flops=4 * rows * own * feature, bytes_accessed=2 * (own + 2 * rows) * feature, transcendentals=rows * own
        ),
        name="attend",
    )(queries, docs, *fixed)


def exchange(x):
    return lax.all_to_all(x, "docs", split_axis=0, concat_axis=0, tiled=True)


def shards(sentences, sent_doc, images, image_owner, anchor, loader_shard):
    members = lax.axis_size("docs")
    me = lax.axis_index("docs")
    own, feature = sentences.shape
    n = images.shape[0]
    cap = max(4, 2 * n // members)
    owner, shard = image_owner[:, 0], loader_shard[:, 0]

    packed = (owner * members + shard) * own + anchor
    every = lax.all_gather(packed, "docs", axis=0, tiled=False)

    spot = jnp.arange(n, dtype=jnp.int32)
    earlier = (owner[:, None] == owner[None, :]) & (spot[None, :] < spot[:, None])
    rank = jnp.sum(earlier.astype(jnp.int32), axis=1)
    slot = jnp.arange(members * cap, dtype=jnp.int32)[:, None]

    def buckets(targets):
        table = (slot == (targets * cap + rank)[None, :]).astype(jnp.bfloat16)
        out = jnp.dot(table, images, preferred_element_type=jnp.float32).astype(jnp.bfloat16)
        return out.reshape(members, cap, feature)

    queries = exchange(buckets(owner)).reshape(members * cap, feature)
    loaded_images = exchange(buckets(shard)).reshape(members * cap, feature)
    before, after = halo_of(sentences)

    spot_of = every % own
    shard_of = every // own % members
    owner_of = every // (own * members)
    mine = owner_of == me
    sooner = (spot[:, None] < spot[None, :]).astype(jnp.bfloat16)
    place = jnp.dot(mine.astype(jnp.bfloat16), sooner, preferred_element_type=jnp.float32).astype(jnp.int32)
    slots = jnp.arange(cap, dtype=jnp.int32)
    hit = mine[:, None, :] & (place[:, None, :] == slots[None, :, None])
    spots = jnp.sum(jnp.where(hit, spot_of[:, None, :] + 1, 0), axis=2).reshape(members * cap) - 1
    docs = jnp.where(spots >= 0, sent_doc[me * own + jnp.maximum(spots, 0)], -2)
    ids = lax.dynamic_slice_in_dim(sent_doc, me * own, own)
    padded = jnp.pad(sent_doc, (MOST_SENT, MOST_SENT), constant_values=-1)
    id_before = lax.dynamic_slice_in_dim(padded, me * own, MOST_SENT)
    id_after = lax.dynamic_slice_in_dim(padded, me * own + own + MOST_SENT, MOST_SENT)
    aligned = attend(queries, docs[:, None], sentences, before, after, ids[None], id_before[None], id_after[None])

    goes = jnp.max(jnp.where(mine, shard_of + 1, 0), axis=1) - 1
    comes = jnp.max(jnp.where(shard_of == me, owner_of + 1, 0), axis=1) - 1

    def move(target, source, rows):
        to, frm = target[:, None], source[None, :]
        table = ((to // cap == frm[..., 0]) & (to % cap == frm[..., 1])).astype(jnp.bfloat16)
        return jnp.dot(table, rows, preferred_element_type=jnp.float32).astype(jnp.bfloat16)

    row = jnp.arange(members * cap, dtype=jnp.int32)
    from_block = jnp.stack([jnp.repeat(goes, cap), row % cap], axis=-1)
    sent = move(row, from_block, aligned).reshape(members, cap, feature)
    got = exchange(sent).reshape(members * cap, feature)
    takes = (jnp.repeat(comes, cap) * cap + row % cap)[:, None] == row[None, :]
    takes = (takes & (jnp.repeat(comes, cap) >= 0)[:, None]).astype(jnp.bfloat16)
    loaded_text = jnp.dot(takes, got, preferred_element_type=jnp.float32).astype(jnp.bfloat16)
    return loaded_images, loaded_text


def solution(mesh):
    split = P(("groups", "docs"))
    rows = P(("groups", "docs"), None)
    return jax.shard_map(
        shards,
        mesh=mesh,
        in_specs=(rows, P("groups"), rows, rows, split, rows),
        out_specs=(rows, rows),
        check_vma=False,
    )
```

time: 173 us -> 130 us (0.75)
  waiting for transfers between devices: 79.5 us -> 37.7 us
  blocking collectives: 0 us -> 35 us
  starting transfers between devices: 45.5 us -> 21.3 us
  Pallas kernels: 0 us -> 14.7 us
  matrix products: 18.8 us -> 7.3 us
  local copies, waits for them, and re-layouts: 18.1 us -> 10.1 us
  other arithmetic: 9.28 us -> 2.27 us
    all_to_all x7 -> x3, waiting for transfers between devices: 79.5 us -> 37.7 us  [exchange(): return lax.all_to_all(x, 'docs', split_axis=0, concat_axis=0, tiled=True)]
    all_gather x0 -> x1, blocking collectives: none -> 35 us  [shards(): every = lax.all_gather(packed, 'docs', axis=0, tiled=False)]
    all_to_all x7 -> x3, starting transfers between devices: 39.9 us -> 17 us  [exchange(): return lax.all_to_all(x, 'docs', split_axis=0, concat_axis=0, tiled=True)]
    pallas_call x0 -> x1, Pallas kernels: none -> 14.7 us  [attend(): pl.pallas_call(functools.partial(attend_kernel, feature ** (-0.5)), grid=...]
    dot_general x7 -> x5, matrix products: 18.8 us -> 7.3 us  [the longest x2 3.15 us: buckets(): jnp.dot(table, images, preferred_element_type=jnp.float32)]
    convert_element_type x2 -> x0, local copies, waits for them, and re-layouts: 2.88 us -> none  [the longest x1 1.44 us: shards(): text_fwd = jnp.einsum('sdj,sje->dje', route_weights, aligned, preferred_e...]
    sub x4 -> x0, local copies, waits for them, and re-layouts: 2.7 us -> none  [the longest x3 2.03 us: spread_values(): return jnp.sum(jnp.where(table, values[None, :] + 1, 0), axis=1) - 1]
    reduce_sum x5 -> x2, other arithmetic: 3.79 us -> 1.3 us  [the longest x1 0.94 us: shards(): rank = jnp.sum(earlier.astype(jnp.int32), axis=1)]
  transfers between devices with their start and end apart: 9 -> 5, of which waited for: 5 -> 2; matrix products, arithmetic and copies ran while one was open for 21% -> 7% of each run, Pallas kernels for 0% -> 11%
where the time goes in v1:
time: 130 us; the launch traced here: 129 us
  waiting for transfers between devices  37.7 us (29%)
  blocking collectives  35 us (27%)
  starting transfers between devices  21.3 us (16%)
  Pallas kernels  14.7 us (11%)
  local copies, waits for them, and re-layouts  10.1 us (8%)
  matrix products  7.3 us (6%)
  other arithmetic  2.27 us (2%)
    all_to_all x3, waiting for transfers between devices, exchange(): return lax.all_to_all(x, 'docs', split_axis=0, concat_axis=0, tiled=True)  37.7 us
    all_gather x1, blocking collectives, shards(): every = lax.all_gather(packed, 'docs', axis=0, tiled=False)  35 us
    all_to_all x3, starting transfers between devices, exchange(): return lax.all_to_all(x, 'docs', split_axis=0, concat_axis=0, tiled=True)  17 us
    pallas_call x1, Pallas kernels, attend(): pl.pallas_call(functools.partial(attend_kernel, feature ** (-0.5)), grid=...  14.7 us
    unnamed x7, local copies, waits for them, and re-layouts  4.96 us
    gather x2, local copies, waits for them, and re-layouts, shards(): docs = jnp.where(spots >= 0, sent_doc[me * own + jnp.maximum(spots, 0)], -2)  3.29 us
    dot_general x2, matrix products, buckets(): jnp.dot(table, images, preferred_element_type=jnp.float32)  3.15 us
  transfers between devices with their start and end apart: 5, of which 2 were waited for; matrix products, arithmetic and copies ran while one was open for 7% of the time, Pallas kernels for 11%

profile of v1, /device:TPU:14, one launch (start us, length us, event | category | flops | bytes accessed | tf_op | source)
XLA Modules:
  0.0 129.1 jit_solution(2915044528584830084)
XLA Ops:
  0.6 0.9 convert_reduce_fusion
  1.6 0.7 multiply_add_fusion.1
  2.3 1.6 %convolution_convert_fusion.2 = bf16[512,1280]{1,0:T(8,128)(2,1)} fusion(bf16[256,1280]{1,0:T(8,128)(2,1)S(1)} %copy-done, s32[256]{0:T(256)S(1)} %get-tuple-element.13), kind=kOutput, calls=%fused_computation.3 | convolution fusion | flops 336330752 | bytes 1967104 | tf_op jit(solution)/shard_map/dot_general | solution.py:86
  3.9 6.2 %all-to-all-start.1 = ((bf16[16,32,1280]{2,1,0:T(8,128)(2,1)}), bf16[16,32,1280]{2,1,0:T(8,128)(2,1)S(1)}, u32[]{:S(2)}, u32[]{:S(2)}) async-start(bf16[16,32,1280]{2,1,0:T(8,128)(2,1)} %bitcast.8), calls=%async_computation.1 | async-start | bytes 2621440 | tf_op jit(solution)/shard_map/all_to_all | solution.py:65
  10.1 0.9 fusion.29
  11.1 2.2 %collective-permute-start.1 = (bf16[32,1280]{1,0:T(8,128)(2,1)S(1)}, bf16[32,1280]{1,0:T(8,128)(2,1)S(1)}, u32[]{:S(2)}, u32[]{:S(2)}) collective-permute-start(bf16[32,1280]{1,0:T(8,128)(2,1)S(1)} %get-tuple-element.5), channel_id=1, source_target_pairs={{1,0},{2,1},{3,2},{4,3},{5,4},{6,5},{7,6},{8,7},{9,8},{10,9},{11,1... | collective-permute-start | bytes 245768 | tf_op jit(solution)/shard_map/ppermute | solution.py:18
  13.3 2.1 %collective-permute-start = (bf16[32,1280]{1,0:T(8,128)(2,1)S(1)}, bf16[32,1280]{1,0:T(8,128)(2,1)S(1)}, u32[]{:S(2)}, u32[]{:S(2)}) collective-permute-start(bf16[32,1280]{1,0:T(8,128)(2,1)S(1)} %get-tuple-element.6), channel_id=1, source_target_pairs={{0,1},{1,2},{2,3},{3,4},{4,5},{5,6},{6,7},{7,8},{8,9},{9,10},{10,1... | collective-permute-start | bytes 245768 | tf_op jit(solution)/shard_map/ppermute | solution.py:17
  15.4 35.0 %all-gather.1 = s32[16,1,256]{2,1,0:T(1,128)S(1)} all-gather(s32[1,1,256]{2,1,0:T(1,128)S(1)} %bitcast.68), channel_id=2, replica_groups=mesh['groups'=2,'docs'=16] {'docs'}, dimensions={0}, use_global_device_ids=true | all-gather | bytes 17408 | tf_op jit(solution)/shard_map/all_gather | solution.py:77
  50.4 0.2 select_reduce_fusion.2
  50.7 0.1 convolution_convert_fusion.4
  50.9 0.4 select_reduce_fusion
  51.2 1.6 %convolution_convert_fusion.3 = bf16[512,1280]{1,0:T(8,128)(2,1)} fusion(bf16[256,1280]{1,0:T(8,128)(2,1)S(1)} %copy-done, s32[256]{0:T(256)S(1)} %get-tuple-element.14), kind=kOutput, calls=%fused_computation.4 | convolution fusion | flops 336330752 | bytes 1967104 | tf_op jit(solution)/shard_map/dot_general | solution.py:86
  52.8 5.7 %all-to-all-start = ((bf16[16,32,1280]{2,1,0:T(8,128)(2,1)}), bf16[16,32,1280]{2,1,0:T(8,128)(2,1)}, u32[]{:S(2)}, u32[]{:S(2)}) async-start(bf16[16,32,1280]{2,1,0:T(8,128)(2,1)} %bitcast.62), calls=%async_computation | async-start | bytes 2621440 | tf_op jit(solution)/shard_map/all_to_all | solution.py:65
  58.6 3.1 %gather_fusion = s32[512]{0:T(512)S(1)} fusion(s32[32768]{0:T(1024)S(1)} %copy-done.2, s32[1024]{0:T(1024)S(1)} %pad_clamp_fusion), kind=kCustom, calls=%fused_computation | custom fusion | bytes 6144 | tf_op jit(solution)/shard_map/gather | solution.py:102
  61.8 0.3 ge.28
  62.1 0.1 copy.13
  62.4 2.5 %copy-done.1 = bf16[2048,1280]{1,0:T(8,128)(2,1)S(1)} copy-done((bf16[2048,1280]{1,0:T(8,128)(2,1)S(1)}, bf16[2048,1280]{1,0:T(8,128)(2,1)}, u32[]{:S(2)}) %copy-start.1) | copy-done | bytes 5242904
  64.9 14.7 %attend.1 = bf16[512,1280]{1,0:T(8,128)(2,1)S(1)} custom-call(bf16[512,1280]{1,0:T(8,128)(2,1)S(1)} %bitcast.60, s32[512,1]{1,0:T(8,128)S(1)} %broadcast_select_fusion.doc_ref, bf16[2048,1280]{1,0:T(8,128)(2,1)S(1)} %copy-done.1, bf16[32,1280]{1,0:T(8,128)(2,1)S(1)} %collective-permute-done.before_ref, ...), custom_call_target="tpu_custom_call" | custom-call | flops 5368709120 | bytes 7864320 | tf_op jit(solution)/shard_map/attend/pallas_call | solution.py:46
  79.6 2.0 %convolution_convert_fusion.1 = bf16[512,1280]{1,0:T(8,128)(2,1)} fusion(bf16[512,1280]{1,0:T(8,128)(2,1)S(1)} %attend.1, s32[512]{0:T(512)S(1)} %bitcast.70, s32[512]{0:T(512)S(1)} %bitcast.69, s32[512]{0:T(512)S(1)} %get-tuple-element.18, s32[512]{0:T(512)S(1)} %get-tuple-element.17), kind=kOutput, calls=%fused_computation.2 | convolution fusion | flops 672530432 | bytes 2629632 | tf_op jit(solution)/shard_map/dot_general | solution.py:115
  81.6 7.6 %all-to-all-done = bf16[16,32,1280]{2,1,0:T(8,128)(2,1)} async-done(((bf16[16,32,1280]{2,1,0:T(8,128)(2,1)}), bf16[16,32,1280]{2,1,0:T(8,128)(2,1)}, u32[]{:S(2)}, u32[]{:S(2)}) %all-to-all-start) | async-done | bytes 1310752 | tf_op jit(solution)/shard_map/all_to_all | solution.py:65
  89.2 5.1 %all-to-all-start.2 = ((bf16[16,32,1280]{2,1,0:T(8,128)(2,1)}), bf16[16,32,1280]{2,1,0:T(8,128)(2,1)S(1)}, u32[]{:S(2)}, u32[]{:S(2)}) async-start(bf16[16,32,1280]{2,1,0:T(8,128)(2,1)} %bitcast.15), calls=%async_computation.2 | async-start | bytes 2621440 | tf_op jit(solution)/shard_map/all_to_all | solution.py:65
  94.6 30.1 %all-to-all-done.2 = bf16[16,32,1280]{2,1,0:T(8,128)(2,1)S(1)} async-done(((bf16[16,32,1280]{2,1,0:T(8,128)(2,1)}), bf16[16,32,1280]{2,1,0:T(8,128)(2,1)S(1)}, u32[]{:S(2)}, u32[]{:S(2)}) %all-to-all-start.2) | async-done | bytes 1310752 | tf_op jit(solution)/shard_map/all_to_all | solution.py:65
  124.7 2.0 %convolution_convert_fusion = bf16[512,1280]{1,0:T(8,128)(2,1)} fusion(bf16[512,1280]{1,0:T(8,128)(2,1)S(1)} %bitcast.63, s32[512]{0:T(512)S(1)} %fusion.26, pred[512]{0:T(512)(128)(4,1)S(1)} %ge.25), kind=kOutput, calls=%fused_computation.1 | convolution fusion | flops 672268288 | bytes 2624000 | tf_op jit(solution)/shard_map/dot_general | solution.py:123
  126.7 2.5 %copy.37 = bf16[512,1280]{1,0:T(8,128)(2,1)} copy(bf16[512,1280]{1,0:T(8,128)(2,1)} %bitcast.3) | data formatting | bytes 2621440
  (29 shorter events, 0.8 us)
Async XLA Ops:
  0.6 1.7 %copy-start = (bf16[256,1280]{1,0:T(8,128)(2,1)S(1)}, bf16[256,1280]{1,0:T(8,128)(2,1)}, u32[]{:S(2)}) copy-start(bf16[256,1280]{1,0:T(8,128)(2,1)} %param.8) | copy-start | bytes 1966084
  3.9 48.9 %all-to-all-start.1 = ((bf16[16,32,1280]{2,1,0:T(8,128)(2,1)}), bf16[16,32,1280]{2,1,0:T(8,128)(2,1)S(1)}, u32[]{:S(2)}, u32[]{:S(2)}) async-start(bf16[16,32,1280]{2,1,0:T(8,128)(2,1)} %bitcast.8), calls=%async_computation.1 | async-start | bytes 2621440 | tf_op jit(solution)/shard_map/all_to_all | solution.py:65
  11.1 51.3 %collective-permute-start.1 = (bf16[32,1280]{1,0:T(8,128)(2,1)S(1)}, bf16[32,1280]{1,0:T(8,128)(2,1)S(1)}, u32[]{:S(2)}, u32[]{:S(2)}) collective-permute-start(bf16[32,1280]{1,0:T(8,128)(2,1)S(1)} %get-tuple-element.5), channel_id=1, source_target_pairs={{1,0},{2,1},{3,2},{4,3},{5,4},{6,5},{7,6},{8,7},{9,8},{10,9},{11,1... | collective-permute-start | bytes 245768 | tf_op jit(solution)/shard_map/ppermute | solution.py:18
  13.3 49.1 %collective-permute-start = (bf16[32,1280]{1,0:T(8,128)(2,1)S(1)}, bf16[32,1280]{1,0:T(8,128)(2,1)S(1)}, u32[]{:S(2)}, u32[]{:S(2)}) collective-permute-start(bf16[32,1280]{1,0:T(8,128)(2,1)S(1)} %get-tuple-element.6), channel_id=1, source_target_pairs={{0,1},{1,2},{2,3},{3,4},{4,5},{5,6},{6,7},{7,8},{8,9},{9,10},{10,1... | collective-permute-start | bytes 245768 | tf_op jit(solution)/shard_map/ppermute | solution.py:17
  52.8 5.8 %copy-start.2 = (s32[32768]{0:T(1024)S(1)}, s32[32768]{0:T(1024)}, u32[]{:S(2)}) copy-start(s32[32768]{0:T(1024)} %param.7) | copy-start | bytes 393220
  52.8 36.4 %all-to-all-start = ((bf16[16,32,1280]{2,1,0:T(8,128)(2,1)}), bf16[16,32,1280]{2,1,0:T(8,128)(2,1)}, u32[]{:S(2)}, u32[]{:S(2)}) async-start(bf16[16,32,1280]{2,1,0:T(8,128)(2,1)} %bitcast.62), calls=%async_computation | async-start | bytes 2621440 | tf_op jit(solution)/shard_map/all_to_all | solution.py:65
  62.4 2.5 %copy-start.1 = (bf16[2048,1280]{1,0:T(8,128)(2,1)S(1)}, bf16[2048,1280]{1,0:T(8,128)(2,1)}, u32[]{:S(2)}) copy-start(bf16[2048,1280]{1,0:T(8,128)(2,1)} %k_ref.1) | copy-start | bytes 15728644
  89.2 35.5 %all-to-all-start.2 = ((bf16[16,32,1280]{2,1,0:T(8,128)(2,1)}), bf16[16,32,1280]{2,1,0:T(8,128)(2,1)S(1)}, u32[]{:S(2)}, u32[]{:S(2)}) async-start(bf16[16,32,1280]{2,1,0:T(8,128)(2,1)} %bitcast.15), calls=%async_computation.2 | async-start | bytes 2621440 | tf_op jit(solution)/shard_map/all_to_all | solution.py:65

commit v2 on v1

--- a/solution.py
+++ b/solution.py
@@ -61,6 +61,38 @@
     )(queries, docs, *fixed)
 
 
+def every_device(row):
+    peers, me = lax.axis_size("docs"), lax.axis_index("docs")
+    if peers & (peers - 1):
+        return lax.all_gather(row, "docs", axis=0, tiled=False)
+    held, step = row[None], 1
+    while step < peers:
+        held = jnp.concatenate([held, lax.ppermute(held, "docs", [(i, i ^ step) for i in range(peers)])], axis=0)
+        step *= 2
+    label = jnp.arange(peers, dtype=jnp.int32)
+    pick = (label ^ me)[:, None] == label[None, :]
+    return jnp.sum(jnp.where(pick[:, :, None], held[None], 0), axis=1)
+
+
+def copy_kernel(x_ref, o_ref):
+    o_ref[...] = x_ref[...]
+
+
+def write_out(x):
+    rows, feature = x.shape
+    block = min(128, rows)
+    spec = pl.BlockSpec((block, feature), lambda i: (i, 0))
+    return pl.pallas_call(
+        copy_kernel,
+        grid=(rows // block,),
+        in_specs=[spec],
+        out_specs=spec,
+        out_shape=jax.ShapeDtypeStruct(x.shape, x.dtype),
+        cost_estimate=pl.CostEstimate(flops=0, bytes_accessed=4 * rows * feature, transcendentals=0),
+        name="write_out",
+    )(x)
+
+
 def exchange(x):
     return lax.all_to_all(x, "docs", split_axis=0, concat_axis=0, tiled=True)
 
@@ -74,7 +106,7 @@
     owner, shard = image_owner[:, 0], loader_shard[:, 0]
 
     packed = (owner * members + shard) * own + anchor
-    every = lax.all_gather(packed, "docs", axis=0, tiled=False)
+    every = every_device(packed)
 
     spot = jnp.arange(n, dtype=jnp.int32)
     earlier = (owner[:, None] == owner[None, :]) & (spot[None, :] < spot[:, None])
@@ -87,7 +119,7 @@
         return out.reshape(members, cap, feature)
 
     queries = exchange(buckets(owner)).reshape(members * cap, feature)
-    loaded_images = exchange(buckets(shard)).reshape(members * cap, feature)
+    loaded_images = write_out(exchange(buckets(shard)).reshape(members * cap, feature))
     before, after = halo_of(sentences)
 
     spot_of = every % own
@@ -109,14 +141,10 @@
     goes = jnp.max(jnp.where(mine, shard_of + 1, 0), axis=1) - 1
     comes = jnp.max(jnp.where(shard_of == me, owner_of + 1, 0), axis=1) - 1
 
-    def move(target, source, rows):
-        to, frm = target[:, None], source[None, :]
-        table = ((to // cap == frm[..., 0]) & (to % cap == frm[..., 1])).astype(jnp.bfloat16)
-        return jnp.dot(table, rows, preferred_element_type=jnp.float32).astype(jnp.bfloat16)
-
     row = jnp.arange(members * cap, dtype=jnp.int32)
-    from_block = jnp.stack([jnp.repeat(goes, cap), row % cap], axis=-1)
-    sent = move(row, from_block, aligned).reshape(members, cap, feature)
+    puts = row[:, None] == (jnp.repeat(goes, cap) * cap + row % cap)[None, :]
+    puts = (puts & (jnp.repeat(goes, cap) >= 0)[None, :]).astype(jnp.bfloat16)
+    sent = jnp.dot(puts, aligned, preferred_element_type=jnp.float32).astype(jnp.bfloat16).reshape(members, cap, feature)
     got = exchange(sent).reshape(members * cap, feature)
     takes = (jnp.repeat(comes, cap) * cap + row % cap)[:, None] == row[None, :]
     takes = (takes & (jnp.repeat(comes, cap) >= 0)[:, None]).astype(jnp.bfloat16)

time: 130 us -> 117 us (0.900)
  blocking collectives: 35 us -> 0 us
  waiting for transfers between devices: 37.7 us -> 53.5 us
  starting transfers between devices: 21.3 us -> 26.4 us
  Pallas kernels: 14.7 us -> 18 us
  local copies, waits for them, and re-layouts: 10.1 us -> 7.82 us
    all_gather x1 -> x0, blocking collectives: 35 us -> none  [shards(): every = lax.all_gather(packed, 'docs', axis=0, tiled=False)]
    ppermute x0 -> x4, waiting for transfers between devices: none -> 19.4 us  [every_device(): lax.ppermute(held, 'docs', [(i, i ^ step) for i in range(peers)])]
    all_to_all x3, waiting for transfers between devices: 37.7 us -> 34.1 us  [exchange(): return lax.all_to_all(x, 'docs', split_axis=0, concat_axis=0, tiled=True)]
    pallas_call x0 -> x1, Pallas kernels: none -> 3.46 us  [write_out(): pl.pallas_call(copy_kernel, grid=(rows // block,), in_specs=[spec], out_s...]
    ppermute x0 -> x4, starting transfers between devices: none -> 3.23 us  [every_device(): lax.ppermute(held, 'docs', [(i, i ^ step) for i in range(peers)])]
    unnamed x7 -> x6, local copies, waits for them, and re-layouts: 4.96 us -> 2.5 us
    all_to_all x3, starting transfers between devices: 17 us -> 18.8 us  [exchange(): return lax.all_to_all(x, 'docs', split_axis=0, concat_axis=0, tiled=True)]
  transfers between devices with their start and end apart: 5 -> 9, of which waited for: 2 -> 6; matrix products, arithmetic and copies ran while one was open for 7% -> 8% of each run, Pallas kernels for 11% -> 15%
where the time goes in v2:
time: 117 us; the launch traced here: 116 us
  waiting for transfers between devices  53.5 us (46%)
  starting transfers between devices  26.4 us (23%)
  Pallas kernels  18 us (15%)
  local copies, waits for them, and re-layouts  7.82 us (7%)
  matrix products  7.25 us (6%)
  other arithmetic  2.48 us (2%)
    all_to_all x3, waiting for transfers between devices, exchange(): return lax.all_to_all(x, 'docs', split_axis=0, concat_axis=0, tiled=True)  34.1 us
    ppermute x4, waiting for transfers between devices, every_device(): lax.ppermute(held, 'docs', [(i, i ^ step) for i in range(peers)])  19.4 us
    all_to_all x3, starting transfers between devices, exchange(): return lax.all_to_all(x, 'docs', split_axis=0, concat_axis=0, tiled=True)  18.8 us
    pallas_call x1, Pallas kernels, attend(): pl.pallas_call(functools.partial(attend_kernel, feature ** (-0.5)), grid=...  14.5 us
    pallas_call x1, Pallas kernels, write_out(): pl.pallas_call(copy_kernel, grid=(rows // block,), in_specs=[spec], out_s...  3.46 us
    gather x2, local copies, waits for them, and re-layouts, shards(): docs = jnp.where(spots >= 0, sent_doc[me * own + jnp.maximum(spots, 0)], -2)  3.28 us
    ppermute x4, starting transfers between devices, every_device(): lax.ppermute(held, 'docs', [(i, i ^ step) for i in range(peers)])  3.23 us
    dot_general x2, matrix products, buckets(): jnp.dot(table, images, preferred_element_type=jnp.float32)  3.15 us
  transfers between devices with their start and end apart: 9, of which 6 were waited for; matrix products, arithmetic and copies ran while one was open for 8% of the time, Pallas kernels for 15%

profile of v2, /device:TPU:14, one launch (start us, length us, event | category | flops | bytes accessed | tf_op | source)
XLA Modules:
  0.0 116.2 jit_solution(10192717541864649693)
XLA Ops:
  0.6 0.9 convert_reduce_fusion
  1.6 0.7 multiply_add_fusion.1
  2.3 1.6 %convolution_convert_fusion.2 = bf16[512,1280]{1,0:T(8,128)(2,1)} fusion(bf16[256,1280]{1,0:T(8,128)(2,1)S(1)} %copy-done, s32[256]{0:T(256)S(1)} %get-tuple-element.11), kind=kOutput, calls=%fused_computation.3 | convolution fusion | flops 336330752 | bytes 1967104 | tf_op jit(solution)/shard_map/dot_general | solution.py:118
  3.9 6.2 %all-to-all-start.1 = ((bf16[16,32,1280]{2,1,0:T(8,128)(2,1)}), bf16[16,32,1280]{2,1,0:T(8,128)(2,1)S(1)}, u32[]{:S(2)}, u32[]{:S(2)}) async-start(bf16[16,32,1280]{2,1,0:T(8,128)(2,1)} %bitcast.24), calls=%async_computation.1 | async-start | bytes 2621440 | tf_op jit(solution)/shard_map/all_to_all | solution.py:97
  10.3 0.9 fusion.24
  11.3 2.4 %collective-permute-start.5 = (bf16[32,1280]{1,0:T(8,128)(2,1)S(1)}, bf16[32,1280]{1,0:T(8,128)(2,1)S(1)}, u32[]{:S(2)}, u32[]{:S(2)}) collective-permute-start(bf16[32,1280]{1,0:T(8,128)(2,1)S(1)} %get-tuple-element.5), channel_id=1, source_target_pairs={{1,0},{2,1},{3,2},{4,3},{5,4},{6,5},{7,6},{8,7},{9,8},{10,9},{11,1... | collective-permute-start | bytes 245768 | tf_op jit(solution)/shard_map/ppermute | solution.py:18
  13.7 1.9 %collective-permute-start.4 = (bf16[32,1280]{1,0:T(8,128)(2,1)S(1)}, bf16[32,1280]{1,0:T(8,128)(2,1)S(1)}, u32[]{:S(2)}, u32[]{:S(2)}) collective-permute-start(bf16[32,1280]{1,0:T(8,128)(2,1)S(1)} %get-tuple-element.6), channel_id=1, source_target_pairs={{0,1},{1,2},{2,3},{3,4},{4,5},{5,6},{6,7},{7,8},{8,9},{9,10},{10,1... | collective-permute-start | bytes 245768 | tf_op jit(solution)/shard_map/ppermute | solution.py:17
  15.7 1.6 %convolution_convert_fusion.3 = bf16[512,1280]{1,0:T(8,128)(2,1)} fusion(bf16[256,1280]{1,0:T(8,128)(2,1)S(1)} %copy-done, s32[256]{0:T(256)S(1)} %get-tuple-element.12), kind=kOutput, calls=%fused_computation.4 | convolution fusion | flops 336330752 | bytes 1967104 | tf_op jit(solution)/shard_map/dot_general | solution.py:118
  17.2 1.5 %collective-permute-start.1 = (s32[2,256]{1,0:T(2,128)S(1)}, s32[2,256]{1,0:T(2,128)S(1)}, u32[]{:S(2)}, u32[]{:S(2)}) collective-permute-start(s32[2,256]{1,0:T(2,128)S(1)} %pad_add_fusion.2), channel_id=1, source_target_pairs={{0,2},{1,3},{2,0},{3,1},{4,6},{5,7},{6,4},{7,5},{8,10},{9,11},{10,... | collective-permute-start | bytes 6152 | tf_op jit(solution)/shard_map/ppermute | solution.py:70
  18.8 2.3 %collective-permute-done.1 = s32[2,256]{1,0:T(2,128)S(1)} collective-permute-done((s32[2,256]{1,0:T(2,128)S(1)}, s32[2,256]{1,0:T(2,128)S(1)}, u32[]{:S(2)}, u32[]{:S(2)}) %collective-permute-start.1) | collective-permute-done | bytes 2080 | tf_op jit(solution)/shard_map/ppermute | solution.py:70
  21.1 0.4 collective-permute-start.2
  21.6 12.0 %collective-permute-done.2 = s32[4,256]{1,0:T(4,128)S(1)} collective-permute-done((s32[4,256]{1,0:T(4,128)S(1)}, s32[4,256]{1,0:T(4,128)S(1)}, u32[]{:S(2)}, u32[]{:S(2)}) %collective-permute-start.2) | collective-permute-done | bytes 4128 | tf_op jit(solution)/shard_map/ppermute | solution.py:70
  33.7 1.1 collective-permute-start.3
  34.8 5.0 %collective-permute-done.3 = s32[8,256]{1,0:T(8,128)S(1)} collective-permute-done((s32[8,256]{1,0:T(8,128)S(1)}, s32[8,256]{1,0:T(8,128)S(1)}, u32[]{:S(2)}, u32[]{:S(2)}) %collective-permute-start.3) | collective-permute-done | bytes 8224 | tf_op jit(solution)/shard_map/ppermute | solution.py:70
  40.7 7.6 %all-to-all-start = ((bf16[16,32,1280]{2,1,0:T(8,128)(2,1)}), bf16[16,32,1280]{2,1,0:T(8,128)(2,1)}, u32[]{:S(2)}, u32[]{:S(2)}) async-start(bf16[16,32,1280]{2,1,0:T(8,128)(2,1)} %bitcast.23), calls=%async_computation | async-start | bytes 2621440 | tf_op jit(solution)/shard_map/all_to_all | solution.py:97
  48.9 3.1 %gather_fusion = s32[512]{0:T(512)S(1)} fusion(s32[32768]{0:T(1024)S(1)} %copy-done.2, s32[1024]{0:T(1024)S(1)} %pad_clamp_fusion), kind=kCustom, calls=%fused_computation | custom fusion | bytes 6144 | tf_op jit(solution)/shard_map/gather | solution.py:134
  52.8 2.5 %copy-done.1 = bf16[2048,1280]{1,0:T(8,128)(2,1)S(1)} copy-done((bf16[2048,1280]{1,0:T(8,128)(2,1)S(1)}, bf16[2048,1280]{1,0:T(8,128)(2,1)}, u32[]{:S(2)}) %copy-start.1) | copy-done | bytes 5242904
  55.3 14.5 %attend.1 = bf16[512,1280]{1,0:T(8,128)(2,1)S(1)} custom-call(bf16[512,1280]{1,0:T(8,128)(2,1)S(1)} %bitcast.21, s32[512,1]{1,0:T(8,128)S(1)} %broadcast_select_fusion.doc_ref, bf16[2048,1280]{1,0:T(8,128)(2,1)S(1)} %copy-done.1, bf16[32,1280]{1,0:T(8,128)(2,1)S(1)} %collective-permute-done.4.before_ref, ...), custom_call_target="tpu_custom_call" | custom-call | flops 5368709120 | bytes 7864320 | tf_op jit(solution)/shard_map/attend/pallas_call | solution.py:46
  69.8 2.0 %convolution_convert_fusion.1 = bf16[512,1280]{1,0:T(8,128)(2,1)} fusion(bf16[512,1280]{1,0:T(8,128)(2,1)S(1)} %attend.1, s32[512]{0:T(512)S(1)} %fusion.19, pred[512]{0:T(512)(128)(4,1)S(1)} %ge.38), kind=kOutput, calls=%fused_computation.2 | convolution fusion | flops 672268288 | bytes 2624000 | tf_op jit(solution)/shard_map/dot_general | solution.py:147
  71.8 7.1 %all-to-all-done = bf16[16,32,1280]{2,1,0:T(8,128)(2,1)} async-done(((bf16[16,32,1280]{2,1,0:T(8,128)(2,1)}), bf16[16,32,1280]{2,1,0:T(8,128)(2,1)}, u32[]{:S(2)}, u32[]{:S(2)}) %all-to-all-start) | async-done | bytes 1310752 | tf_op jit(solution)/shard_map/all_to_all | solution.py:97
  78.8 5.0 %all-to-all-start.2 = ((bf16[16,32,1280]{2,1,0:T(8,128)(2,1)}), bf16[16,32,1280]{2,1,0:T(8,128)(2,1)S(1)}, u32[]{:S(2)}, u32[]{:S(2)}) async-start(bf16[16,32,1280]{2,1,0:T(8,128)(2,1)} %bitcast.12), calls=%async_computation.2 | async-start | bytes 2621440 | tf_op jit(solution)/shard_map/all_to_all | solution.py:97
  84.1 3.5 %write_out.1 = bf16[512,1280]{1,0:T(8,128)(2,1)} custom-call(bf16[512,1280]{1,0:T(8,128)(2,1)} %bitcast.3.x_ref), custom_call_target="tpu_custom_call" | custom-call | bytes 2621440 | tf_op jit(solution)/shard_map/write_out/pallas_call | solution.py:85
  87.6 26.6 %all-to-all-done.2 = bf16[16,32,1280]{2,1,0:T(8,128)(2,1)S(1)} async-done(((bf16[16,32,1280]{2,1,0:T(8,128)(2,1)}), bf16[16,32,1280]{2,1,0:T(8,128)(2,1)S(1)}, u32[]{:S(2)}, u32[]{:S(2)}) %all-to-all-start.2) | async-done | bytes 1310752 | tf_op jit(solution)/shard_map/all_to_all | solution.py:97
  114.2 2.0 %convolution_convert_fusion = bf16[512,1280]{1,0:T(8,128)(2,1)} fusion(bf16[512,1280]{1,0:T(8,128)(2,1)S(1)} %bitcast.25, s32[512]{0:T(512)S(1)} %fusion.20, pred[512]{0:T(512)(128)(4,1)S(1)} %ge.36), kind=kOutput, calls=%fused_computation.1 | convolution fusion | flops 672268288 | bytes 2624000 | tf_op jit(solution)/shard_map/dot_general | solution.py:151
  (42 shorter events, 2.9 us)
Async XLA Ops:
  0.6 1.7 %copy-start = (bf16[256,1280]{1,0:T(8,128)(2,1)S(1)}, bf16[256,1280]{1,0:T(8,128)(2,1)}, u32[]{:S(2)}) copy-start(bf16[256,1280]{1,0:T(8,128)(2,1)} %param.8) | copy-start | bytes 1966084
  3.9 36.8 %all-to-all-start.1 = ((bf16[16,32,1280]{2,1,0:T(8,128)(2,1)}), bf16[16,32,1280]{2,1,0:T(8,128)(2,1)S(1)}, u32[]{:S(2)}, u32[]{:S(2)}) async-start(bf16[16,32,1280]{2,1,0:T(8,128)(2,1)} %bitcast.24), calls=%async_computation.1 | async-start | bytes 2621440 | tf_op jit(solution)/shard_map/all_to_all | solution.py:97
  10.1 24.6 %copy-start.2 = (s32[32768]{0:T(1024)S(1)}, s32[32768]{0:T(1024)}, u32[]{:S(2)}) copy-start(s32[32768]{0:T(1024)} %param.7) | copy-start | bytes 393220
  10.1 7.1 %collective-permute-start = (s32[1,256]{1,0:T(1,128)S(1)}, s32[1,256]{1,0:T(1,128)S(1)}, u32[]{:S(2)}, u32[]{:S(2)}) collective-permute-start(s32[1,256]{1,0:T(1,128)S(1)} %bitcast.26), channel_id=1, source_target_pairs={{0,1},{1,0},{2,3},{3,2},{4,5},{5,4},{6,7},{7,6},{8,9},{9,8},{10,11... | collective-permute-start | bytes 3080 | tf_op jit(solution)/shard_map/ppermute | solution.py:70
  11.3 41.5 %collective-permute-start.5 = (bf16[32,1280]{1,0:T(8,128)(2,1)S(1)}, bf16[32,1280]{1,0:T(8,128)(2,1)S(1)}, u32[]{:S(2)}, u32[]{:S(2)}) collective-permute-start(bf16[32,1280]{1,0:T(8,128)(2,1)S(1)} %get-tuple-element.5), channel_id=1, source_target_pairs={{1,0},{2,1},{3,2},{4,3},{5,4},{6,5},{7,6},{8,7},{9,8},{10,9},{11,1... | collective-permute-start | bytes 245768 | tf_op jit(solution)/shard_map/ppermute | solution.py:18
  13.7 39.0 %collective-permute-start.4 = (bf16[32,1280]{1,0:T(8,128)(2,1)S(1)}, bf16[32,1280]{1,0:T(8,128)(2,1)S(1)}, u32[]{:S(2)}, u32[]{:S(2)}) collective-permute-start(bf16[32,1280]{1,0:T(8,128)(2,1)S(1)} %get-tuple-element.6), channel_id=1, source_target_pairs={{0,1},{1,2},{2,3},{3,4},{4,5},{5,6},{6,7},{7,8},{8,9},{9,10},{10,1... | collective-permute-start | bytes 245768 | tf_op jit(solution)/shard_map/ppermute | solution.py:17
  17.2 3.8 %collective-permute-start.1 = (s32[2,256]{1,0:T(2,128)S(1)}, s32[2,256]{1,0:T(2,128)S(1)}, u32[]{:S(2)}, u32[]{:S(2)}) collective-permute-start(s32[2,256]{1,0:T(2,128)S(1)} %pad_add_fusion.2), channel_id=1, source_target_pairs={{0,2},{1,3},{2,0},{3,1},{4,6},{5,7},{6,4},{7,5},{8,10},{9,11},{10,... | collective-permute-start | bytes 6152 | tf_op jit(solution)/shard_map/ppermute | solution.py:70
  21.1 12.5 %collective-permute-start.2 = (s32[4,256]{1,0:T(4,128)S(1)}, s32[4,256]{1,0:T(4,128)S(1)}, u32[]{:S(2)}, u32[]{:S(2)}) collective-permute-start(s32[4,256]{1,0:T(4,128)S(1)} %pad_add_fusion.1), channel_id=1, source_target_pairs={{0,4},{1,5},{2,6},{3,7},{4,0},{5,1},{6,2},{7,3},{8,12},{9,13},{10,... | collective-permute-start | bytes 12296 | tf_op jit(solution)/shard_map/ppermute | solution.py:70
  33.7 6.2 %collective-permute-start.3 = (s32[8,256]{1,0:T(8,128)S(1)}, s32[8,256]{1,0:T(8,128)S(1)}, u32[]{:S(2)}, u32[]{:S(2)}) collective-permute-start(s32[8,256]{1,0:T(8,128)S(1)} %pad_add_fusion), channel_id=1, source_target_pairs={{0,8},{1,9},{2,10},{3,11},{4,12},{5,13},{6,14},{7,15},{8,0},{9,1},... | collective-permute-start | bytes 24584 | tf_op jit(solution)/shard_map/ppermute | solution.py:70
  40.7 38.1 %all-to-all-start = ((bf16[16,32,1280]{2,1,0:T(8,128)(2,1)}), bf16[16,32,1280]{2,1,0:T(8,128)(2,1)}, u32[]{:S(2)}, u32[]{:S(2)}) async-start(bf16[16,32,1280]{2,1,0:T(8,128)(2,1)} %bitcast.23), calls=%async_computation | async-start | bytes 2621440 | tf_op jit(solution)/shard_map/all_to_all | solution.py:97
  52.8 2.5 %copy-start.1 = (bf16[2048,1280]{1,0:T(8,128)(2,1)S(1)}, bf16[2048,1280]{1,0:T(8,128)(2,1)}, u32[]{:S(2)}) copy-start(bf16[2048,1280]{1,0:T(8,128)(2,1)} %k_ref.1) | copy-start | bytes 15728644
  78.8 35.4 %all-to-all-start.2 = ((bf16[16,32,1280]{2,1,0:T(8,128)(2,1)}), bf16[16,32,1280]{2,1,0:T(8,128)(2,1)S(1)}, u32[]{:S(2)}, u32[]{:S(2)}) async-start(bf16[16,32,1280]{2,1,0:T(8,128)(2,1)} %bitcast.12), calls=%async_computation.2 | async-start | bytes 2621440 | tf_op jit(solution)/shard_map/all_to_all | solution.py:97

commit v3 on v1

v3 whole, which is shorter than its diff:
```python
import functools

import jax
import jax.numpy as jnp
from jax import lax
from jax.experimental import pallas as pl
from jax.experimental.pallas import tpu as pltpu
from jax.sharding import PartitionSpec as P

MOST_SENT = 32
TILE = 16


def halo_of(sentences):
    peers = lax.axis_size("docs")
    up = [(i, i + 1) for i in range(peers - 1)]
    down = [(j, i) for i, j in up]
    before = lax.ppermute(sentences[-MOST_SENT:], "docs", up)
    after = lax.ppermute(sentences[:MOST_SENT], "docs", down)
    return before, after


def every_device(row, order):
    peers, me = lax.axis_size("docs"), lax.axis_index("docs")
    half = peers // 2
    if peers & (peers - 1):
        held = lax.all_gather(row, "docs", axis=0, tiled=False)
        mirror = lax.ppermute(row, "docs", [(i, (i + half) % peers) for i in range(peers)])
        source = jnp.arange(peers, dtype=jnp.int32)
    else:
        held, apart, step = row[None], [0], half
        while step:
            held = jnp.concatenate([held, lax.ppermute(held, "docs", [(i, i ^ step) for i in range(peers)])], axis=0)
            apart += [a ^ step for a in apart]
            mirror = held[1] if step == half else mirror
            step //= 2
        source = jnp.array(apart, jnp.int32) ^ me
    pick = order[:, None] == source[None, :]
    return jnp.sum(jnp.where(pick[:, :, None], held[None], 0), axis=1), mirror


def one_hot_dot(table, rows):
    return jnp.dot(table.astype(jnp.bfloat16), rows, preferred_element_type=jnp.float32).astype(jnp.bfloat16)


class Arriving:
    def __init__(self, source, held, sems):
        length = source.shape[0] // sems.shape[0]
        self.spans = [pl.ds(i * length, length) for i in range(sems.shape[0])]
        self.held = held
        self.copies = [pltpu.make_async_copy(source.at[s], held.at[s], sems.at[i]) for i, s in enumerate(self.spans)]
        for c in self.copies:
            c.start()

    def parts(self, ids):
        return [(self.held.at[s], ids.at[:, s], c.wait) for s, c in zip(self.spans, self.copies)]


def softmax_rows(temper, q, doc, parts):
    scores = []
    for rows, ids, ready in parts:
        ready()
        s = lax.dot_general(q, rows[...], (((1,), (1,)), ((), ())), preferred_element_type=jnp.float32) * temper
        scores.append(jnp.where(doc == ids[...], s, -1e30))
    peak = functools.reduce(jnp.maximum, [jnp.max(s, axis=1, keepdims=True) for s in scores])
    raised = [jnp.where(doc == ids[...], jnp.exp(s - peak), 0.0) for s, (_, ids, _) in zip(scores, parts)]
    total = sum(jnp.sum(r, axis=1, keepdims=True) for r in raised)
    total = jnp.where(total > 0.0, total, 1.0)
    return sum(
        jnp.dot((r / total).astype(jnp.bfloat16), rows[...], preferred_element_type=jnp.float32)
        for r, (rows, _, _) in zip(raised, parts)
    ).astype(jnp.bfloat16)


def attended(temper, count, q_ref, doc_ref, k, before_ref, after_ref, id_ref, id_before_ref, id_after_ref):
    q = q_ref[:, :count].reshape(doc_ref.shape[0], -1)
    here = lambda: None
    parts = [*k.parts(id_ref), (before_ref, id_before_ref, here), (after_ref, id_after_ref, here)]
    return softmax_rows(temper, q, doc_ref[...], parts)


def attend_kernel(temper, count, q_ref, doc_ref, k_ref, *rest):
    *known, o_ref, held, k_sem = rest
    k = Arriving(k_ref, held, k_sem)
    o_ref[...] = attended(temper, count, q_ref, doc_ref, k, *known)


def attend_route_kernel(temper, count, goes_ref, taken_ref, q_ref, doc_ref, k_ref, *rest):
    *known, own_ref, o_ref, held, out, zero, k_sem, own_sem, out_sem, zero_sem = rest
    half, members = q_ref.shape[0], o_ref.shape[0]
    k = Arriving(k_ref, held, k_sem)
    zero[...] = jnp.zeros_like(zero)
    block = lambda j: pl.ds(j * count, count)
    place = lambda j: jnp.maximum(goes_ref[j], 0)
    owns = [pltpu.make_async_copy(own_ref.at[block(j)], o_ref.at[place(j)], own_sem.at[j]) for j in range(half)]
    outs = [pltpu.make_async_copy(out.at[block(j)], o_ref.at[place(half + j)], out_sem.at[j]) for j in range(half)]
    zeros = [pltpu.make_async_copy(zero, o_ref.at[d], zero_sem.at[d]) for d in range(members)]
    for j in range(half):
        pl.when(goes_ref[j] >= 0)(owns[j].start)
    for d in range(members):
        pl.when(taken_ref[d] < 0)(zeros[d].start)
    out[...] = attended(temper, count, q_ref, doc_ref, k, *known)
    for j in range(half):
        pl.when(goes_ref[half + j] >= 0)(outs[j].start)
    for j in range(half):
        pl.when(goes_ref[j] >= 0)(owns[j].wait)
    for d in range(members):
        pl.when(taken_ref[d] < 0)(zeros[d].wait)
    for j in range(half):
        pl.when(goes_ref[half + j] >= 0)(outs[j].wait)


VMEM, SMEM, ANY, HBM = (pl.BlockSpec(memory_space=m) for m in (pltpu.VMEM, pltpu.SMEM, pl.ANY, pltpu.HBM))


def attend(queries, cap, docs, known, own=None, goes=None):
    blocks, _, feature = queries.shape
    rows = blocks * cap
    if cap % TILE:
        queries = queries[:, :cap].reshape(1, rows, feature)
    routed = own is not None and cap % TILE == 0
    count = queries.shape[1] if cap % TILE else cap
    length = known[0].shape[0]
    chunks = 4
    args = (queries, docs[:, None], *known)
    specs = [VMEM, VMEM, HBM] + [VMEM] * (len(known) - 1)
    held, dma = pltpu.VMEM((length, feature), jnp.bfloat16), pltpu.SemaphoreType.DMA
    if routed:
        taken = jnp.max(jnp.where(goes[None, :] == jnp.arange(2 * blocks)[:, None], 1, -1), axis=1)
        args, specs = (goes, taken, *args, own), [SMEM, SMEM, *specs, ANY]
        shape = (2 * blocks, cap, feature)
        scratch = [
            held,
            pltpu.VMEM((rows, feature), jnp.bfloat16),
            pltpu.VMEM((cap, feature), jnp.bfloat16),
            dma((chunks,)),
            dma((blocks,)),
            dma((blocks,)),
            dma((2 * blocks,)),
        ]
    else:
        shape = (rows, feature)
        scratch = [held, dma((chunks,))]
    out = pl.pallas_call(
        functools.partial(attend_route_kernel if routed else attend_kernel, feature**-0.5, count),
        in_specs=specs,
        out_specs=HBM if routed else pl.BlockSpec(),
        out_shape=jax.ShapeDtypeStruct(shape, jnp.bfloat16),
        scratch_shapes=scratch,
        compiler_params=pltpu.CompilerParams(vmem_limit_bytes=59 * 1024 * 1024),
        cost_estimate=pl.CostEstimate(
            flops=4 * rows * length * feature, bytes_accessed=2 * (length + 2 * rows) * feature, transcendentals=rows * length
        ),
        name="attend_route" if routed else "attend",
    )(*args)
    if own is None or routed:
        return out
    both = jnp.concatenate([own, out])
    row = jnp.arange(2 * rows, dtype=jnp.int32)
    block = jnp.repeat(goes, cap)
    puts = (row[:, None] == (block * cap + row % cap)[None, :]) & (block >= 0)[None, :]
    return one_hot_dot(puts, both).reshape(2 * blocks, cap, feature)


def place_kernel(comes_ref, x_ref, o_ref, zero, sem):
    zero[...] = jnp.zeros_like(zero)
    members = x_ref.shape[0]
    moves = [pltpu.make_async_copy(x_ref.at[jnp.maximum(comes_ref[d], 0)], o_ref.at[d], sem.at[d]) for d in range(members)]
    clears = [pltpu.make_async_copy(zero, o_ref.at[d], sem.at[d]) for d in range(members)]
    for d in range(members):
        pl.when(comes_ref[d] >= 0)(moves[d].start)
        pl.when(comes_ref[d] < 0)(clears[d].start)
    for d in range(members):
        pl.when(comes_ref[d] >= 0)(moves[d].wait)
        pl.when(comes_ref[d] < 0)(clears[d].wait)


def place(x, comes):
    members, cap, feature = x.shape
    if cap % TILE:
        row = jnp.arange(members * cap, dtype=jnp.int32)
        block = jnp.repeat(comes, cap)
        takes = ((block * cap + row % cap)[:, None] == row[None, :]) & (block >= 0)[:, None]
        return one_hot_dot(takes, x.reshape(members * cap, feature))
    return pl.pallas_call(
        place_kernel,
        in_specs=[SMEM, ANY],
        out_specs=ANY,
        out_shape=jax.ShapeDtypeStruct(x.shape, x.dtype),
        scratch_shapes=[pltpu.VMEM((cap, feature), x.dtype), pltpu.SemaphoreType.DMA((members,))],
        cost_estimate=pl.CostEstimate(flops=0, bytes_accessed=4 * x.size, transcendentals=0),
        name="place",
    )(comes, x).reshape(members * cap, feature)


def shards(sentences, sent_doc, images, image_owner, anchor, loader_shard):
    members = lax.axis_size("docs")
    me = lax.axis_index("docs")
    own, feature = sentences.shape
    n = images.shape[0]
    cap = max(4, 2 * n // members)
    half = members // 2
    first = me // half * half
    halves = [list(range(half)), list(range(half, members))]

    mirrored = lax.ppermute(images, "docs", [(i, (i + half) % members) for i in range(members)])
    packed = (image_owner[:, 0] * members + loader_shard[:, 0]) * own + anchor
    order = (first + jnp.arange(members, dtype=jnp.int32)) % members
    every, packed_mirror = every_device(packed, order)
    before, after = halo_of(sentences)

    spot = jnp.arange(n, dtype=jnp.int32)

    def deal(rows, codes):
        owner, shard = codes // (own * members), codes // own % members
        earlier = (owner[:, None] == owner[None, :]) & (spot[None, :] < spot[:, None])
        rank = jnp.sum(earlier.astype(jnp.int32), axis=1)
        slot = jnp.arange(half * 2 * cap, dtype=jnp.int32)[:, None]
        owned = (owner - first) * (2 * cap) + rank
        loads = (shard - first) * (2 * cap) + cap + rank
        table = (slot == owned[None, :]) & (owner // half * half == first)[None, :]
        table |= (slot == loads[None, :]) & (shard // half * half == first)[None, :]
        out = one_hot_dot(table, rows).reshape(half, 2 * cap, feature)
        return lax.all_to_all(out, "docs", split_axis=0, concat_axis=0, tiled=True, axis_index_groups=halves)

    near = deal(images, packed)
    far = deal(mirrored, packed_mirror)

    spot_of, shard_of, owner_of = every % own, every // own % members, every // (own * members)
    mine = owner_of == me
    sooner = (spot[:, None] < spot[None, :]).astype(jnp.bfloat16)
    ranks = jnp.dot(mine.astype(jnp.bfloat16), sooner, preferred_element_type=jnp.float32).astype(jnp.int32)
    slots = jnp.arange(cap, dtype=jnp.int32)
    hit = mine[:, None, :] & (ranks[:, None, :] == slots[None, :, None])
    spots = jnp.sum(jnp.where(hit, spot_of[:, None, :] + 1, 0), axis=2).reshape(members * cap) - 1
    docs = jnp.where(spots >= 0, sent_doc[me * own + jnp.maximum(spots, 0)], -2)
    ids = lax.dynamic_slice_in_dim(sent_doc, me * own, own)
    padded = jnp.pad(sent_doc, (MOST_SENT, MOST_SENT), constant_values=-1)
    id_before = lax.dynamic_slice_in_dim(padded, me * own, MOST_SENT)
    id_after = lax.dynamic_slice_in_dim(padded, me * own + own + MOST_SENT, MOST_SENT)
    known = (sentences, before, after, ids[None], id_before[None], id_after[None])

    goes = jnp.max(jnp.where(mine, shard_of + 1, 0), axis=1) - 1
    comes = jnp.roll(jnp.max(jnp.where(shard_of == me, owner_of + 1, 0), axis=1) - 1, first)

    aligned_near = attend(near, cap, docs[: half * cap], known)
    sent = attend(far, cap, docs[half * cap :], known, aligned_near, goes)
    got = lax.all_to_all(sent, "docs", split_axis=0, concat_axis=0, tiled=True)

    low = first == 0
    near_images, far_images = near[:, cap:], far[:, cap:]
    loaded_images = jnp.concatenate(
        [jnp.where(low, near_images, far_images), jnp.where(low, far_images, near_images)]
    ).reshape(members * cap, feature)
    loaded_text = place(got, comes)
    return loaded_images, loaded_text


def solution(mesh):
    split = P(("groups", "docs"))
    rows = P(("groups", "docs"), None)
    return jax.shard_map(
        shards,
        mesh=mesh,
        in_specs=(rows, P("groups"), rows, rows, split, rows),
        out_specs=(rows, rows),
        check_vma=False,
    )
```

time: 130 us -> 164 us (1.26)
  Pallas kernels: 14.7 us -> 63.6 us
  blocking collectives: 35 us -> 0 us
  waiting for transfers between devices: 37.7 us -> 51.1 us
  starting transfers between devices: 21.3 us -> 26.6 us
  other arithmetic: 2.27 us -> 5.73 us
  matrix products: 7.3 us -> 4.52 us
    pallas_call x1 -> x3, Pallas kernels: 14.7 us -> 63.6 us  [the longest x2 31.9 us: attend(): pl.pallas_call(functools.partial(attend_route_kernel if routed else atten...]
    all_gather x1 -> x0, blocking collectives: 35 us -> none  [shards(): every = lax.all_gather(packed, 'docs', axis=0, tiled=False)]
    ppermute x0 -> x5, waiting for transfers between devices: none -> 23.7 us  [the longest x4 23.7 us: every_device(): lax.ppermute(held, 'docs', [(i, i ^ step) for i in range(peers)])]
    all_to_all x3, waiting for transfers between devices: 37.7 us -> 27.4 us  [the longest x1 27.4 us: shards(): got = lax.all_to_all(sent, 'docs', split_axis=0, concat_axis=0, tiled=True)]
    ppermute x0 -> x5, starting transfers between devices: none -> 5.04 us  [the longest x4 4.71 us: every_device(): lax.ppermute(held, 'docs', [(i, i ^ step) for i in range(peers)])]
    dot_general x4 -> x2, matrix products: 7.15 us -> 4.37 us  [one_hot_dot(): jnp.dot(table.astype(jnp.bfloat16), rows, preferred_element_type=jnp.floa...]
    unnamed x7 -> x16, local copies, waits for them, and re-layouts: 4.96 us -> 2.8 us
    gather x2 -> x1, local copies, waits for them, and re-layouts: 3.29 us -> 3.14 us  [shards(): docs = jnp.where(spots >= 0, sent_doc[me * own + jnp.maximum(spots, 0)], -2)]
  transfers between devices with their start and end apart: 5 -> 10, of which waited for: 2 -> 4; matrix products, arithmetic and copies ran while one was open for 7% -> 10% of each run, Pallas kernels for 11% -> 6%
where the time goes in v3:
time: 164 us; the launch traced here: 163 us
  Pallas kernels  63.6 us (39%)
  waiting for transfers between devices  51.1 us (31%)
  starting transfers between devices  26.6 us (16%)
  local copies, waits for them, and re-layouts  10.5 us (6%)
  other arithmetic  5.73 us (3%)
  matrix products  4.52 us (3%)
    pallas_call x2, Pallas kernels, attend(): pl.pallas_call(functools.partial(attend_route_kernel if routed else atten...  31.9 us
    pallas_call x1, Pallas kernels, place(): pl.pallas_call(place_kernel, in_specs=[SMEM, ANY], out_specs=ANY, out_sha...  31.7 us
    all_to_all x1, waiting for transfers between devices, shards(): got = lax.all_to_all(sent, 'docs', split_axis=0, concat_axis=0, tiled=True)  27.4 us
    ppermute x4, waiting for transfers between devices, every_device(): lax.ppermute(held, 'docs', [(i, i ^ step) for i in range(peers)])  23.7 us
    all_to_all x2, starting transfers between devices, deal(): lax.all_to_all(out, 'docs', split_axis=0, concat_axis=0, tiled=True, axis...  11.8 us
    all_to_all x1, starting transfers between devices, shards(): got = lax.all_to_all(sent, 'docs', split_axis=0, concat_axis=0, tiled=True)  5.35 us
    ppermute x4, starting transfers between devices, every_device(): lax.ppermute(held, 'docs', [(i, i ^ step) for i in range(peers)])  4.71 us
    dot_general x2, matrix products, one_hot_dot(): jnp.dot(table.astype(jnp.bfloat16), rows, preferred_element_type=jnp.floa...  4.37 us
  transfers between devices with their start and end apart: 10, of which 4 were waited for; matrix products, arithmetic and copies ran while one was open for 10% of the time, Pallas kernels for 6%

profile of v3, /device:TPU:14, one launch (start us, length us, event | category | flops | bytes accessed | tf_op | source)
XLA Modules:
  0.0 162.9 jit_solution(143414679194245437)
XLA Ops:
  2.0 2.7 %collective-permute-start = (s32[1,256]{1,0:T(1,128)S(1)}, s32[1,256]{1,0:T(1,128)S(1)}, u32[]{:S(2)}, u32[]{:S(2)}) collective-permute-start(s32[1,256]{1,0:T(1,128)S(1)} %bitcast.24), channel_id=1, source_target_pairs={{0,8},{1,9},{2,10},{3,11},{4,12},{5,13},{6,14},{7,15},{8,0},{9,1},... | collective-permute-start | bytes 3080 | tf_op jit(solution)/shard_map/ppermute | solution.py:33
  5.3 2.7 %convolution_convert_fusion.1 = bf16[512,1280]{1,0:T(8,128)(2,1)} fusion(bf16[256,1280]{1,0:T(8,128)(2,1)} %param.9, s32[256]{0:T(256)S(1)} %get-tuple-element.24, s32[256]{0:T(256)S(1)} %get-tuple-element.23, pred[256]{0:T(512)(128)(4,1)S(1)} %get-tuple-element.8, pred[256]{0:T(512)(128)(4,1)S(1)} %get-tuple-element.5), kind=kOutput, calls=%fused_computation.2 | convolution fusion | flops 336855040 | bytes 1968640 | tf_op jit(solution)/shard_map/dot_general | solution.py:43
  8.0 4.3 %all-to-all-start = ((bf16[8,64,1280]{2,1,0:T(8,128)(2,1)}), bf16[8,64,1280]{2,1,0:T(8,128)(2,1)S(1)}, u32[]{:S(2)}, u32[]{:S(2)}) async-start(bf16[8,64,1280]{2,1,0:T(8,128)(2,1)} %bitcast.1), calls=%async_computation | async-start | bytes 2621440 | tf_op jit(solution)/shard_map/all_to_all | solution.py:224
  12.3 0.9 fusion.31
  13.3 2.2 %collective-permute-start.6 = (bf16[32,1280]{1,0:T(8,128)(2,1)S(1)}, bf16[32,1280]{1,0:T(8,128)(2,1)S(1)}, u32[]{:S(2)}, u32[]{:S(2)}) collective-permute-start(bf16[32,1280]{1,0:T(8,128)(2,1)S(1)} %get-tuple-element.14), channel_id=1, source_target_pairs={{1,0},{2,1},{3,2},{4,3},{5,4},{6,5},{7,6},{8,7},{9,8},{10,9},{11,1... | collective-permute-start | bytes 245768 | tf_op jit(solution)/shard_map/ppermute | solution.py:19
  15.5 2.1 %collective-permute-start.5 = (bf16[32,1280]{1,0:T(8,128)(2,1)S(1)}, bf16[32,1280]{1,0:T(8,128)(2,1)S(1)}, u32[]{:S(2)}, u32[]{:S(2)}) collective-permute-start(bf16[32,1280]{1,0:T(8,128)(2,1)S(1)} %get-tuple-element.15), channel_id=1, source_target_pairs={{0,1},{1,2},{2,3},{3,4},{4,5},{5,6},{6,7},{7,8},{8,9},{9,10},{10,1... | collective-permute-start | bytes 245768 | tf_op jit(solution)/shard_map/ppermute | solution.py:18
  19.7 20.5 %collective-permute-done.2 = s32[2,256]{1,0:T(2,128)S(1)} collective-permute-done((s32[2,256]{1,0:T(2,128)S(1)}, s32[2,256]{1,0:T(2,128)S(1)}, u32[]{:S(2)}, u32[]{:S(2)}) %collective-permute-start.2) | collective-permute-done | bytes 2080 | tf_op jit(solution)/shard_map/ppermute | solution.py:33
  40.2 1.4 collective-permute-start.3
  41.7 2.1 %collective-permute-done.3 = s32[4,256]{1,0:T(4,128)S(1)} collective-permute-done((s32[4,256]{1,0:T(4,128)S(1)}, s32[4,256]{1,0:T(4,128)S(1)}, u32[]{:S(2)}, u32[]{:S(2)}) %collective-permute-start.3) | collective-permute-done | bytes 4128 | tf_op jit(solution)/shard_map/ppermute | solution.py:33
  43.9 1.1 collective-permute-done.4
  45.2 1.6 %convolution_convert_fusion = bf16[512,1280]{1,0:T(8,128)(2,1)} fusion(bf16[256,1280]{1,0:T(8,128)(2,1)S(1)} %collective-permute-done.1, s32[256]{0:T(256)S(1)} %bitcast.35, s32[256]{0:T(256)S(1)} %bitcast.34, pred[256]{0:T(512)(128)(4,1)S(1)} %get-tuple-element.12, pred[256]{0:T(512)(128)(4,1)S(1)} %get-tuple-element.27), kind=kOutput, calls=%fused_computation.1 | convolution fusion | flops 336855040 | bytes 1968640 | tf_op jit(solution)/shard_map/dot_general | solution.py:43
  46.9 1.1 copy-done.2
  47.9 7.5 %all-to-all-start.1 = ((bf16[8,64,1280]{2,1,0:T(8,128)(2,1)}), bf16[8,64,1280]{2,1,0:T(8,128)(2,1)}, u32[]{:S(2)}, u32[]{:S(2)}) async-start(bf16[8,64,1280]{2,1,0:T(8,128)(2,1)} %bitcast.8), calls=%async_computation.1 | async-start | bytes 2621440 | tf_op jit(solution)/shard_map/all_to_all | solution.py:224
  56.3 3.1 %gather_fusion = s32[512]{0:T(512)S(1)} fusion(s32[32768]{0:T(1024)S(1)} %copy-done, s32[1024]{0:T(1024)S(1)} %pad_clamp_fusion), kind=kCustom, calls=%fused_computation | custom fusion | bytes 6144 | tf_op jit(solution)/shard_map/gather | solution.py:236
  59.5 0.8 copy.12.doc_ref
  60.3 0.8 copy.11.doc_ref
  62.4 9.2 %attend.1.rest_5_ = bf16[256,1280]{1,0:T(8,128)(2,1)} custom-call(bf16[8,64,1280]{2,1,0:T(8,128)(2,1)} %copy-done.2, s32[256,1]{1,0:T(8,128)} %copy.11.doc_ref, bf16[2048,1280]{1,0:T(8,128)(2,1)} %k_ref.3, bf16[32,1280]{1,0:T(8,128)(2,1)} %copy-done.6, bf16[32,1280]{1,0:T(8,128)(2,1)} %copy-done.5, s32[1,2048]{1,0:T(1,128)} %bitcast.32, ...), custom_call_target="tpu_custom_call" | custom-call | flops 2684354560 | bytes 6553600 | tf_op jit(solution)/shard_map/attend/pallas_call | solution.py:144
  71.6 22.8 %attend_route.1 = bf16[16,32,1280]{2,1,0:T(8,128)(2,1)} custom-call(s32[16]{0:T(128)} %copy-done.7, s32[16]{0:T(128)} %select_reduce_fusion.4.taken_ref, bf16[8,64,1280]{2,1,0:T(8,128)(2,1)} %all-to-all-done.1.q_ref, s32[256,1]{1,0:T(8,128)} %copy.12.doc_ref, bf16[2048,1280]{1,0:T(8,128)(2,1)} %k_ref.3, bf16[32,1280]{1,0:T(8,128)(2,1)} %copy-done.6, ...), custom_call_target="tpu_custom_call" | custom-call | flops 2684354560 | bytes 6553600 | tf_op jit(solution)/shard_map/attend_route/pallas_call | solution.py:144
  94.4 5.3 %all-to-all-start.2 = ((bf16[16,32,1280]{2,1,0:T(8,128)(2,1)}), bf16[16,32,1280]{2,1,0:T(8,128)(2,1)S(1)}, u32[]{:S(2)}, u32[]{:S(2)}) async-start(bf16[16,32,1280]{2,1,0:T(8,128)(2,1)} %attend_route.1), calls=%async_computation.2 | async-start | bytes 2621440 | tf_op jit(solution)/shard_map/all_to_all | solution.py:248
  100.4 1.2 broadcast_select_fusion.1
  101.6 1.2 pad_maximum_fusion
  102.7 27.4 %all-to-all-done.2.x_ref = bf16[16,32,1280]{2,1,0:T(8,128)(2,1)S(1)} async-done(((bf16[16,32,1280]{2,1,0:T(8,128)(2,1)}), bf16[16,32,1280]{2,1,0:T(8,128)(2,1)S(1)}, u32[]{:S(2)}, u32[]{:S(2)}) %all-to-all-start.2) | async-done | bytes 1310752 | tf_op jit(solution)/shard_map/all_to_all | solution.py:248
  130.2 1.1 copy-done.1
  131.2 31.7 %place.1 = bf16[16,32,1280]{2,1,0:T(8,128)(2,1)} custom-call(s32[16]{0:T(128)} %dynamic_slice.13.comes_ref, bf16[16,32,1280]{2,1,0:T(8,128)(2,1)} %copy-done.1), custom_call_target="tpu_custom_call" | custom-call | bytes 2621440 | tf_op jit(solution)/shard_map/place/pallas_call | solution.py:185
  (57 shorter events, 7.3 us)
Async XLA Ops:
  2.0 16.9 %collective-permute-start = (s32[1,256]{1,0:T(1,128)S(1)}, s32[1,256]{1,0:T(1,128)S(1)}, u32[]{:S(2)}, u32[]{:S(2)}) collective-permute-start(s32[1,256]{1,0:T(1,128)S(1)} %bitcast.24), channel_id=1, source_target_pairs={{0,8},{1,9},{2,10},{3,11},{4,12},{5,13},{6,14},{7,15},{8,0},{9,1},... | collective-permute-start | bytes 3080 | tf_op jit(solution)/shard_map/ppermute | solution.py:33
  4.7 40.5 %collective-permute-start.1 = (bf16[256,1280]{1,0:T(8,128)(2,1)}, bf16[256,1280]{1,0:T(8,128)(2,1)S(1)}, u32[]{:S(2)}, u32[]{:S(2)}) collective-permute-start(bf16[256,1280]{1,0:T(8,128)(2,1)} %param.9), channel_id=1, source_target_pairs={{0,8},{1,9},{2,10},{3,11},{4,12},{5,13},{6,14},{7,15},{8,0},{9,1},... | collective-permute-start | bytes 1966088 | tf_op jit(solution)/shard_map/ppermute | solution.py:206
  8.0 9.6 %copy-start.4 = (s32[16]{0:T(128)S(1)}, s32[16]{0:T(128)}, u32[]{:S(2)}) copy-start(s32[16]{0:T(128)} %constant.195.clone) | copy-start | bytes 196
  8.0 9.7 %copy-start = (s32[32768]{0:T(1024)S(1)}, s32[32768]{0:T(1024)}, u32[]{:S(2)}) copy-start(s32[32768]{0:T(1024)} %param.8) | copy-start | bytes 393220
  8.0 38.9 %all-to-all-start = ((bf16[8,64,1280]{2,1,0:T(8,128)(2,1)}), bf16[8,64,1280]{2,1,0:T(8,128)(2,1)S(1)}, u32[]{:S(2)}, u32[]{:S(2)}) async-start(bf16[8,64,1280]{2,1,0:T(8,128)(2,1)} %bitcast.1), calls=%async_computation | async-start | bytes 2621440 | tf_op jit(solution)/shard_map/all_to_all | solution.py:224
  13.3 48.5 %collective-permute-start.6 = (bf16[32,1280]{1,0:T(8,128)(2,1)S(1)}, bf16[32,1280]{1,0:T(8,128)(2,1)S(1)}, u32[]{:S(2)}, u32[]{:S(2)}) collective-permute-start(bf16[32,1280]{1,0:T(8,128)(2,1)S(1)} %get-tuple-element.14), channel_id=1, source_target_pairs={{1,0},{2,1},{3,2},{4,3},{5,4},{6,5},{7,6},{8,7},{9,8},{10,9},{11,1... | collective-permute-start | bytes 245768 | tf_op jit(solution)/shard_map/ppermute | solution.py:19
  15.5 46.2 %collective-permute-start.5 = (bf16[32,1280]{1,0:T(8,128)(2,1)S(1)}, bf16[32,1280]{1,0:T(8,128)(2,1)S(1)}, u32[]{:S(2)}, u32[]{:S(2)}) collective-permute-start(bf16[32,1280]{1,0:T(8,128)(2,1)S(1)} %get-tuple-element.15), channel_id=1, source_target_pairs={{0,1},{1,2},{2,3},{3,4},{4,5},{5,6},{6,7},{7,8},{8,9},{9,10},{10,1... | collective-permute-start | bytes 245768 | tf_op jit(solution)/shard_map/ppermute | solution.py:18
  19.0 21.2 %collective-permute-start.2 = (s32[2,256]{1,0:T(2,128)S(1)}, s32[2,256]{1,0:T(2,128)S(1)}, u32[]{:S(2)}, u32[]{:S(2)}) collective-permute-start(s32[2,256]{1,0:T(2,128)S(1)} %pad_add_fusion.2), channel_id=1, source_target_pairs={{0,4},{1,5},{2,6},{3,7},{4,0},{5,1},{6,2},{7,3},{8,12},{9,13},{10,... | collective-permute-start | bytes 6152 | tf_op jit(solution)/shard_map/ppermute | solution.py:33
  40.2 3.6 %collective-permute-start.3 = (s32[4,256]{1,0:T(4,128)S(1)}, s32[4,256]{1,0:T(4,128)S(1)}, u32[]{:S(2)}, u32[]{:S(2)}) collective-permute-start(s32[4,256]{1,0:T(4,128)S(1)} %pad_add_fusion.1), channel_id=1, source_target_pairs={{0,2},{1,3},{2,0},{3,1},{4,6},{5,7},{6,4},{7,5},{8,10},{9,11},{10,... | collective-permute-start | bytes 12296 | tf_op jit(solution)/shard_map/ppermute | solution.py:33
  43.8 1.2 collective-permute-start.4
  46.9 1.1 copy-start.2
  47.9 23.7 %all-to-all-start.1 = ((bf16[8,64,1280]{2,1,0:T(8,128)(2,1)}), bf16[8,64,1280]{2,1,0:T(8,128)(2,1)}, u32[]{:S(2)}, u32[]{:S(2)}) async-start(bf16[8,64,1280]{2,1,0:T(8,128)(2,1)} %bitcast.8), calls=%async_computation.1 | async-start | bytes 2621440 | tf_op jit(solution)/shard_map/all_to_all | solution.py:224
  61.1 10.5 %copy-start.7 = (s32[16]{0:T(128)}, s32[16]{0:T(128)S(1)}, u32[]{:S(2)}) copy-start(s32[16]{0:T(128)S(1)} %broadcast_add_fusion.goes_ref) | copy-start | bytes 196
  61.7 0.6 copy-start.5
  61.7 0.7 copy-start.6
  94.4 6.0 %copy-start.3 = (bf16[8,64,1280]{2,1,0:T(8,128)(2,1)S(1)}, bf16[8,64,1280]{2,1,0:T(8,128)(2,1)}, u32[]{:S(2)}) copy-start(bf16[8,64,1280]{2,1,0:T(8,128)(2,1)} %copy-done.2) | copy-start | bytes 3932164
  94.4 35.8 %all-to-all-start.2 = ((bf16[16,32,1280]{2,1,0:T(8,128)(2,1)}), bf16[16,32,1280]{2,1,0:T(8,128)(2,1)S(1)}, u32[]{:S(2)}, u32[]{:S(2)}) async-start(bf16[16,32,1280]{2,1,0:T(8,128)(2,1)} %attend_route.1), calls=%async_computation.2 | async-start | bytes 2621440 | tf_op jit(solution)/shard_map/all_to_all | solution.py:248
  130.2 1.1 copy-start.1

commit v4 on v2

--- a/solution.py
+++ b/solution.py
@@ -8,6 +8,8 @@
 from jax.sharding import PartitionSpec as P
 
 MOST_SENT = 32
+TILE = 16
+VMEM, SMEM, HBM = (pl.BlockSpec(memory_space=m) for m in (pltpu.VMEM, pltpu.SMEM, pltpu.HBM))
 
 
 def halo_of(sentences):
@@ -40,7 +42,7 @@
 def attend(queries, docs, sentences, before, after, ids, id_before, id_after):
     rows, feature = queries.shape
     own = sentences.shape[0]
-    block = min(128, rows)
+    block = min(256, rows)
     whole = lambda a: pl.BlockSpec(a.shape, lambda i: (0, 0))
     fixed = (sentences, before, after, ids, id_before, id_after)
     return pl.pallas_call(
@@ -61,17 +63,19 @@
     )(queries, docs, *fixed)
 
 
-def every_device(row):
+def every_device(row, late):
     peers, me = lax.axis_size("docs"), lax.axis_index("docs")
     if peers & (peers - 1):
-        return lax.all_gather(row, "docs", axis=0, tiled=False)
+        return lax.all_gather(row, "docs", axis=0, tiled=False), late
     held, step = row[None], 1
     while step < peers:
+        if 2 * step == peers:
+            held, late = lax.optimization_barrier((held, late))
         held = jnp.concatenate([held, lax.ppermute(held, "docs", [(i, i ^ step) for i in range(peers)])], axis=0)
         step *= 2
     label = jnp.arange(peers, dtype=jnp.int32)
     pick = (label ^ me)[:, None] == label[None, :]
-    return jnp.sum(jnp.where(pick[:, :, None], held[None], 0), axis=1)
+    return jnp.sum(jnp.where(pick[:, :, None], held[None], 0), axis=1), late
 
 
 def copy_kernel(x_ref, o_ref):
@@ -88,6 +92,7 @@
         in_specs=[spec],
         out_specs=spec,
         out_shape=jax.ShapeDtypeStruct(x.shape, x.dtype),
+        compiler_params=pltpu.CompilerParams(vmem_limit_bytes=8 * 1024 * 1024),
         cost_estimate=pl.CostEstimate(flops=0, bytes_accessed=4 * rows * feature, transcendentals=0),
         name="write_out",
     )(x)
@@ -95,6 +100,40 @@
 
 def exchange(x):
     return lax.all_to_all(x, "docs", split_axis=0, concat_axis=0, tiled=True)
+
+
+def place_kernel(comes_ref, x_ref, o_ref, zero, sem):
+    zero[...] = jnp.zeros_like(zero)
+    members = x_ref.shape[0]
+    moves = [pltpu.make_async_copy(x_ref.at[jnp.maximum(comes_ref[d], 0)], o_ref.at[d], sem.at[d]) for d in range(members)]
+    clears = [pltpu.make_async_copy(zero, o_ref.at[d], sem.at[d]) for d in range(members)]
+    for d in range(members):
+        pl.when(comes_ref[d] >= 0)(moves[d].start)
+        pl.when(comes_ref[d] < 0)(clears[d].start)
+    for d in range(members):
+        pl.when(comes_ref[d] >= 0)(moves[d].wait)
+        pl.when(comes_ref[d] < 0)(clears[d].wait)
+
+
+def place(x, comes):
+    members, cap, feature = x.shape
+    if cap % TILE:
+        row = jnp.arange(members * cap, dtype=jnp.int32)
+        block = jnp.repeat(comes, cap)
+        takes = ((block * cap + row % cap)[:, None] == row[None, :]) & (block >= 0)[:, None]
+        table = takes.astype(jnp.bfloat16)
+        rows = x.reshape(members * cap, feature)
+        return jnp.dot(table, rows, preferred_element_type=jnp.float32).astype(jnp.bfloat16)
+    return pl.pallas_call(
+        place_kernel,
+        in_specs=[SMEM, VMEM],
+        out_specs=HBM,
+        out_shape=jax.ShapeDtypeStruct(x.shape, x.dtype),
+        scratch_shapes=[pltpu.VMEM((cap, feature), x.dtype), pltpu.SemaphoreType.DMA((members,))],
+        compiler_params=pltpu.CompilerParams(vmem_limit_bytes=8 * 1024 * 1024),
+        cost_estimate=pl.CostEstimate(flops=0, bytes_accessed=4 * x.size, transcendentals=0),
+        name="place",
+    )(comes, x).reshape(members * cap, feature)
 
 
 def shards(sentences, sent_doc, images, image_owner, anchor, loader_shard):
@@ -106,7 +145,6 @@
     owner, shard = image_owner[:, 0], loader_shard[:, 0]
 
     packed = (owner * members + shard) * own + anchor
-    every = every_device(packed)
 
     spot = jnp.arange(n, dtype=jnp.int32)
     earlier = (owner[:, None] == owner[None, :]) & (spot[None, :] < spot[:, None])
@@ -118,7 +156,8 @@
         out = jnp.dot(table, images, preferred_element_type=jnp.float32).astype(jnp.bfloat16)
         return out.reshape(members, cap, feature)
 
-    queries = exchange(buckets(owner)).reshape(members * cap, feature)
+    every, arrived = every_device(packed, exchange(buckets(owner)))
+    queries = arrived.reshape(members * cap, feature)
     loaded_images = write_out(exchange(buckets(shard)).reshape(members * cap, feature))
     before, after = halo_of(sentences)
 
@@ -127,12 +166,13 @@
     owner_of = every // (own * members)
     mine = owner_of == me
     sooner = (spot[:, None] < spot[None, :]).astype(jnp.bfloat16)
-    place = jnp.dot(mine.astype(jnp.bfloat16), sooner, preferred_element_type=jnp.float32).astype(jnp.int32)
+    ranks = jnp.dot(mine.astype(jnp.bfloat16), sooner, preferred_element_type=jnp.float32).astype(jnp.int32)
     slots = jnp.arange(cap, dtype=jnp.int32)
-    hit = mine[:, None, :] & (place[:, None, :] == slots[None, :, None])
+    hit = mine[:, None, :] & (ranks[:, None, :] == slots[None, :, None])
     spots = jnp.sum(jnp.where(hit, spot_of[:, None, :] + 1, 0), axis=2).reshape(members * cap) - 1
-    docs = jnp.where(spots >= 0, sent_doc[me * own + jnp.maximum(spots, 0)], -2)
     ids = lax.dynamic_slice_in_dim(sent_doc, me * own, own)
+    here = spots[:, None] == jnp.arange(own, dtype=jnp.int32)[None, :]
+    docs = jnp.max(jnp.where(here, ids[None, :], -2), axis=1)
     padded = jnp.pad(sent_doc, (MOST_SENT, MOST_SENT), constant_values=-1)
     id_before = lax.dynamic_slice_in_dim(padded, me * own, MOST_SENT)
     id_after = lax.dynamic_slice_in_dim(padded, me * own + own + MOST_SENT, MOST_SENT)
@@ -145,10 +185,7 @@
     puts = row[:, None] == (jnp.repeat(goes, cap) * cap + row % cap)[None, :]
     puts = (puts & (jnp.repeat(goes, cap) >= 0)[None, :]).astype(jnp.bfloat16)
     sent = jnp.dot(puts, aligned, preferred_element_type=jnp.float32).astype(jnp.bfloat16).reshape(members, cap, feature)
-    got = exchange(sent).reshape(members * cap, feature)
-    takes = (jnp.repeat(comes, cap) * cap + row % cap)[:, None] == row[None, :]
-    takes = (takes & (jnp.repeat(comes, cap) >= 0)[:, None]).astype(jnp.bfloat16)
-    loaded_text = jnp.dot(takes, got, preferred_element_type=jnp.float32).astype(jnp.bfloat16)
+    loaded_text = place(exchange(sent), comes)
     return loaded_images, loaded_text
 
 

time: 117 us -> 136 us (1.16)
  waiting for transfers between devices: 53.5 us -> 76.2 us
  Pallas kernels: 18 us -> 14.4 us
  other arithmetic: 2.48 us -> 4.93 us
  matrix products: 7.25 us -> 5.26 us
  local copies, waits for them, and re-layouts: 7.82 us -> 5.98 us
    ppermute x4, waiting for transfers between devices: 19.4 us -> 40.5 us  [every_device(): lax.ppermute(held, 'docs', [(i, i ^ step) for i in range(peers)])]
    pallas_call x1, Pallas kernels: 14.5 us -> 11 us  [attend(): pl.pallas_call(functools.partial(attend_kernel, feature ** (-0.5)), grid=...]
    gather x2 -> x0, local copies, waits for them, and re-layouts: 3.28 us -> none  [shards(): docs = jnp.where(spots >= 0, sent_doc[me * own + jnp.maximum(spots, 0)], -2)]
    dot_general x1 -> x0, matrix products: 1.99 us -> none  [shards(): jnp.dot(takes, got, preferred_element_type=jnp.float32).astype(jnp.bfloat16)]
    reduce_max x1 -> x2, other arithmetic: 0.15 us -> 2.1 us  [the longest x1 1.37 us: shards(): docs = jnp.max(jnp.where(here, ids[None, :], -2), axis=1)]
    pallas_call x1, Pallas kernels: 3.46 us -> 1.63 us  [write_out(): pl.pallas_call(copy_kernel, grid=(rows // block,), in_specs=[spec], out_s...]
    pallas_call x0 -> x1, Pallas kernels: none -> 1.73 us  [place(): pl.pallas_call(place_kernel, in_specs=[SMEM, VMEM], out_specs=HBM, out_sh...]
    all_to_all x3, waiting for transfers between devices: 34.1 us -> 35.7 us  [exchange(): return lax.all_to_all(x, 'docs', split_axis=0, concat_axis=0, tiled=True)]
  transfers between devices with their start and end apart: 9 -> 9, of which waited for: 6 -> 5; matrix products, arithmetic and copies ran while one was open for 8% -> 8% of each run, Pallas kernels for 15% -> 9%
where the time goes in v4:
time: 136 us; the launch traced here: 135 us
  waiting for transfers between devices  76.2 us (56%)
  starting transfers between devices  27.4 us (20%)
  Pallas kernels  14.4 us (11%)
  local copies, waits for them, and re-layouts  5.98 us (4%)
  matrix products  5.26 us (4%)
  other arithmetic  4.93 us (4%)
    ppermute x4, waiting for transfers between devices, every_device(): lax.ppermute(held, 'docs', [(i, i ^ step) for i in range(peers)])  40.5 us
    all_to_all x3, waiting for transfers between devices, exchange(): return lax.all_to_all(x, 'docs', split_axis=0, concat_axis=0, tiled=True)  35.7 us
    all_to_all x3, starting transfers between devices, exchange(): return lax.all_to_all(x, 'docs', split_axis=0, concat_axis=0, tiled=True)  18.5 us
    pallas_call x1, Pallas kernels, attend(): pl.pallas_call(functools.partial(attend_kernel, feature ** (-0.5)), grid=...  11 us
    ppermute x4, starting transfers between devices, every_device(): lax.ppermute(held, 'docs', [(i, i ^ step) for i in range(peers)])  4.55 us
    dot_general x2, matrix products, buckets(): jnp.dot(table, images, preferred_element_type=jnp.float32)  3.15 us
  transfers between devices with their start and end apart: 9, of which 5 were waited for; matrix products, arithmetic and copies ran while one was open for 8% of the time, Pallas kernels for 9%

profile of v4, /device:TPU:14, one launch (start us, length us, event | category | flops | bytes accessed | tf_op | source)
XLA Modules:
  0.0 134.9 jit_solution(13802563976618303684)
XLA Ops:
  0.6 0.9 convert_reduce_fusion
  2.3 1.6 %convolution_convert_fusion.1 = bf16[512,1280]{1,0:T(8,128)(2,1)} fusion(bf16[256,1280]{1,0:T(8,128)(2,1)S(1)} %copy-done, s32[256]{0:T(256)S(1)} %get-tuple-element.14), kind=kOutput, calls=%fused_computation.3 | convolution fusion | flops 336330752 | bytes 1967104 | tf_op jit(solution)/shard_map/dot_general | solution.py:156
  3.9 6.2 %all-to-all-start.1 = ((bf16[16,32,1280]{2,1,0:T(8,128)(2,1)}), bf16[16,32,1280]{2,1,0:T(8,128)(2,1)S(1)}, u32[]{:S(2)}, u32[]{:S(2)}) async-start(bf16[16,32,1280]{2,1,0:T(8,128)(2,1)} %bitcast.5), calls=%async_computation.1 | async-start | bytes 2621440 | tf_op jit(solution)/shard_map/all_to_all | solution.py:102
  10.3 1.6 %fusion.19 = (bf16[32,1280]{1,0:T(8,128)(2,1)}, bf16[32,1280]{1,0:T(8,128)(2,1)}) fusion(bf16[2048,1280]{1,0:T(8,128)(2,1)} %k_ref.1), kind=kLoop, calls=%fused_computation.65 | loop fusion | bytes 327680 | tf_op jit(solution)/shard_map/slice | solution.py:20
  11.9 2.4 %collective-permute-start.5 = (bf16[32,1280]{1,0:T(8,128)(2,1)}, bf16[32,1280]{1,0:T(8,128)(2,1)}, u32[]{:S(2)}, u32[]{:S(2)}) collective-permute-start(bf16[32,1280]{1,0:T(8,128)(2,1)} %get-tuple-element.9), channel_id=1, source_target_pairs={{1,0},{2,1},{3,2},{4,3},{5,4},{6,5},{7,6},{8,7},{9,8},{10,9},{11,1... | collective-permute-start | bytes 245768 | tf_op jit(solution)/shard_map/ppermute | solution.py:20
  14.3 1.9 %collective-permute-start.4 = (bf16[32,1280]{1,0:T(8,128)(2,1)}, bf16[32,1280]{1,0:T(8,128)(2,1)}, u32[]{:S(2)}, u32[]{:S(2)}) collective-permute-start(bf16[32,1280]{1,0:T(8,128)(2,1)} %get-tuple-element.10), channel_id=1, source_target_pairs={{0,1},{1,2},{2,3},{3,4},{4,5},{5,6},{6,7},{7,8},{8,9},{9,10},{10,1... | collective-permute-start | bytes 245768 | tf_op jit(solution)/shard_map/ppermute | solution.py:19
  16.2 1.6 %convolution_convert_fusion.2 = bf16[512,1280]{1,0:T(8,128)(2,1)} fusion(bf16[256,1280]{1,0:T(8,128)(2,1)S(1)} %copy-done, s32[256]{0:T(256)S(1)} %get-tuple-element.16), kind=kOutput, calls=%fused_computation.4 | convolution fusion | flops 336330752 | bytes 1967104 | tf_op jit(solution)/shard_map/dot_general | solution.py:156
  17.8 1.5 %collective-permute-start.1 = (s32[2,256]{1,0:T(2,128)S(1)}, s32[2,256]{1,0:T(2,128)S(1)}, u32[]{:S(2)}, u32[]{:S(2)}) collective-permute-start(s32[2,256]{1,0:T(2,128)S(1)} %pad_add_fusion.3), channel_id=1, source_target_pairs={{0,2},{1,3},{2,0},{3,1},{4,6},{5,7},{6,4},{7,5},{8,10},{9,11},{10,... | collective-permute-start | bytes 6152 | tf_op jit(solution)/shard_map/ppermute | solution.py:74
  19.3 2.2 %collective-permute-done.1 = s32[2,256]{1,0:T(2,128)S(1)} collective-permute-done((s32[2,256]{1,0:T(2,128)S(1)}, s32[2,256]{1,0:T(2,128)S(1)}, u32[]{:S(2)}, u32[]{:S(2)}) %collective-permute-start.1) | collective-permute-done | bytes 2080 | tf_op jit(solution)/shard_map/ppermute | solution.py:74
  22.1 11.5 %collective-permute-done.2 = s32[4,256]{1,0:T(4,128)S(1)} collective-permute-done((s32[4,256]{1,0:T(4,128)S(1)}, s32[4,256]{1,0:T(4,128)S(1)}, u32[]{:S(2)}, u32[]{:S(2)}) %collective-permute-start.2) | collective-permute-done | bytes 4128 | tf_op jit(solution)/shard_map/ppermute | solution.py:74
  33.7 6.9 %all-to-all-done.1 = bf16[16,32,1280]{2,1,0:T(8,128)(2,1)S(1)} async-done(((bf16[16,32,1280]{2,1,0:T(8,128)(2,1)}), bf16[16,32,1280]{2,1,0:T(8,128)(2,1)S(1)}, u32[]{:S(2)}, u32[]{:S(2)}) %all-to-all-start.1) | async-done | bytes 1310752 | tf_op jit(solution)/shard_map/all_to_all | solution.py:102
  40.5 5.3 %all-to-all-start = ((bf16[16,32,1280]{2,1,0:T(8,128)(2,1)}), bf16[16,32,1280]{2,1,0:T(8,128)(2,1)S(1)}, u32[]{:S(2)}, u32[]{:S(2)}) async-start(bf16[16,32,1280]{2,1,0:T(8,128)(2,1)} %bitcast.22), calls=%async_computation | async-start | bytes 2621440 | tf_op jit(solution)/shard_map/all_to_all | solution.py:102
  45.8 2.4 %collective-permute-start.3 = (s32[8,256]{1,0:T(8,128)S(1)}, s32[8,256]{1,0:T(8,128)S(1)}, u32[]{:S(2)}, u32[]{:S(2)}) collective-permute-start(s32[8,256]{1,0:T(8,128)S(1)} %pad_add_fusion.1), channel_id=1, source_target_pairs={{0,8},{1,9},{2,10},{3,11},{4,12},{5,13},{6,14},{7,15},{8,0},{9,1},... | collective-permute-start | bytes 24584 | tf_op jit(solution)/shard_map/ppermute | solution.py:74
  48.3 26.8 %collective-permute-done.3 = s32[8,256]{1,0:T(8,128)S(1)} collective-permute-done((s32[8,256]{1,0:T(8,128)S(1)}, s32[8,256]{1,0:T(8,128)S(1)}, u32[]{:S(2)}, u32[]{:S(2)}) %collective-permute-start.3) | collective-permute-done | bytes 8224 | tf_op jit(solution)/shard_map/ppermute | solution.py:74
  75.2 0.7 select_reduce_fusion.3
  77.3 1.4 %select_reduce_fusion = s32[512]{0:T(512)} fusion(s32[2048]{0:T(1024)S(1)} %dynamic_slice.9, s32[512]{0:T(512)S(1)} %sub.27), kind=kLoop, calls=%fused_computation | loop fusion | flops 3145216 | bytes 12288 | tf_op jit(solution)/shard_map/reduce_max | solution.py:175
  79.4 0.8 copy.9.doc_ref
  80.2 2.5 %copy-done.1 = bf16[2048,1280]{1,0:T(8,128)(2,1)S(1)} copy-done((bf16[2048,1280]{1,0:T(8,128)(2,1)S(1)}, bf16[2048,1280]{1,0:T(8,128)(2,1)}, u32[]{:S(2)}) %copy-start.1) | copy-done | bytes 5242904
  82.7 11.0 %attend.1 = bf16[512,1280]{1,0:T(8,128)(2,1)S(1)} custom-call(bf16[512,1280]{1,0:T(8,128)(2,1)S(1)} %bitcast.20, s32[512,1]{1,0:T(8,128)S(1)} %copy.9.doc_ref, bf16[2048,1280]{1,0:T(8,128)(2,1)S(1)} %copy-done.1, bf16[32,1280]{1,0:T(8,128)(2,1)} %collective-permute-done.4.before_ref, bf16[32,1280]{1,0:T(8,128)(2,1)} %collective-permute-done.5.after_ref, ...), custom_call_target="tpu_custom_call" | custom-call | flops 5368709120 | bytes 7864320 | tf_op jit(solution)/shard_map/attend/pallas_call | solution.py:48
  93.8 2.0 %convolution_convert_fusion = bf16[512,1280]{1,0:T(8,128)(2,1)} fusion(bf16[512,1280]{1,0:T(8,128)(2,1)S(1)} %attend.1, s32[512]{0:T(512)S(1)} %copy-done.3, pred[512]{0:T(512)(128)(4,1)S(1)} %copy-done.5), kind=kOutput, calls=%fused_computation.2 | convolution fusion | flops 672268288 | bytes 2624000 | tf_op jit(solution)/shard_map/dot_general | solution.py:187
  95.7 7.0 %all-to-all-start.2 = ((bf16[16,32,1280]{2,1,0:T(8,128)(2,1)}), bf16[16,32,1280]{2,1,0:T(8,128)(2,1)S(1)}, u32[]{:S(2)}, u32[]{:S(2)}) async-start(bf16[16,32,1280]{2,1,0:T(8,128)(2,1)} %bitcast.23), calls=%async_computation.2 | async-start | bytes 2621440 | tf_op jit(solution)/shard_map/all_to_all | solution.py:102
  102.8 1.6 %write_out.1 = bf16[512,1280]{1,0:T(8,128)(2,1)} custom-call(bf16[512,1280]{1,0:T(8,128)(2,1)S(1)} %bitcast.19), custom_call_target="tpu_custom_call" | custom-call | bytes 2621440 | tf_op jit(solution)/shard_map/write_out/pallas_call | solution.py:89
  104.4 28.8 %all-to-all-done.2.x_ref = bf16[16,32,1280]{2,1,0:T(8,128)(2,1)S(1)} async-done(((bf16[16,32,1280]{2,1,0:T(8,128)(2,1)}), bf16[16,32,1280]{2,1,0:T(8,128)(2,1)S(1)}, u32[]{:S(2)}, u32[]{:S(2)}) %all-to-all-start.2) | async-done | bytes 1310752 | tf_op jit(solution)/shard_map/all_to_all | solution.py:102
  133.2 1.7 %place.1 = bf16[16,32,1280]{2,1,0:T(8,128)(2,1)} custom-call(s32[16]{0:T(128)S(1)} %broadcast_add_fusion.1.comes_ref, bf16[16,32,1280]{2,1,0:T(8,128)(2,1)S(1)} %all-to-all-done.2.x_ref), custom_call_target="tpu_custom_call" | custom-call | bytes 2621440 | tf_op jit(solution)/shard_map/place/pallas_call | solution.py:127
  (39 shorter events, 3.8 us)
Async XLA Ops:
  0.6 1.7 %copy-start = (bf16[256,1280]{1,0:T(8,128)(2,1)S(1)}, bf16[256,1280]{1,0:T(8,128)(2,1)}, u32[]{:S(2)}) copy-start(bf16[256,1280]{1,0:T(8,128)(2,1)} %param.8) | copy-start | bytes 1966084
  3.9 36.7 %all-to-all-start.1 = ((bf16[16,32,1280]{2,1,0:T(8,128)(2,1)}), bf16[16,32,1280]{2,1,0:T(8,128)(2,1)S(1)}, u32[]{:S(2)}, u32[]{:S(2)}) async-start(bf16[16,32,1280]{2,1,0:T(8,128)(2,1)} %bitcast.5), calls=%async_computation.1 | async-start | bytes 2621440 | tf_op jit(solution)/shard_map/all_to_all | solution.py:102
  10.1 7.7 %collective-permute-start = (s32[1,256]{1,0:T(1,128)S(1)}, s32[1,256]{1,0:T(1,128)S(1)}, u32[]{:S(2)}, u32[]{:S(2)}) collective-permute-start(s32[1,256]{1,0:T(1,128)S(1)} %bitcast.25), channel_id=1, source_target_pairs={{0,1},{1,0},{2,3},{3,2},{4,5},{5,4},{6,7},{7,6},{8,9},{9,8},{10,11... | collective-permute-start | bytes 3080 | tf_op jit(solution)/shard_map/ppermute | solution.py:74
  11.9 68.3 %collective-permute-start.5 = (bf16[32,1280]{1,0:T(8,128)(2,1)}, bf16[32,1280]{1,0:T(8,128)(2,1)}, u32[]{:S(2)}, u32[]{:S(2)}) collective-permute-start(bf16[32,1280]{1,0:T(8,128)(2,1)} %get-tuple-element.9), channel_id=1, source_target_pairs={{1,0},{2,1},{3,2},{4,3},{5,4},{6,5},{7,6},{8,7},{9,8},{10,9},{11,1... | collective-permute-start | bytes 245768 | tf_op jit(solution)/shard_map/ppermute | solution.py:20
  14.3 65.9 %collective-permute-start.4 = (bf16[32,1280]{1,0:T(8,128)(2,1)}, bf16[32,1280]{1,0:T(8,128)(2,1)}, u32[]{:S(2)}, u32[]{:S(2)}) collective-permute-start(bf16[32,1280]{1,0:T(8,128)(2,1)} %get-tuple-element.10), channel_id=1, source_target_pairs={{0,1},{1,2},{2,3},{3,4},{4,5},{5,6},{6,7},{7,8},{8,9},{9,10},{10,1... | collective-permute-start | bytes 245768 | tf_op jit(solution)/shard_map/ppermute | solution.py:19
  17.8 3.7 %collective-permute-start.1 = (s32[2,256]{1,0:T(2,128)S(1)}, s32[2,256]{1,0:T(2,128)S(1)}, u32[]{:S(2)}, u32[]{:S(2)}) collective-permute-start(s32[2,256]{1,0:T(2,128)S(1)} %pad_add_fusion.3), channel_id=1, source_target_pairs={{0,2},{1,3},{2,0},{3,1},{4,6},{5,7},{6,4},{7,5},{8,10},{9,11},{10,... | collective-permute-start | bytes 6152 | tf_op jit(solution)/shard_map/ppermute | solution.py:74
  21.6 12.1 %collective-permute-start.2 = (s32[4,256]{1,0:T(4,128)S(1)}, s32[4,256]{1,0:T(4,128)S(1)}, u32[]{:S(2)}, u32[]{:S(2)}) collective-permute-start(s32[4,256]{1,0:T(4,128)S(1)} %pad_add_fusion.2), channel_id=1, source_target_pairs={{0,4},{1,5},{2,6},{3,7},{4,0},{5,1},{6,2},{7,3},{8,12},{9,13},{10,... | collective-permute-start | bytes 12296 | tf_op jit(solution)/shard_map/ppermute | solution.py:74
  40.5 7.6 %copy-start.2 = (s32[32768]{0:T(1024)S(1)}, s32[32768]{0:T(1024)}, u32[]{:S(2)}) copy-start(s32[32768]{0:T(1024)} %param.7) | copy-start | bytes 393220
  40.5 55.2 %all-to-all-start = ((bf16[16,32,1280]{2,1,0:T(8,128)(2,1)}), bf16[16,32,1280]{2,1,0:T(8,128)(2,1)S(1)}, u32[]{:S(2)}, u32[]{:S(2)}) async-start(bf16[16,32,1280]{2,1,0:T(8,128)(2,1)} %bitcast.22), calls=%async_computation | async-start | bytes 2621440 | tf_op jit(solution)/shard_map/all_to_all | solution.py:102
  45.8 29.2 %collective-permute-start.3 = (s32[8,256]{1,0:T(8,128)S(1)}, s32[8,256]{1,0:T(8,128)S(1)}, u32[]{:S(2)}, u32[]{:S(2)}) collective-permute-start(s32[8,256]{1,0:T(8,128)S(1)} %pad_add_fusion.1), channel_id=1, source_target_pairs={{0,8},{1,9},{2,10},{3,11},{4,12},{5,13},{6,14},{7,15},{8,0},{9,1},... | collective-permute-start | bytes 24584 | tf_op jit(solution)/shard_map/ppermute | solution.py:74
  80.2 2.5 %copy-start.1 = (bf16[2048,1280]{1,0:T(8,128)(2,1)S(1)}, bf16[2048,1280]{1,0:T(8,128)(2,1)}, u32[]{:S(2)}) copy-start(bf16[2048,1280]{1,0:T(8,128)(2,1)} %k_ref.1) | copy-start | bytes 15728644
  82.7 11.0 %copy-start.3 = (s32[512]{0:T(512)S(1)}, s32[512]{0:T(512)}, u32[]{:S(2)}) copy-start(s32[512]{0:T(512)} %fusion.13) | copy-start | bytes 6148
  82.7 11.0 %copy-start.5 = (pred[512]{0:T(512)(128)(4,1)S(1)}, pred[512]{0:T(512)(128)(4,1)}, u32[]{:S(2)}) copy-start(pred[512]{0:T(512)(128)(4,1)} %ge.13) | copy-start | bytes 1540
  95.7 37.4 %all-to-all-start.2 = ((bf16[16,32,1280]{2,1,0:T(8,128)(2,1)}), bf16[16,32,1280]{2,1,0:T(8,128)(2,1)S(1)}, u32[]{:S(2)}, u32[]{:S(2)}) async-start(bf16[16,32,1280]{2,1,0:T(8,128)(2,1)} %bitcast.23), calls=%async_computation.2 | async-start | bytes 2621440 | tf_op jit(solution)/shard_map/all_to_all | solution.py:102
  102.8 1.6 %copy-start.4 = (s32[16]{0:T(128)S(1)}, s32[16]{0:T(128)}, u32[]{:S(2)}) copy-start(s32[16]{0:T(128)} %get-tuple-element.7) | copy-start | bytes 196

commit v5 on v4

--- a/solution.py
+++ b/solution.py
@@ -63,19 +63,21 @@
     )(queries, docs, *fixed)
 
 
-def every_device(row, late):
+def every_device(row, after):
     peers, me = lax.axis_size("docs"), lax.axis_index("docs")
     if peers & (peers - 1):
-        return lax.all_gather(row, "docs", axis=0, tiled=False), late
-    held, step = row[None], 1
-    while step < peers:
-        if 2 * step == peers:
-            held, late = lax.optimization_barrier((held, late))
+        return lax.all_gather(row, "docs", axis=0, tiled=False), after
+    step = max(1, peers // 4)
+    apart = list(range(0, peers, step))
+    rows = [lax.ppermute(row, "docs", [(i, i ^ a) for i in range(peers)]) if a else row for a in apart]
+    held, after = lax.optimization_barrier((jnp.stack(rows), after))
+    while step > 1:
+        step //= 2
         held = jnp.concatenate([held, lax.ppermute(held, "docs", [(i, i ^ step) for i in range(peers)])], axis=0)
-        step *= 2
-    label = jnp.arange(peers, dtype=jnp.int32)
-    pick = (label ^ me)[:, None] == label[None, :]
-    return jnp.sum(jnp.where(pick[:, :, None], held[None], 0), axis=1), late
+        apart = apart + [a ^ step for a in apart]
+    source = jnp.array(apart, dtype=jnp.int32) ^ me
+    pick = jnp.arange(peers, dtype=jnp.int32)[:, None] == source[None, :]
+    return jnp.sum(jnp.where(pick[:, :, None], held[None], 0), axis=1), after
 
 
 def copy_kernel(x_ref, o_ref):
@@ -156,8 +158,8 @@
         out = jnp.dot(table, images, preferred_element_type=jnp.float32).astype(jnp.bfloat16)
         return out.reshape(members, cap, feature)
 
-    every, arrived = every_device(packed, exchange(buckets(owner)))
-    queries = arrived.reshape(members * cap, feature)
+    every, leaving = every_device(packed, buckets(owner))
+    queries = exchange(leaving).reshape(members * cap, feature)
     loaded_images = write_out(exchange(buckets(shard)).reshape(members * cap, feature))
     before, after = halo_of(sentences)
 

time: 136 us -> 119 us (0.88)
  waiting for transfers between devices: 76.2 us -> 59.4 us
    ppermute x4 -> x2, waiting for transfers between devices: 40.5 us -> 3.18 us  [every_device(): lax.ppermute(held, 'docs', [(i, i ^ step) for i in range(peers)])]
    all_to_all x3, waiting for transfers between devices: 35.7 us -> 55.5 us  [exchange(): return lax.all_to_all(x, 'docs', split_axis=0, concat_axis=0, tiled=True)]
    ppermute x0 -> x3, starting transfers between devices: none -> 4.05 us  [every_device(): lax.ppermute(row, 'docs', [(i, i ^ a) for i in range(peers)])]
    ppermute x4 -> x2, starting transfers between devices: 4.55 us -> 2.59 us  [every_device(): lax.ppermute(held, 'docs', [(i, i ^ step) for i in range(peers)])]
    all_to_all x3, starting transfers between devices: 18.5 us -> 16.6 us  [exchange(): return lax.all_to_all(x, 'docs', split_axis=0, concat_axis=0, tiled=True)]
  transfers between devices with their start and end apart: 9 -> 10, of which waited for: 5 -> 7; matrix products, arithmetic and copies ran while one was open for 8% -> 10% of each run, Pallas kernels for 9% -> 11%
where the time goes in v5:
time: 119 us; the launch traced here: 118 us
  waiting for transfers between devices  59.4 us (50%)
  starting transfers between devices  27.6 us (23%)
  Pallas kernels  14.4 us (12%)
  local copies, waits for them, and re-layouts  6.02 us (5%)
  matrix products  5.27 us (4%)
  other arithmetic  4.88 us (4%)
    all_to_all x3, waiting for transfers between devices, exchange(): return lax.all_to_all(x, 'docs', split_axis=0, concat_axis=0, tiled=True)  55.5 us
    all_to_all x3, starting transfers between devices, exchange(): return lax.all_to_all(x, 'docs', split_axis=0, concat_axis=0, tiled=True)  16.6 us
    pallas_call x1, Pallas kernels, attend(): pl.pallas_call(functools.partial(attend_kernel, feature ** (-0.5)), grid=...  11 us
    ppermute x3, starting transfers between devices, every_device(): lax.ppermute(row, 'docs', [(i, i ^ a) for i in range(peers)])  4.05 us
    ppermute x2, waiting for transfers between devices, every_device(): lax.ppermute(held, 'docs', [(i, i ^ step) for i in range(peers)])  3.18 us
    dot_general x2, matrix products, buckets(): jnp.dot(table, images, preferred_element_type=jnp.float32)  3.15 us
    ppermute x2, starting transfers between devices, every_device(): lax.ppermute(held, 'docs', [(i, i ^ step) for i in range(peers)])  2.59 us
    unnamed x14, local copies, waits for them, and re-layouts  2.51 us
  transfers between devices with their start and end apart: 10, of which 7 were waited for; matrix products, arithmetic and copies ran while one was open for 10% of the time, Pallas kernels for 11%

profile of v5, /device:TPU:14, one launch (start us, length us, event | category | flops | bytes accessed | tf_op | source)
XLA Modules:
  0.0 118.3 jit_solution(4425123144569000967)
XLA Ops:
  0.6 0.9 convert_reduce_fusion
  2.3 1.6 %collective-permute-start.2 = (s32[256]{0:T(256)S(1)}, s32[256]{0:T(256)S(1)}, u32[]{:S(2)}, u32[]{:S(2)}) collective-permute-start(s32[256]{0:T(256)S(1)} %get-tuple-element.15), channel_id=1, source_target_pairs={{0,12},{1,13},{2,14},{3,15},{4,8},{5,9},{6,10},{7,11},{8,4},{9,5},... | collective-permute-start | bytes 3080 | tf_op jit(solution)/shard_map/ppermute | solution.py:72
  3.9 1.2 %collective-permute-start.1 = (s32[256]{0:T(256)S(1)}, s32[256]{0:T(256)S(1)}, u32[]{:S(2)}, u32[]{:S(2)}) collective-permute-start(s32[256]{0:T(256)S(1)} %get-tuple-element.15), channel_id=1, source_target_pairs={{0,8},{1,9},{2,10},{3,11},{4,12},{5,13},{6,14},{7,15},{8,0},{9,1},... | collective-permute-start | bytes 3080 | tf_op jit(solution)/shard_map/ppermute | solution.py:72
  5.1 1.2 %collective-permute-start = (s32[256]{0:T(256)S(1)}, s32[256]{0:T(256)S(1)}, u32[]{:S(2)}, u32[]{:S(2)}) collective-permute-start(s32[256]{0:T(256)S(1)} %get-tuple-element.15), channel_id=1, source_target_pairs={{0,4},{1,5},{2,6},{3,7},{4,0},{5,1},{6,2},{7,3},{8,12},{9,13},{10,... | collective-permute-start | bytes 3080 | tf_op jit(solution)/shard_map/ppermute | solution.py:72
  6.4 1.6 %convolution_convert_fusion.1 = bf16[512,1280]{1,0:T(8,128)(2,1)} fusion(bf16[256,1280]{1,0:T(8,128)(2,1)S(1)} %copy-done, s32[256]{0:T(256)S(1)} %get-tuple-element.14), kind=kOutput, calls=%fused_computation.3 | convolution fusion | flops 336330752 | bytes 1967104 | tf_op jit(solution)/shard_map/dot_general | solution.py:158
  8.7 6.4 %all-to-all-start.1 = ((bf16[16,32,1280]{2,1,0:T(8,128)(2,1)}), bf16[16,32,1280]{2,1,0:T(8,128)(2,1)S(1)}, u32[]{:S(2)}, u32[]{:S(2)}) async-start(bf16[16,32,1280]{2,1,0:T(8,128)(2,1)} %bitcast.8), calls=%async_computation.1 | async-start | bytes 2621440 | tf_op jit(solution)/shard_map/all_to_all | solution.py:104
  15.1 1.6 %fusion.19 = (bf16[32,1280]{1,0:T(8,128)(2,1)}, bf16[32,1280]{1,0:T(8,128)(2,1)}) fusion(bf16[2048,1280]{1,0:T(8,128)(2,1)} %k_ref.1), kind=kLoop, calls=%fused_computation.64 | loop fusion | bytes 327680 | tf_op jit(solution)/shard_map/slice | solution.py:20
  16.7 2.2 %collective-permute-start.6 = (bf16[32,1280]{1,0:T(8,128)(2,1)}, bf16[32,1280]{1,0:T(8,128)(2,1)}, u32[]{:S(2)}, u32[]{:S(2)}) collective-permute-start(bf16[32,1280]{1,0:T(8,128)(2,1)} %get-tuple-element.9), channel_id=1, source_target_pairs={{1,0},{2,1},{3,2},{4,3},{5,4},{6,5},{7,6},{8,7},{9,8},{10,9},{11,1... | collective-permute-start | bytes 245768 | tf_op jit(solution)/shard_map/ppermute | solution.py:20
  18.9 2.1 %collective-permute-start.5 = (bf16[32,1280]{1,0:T(8,128)(2,1)}, bf16[32,1280]{1,0:T(8,128)(2,1)}, u32[]{:S(2)}, u32[]{:S(2)}) collective-permute-start(bf16[32,1280]{1,0:T(8,128)(2,1)} %get-tuple-element.10), channel_id=1, source_target_pairs={{0,1},{1,2},{2,3},{3,4},{4,5},{5,6},{6,7},{7,8},{8,9},{9,10},{10,1... | collective-permute-start | bytes 245768 | tf_op jit(solution)/shard_map/ppermute | solution.py:19
  21.1 1.6 %convolution_convert_fusion.2 = bf16[512,1280]{1,0:T(8,128)(2,1)} fusion(bf16[256,1280]{1,0:T(8,128)(2,1)S(1)} %copy-done, s32[256]{0:T(256)S(1)} %get-tuple-element.16), kind=kOutput, calls=%fused_computation.4 | convolution fusion | flops 336330752 | bytes 1967104 | tf_op jit(solution)/shard_map/dot_general | solution.py:158
  22.7 1.3 %collective-permute-start.3 = (s32[4,256]{1,0:T(4,128)S(1)}, s32[4,256]{1,0:T(4,128)S(1)}, u32[]{:S(2)}, u32[]{:S(2)}) collective-permute-start(s32[4,256]{1,0:T(4,128)S(1)} %pad_add_fusion.2), channel_id=1, source_target_pairs={{0,2},{1,3},{2,0},{3,1},{4,6},{5,7},{6,4},{7,5},{8,10},{9,11},{10,... | collective-permute-start | bytes 12296 | tf_op jit(solution)/shard_map/ppermute | solution.py:76
  23.9 2.4 %collective-permute-done.3 = s32[4,256]{1,0:T(4,128)S(1)} collective-permute-done((s32[4,256]{1,0:T(4,128)S(1)}, s32[4,256]{1,0:T(4,128)S(1)}, u32[]{:S(2)}, u32[]{:S(2)}) %collective-permute-start.3) | collective-permute-done | bytes 4128 | tf_op jit(solution)/shard_map/ppermute | solution.py:76
  26.4 1.3 %collective-permute-start.4 = (s32[8,256]{1,0:T(8,128)S(1)}, s32[8,256]{1,0:T(8,128)S(1)}, u32[]{:S(2)}, u32[]{:S(2)}) collective-permute-start(s32[8,256]{1,0:T(8,128)S(1)} %pad_add_fusion.1), channel_id=1, source_target_pairs={{0,1},{1,0},{2,3},{3,2},{4,5},{5,4},{6,7},{7,6},{8,9},{9,8},{10,11... | collective-permute-start | bytes 24584 | tf_op jit(solution)/shard_map/ppermute | solution.py:76
  28.7 16.8 %all-to-all-done.1 = bf16[16,32,1280]{2,1,0:T(8,128)(2,1)S(1)} async-done(((bf16[16,32,1280]{2,1,0:T(8,128)(2,1)}), bf16[16,32,1280]{2,1,0:T(8,128)(2,1)S(1)}, u32[]{:S(2)}, u32[]{:S(2)}) %all-to-all-start.1) | async-done | bytes 1310752 | tf_op jit(solution)/shard_map/all_to_all | solution.py:104
  45.5 5.1 %all-to-all-start = ((bf16[16,32,1280]{2,1,0:T(8,128)(2,1)}), bf16[16,32,1280]{2,1,0:T(8,128)(2,1)S(1)}, u32[]{:S(2)}, u32[]{:S(2)}) async-start(bf16[16,32,1280]{2,1,0:T(8,128)(2,1)} %bitcast.25), calls=%async_computation | async-start | bytes 2621440 | tf_op jit(solution)/shard_map/all_to_all | solution.py:104
  52.7 1.4 %select_reduce_fusion = s32[512]{0:T(512)} fusion(s32[2048]{0:T(1024)S(1)} %dynamic_slice.9, s32[512]{0:T(512)S(1)} %sub.27), kind=kLoop, calls=%fused_computation | loop fusion | flops 3145216 | bytes 12288 | tf_op jit(solution)/shard_map/reduce_max | solution.py:177
  55.6 2.5 %copy-done.1 = bf16[2048,1280]{1,0:T(8,128)(2,1)S(1)} copy-done((bf16[2048,1280]{1,0:T(8,128)(2,1)S(1)}, bf16[2048,1280]{1,0:T(8,128)(2,1)}, u32[]{:S(2)}) %copy-start.1) | copy-done | bytes 5242904
  58.1 11.0 %attend.1 = bf16[512,1280]{1,0:T(8,128)(2,1)S(1)} custom-call(bf16[512,1280]{1,0:T(8,128)(2,1)S(1)} %bitcast.23, s32[512,1]{1,0:T(8,128)S(1)} %copy.10.doc_ref, bf16[2048,1280]{1,0:T(8,128)(2,1)S(1)} %copy-done.1, bf16[32,1280]{1,0:T(8,128)(2,1)} %collective-permute-done.5.before_ref, bf16[32,1280]{1,0:T(8,128)(2,1)} %collective-permute-done.6.after_ref, ...), custom_call_target="tpu_custom_call" | custom-call | flops 5368709120 | bytes 7864320 | tf_op jit(solution)/shard_map/attend/pallas_call | solution.py:48
  69.2 2.0 %convolution_convert_fusion = bf16[512,1280]{1,0:T(8,128)(2,1)} fusion(bf16[512,1280]{1,0:T(8,128)(2,1)S(1)} %attend.1, s32[512]{0:T(512)S(1)} %copy-done.3, pred[512]{0:T(512)(128)(4,1)S(1)} %copy-done.5), kind=kOutput, calls=%fused_computation.2 | convolution fusion | flops 672268288 | bytes 2624000 | tf_op jit(solution)/shard_map/dot_general | solution.py:189
  71.1 9.9 %all-to-all-done = bf16[16,32,1280]{2,1,0:T(8,128)(2,1)S(1)} async-done(((bf16[16,32,1280]{2,1,0:T(8,128)(2,1)}), bf16[16,32,1280]{2,1,0:T(8,128)(2,1)S(1)}, u32[]{:S(2)}, u32[]{:S(2)}) %all-to-all-start) | async-done | bytes 1310752 | tf_op jit(solution)/shard_map/all_to_all | solution.py:104
  81.0 5.1 %all-to-all-start.2 = ((bf16[16,32,1280]{2,1,0:T(8,128)(2,1)}), bf16[16,32,1280]{2,1,0:T(8,128)(2,1)S(1)}, u32[]{:S(2)}, u32[]{:S(2)}) async-start(bf16[16,32,1280]{2,1,0:T(8,128)(2,1)} %bitcast.26), calls=%async_computation.2 | async-start | bytes 2621440 | tf_op jit(solution)/shard_map/all_to_all | solution.py:104
  86.2 1.6 %write_out.1 = bf16[512,1280]{1,0:T(8,128)(2,1)} custom-call(bf16[512,1280]{1,0:T(8,128)(2,1)S(1)} %bitcast.22), custom_call_target="tpu_custom_call" | custom-call | bytes 2621440 | tf_op jit(solution)/shard_map/write_out/pallas_call | solution.py:91
  87.8 28.8 %all-to-all-done.2.x_ref = bf16[16,32,1280]{2,1,0:T(8,128)(2,1)S(1)} async-done(((bf16[16,32,1280]{2,1,0:T(8,128)(2,1)}), bf16[16,32,1280]{2,1,0:T(8,128)(2,1)S(1)}, u32[]{:S(2)}, u32[]{:S(2)}) %all-to-all-start.2) | async-done | bytes 1310752 | tf_op jit(solution)/shard_map/all_to_all | solution.py:104
  116.6 1.7 %place.1 = bf16[16,32,1280]{2,1,0:T(8,128)(2,1)} custom-call(s32[16]{0:T(128)S(1)} %broadcast_add_fusion.1.comes_ref, bf16[16,32,1280]{2,1,0:T(8,128)(2,1)S(1)} %all-to-all-done.2.x_ref), custom_call_target="tpu_custom_call" | custom-call | bytes 2621440 | tf_op jit(solution)/shard_map/place/pallas_call | solution.py:129
  (42 shorter events, 6.1 us)
Async XLA Ops:
  0.6 5.7 %copy-start = (bf16[256,1280]{1,0:T(8,128)(2,1)S(1)}, bf16[256,1280]{1,0:T(8,128)(2,1)}, u32[]{:S(2)}) copy-start(bf16[256,1280]{1,0:T(8,128)(2,1)} %param.9) | copy-start | bytes 1966084
  2.3 5.6 %collective-permute-start.2 = (s32[256]{0:T(256)S(1)}, s32[256]{0:T(256)S(1)}, u32[]{:S(2)}, u32[]{:S(2)}) collective-permute-start(s32[256]{0:T(256)S(1)} %get-tuple-element.15), channel_id=1, source_target_pairs={{0,12},{1,13},{2,14},{3,15},{4,8},{5,9},{6,10},{7,11},{8,4},{9,5},... | collective-permute-start | bytes 3080 | tf_op jit(solution)/shard_map/ppermute | solution.py:72
  3.9 4.5 %collective-permute-start.1 = (s32[256]{0:T(256)S(1)}, s32[256]{0:T(256)S(1)}, u32[]{:S(2)}, u32[]{:S(2)}) collective-permute-start(s32[256]{0:T(256)S(1)} %get-tuple-element.15), channel_id=1, source_target_pairs={{0,8},{1,9},{2,10},{3,11},{4,12},{5,13},{6,14},{7,15},{8,0},{9,1},... | collective-permute-start | bytes 3080 | tf_op jit(solution)/shard_map/ppermute | solution.py:72
  5.1 3.6 %collective-permute-start = (s32[256]{0:T(256)S(1)}, s32[256]{0:T(256)S(1)}, u32[]{:S(2)}, u32[]{:S(2)}) collective-permute-start(s32[256]{0:T(256)S(1)} %get-tuple-element.15), channel_id=1, source_target_pairs={{0,4},{1,5},{2,6},{3,7},{4,0},{5,1},{6,2},{7,3},{8,12},{9,13},{10,... | collective-permute-start | bytes 3080 | tf_op jit(solution)/shard_map/ppermute | solution.py:72
  8.7 12.4 %copy-start.6 = (s32[16]{0:T(128)S(1)}, s32[16]{0:T(128)}, u32[]{:S(2)}) copy-start(s32[16]{0:T(128)} %constant.95.clone) | copy-start | bytes 196
  8.7 36.8 %all-to-all-start.1 = ((bf16[16,32,1280]{2,1,0:T(8,128)(2,1)}), bf16[16,32,1280]{2,1,0:T(8,128)(2,1)S(1)}, u32[]{:S(2)}, u32[]{:S(2)}) async-start(bf16[16,32,1280]{2,1,0:T(8,128)(2,1)} %bitcast.8), calls=%async_computation.1 | async-start | bytes 2621440 | tf_op jit(solution)/shard_map/all_to_all | solution.py:104
  15.1 12.6 %copy-start.2 = (s32[32768]{0:T(1024)S(1)}, s32[32768]{0:T(1024)}, u32[]{:S(2)}) copy-start(s32[32768]{0:T(1024)} %param.8) | copy-start | bytes 393220
  16.7 38.9 %collective-permute-start.6 = (bf16[32,1280]{1,0:T(8,128)(2,1)}, bf16[32,1280]{1,0:T(8,128)(2,1)}, u32[]{:S(2)}, u32[]{:S(2)}) collective-permute-start(bf16[32,1280]{1,0:T(8,128)(2,1)} %get-tuple-element.9), channel_id=1, source_target_pairs={{1,0},{2,1},{3,2},{4,3},{5,4},{6,5},{7,6},{8,7},{9,8},{10,9},{11,1... | collective-permute-start | bytes 245768 | tf_op jit(solution)/shard_map/ppermute | solution.py:20
  18.9 36.7 %collective-permute-start.5 = (bf16[32,1280]{1,0:T(8,128)(2,1)}, bf16[32,1280]{1,0:T(8,128)(2,1)}, u32[]{:S(2)}, u32[]{:S(2)}) collective-permute-start(bf16[32,1280]{1,0:T(8,128)(2,1)} %get-tuple-element.10), channel_id=1, source_target_pairs={{0,1},{1,2},{2,3},{3,4},{4,5},{5,6},{6,7},{7,8},{8,9},{9,10},{10,1... | collective-permute-start | bytes 245768 | tf_op jit(solution)/shard_map/ppermute | solution.py:19
  22.7 3.7 %collective-permute-start.3 = (s32[4,256]{1,0:T(4,128)S(1)}, s32[4,256]{1,0:T(4,128)S(1)}, u32[]{:S(2)}, u32[]{:S(2)}) collective-permute-start(s32[4,256]{1,0:T(4,128)S(1)} %pad_add_fusion.2), channel_id=1, source_target_pairs={{0,2},{1,3},{2,0},{3,1},{4,6},{5,7},{6,4},{7,5},{8,10},{9,11},{10,... | collective-permute-start | bytes 12296 | tf_op jit(solution)/shard_map/ppermute | solution.py:76
  26.4 2.1 %collective-permute-start.4 = (s32[8,256]{1,0:T(8,128)S(1)}, s32[8,256]{1,0:T(8,128)S(1)}, u32[]{:S(2)}, u32[]{:S(2)}) collective-permute-start(s32[8,256]{1,0:T(8,128)S(1)} %pad_add_fusion.1), channel_id=1, source_target_pairs={{0,1},{1,0},{2,3},{3,2},{4,5},{5,4},{6,7},{7,6},{8,9},{9,8},{10,11... | collective-permute-start | bytes 24584 | tf_op jit(solution)/shard_map/ppermute | solution.py:76
  45.5 35.5 %all-to-all-start = ((bf16[16,32,1280]{2,1,0:T(8,128)(2,1)}), bf16[16,32,1280]{2,1,0:T(8,128)(2,1)S(1)}, u32[]{:S(2)}, u32[]{:S(2)}) async-start(bf16[16,32,1280]{2,1,0:T(8,128)(2,1)} %bitcast.25), calls=%async_computation | async-start | bytes 2621440 | tf_op jit(solution)/shard_map/all_to_all | solution.py:104
  55.6 2.5 %copy-start.1 = (bf16[2048,1280]{1,0:T(8,128)(2,1)S(1)}, bf16[2048,1280]{1,0:T(8,128)(2,1)}, u32[]{:S(2)}) copy-start(bf16[2048,1280]{1,0:T(8,128)(2,1)} %k_ref.1) | copy-start | bytes 15728644
  58.1 11.0 %copy-start.3 = (s32[512]{0:T(512)S(1)}, s32[512]{0:T(512)}, u32[]{:S(2)}) copy-start(s32[512]{0:T(512)} %fusion.13) | copy-start | bytes 6148
  58.1 11.0 %copy-start.5 = (pred[512]{0:T(512)(128)(4,1)S(1)}, pred[512]{0:T(512)(128)(4,1)}, u32[]{:S(2)}) copy-start(pred[512]{0:T(512)(128)(4,1)} %ge.13) | copy-start | bytes 1540
  81.0 5.2 %copy-start.4 = (s32[16]{0:T(128)S(1)}, s32[16]{0:T(128)}, u32[]{:S(2)}) copy-start(s32[16]{0:T(128)} %get-tuple-element.7) | copy-start | bytes 196
  81.0 35.6 %all-to-all-start.2 = ((bf16[16,32,1280]{2,1,0:T(8,128)(2,1)}), bf16[16,32,1280]{2,1,0:T(8,128)(2,1)S(1)}, u32[]{:S(2)}, u32[]{:S(2)}) async-start(bf16[16,32,1280]{2,1,0:T(8,128)(2,1)} %bitcast.26), calls=%async_computation.2 | async-start | bytes 2621440 | tf_op jit(solution)/shard_map/all_to_all | solution.py:104

commit v6 on v5

--- a/solution.py
+++ b/solution.py
@@ -67,14 +67,15 @@
     peers, me = lax.axis_size("docs"), lax.axis_index("docs")
     if peers & (peers - 1):
         return lax.all_gather(row, "docs", axis=0, tiled=False), after
-    step = max(1, peers // 4)
-    apart = list(range(0, peers, step))
-    rows = [lax.ppermute(row, "docs", [(i, i ^ a) for i in range(peers)]) if a else row for a in apart]
-    held, after = lax.optimization_barrier((jnp.stack(rows), after))
-    while step > 1:
+    step = peers // 2
+    held, after = lax.optimization_barrier((row[None], after))
+    apart = [0]
+    while step:
+        held = jnp.concatenate([held, lax.ppermute(held, "docs", [(i, i ^ step) for i in range(peers)])], axis=0)
+        if len(apart) == 1:
+            held, after = lax.optimization_barrier((held, after))
+        apart = apart + [a ^ step for a in apart]
         step //= 2
-        held = jnp.concatenate([held, lax.ppermute(held, "docs", [(i, i ^ step) for i in range(peers)])], axis=0)
-        apart = apart + [a ^ step for a in apart]
     source = jnp.array(apart, dtype=jnp.int32) ^ me
     pick = jnp.arange(peers, dtype=jnp.int32)[:, None] == source[None, :]
     return jnp.sum(jnp.where(pick[:, :, None], held[None], 0), axis=1), after

time: 119 us -> 119 us (level)
  starting transfers between devices: 27.6 us -> 24 us
  waiting for transfers between devices: 59.4 us -> 62.6 us
    ppermute x2 -> x4, waiting for transfers between devices: 3.18 us -> 21.9 us  [every_device(): lax.ppermute(held, 'docs', [(i, i ^ step) for i in range(peers)])]
    all_to_all x3, waiting for transfers between devices: 55.5 us -> 40.7 us  [exchange(): return lax.all_to_all(x, 'docs', split_axis=0, concat_axis=0, tiled=True)]
    ppermute x3 -> x0, starting transfers between devices: 4.05 us -> none  [every_device(): lax.ppermute(row, 'docs', [(i, i ^ a) for i in range(peers)])]
    ppermute x2 -> x4, starting transfers between devices: 2.59 us -> 3.22 us  [every_device(): lax.ppermute(held, 'docs', [(i, i ^ step) for i in range(peers)])]
  transfers between devices with their start and end apart: 10 -> 9, of which waited for: 7 -> 7; matrix products, arithmetic and copies ran while one was open for 10% -> 9% of each run, Pallas kernels for 11% -> 11%
where the time goes in v6:
time: 119 us; the launch traced here: 118 us
  waiting for transfers between devices  62.6 us (53%)
  starting transfers between devices  24 us (20%)
  Pallas kernels  14.4 us (12%)
  local copies, waits for them, and re-layouts  5.96 us (5%)
  matrix products  5.25 us (4%)
  other arithmetic  4.81 us (4%)
    all_to_all x3, waiting for transfers between devices, exchange(): return lax.all_to_all(x, 'docs', split_axis=0, concat_axis=0, tiled=True)  40.7 us
    ppermute x4, waiting for transfers between devices, every_device(): lax.ppermute(held, 'docs', [(i, i ^ step) for i in range(peers)])  21.9 us
    all_to_all x3, starting transfers between devices, exchange(): return lax.all_to_all(x, 'docs', split_axis=0, concat_axis=0, tiled=True)  16.5 us
    pallas_call x1, Pallas kernels, attend(): pl.pallas_call(functools.partial(attend_kernel, feature ** (-0.5)), grid=...  11 us
    ppermute x4, starting transfers between devices, every_device(): lax.ppermute(held, 'docs', [(i, i ^ step) for i in range(peers)])  3.22 us
    dot_general x2, matrix products, buckets(): jnp.dot(table, images, preferred_element_type=jnp.float32)  3.15 us
    unnamed x14, local copies, waits for them, and re-layouts  2.51 us
  transfers between devices with their start and end apart: 9, of which 7 were waited for; matrix products, arithmetic and copies ran while one was open for 9% of the time, Pallas kernels for 11%

profile of v6, /device:TPU:14, one launch (start us, length us, event | category | flops | bytes accessed | tf_op | source)
XLA Modules:
  0.0 117.8 jit_solution(10377136987999769574)
XLA Ops:
  0.6 0.9 convert_reduce_fusion
  2.3 1.6 %convolution_convert_fusion.1 = bf16[512,1280]{1,0:T(8,128)(2,1)} fusion(bf16[256,1280]{1,0:T(8,128)(2,1)S(1)} %copy-done, s32[256]{0:T(256)S(1)} %get-tuple-element.18), kind=kOutput, calls=%fused_computation.3 | convolution fusion | flops 336330752 | bytes 1967104 | tf_op jit(solution)/shard_map/dot_general | solution.py:159
  3.9 2.6 %collective-permute-start = (s32[1,256]{1,0:T(1,128)S(1)}, s32[1,256]{1,0:T(1,128)S(1)}, u32[]{:S(2)}, u32[]{:S(2)}) collective-permute-start(s32[1,256]{1,0:T(1,128)S(1)} %bitcast.28), channel_id=1, source_target_pairs={{0,8},{1,9},{2,10},{3,11},{4,12},{5,13},{6,14},{7,15},{8,0},{9,1},... | collective-permute-start | bytes 3080 | tf_op jit(solution)/shard_map/ppermute | solution.py:74
  6.5 1.9 %collective-permute-done = s32[1,256]{1,0:T(1,128)S(1)} collective-permute-done((s32[1,256]{1,0:T(1,128)S(1)}, s32[1,256]{1,0:T(1,128)S(1)}, u32[]{:S(2)}, u32[]{:S(2)}) %collective-permute-start) | collective-permute-done | bytes 1056 | tf_op jit(solution)/shard_map/ppermute | solution.py:74
  8.4 6.2 %all-to-all-start.1 = ((bf16[16,32,1280]{2,1,0:T(8,128)(2,1)}), bf16[16,32,1280]{2,1,0:T(8,128)(2,1)S(1)}, u32[]{:S(2)}, u32[]{:S(2)}) async-start(bf16[16,32,1280]{2,1,0:T(8,128)(2,1)} %bitcast.5), calls=%async_computation.1 | async-start | bytes 2621440 | tf_op jit(solution)/shard_map/all_to_all | solution.py:105
  14.6 1.6 %fusion.19 = (bf16[32,1280]{1,0:T(8,128)(2,1)}, bf16[32,1280]{1,0:T(8,128)(2,1)}) fusion(bf16[2048,1280]{1,0:T(8,128)(2,1)} %k_ref.1), kind=kLoop, calls=%fused_computation.65 | loop fusion | bytes 327680 | tf_op jit(solution)/shard_map/slice | solution.py:20
  16.3 2.2 %collective-permute-start.5 = (bf16[32,1280]{1,0:T(8,128)(2,1)}, bf16[32,1280]{1,0:T(8,128)(2,1)}, u32[]{:S(2)}, u32[]{:S(2)}) collective-permute-start(bf16[32,1280]{1,0:T(8,128)(2,1)} %get-tuple-element.13), channel_id=1, source_target_pairs={{1,0},{2,1},{3,2},{4,3},{5,4},{6,5},{7,6},{8,7},{9,8},{10,9},{11,1... | collective-permute-start | bytes 245768 | tf_op jit(solution)/shard_map/ppermute | solution.py:20
  18.5 2.1 %collective-permute-start.4 = (bf16[32,1280]{1,0:T(8,128)(2,1)}, bf16[32,1280]{1,0:T(8,128)(2,1)}, u32[]{:S(2)}, u32[]{:S(2)}) collective-permute-start(bf16[32,1280]{1,0:T(8,128)(2,1)} %get-tuple-element.14), channel_id=1, source_target_pairs={{0,1},{1,2},{2,3},{3,4},{4,5},{5,6},{6,7},{7,8},{8,9},{9,10},{10,1... | collective-permute-start | bytes 245768 | tf_op jit(solution)/shard_map/ppermute | solution.py:19
  20.6 1.6 %convolution_convert_fusion.2 = bf16[512,1280]{1,0:T(8,128)(2,1)} fusion(bf16[256,1280]{1,0:T(8,128)(2,1)S(1)} %copy-done, s32[256]{0:T(256)S(1)} %get-tuple-element.20), kind=kOutput, calls=%fused_computation.4 | convolution fusion | flops 336330752 | bytes 1967104 | tf_op jit(solution)/shard_map/dot_general | solution.py:159
  22.7 15.3 %collective-permute-done.1 = s32[2,256]{1,0:T(2,128)S(1)} collective-permute-done((s32[2,256]{1,0:T(2,128)S(1)}, s32[2,256]{1,0:T(2,128)S(1)}, u32[]{:S(2)}, u32[]{:S(2)}) %collective-permute-start.1) | collective-permute-done | bytes 2080 | tf_op jit(solution)/shard_map/ppermute | solution.py:74
  38.1 3.6 %collective-permute-done.2 = s32[4,256]{1,0:T(4,128)S(1)} collective-permute-done((s32[4,256]{1,0:T(4,128)S(1)}, s32[4,256]{1,0:T(4,128)S(1)}, u32[]{:S(2)}, u32[]{:S(2)}) %collective-permute-start.2) | collective-permute-done | bytes 4128 | tf_op jit(solution)/shard_map/ppermute | solution.py:74
  41.9 1.1 collective-permute-done.3
  43.1 1.9 %all-to-all-done.1 = bf16[16,32,1280]{2,1,0:T(8,128)(2,1)S(1)} async-done(((bf16[16,32,1280]{2,1,0:T(8,128)(2,1)}), bf16[16,32,1280]{2,1,0:T(8,128)(2,1)S(1)}, u32[]{:S(2)}, u32[]{:S(2)}) %all-to-all-start.1) | async-done | bytes 1310752 | tf_op jit(solution)/shard_map/all_to_all | solution.py:105
  45.0 5.1 %all-to-all-start = ((bf16[16,32,1280]{2,1,0:T(8,128)(2,1)}), bf16[16,32,1280]{2,1,0:T(8,128)(2,1)S(1)}, u32[]{:S(2)}, u32[]{:S(2)}) async-start(bf16[16,32,1280]{2,1,0:T(8,128)(2,1)} %bitcast.22), calls=%async_computation | async-start | bytes 2621440 | tf_op jit(solution)/shard_map/all_to_all | solution.py:105
  52.1 1.4 %select_reduce_fusion = s32[512]{0:T(512)} fusion(s32[2048]{0:T(1024)S(1)} %dynamic_slice.9, s32[512]{0:T(512)S(1)} %sub.27), kind=kLoop, calls=%fused_computation | loop fusion | flops 3145216 | bytes 12288 | tf_op jit(solution)/shard_map/reduce_max | solution.py:178
  54.2 0.8 copy.10.doc_ref
  55.0 2.5 %copy-done.1 = bf16[2048,1280]{1,0:T(8,128)(2,1)S(1)} copy-done((bf16[2048,1280]{1,0:T(8,128)(2,1)S(1)}, bf16[2048,1280]{1,0:T(8,128)(2,1)}, u32[]{:S(2)}) %copy-start.1) | copy-done | bytes 5242904
  57.5 11.0 %attend.1 = bf16[512,1280]{1,0:T(8,128)(2,1)S(1)} custom-call(bf16[512,1280]{1,0:T(8,128)(2,1)S(1)} %bitcast.20, s32[512,1]{1,0:T(8,128)S(1)} %copy.10.doc_ref, bf16[2048,1280]{1,0:T(8,128)(2,1)S(1)} %copy-done.1, bf16[32,1280]{1,0:T(8,128)(2,1)} %collective-permute-done.4.before_ref, bf16[32,1280]{1,0:T(8,128)(2,1)} %collective-permute-done.5.after_ref, ...), custom_call_target="tpu_custom_call" | custom-call | flops 5368709120 | bytes 7864320 | tf_op jit(solution)/shard_map/attend/pallas_call | solution.py:48
  68.6 2.0 %convolution_convert_fusion = bf16[512,1280]{1,0:T(8,128)(2,1)} fusion(bf16[512,1280]{1,0:T(8,128)(2,1)S(1)} %attend.1, s32[512]{0:T(512)S(1)} %copy-done.3, pred[512]{0:T(512)(128)(4,1)S(1)} %copy-done.5), kind=kOutput, calls=%fused_computation.2 | convolution fusion | flops 672268288 | bytes 2624000 | tf_op jit(solution)/shard_map/dot_general | solution.py:190
  70.5 10.0 %all-to-all-done = bf16[16,32,1280]{2,1,0:T(8,128)(2,1)S(1)} async-done(((bf16[16,32,1280]{2,1,0:T(8,128)(2,1)}), bf16[16,32,1280]{2,1,0:T(8,128)(2,1)S(1)}, u32[]{:S(2)}, u32[]{:S(2)}) %all-to-all-start) | async-done | bytes 1310752 | tf_op jit(solution)/shard_map/all_to_all | solution.py:105
  80.5 5.1 %all-to-all-start.2 = ((bf16[16,32,1280]{2,1,0:T(8,128)(2,1)}), bf16[16,32,1280]{2,1,0:T(8,128)(2,1)S(1)}, u32[]{:S(2)}, u32[]{:S(2)}) async-start(bf16[16,32,1280]{2,1,0:T(8,128)(2,1)} %bitcast.23), calls=%async_computation.2 | async-start | bytes 2621440 | tf_op jit(solution)/shard_map/all_to_all | solution.py:105
  85.7 1.6 %write_out.1 = bf16[512,1280]{1,0:T(8,128)(2,1)} custom-call(bf16[512,1280]{1,0:T(8,128)(2,1)S(1)} %bitcast.19), custom_call_target="tpu_custom_call" | custom-call | bytes 2621440 | tf_op jit(solution)/shard_map/write_out/pallas_call | solution.py:92
  87.3 28.8 %all-to-all-done.2.x_ref = bf16[16,32,1280]{2,1,0:T(8,128)(2,1)S(1)} async-done(((bf16[16,32,1280]{2,1,0:T(8,128)(2,1)}), bf16[16,32,1280]{2,1,0:T(8,128)(2,1)S(1)}, u32[]{:S(2)}, u32[]{:S(2)}) %all-to-all-start.2) | async-done | bytes 1310752 | tf_op jit(solution)/shard_map/all_to_all | solution.py:105
  116.1 1.7 %place.1 = bf16[16,32,1280]{2,1,0:T(8,128)(2,1)} custom-call(s32[16]{0:T(128)S(1)} %broadcast_add_fusion.1.comes_ref, bf16[16,32,1280]{2,1,0:T(8,128)(2,1)S(1)} %all-to-all-done.2.x_ref), custom_call_target="tpu_custom_call" | custom-call | bytes 2621440 | tf_op jit(solution)/shard_map/place/pallas_call | solution.py:130
  (41 shorter events, 4.3 us)
Async XLA Ops:
  0.6 1.7 %copy-start = (bf16[256,1280]{1,0:T(8,128)(2,1)S(1)}, bf16[256,1280]{1,0:T(8,128)(2,1)}, u32[]{:S(2)}) copy-start(bf16[256,1280]{1,0:T(8,128)(2,1)} %param.9) | copy-start | bytes 1966084
  3.9 4.5 %collective-permute-start = (s32[1,256]{1,0:T(1,128)S(1)}, s32[1,256]{1,0:T(1,128)S(1)}, u32[]{:S(2)}, u32[]{:S(2)}) collective-permute-start(s32[1,256]{1,0:T(1,128)S(1)} %bitcast.28), channel_id=1, source_target_pairs={{0,8},{1,9},{2,10},{3,11},{4,12},{5,13},{6,14},{7,15},{8,0},{9,1},... | collective-permute-start | bytes 3080 | tf_op jit(solution)/shard_map/ppermute | solution.py:74
  8.4 36.7 %all-to-all-start.1 = ((bf16[16,32,1280]{2,1,0:T(8,128)(2,1)}), bf16[16,32,1280]{2,1,0:T(8,128)(2,1)S(1)}, u32[]{:S(2)}, u32[]{:S(2)}) async-start(bf16[16,32,1280]{2,1,0:T(8,128)(2,1)} %bitcast.5), calls=%async_computation.1 | async-start | bytes 2621440 | tf_op jit(solution)/shard_map/all_to_all | solution.py:105
  14.6 8.1 %copy-start.6 = (s32[16]{0:T(128)S(1)}, s32[16]{0:T(128)}, u32[]{:S(2)}) copy-start(s32[16]{0:T(128)} %constant.95.clone) | copy-start | bytes 196
  14.6 27.2 %copy-start.2 = (s32[32768]{0:T(1024)S(1)}, s32[32768]{0:T(1024)}, u32[]{:S(2)}) copy-start(s32[32768]{0:T(1024)} %param.8) | copy-start | bytes 393220
  16.3 38.7 %collective-permute-start.5 = (bf16[32,1280]{1,0:T(8,128)(2,1)}, bf16[32,1280]{1,0:T(8,128)(2,1)}, u32[]{:S(2)}, u32[]{:S(2)}) collective-permute-start(bf16[32,1280]{1,0:T(8,128)(2,1)} %get-tuple-element.13), channel_id=1, source_target_pairs={{1,0},{2,1},{3,2},{4,3},{5,4},{6,5},{7,6},{8,7},{9,8},{10,9},{11,1... | collective-permute-start | bytes 245768 | tf_op jit(solution)/shard_map/ppermute | solution.py:20
  18.5 36.5 %collective-permute-start.4 = (bf16[32,1280]{1,0:T(8,128)(2,1)}, bf16[32,1280]{1,0:T(8,128)(2,1)}, u32[]{:S(2)}, u32[]{:S(2)}) collective-permute-start(bf16[32,1280]{1,0:T(8,128)(2,1)} %get-tuple-element.14), channel_id=1, source_target_pairs={{0,1},{1,2},{2,3},{3,4},{4,5},{5,6},{6,7},{7,8},{8,9},{9,10},{10,1... | collective-permute-start | bytes 245768 | tf_op jit(solution)/shard_map/ppermute | solution.py:19
  22.2 15.9 %collective-permute-start.1 = (s32[2,256]{1,0:T(2,128)S(1)}, s32[2,256]{1,0:T(2,128)S(1)}, u32[]{:S(2)}, u32[]{:S(2)}) collective-permute-start(s32[2,256]{1,0:T(2,128)S(1)} %pad_add_fusion.3), channel_id=1, source_target_pairs={{0,4},{1,5},{2,6},{3,7},{4,0},{5,1},{6,2},{7,3},{8,12},{9,13},{10,... | collective-permute-start | bytes 6152 | tf_op jit(solution)/shard_map/ppermute | solution.py:74
  38.1 3.6 %collective-permute-start.2 = (s32[4,256]{1,0:T(4,128)S(1)}, s32[4,256]{1,0:T(4,128)S(1)}, u32[]{:S(2)}, u32[]{:S(2)}) collective-permute-start(s32[4,256]{1,0:T(4,128)S(1)} %pad_add_fusion.2), channel_id=1, source_target_pairs={{0,2},{1,3},{2,0},{3,1},{4,6},{5,7},{6,4},{7,5},{8,10},{9,11},{10,... | collective-permute-start | bytes 12296 | tf_op jit(solution)/shard_map/ppermute | solution.py:74
  41.7 1.2 %collective-permute-start.3 = (s32[8,256]{1,0:T(8,128)S(1)}, s32[8,256]{1,0:T(8,128)S(1)}, u32[]{:S(2)}, u32[]{:S(2)}) collective-permute-start(s32[8,256]{1,0:T(8,128)S(1)} %pad_add_fusion.1), channel_id=1, source_target_pairs={{0,1},{1,0},{2,3},{3,2},{4,5},{5,4},{6,7},{7,6},{8,9},{9,8},{10,11... | collective-permute-start | bytes 24584 | tf_op jit(solution)/shard_map/ppermute | solution.py:74
  45.0 35.5 %all-to-all-start = ((bf16[16,32,1280]{2,1,0:T(8,128)(2,1)}), bf16[16,32,1280]{2,1,0:T(8,128)(2,1)S(1)}, u32[]{:S(2)}, u32[]{:S(2)}) async-start(bf16[16,32,1280]{2,1,0:T(8,128)(2,1)} %bitcast.22), calls=%async_computation | async-start | bytes 2621440 | tf_op jit(solution)/shard_map/all_to_all | solution.py:105
  55.0 2.5 %copy-start.1 = (bf16[2048,1280]{1,0:T(8,128)(2,1)S(1)}, bf16[2048,1280]{1,0:T(8,128)(2,1)}, u32[]{:S(2)}) copy-start(bf16[2048,1280]{1,0:T(8,128)(2,1)} %k_ref.1) | copy-start | bytes 15728644
  57.5 11.0 %copy-start.3 = (s32[512]{0:T(512)S(1)}, s32[512]{0:T(512)}, u32[]{:S(2)}) copy-start(s32[512]{0:T(512)} %fusion.13) | copy-start | bytes 6148
  57.5 11.0 %copy-start.5 = (pred[512]{0:T(512)(128)(4,1)S(1)}, pred[512]{0:T(512)(128)(4,1)}, u32[]{:S(2)}) copy-start(pred[512]{0:T(512)(128)(4,1)} %ge.13) | copy-start | bytes 1540
  80.5 5.2 %copy-start.4 = (s32[16]{0:T(128)S(1)}, s32[16]{0:T(128)}, u32[]{:S(2)}) copy-start(s32[16]{0:T(128)} %get-tuple-element.11) | copy-start | bytes 196
  80.5 35.6 %all-to-all-start.2 = ((bf16[16,32,1280]{2,1,0:T(8,128)(2,1)}), bf16[16,32,1280]{2,1,0:T(8,128)(2,1)S(1)}, u32[]{:S(2)}, u32[]{:S(2)}) async-start(bf16[16,32,1280]{2,1,0:T(8,128)(2,1)} %bitcast.23), calls=%async_computation.2 | async-start | bytes 2621440 | tf_op jit(solution)/shard_map/all_to_all | solution.py:105

commit v7 on v5

--- a/solution.py
+++ b/solution.py
@@ -63,21 +63,21 @@
     )(queries, docs, *fixed)
 
 
-def every_device(row, after):
+def every_device(row, arrived):
     peers, me = lax.axis_size("docs"), lax.axis_index("docs")
     if peers & (peers - 1):
-        return lax.all_gather(row, "docs", axis=0, tiled=False), after
+        return lax.all_gather(row, "docs", axis=0, tiled=False), arrived
     step = max(1, peers // 4)
     apart = list(range(0, peers, step))
     rows = [lax.ppermute(row, "docs", [(i, i ^ a) for i in range(peers)]) if a else row for a in apart]
-    held, after = lax.optimization_barrier((jnp.stack(rows), after))
+    held, arrived = lax.optimization_barrier((jnp.stack(rows), arrived))
     while step > 1:
         step //= 2
         held = jnp.concatenate([held, lax.ppermute(held, "docs", [(i, i ^ step) for i in range(peers)])], axis=0)
         apart = apart + [a ^ step for a in apart]
     source = jnp.array(apart, dtype=jnp.int32) ^ me
     pick = jnp.arange(peers, dtype=jnp.int32)[:, None] == source[None, :]
-    return jnp.sum(jnp.where(pick[:, :, None], held[None], 0), axis=1), after
+    return jnp.sum(jnp.where(pick[:, :, None], held[None], 0), axis=1), arrived
 
 
 def copy_kernel(x_ref, o_ref):
@@ -158,8 +158,8 @@
         out = jnp.dot(table, images, preferred_element_type=jnp.float32).astype(jnp.bfloat16)
         return out.reshape(members, cap, feature)
 
-    every, leaving = every_device(packed, buckets(owner))
-    queries = exchange(leaving).reshape(members * cap, feature)
+    every, arrived = every_device(packed, exchange(buckets(owner)))
+    queries = arrived.reshape(members * cap, feature)
     loaded_images = write_out(exchange(buckets(shard)).reshape(members * cap, feature))
     before, after = halo_of(sentences)
 

time: 119 us -> 117 us (0.983)
  waiting for transfers between devices: 59.4 us -> 57.4 us
    all_to_all x3, waiting for transfers between devices: 55.5 us -> 30.2 us  [exchange(): return lax.all_to_all(x, 'docs', split_axis=0, concat_axis=0, tiled=True)]
    ppermute x3, waiting for transfers between devices: 0.75 us -> 19.5 us  [every_device(): lax.ppermute(row, 'docs', [(i, i ^ a) for i in range(peers)])]
    ppermute x2, waiting for transfers between devices: 3.18 us -> 7.61 us  [every_device(): lax.ppermute(held, 'docs', [(i, i ^ step) for i in range(peers)])]
    ppermute x2, starting transfers between devices: 2.59 us -> 0.56 us  [every_device(): lax.ppermute(held, 'docs', [(i, i ^ step) for i in range(peers)])]
    all_to_all x3, starting transfers between devices: 16.6 us -> 18.6 us  [exchange(): return lax.all_to_all(x, 'docs', split_axis=0, concat_axis=0, tiled=True)]
  transfers between devices with their start and end apart: 10 -> 10, of which waited for: 7 -> 5; matrix products, arithmetic and copies ran while one was open for 10% -> 9% of each run, Pallas kernels for 11% -> 11%
where the time goes in v7:
time: 117 us; the launch traced here: 116 us
  waiting for transfers between devices  57.4 us (49%)
  starting transfers between devices  27.4 us (23%)
  Pallas kernels  14.4 us (12%)
  local copies, waits for them, and re-layouts  5.99 us (5%)
  matrix products  5.27 us (5%)
  other arithmetic  4.88 us (4%)
    all_to_all x3, waiting for transfers between devices, exchange(): return lax.all_to_all(x, 'docs', split_axis=0, concat_axis=0, tiled=True)  30.2 us
    ppermute x3, waiting for transfers between devices, every_device(): lax.ppermute(row, 'docs', [(i, i ^ a) for i in range(peers)])  19.5 us
    all_to_all x3, starting transfers between devices, exchange(): return lax.all_to_all(x, 'docs', split_axis=0, concat_axis=0, tiled=True)  18.6 us
    pallas_call x1, Pallas kernels, attend(): pl.pallas_call(functools.partial(attend_kernel, feature ** (-0.5)), grid=...  11 us
    ppermute x2, waiting for transfers between devices, every_device(): lax.ppermute(held, 'docs', [(i, i ^ step) for i in range(peers)])  7.61 us
    ppermute x3, starting transfers between devices, every_device(): lax.ppermute(row, 'docs', [(i, i ^ a) for i in range(peers)])  3.9 us
    dot_general x2, matrix products, buckets(): jnp.dot(table, images, preferred_element_type=jnp.float32)  3.15 us
    unnamed x14, local copies, waits for them, and re-layouts  2.51 us
  transfers between devices with their start and end apart: 10, of which 5 were waited for; matrix products, arithmetic and copies ran while one was open for 9% of the time, Pallas kernels for 11%

profile of v7, /device:TPU:14, one launch (start us, length us, event | category | flops | bytes accessed | tf_op | source)
XLA Modules:
  0.0 116.1 jit_solution(5749857782419443941)
XLA Ops:
  0.6 0.9 convert_reduce_fusion
  2.3 1.6 %convolution_convert_fusion.1 = bf16[512,1280]{1,0:T(8,128)(2,1)} fusion(bf16[256,1280]{1,0:T(8,128)(2,1)S(1)} %copy-done, s32[256]{0:T(256)S(1)} %get-tuple-element.14), kind=kOutput, calls=%fused_computation.3 | convolution fusion | flops 336330752 | bytes 1967104 | tf_op jit(solution)/shard_map/dot_general | solution.py:158
  3.9 6.2 %all-to-all-start.1 = ((bf16[16,32,1280]{2,1,0:T(8,128)(2,1)}), bf16[16,32,1280]{2,1,0:T(8,128)(2,1)S(1)}, u32[]{:S(2)}, u32[]{:S(2)}) async-start(bf16[16,32,1280]{2,1,0:T(8,128)(2,1)} %bitcast.8), calls=%async_computation.1 | async-start | bytes 2621440 | tf_op jit(solution)/shard_map/all_to_all | solution.py:104
  10.1 1.5 %collective-permute-start.2 = (s32[256]{0:T(256)S(1)}, s32[256]{0:T(256)S(1)}, u32[]{:S(2)}, u32[]{:S(2)}) collective-permute-start(s32[256]{0:T(256)S(1)} %get-tuple-element.15), channel_id=1, source_target_pairs={{0,12},{1,13},{2,14},{3,15},{4,8},{5,9},{6,10},{7,11},{8,4},{9,5},... | collective-permute-start | bytes 3080 | tf_op jit(solution)/shard_map/ppermute | solution.py:72
  11.7 1.5 %collective-permute-start.1 = (s32[256]{0:T(256)S(1)}, s32[256]{0:T(256)S(1)}, u32[]{:S(2)}, u32[]{:S(2)}) collective-permute-start(s32[256]{0:T(256)S(1)} %get-tuple-element.15), channel_id=1, source_target_pairs={{0,8},{1,9},{2,10},{3,11},{4,12},{5,13},{6,14},{7,15},{8,0},{9,1},... | collective-permute-start | bytes 3080 | tf_op jit(solution)/shard_map/ppermute | solution.py:72
  13.1 0.9 collective-permute-start
  14.0 1.6 %fusion.19 = (bf16[32,1280]{1,0:T(8,128)(2,1)}, bf16[32,1280]{1,0:T(8,128)(2,1)}) fusion(bf16[2048,1280]{1,0:T(8,128)(2,1)} %k_ref.1), kind=kLoop, calls=%fused_computation.64 | loop fusion | bytes 327680 | tf_op jit(solution)/shard_map/slice | solution.py:20
  15.6 1.9 %collective-permute-start.6 = (bf16[32,1280]{1,0:T(8,128)(2,1)}, bf16[32,1280]{1,0:T(8,128)(2,1)}, u32[]{:S(2)}, u32[]{:S(2)}) collective-permute-start(bf16[32,1280]{1,0:T(8,128)(2,1)} %get-tuple-element.9), channel_id=1, source_target_pairs={{1,0},{2,1},{3,2},{4,3},{5,4},{6,5},{7,6},{8,7},{9,8},{10,9},{11,1... | collective-permute-start | bytes 245768 | tf_op jit(solution)/shard_map/ppermute | solution.py:20
  17.5 2.4 %collective-permute-start.5 = (bf16[32,1280]{1,0:T(8,128)(2,1)}, bf16[32,1280]{1,0:T(8,128)(2,1)}, u32[]{:S(2)}, u32[]{:S(2)}) collective-permute-start(bf16[32,1280]{1,0:T(8,128)(2,1)} %get-tuple-element.10), channel_id=1, source_target_pairs={{0,1},{1,2},{2,3},{3,4},{4,5},{5,6},{6,7},{7,8},{8,9},{9,10},{10,1... | collective-permute-start | bytes 245768 | tf_op jit(solution)/shard_map/ppermute | solution.py:19
  20.0 1.6 %convolution_convert_fusion.2 = bf16[512,1280]{1,0:T(8,128)(2,1)} fusion(bf16[256,1280]{1,0:T(8,128)(2,1)S(1)} %copy-done, s32[256]{0:T(256)S(1)} %get-tuple-element.16), kind=kOutput, calls=%fused_computation.4 | convolution fusion | flops 336330752 | bytes 1967104 | tf_op jit(solution)/shard_map/dot_general | solution.py:158
  21.6 19.5 %collective-permute-done.2 = s32[256]{0:T(256)S(1)} collective-permute-done((s32[256]{0:T(256)S(1)}, s32[256]{0:T(256)S(1)}, u32[]{:S(2)}, u32[]{:S(2)}) %collective-permute-start.2) | collective-permute-done | bytes 1056 | tf_op jit(solution)/shard_map/ppermute | solution.py:72
  41.1 5.6 %all-to-all-start = ((bf16[16,32,1280]{2,1,0:T(8,128)(2,1)}), bf16[16,32,1280]{2,1,0:T(8,128)(2,1)S(1)}, u32[]{:S(2)}, u32[]{:S(2)}) async-start(bf16[16,32,1280]{2,1,0:T(8,128)(2,1)} %bitcast.25), calls=%async_computation | async-start | bytes 2621440 | tf_op jit(solution)/shard_map/all_to_all | solution.py:104
  47.3 6.5 %collective-permute-done.3 = s32[4,256]{1,0:T(4,128)S(1)} collective-permute-done((s32[4,256]{1,0:T(4,128)S(1)}, s32[4,256]{1,0:T(4,128)S(1)}, u32[]{:S(2)}, u32[]{:S(2)}) %collective-permute-start.3) | collective-permute-done | bytes 4128 | tf_op jit(solution)/shard_map/ppermute | solution.py:76
  54.0 1.1 collective-permute-done.4
  57.3 1.4 %select_reduce_fusion = s32[512]{0:T(512)} fusion(s32[2048]{0:T(1024)S(1)} %dynamic_slice.9, s32[512]{0:T(512)S(1)} %sub.27), kind=kLoop, calls=%fused_computation | loop fusion | flops 3145216 | bytes 12288 | tf_op jit(solution)/shard_map/reduce_max | solution.py:177
  59.4 0.8 copy.10.doc_ref
  60.3 2.5 %copy-done.1 = bf16[2048,1280]{1,0:T(8,128)(2,1)S(1)} copy-done((bf16[2048,1280]{1,0:T(8,128)(2,1)S(1)}, bf16[2048,1280]{1,0:T(8,128)(2,1)}, u32[]{:S(2)}) %copy-start.1) | copy-done | bytes 5242904
  62.8 11.0 %attend.1 = bf16[512,1280]{1,0:T(8,128)(2,1)S(1)} custom-call(bf16[512,1280]{1,0:T(8,128)(2,1)S(1)} %bitcast.23, s32[512,1]{1,0:T(8,128)S(1)} %copy.10.doc_ref, bf16[2048,1280]{1,0:T(8,128)(2,1)S(1)} %copy-done.1, bf16[32,1280]{1,0:T(8,128)(2,1)} %collective-permute-done.5.before_ref, bf16[32,1280]{1,0:T(8,128)(2,1)} %collective-permute-done.6.after_ref, ...), custom_call_target="tpu_custom_call" | custom-call | flops 5368709120 | bytes 7864320 | tf_op jit(solution)/shard_map/attend/pallas_call | solution.py:48
  73.8 2.0 %convolution_convert_fusion = bf16[512,1280]{1,0:T(8,128)(2,1)} fusion(bf16[512,1280]{1,0:T(8,128)(2,1)S(1)} %attend.1, s32[512]{0:T(512)S(1)} %copy-done.3, pred[512]{0:T(512)(128)(4,1)S(1)} %copy-done.5), kind=kOutput, calls=%fused_computation.2 | convolution fusion | flops 672268288 | bytes 2624000 | tf_op jit(solution)/shard_map/dot_general | solution.py:189
  75.8 1.4 %all-to-all-done = bf16[16,32,1280]{2,1,0:T(8,128)(2,1)S(1)} async-done(((bf16[16,32,1280]{2,1,0:T(8,128)(2,1)}), bf16[16,32,1280]{2,1,0:T(8,128)(2,1)S(1)}, u32[]{:S(2)}, u32[]{:S(2)}) %all-to-all-start) | async-done | bytes 1310752 | tf_op jit(solution)/shard_map/all_to_all | solution.py:104
  77.2 6.7 %all-to-all-start.2 = ((bf16[16,32,1280]{2,1,0:T(8,128)(2,1)}), bf16[16,32,1280]{2,1,0:T(8,128)(2,1)S(1)}, u32[]{:S(2)}, u32[]{:S(2)}) async-start(bf16[16,32,1280]{2,1,0:T(8,128)(2,1)} %bitcast.26), calls=%async_computation.2 | async-start | bytes 2621440 | tf_op jit(solution)/shard_map/all_to_all | solution.py:104
  83.9 1.6 %write_out.1 = bf16[512,1280]{1,0:T(8,128)(2,1)} custom-call(bf16[512,1280]{1,0:T(8,128)(2,1)S(1)} %bitcast.22), custom_call_target="tpu_custom_call" | custom-call | bytes 2621440 | tf_op jit(solution)/shard_map/write_out/pallas_call | solution.py:91
  85.6 28.8 %all-to-all-done.2.x_ref = bf16[16,32,1280]{2,1,0:T(8,128)(2,1)S(1)} async-done(((bf16[16,32,1280]{2,1,0:T(8,128)(2,1)}), bf16[16,32,1280]{2,1,0:T(8,128)(2,1)S(1)}, u32[]{:S(2)}, u32[]{:S(2)}) %all-to-all-start.2) | async-done | bytes 1310752 | tf_op jit(solution)/shard_map/all_to_all | solution.py:104
  114.3 1.7 %place.1 = bf16[16,32,1280]{2,1,0:T(8,128)(2,1)} custom-call(s32[16]{0:T(128)S(1)} %broadcast_add_fusion.1.comes_ref, bf16[16,32,1280]{2,1,0:T(8,128)(2,1)S(1)} %all-to-all-done.2.x_ref), custom_call_target="tpu_custom_call" | custom-call | bytes 2621440 | tf_op jit(solution)/shard_map/place/pallas_call | solution.py:129
  (42 shorter events, 4.4 us)
Async XLA Ops:
  0.6 1.7 %copy-start = (bf16[256,1280]{1,0:T(8,128)(2,1)S(1)}, bf16[256,1280]{1,0:T(8,128)(2,1)}, u32[]{:S(2)}) copy-start(bf16[256,1280]{1,0:T(8,128)(2,1)} %param.9) | copy-start | bytes 1966084
  3.9 37.2 %all-to-all-start.1 = ((bf16[16,32,1280]{2,1,0:T(8,128)(2,1)}), bf16[16,32,1280]{2,1,0:T(8,128)(2,1)S(1)}, u32[]{:S(2)}, u32[]{:S(2)}) async-start(bf16[16,32,1280]{2,1,0:T(8,128)(2,1)} %bitcast.8), calls=%async_computation.1 | async-start | bytes 2621440 | tf_op jit(solution)/shard_map/all_to_all | solution.py:104
  10.1 11.4 %copy-start.6 = (s32[16]{0:T(128)S(1)}, s32[16]{0:T(128)}, u32[]{:S(2)}) copy-start(s32[16]{0:T(128)} %constant.95.clone) | copy-start | bytes 196
  10.1 31.0 %collective-permute-start.2 = (s32[256]{0:T(256)S(1)}, s32[256]{0:T(256)S(1)}, u32[]{:S(2)}, u32[]{:S(2)}) collective-permute-start(s32[256]{0:T(256)S(1)} %get-tuple-element.15), channel_id=1, source_target_pairs={{0,12},{1,13},{2,14},{3,15},{4,8},{5,9},{6,10},{7,11},{8,4},{9,5},... | collective-permute-start | bytes 3080 | tf_op jit(solution)/shard_map/ppermute | solution.py:72
  11.7 29.4 %collective-permute-start.1 = (s32[256]{0:T(256)S(1)}, s32[256]{0:T(256)S(1)}, u32[]{:S(2)}, u32[]{:S(2)}) collective-permute-start(s32[256]{0:T(256)S(1)} %get-tuple-element.15), channel_id=1, source_target_pairs={{0,8},{1,9},{2,10},{3,11},{4,12},{5,13},{6,14},{7,15},{8,0},{9,1},... | collective-permute-start | bytes 3080 | tf_op jit(solution)/shard_map/ppermute | solution.py:72
  13.1 28.0 %collective-permute-start = (s32[256]{0:T(256)S(1)}, s32[256]{0:T(256)S(1)}, u32[]{:S(2)}, u32[]{:S(2)}) collective-permute-start(s32[256]{0:T(256)S(1)} %get-tuple-element.15), channel_id=1, source_target_pairs={{0,4},{1,5},{2,6},{3,7},{4,0},{5,1},{6,2},{7,3},{8,12},{9,13},{10,... | collective-permute-start | bytes 3080 | tf_op jit(solution)/shard_map/ppermute | solution.py:72
  15.6 44.6 %collective-permute-start.6 = (bf16[32,1280]{1,0:T(8,128)(2,1)}, bf16[32,1280]{1,0:T(8,128)(2,1)}, u32[]{:S(2)}, u32[]{:S(2)}) collective-permute-start(bf16[32,1280]{1,0:T(8,128)(2,1)} %get-tuple-element.9), channel_id=1, source_target_pairs={{1,0},{2,1},{3,2},{4,3},{5,4},{6,5},{7,6},{8,7},{9,8},{10,9},{11,1... | collective-permute-start | bytes 245768 | tf_op jit(solution)/shard_map/ppermute | solution.py:20
  17.5 42.7 %collective-permute-start.5 = (bf16[32,1280]{1,0:T(8,128)(2,1)}, bf16[32,1280]{1,0:T(8,128)(2,1)}, u32[]{:S(2)}, u32[]{:S(2)}) collective-permute-start(bf16[32,1280]{1,0:T(8,128)(2,1)} %get-tuple-element.10), channel_id=1, source_target_pairs={{0,1},{1,2},{2,3},{3,4},{4,5},{5,6},{6,7},{7,8},{8,9},{9,10},{10,1... | collective-permute-start | bytes 245768 | tf_op jit(solution)/shard_map/ppermute | solution.py:19
  41.1 12.8 %copy-start.2 = (s32[32768]{0:T(1024)S(1)}, s32[32768]{0:T(1024)}, u32[]{:S(2)}) copy-start(s32[32768]{0:T(1024)} %param.8) | copy-start | bytes 393220
  41.1 36.1 %all-to-all-start = ((bf16[16,32,1280]{2,1,0:T(8,128)(2,1)}), bf16[16,32,1280]{2,1,0:T(8,128)(2,1)S(1)}, u32[]{:S(2)}, u32[]{:S(2)}) async-start(bf16[16,32,1280]{2,1,0:T(8,128)(2,1)} %bitcast.25), calls=%async_computation | async-start | bytes 2621440 | tf_op jit(solution)/shard_map/all_to_all | solution.py:104
  46.8 7.1 %collective-permute-start.3 = (s32[4,256]{1,0:T(4,128)S(1)}, s32[4,256]{1,0:T(4,128)S(1)}, u32[]{:S(2)}, u32[]{:S(2)}) collective-permute-start(s32[4,256]{1,0:T(4,128)S(1)} %pad_add_fusion.2), channel_id=1, source_target_pairs={{0,2},{1,3},{2,0},{3,1},{4,6},{5,7},{6,4},{7,5},{8,10},{9,11},{10,... | collective-permute-start | bytes 12296 | tf_op jit(solution)/shard_map/ppermute | solution.py:76
  53.9 1.2 %collective-permute-start.4 = (s32[8,256]{1,0:T(8,128)S(1)}, s32[8,256]{1,0:T(8,128)S(1)}, u32[]{:S(2)}, u32[]{:S(2)}) collective-permute-start(s32[8,256]{1,0:T(8,128)S(1)} %pad_add_fusion.1), channel_id=1, source_target_pairs={{0,1},{1,0},{2,3},{3,2},{4,5},{5,4},{6,7},{7,6},{8,9},{9,8},{10,11... | collective-permute-start | bytes 24584 | tf_op jit(solution)/shard_map/ppermute | solution.py:76
  60.3 2.5 %copy-start.1 = (bf16[2048,1280]{1,0:T(8,128)(2,1)S(1)}, bf16[2048,1280]{1,0:T(8,128)(2,1)}, u32[]{:S(2)}) copy-start(bf16[2048,1280]{1,0:T(8,128)(2,1)} %k_ref.1) | copy-start | bytes 15728644
  62.7 11.0 %copy-start.3 = (s32[512]{0:T(512)S(1)}, s32[512]{0:T(512)}, u32[]{:S(2)}) copy-start(s32[512]{0:T(512)} %fusion.13) | copy-start | bytes 6148
  62.7 11.0 %copy-start.5 = (pred[512]{0:T(512)(128)(4,1)S(1)}, pred[512]{0:T(512)(128)(4,1)}, u32[]{:S(2)}) copy-start(pred[512]{0:T(512)(128)(4,1)} %ge.13) | copy-start | bytes 1540
  77.2 37.1 %all-to-all-start.2 = ((bf16[16,32,1280]{2,1,0:T(8,128)(2,1)}), bf16[16,32,1280]{2,1,0:T(8,128)(2,1)S(1)}, u32[]{:S(2)}, u32[]{:S(2)}) async-start(bf16[16,32,1280]{2,1,0:T(8,128)(2,1)} %bitcast.26), calls=%async_computation.2 | async-start | bytes 2621440 | tf_op jit(solution)/shard_map/all_to_all | solution.py:104
  83.9 1.6 %copy-start.4 = (s32[16]{0:T(128)S(1)}, s32[16]{0:T(128)}, u32[]{:S(2)}) copy-start(s32[16]{0:T(128)} %get-tuple-element.7) | copy-start | bytes 196

commit v8 on v7

--- a/solution.py
+++ b/solution.py
@@ -9,6 +9,7 @@
 
 MOST_SENT = 32
 TILE = 16
+LANES = 128
 VMEM, SMEM, HBM = (pl.BlockSpec(memory_space=m) for m in (pltpu.VMEM, pltpu.SMEM, pltpu.HBM))
 
 
@@ -21,7 +22,59 @@
     return before, after
 
 
-def attend_kernel(temper, q_ref, doc_ref, k_ref, before_ref, after_ref, id_ref, id_before_ref, id_after_ref, o_ref):
+def deal_kernel(cap, owner_ref, shard_ref, anchor_ref, rows_ref, o_ref):
+    members = o_ref.shape[0]
+    lines, n = owner_ref.shape[0], rows_ref.shape[0]
+    owner, shard, anchor = owner_ref[...], shard_ref[...], anchor_ref[...]
+    told = jnp.concatenate([owner, shard, anchor // LANES, anchor % LANES], axis=0)
+    told = jnp.concatenate([told, jnp.zeros((TILE - 4 * lines, LANES), jnp.int32)], axis=0)
+    told = told.astype(jnp.float32).astype(jnp.bfloat16)
+    owner = jnp.concatenate([owner[i : i + 1] for i in range(lines)], axis=1)
+    label = lax.broadcasted_iota(jnp.int32, (members, n), 0)
+    theirs = jnp.where(label == owner, 1.0, 0.0)
+    sooner = lax.broadcasted_iota(jnp.int32, (n, n), 0) < lax.broadcasted_iota(jnp.int32, (n, n), 1)
+    before = jnp.dot(
+        theirs.astype(jnp.bfloat16), jnp.where(sooner, 1.0, 0.0).astype(jnp.bfloat16), preferred_element_type=jnp.float32
+    )
+    rank = jnp.sum(theirs * before, axis=0, keepdims=True).astype(jnp.int32)
+    slot = lax.broadcasted_iota(jnp.int32, (members * cap, n), 0)
+    table = jnp.where(slot == owner * cap + rank, 1.0, 0.0).astype(jnp.bfloat16)
+    out = jnp.dot(table, rows_ref[...], preferred_element_type=jnp.float32).astype(jnp.bfloat16)
+    for d in range(members):
+        for t, r, c in tiles(cap, out.shape[1]):
+            o_ref[d, t : t + TILE] = out[d * cap + r : d * cap + r + TILE, c : c + LANES]
+        o_ref[d, cap * out.shape[1] // LANES :] = told
+
+
+def tiles(rows, columns):
+    every = [(r, c) for r in range(0, rows, TILE) for c in range(0, columns, LANES)]
+    return [(i * TILE, r, c) for i, (r, c) in enumerate(every)]
+
+
+def deal(images, owner, shard, anchor, members, cap):
+    n, feature = images.shape
+    lines = lambda a: a.reshape(n // LANES, LANES)
+    shape = (members, cap * feature // LANES + TILE, LANES)
+    return pl.pallas_call(
+        functools.partial(deal_kernel, cap),
+        in_specs=[pl.BlockSpec()] * 4,
+        out_specs=pl.BlockSpec(),
+        out_shape=jax.ShapeDtypeStruct(shape, jnp.bfloat16),
+        compiler_params=pltpu.CompilerParams(vmem_limit_bytes=60 * 1024 * 1024),
+        cost_estimate=pl.CostEstimate(
+            flops=2 * members * cap * n * feature, bytes_accessed=2 * (n + members * cap) * feature, transcendentals=0
+        ),
+        name="deal",
+    )(lines(owner), lines(shard), lines(anchor), images)
+
+
+def attend_kernel(temper, q_ref, doc_ref, k_ref, before_ref, after_ref, id_ref, id_before_ref, id_after_ref, o_ref, *scratch):
+    if scratch:
+        rows, cap = scratch[0], o_ref.shape[0] // q_ref.shape[0]
+        for d in range(q_ref.shape[0]):
+            for t, r, c in tiles(cap, rows.shape[1]):
+                rows[d * cap + r : d * cap + r + TILE, c : c + LANES] = q_ref[d, t : t + TILE]
+        q_ref = rows
     q = q_ref[...]
     doc = doc_ref[...]
     parts = ((k_ref, id_ref), (before_ref, id_before_ref), (after_ref, id_after_ref))
@@ -40,21 +93,26 @@
 
 
 def attend(queries, docs, sentences, before, after, ids, id_before, id_after):
-    rows, feature = queries.shape
-    own = sentences.shape[0]
+    rows, (own, feature) = docs.shape[0], sentences.shape
     block = min(256, rows)
     whole = lambda a: pl.BlockSpec(a.shape, lambda i: (0, 0))
     fixed = (sentences, before, after, ids, id_before, id_after)
+    tiled = queries.ndim == 3
+    queries_spec = pl.BlockSpec((block, feature), lambda i: (i, 0))
+    if tiled:
+        buckets = block * queries.shape[0] // rows
+        queries_spec = pl.BlockSpec((buckets, *queries.shape[1:]), lambda i: (i, 0, 0))
     return pl.pallas_call(
         functools.partial(attend_kernel, feature**-0.5),
         grid=(rows // block,),
         in_specs=[
-            pl.BlockSpec((block, feature), lambda i: (i, 0)),
+            queries_spec,
             pl.BlockSpec((block, 1), lambda i: (i, 0)),
             *[whole(a) for a in fixed],
         ],
         out_specs=pl.BlockSpec((block, feature), lambda i: (i, 0)),
         out_shape=jax.ShapeDtypeStruct((rows, feature), jnp.bfloat16),
+        scratch_shapes=[pltpu.VMEM((block, feature), jnp.bfloat16)] * tiled,
         compiler_params=pltpu.CompilerParams(vmem_limit_bytes=40 * 1024 * 1024),
         cost_estimate=pl.CostEstimate(
             flops=4 * rows * own * feature, bytes_accessed=2 * (own + 2 * rows) * feature, transcendentals=rows * own
@@ -146,8 +204,6 @@
     cap = max(4, 2 * n // members)
     owner, shard = image_owner[:, 0], loader_shard[:, 0]
 
-    packed = (owner * members + shard) * own + anchor
-
     spot = jnp.arange(n, dtype=jnp.int32)
     earlier = (owner[:, None] == owner[None, :]) & (spot[None, :] < spot[:, None])
     rank = jnp.sum(earlier.astype(jnp.int32), axis=1)
@@ -158,14 +214,19 @@
         out = jnp.dot(table, images, preferred_element_type=jnp.float32).astype(jnp.bfloat16)
         return out.reshape(members, cap, feature)
 
-    every, arrived = every_device(packed, exchange(buckets(owner)))
-    queries = arrived.reshape(members * cap, feature)
+    whole_tiles = cap % TILE == 0 and feature % LANES == 0 and n % LANES == 0
+    if whole_tiles and 4 * n <= TILE * LANES and members <= 256 and own <= 256 * LANES:
+        queries = exchange(deal(images, owner, shard, anchor, members, cap))
+        told = queries[:, cap * feature // LANES :][:, : 4 * n // LANES].reshape(members, 4, n).astype(jnp.int32)
+        owner_of, shard_of, spot_of = told[:, 0], told[:, 1], told[:, 2] * LANES + told[:, 3]
+    else:
+        packed = (owner * members + shard) * own + anchor
+        every, arrived = every_device(packed, exchange(buckets(owner)))
+        queries = arrived.reshape(members * cap, feature)
+        owner_of, shard_of, spot_of = every // (own * members), every // own % members, every % own
     loaded_images = write_out(exchange(buckets(shard)).reshape(members * cap, feature))
     before, after = halo_of(sentences)
 
-    spot_of = every % own
-    shard_of = every // own % members
-    owner_of = every // (own * members)
     mine = owner_of == me
     sooner = (spot[:, None] < spot[None, :]).astype(jnp.bfloat16)
     ranks = jnp.dot(mine.astype(jnp.bfloat16), sooner, preferred_element_type=jnp.float32).astype(jnp.int32)

time: 117 us -> 115 us (0.983)
  waiting for transfers between devices: 57.4 us -> 65.8 us
  starting transfers between devices: 27.4 us -> 22 us
  other arithmetic: 4.88 us -> 1.67 us
  Pallas kernels: 14.4 us -> 16.4 us
  local copies, waits for them, and re-layouts: 5.99 us -> 4.12 us
  matrix products: 5.27 us -> 3.68 us
    all_to_all x3, waiting for transfers between devices: 30.2 us -> 65.8 us  [exchange(): return lax.all_to_all(x, 'docs', split_axis=0, concat_axis=0, tiled=True)]
    ppermute x5 -> x0, waiting for transfers between devices: 27.2 us -> none  [the longest x3 19.5 us: every_device(): lax.ppermute(row, 'docs', [(i, i ^ a) for i in range(peers)])]
    ppermute x5 -> x0, starting transfers between devices: 4.46 us -> none  [the longest x3 3.9 us: every_device(): lax.ppermute(row, 'docs', [(i, i ^ a) for i in range(peers)])]
    pallas_call x0 -> x1, Pallas kernels: none -> 2.9 us  [deal(): pl.pallas_call(functools.partial(deal_kernel, cap), in_specs=[pl.BlockSpe...]
    all_to_all x3, starting transfers between devices: 18.6 us -> 16.5 us  [exchange(): return lax.all_to_all(x, 'docs', split_axis=0, concat_axis=0, tiled=True)]
    ppermute x1, starting transfers between devices: 1.91 us -> 3.51 us  [halo_of(): after = lax.ppermute(sentences[:MOST_SENT], 'docs', down)]
    dot_general x2 -> x1, matrix products: 3.15 us -> 1.58 us  [buckets(): jnp.dot(table, images, preferred_element_type=jnp.float32)]
    unnamed x14 -> x11, local copies, waits for them, and re-layouts: 2.51 us -> 2.5 us
  transfers between devices with their start and end apart: 10 -> 5, of which waited for: 5 -> 3; matrix products, arithmetic and copies ran while one was open for 9% -> 6% of each run, Pallas kernels for 11% -> 10%
where the time goes in v8:
time: 115 us; the launch traced here: 114 us
  waiting for transfers between devices  65.8 us (57%)
  starting transfers between devices  22 us (19%)
  Pallas kernels  16.4 us (14%)
  local copies, waits for them, and re-layouts  4.12 us (4%)
  matrix products  3.68 us (3%)
  other arithmetic  1.67 us (1%)
    all_to_all x3, waiting for transfers between devices, exchange(): return lax.all_to_all(x, 'docs', split_axis=0, concat_axis=0, tiled=True)  65.8 us
    all_to_all x3, starting transfers between devices, exchange(): return lax.all_to_all(x, 'docs', split_axis=0, concat_axis=0, tiled=True)  16.5 us
    pallas_call x1, Pallas kernels, attend(): pl.pallas_call(functools.partial(attend_kernel, feature ** (-0.5)), grid=...  10.1 us
    ppermute x1, starting transfers between devices, halo_of(): after = lax.ppermute(sentences[:MOST_SENT], 'docs', down)  3.51 us
    pallas_call x1, Pallas kernels, deal(): pl.pallas_call(functools.partial(deal_kernel, cap), in_specs=[pl.BlockSpe...  2.9 us
    unnamed x11, local copies, waits for them, and re-layouts  2.5 us
  transfers between devices with their start and end apart: 5, of which 3 were waited for; matrix products, arithmetic and copies ran while one was open for 6% of the time, Pallas kernels for 10%

profile of v8, /device:TPU:14, one launch (start us, length us, event | category | flops | bytes accessed | tf_op | source)
XLA Modules:
  0.0 114.4 jit_solution(9241042642182533888)
XLA Ops:
  0.6 2.9 %deal.1 = bf16[16,336,128]{2,1,0:T(8,128)(2,1)} custom-call(s32[2,128]{1,0:T(2,128)} %bitcast.34, s32[2,128]{1,0:T(2,128)} %bitcast.37, s32[2,128]{1,0:T(2,128)} %bitcast.39, bf16[256,1280]{1,0:T(8,128)(2,1)} %rows_ref.1), custom_call_target="tpu_custom_call" | custom-call | flops 335544320 | bytes 1966080 | tf_op jit(solution)/shard_map/deal/pallas_call | solution.py:58
  3.5 6.4 %all-to-all-start.1 = ((bf16[16,336,128]{2,1,0:T(8,128)(2,1)}), bf16[16,336,128]{2,1,0:T(8,128)(2,1)S(1)}, u32[]{:S(2)}, u32[]{:S(2)}) async-start(bf16[16,336,128]{2,1,0:T(8,128)(2,1)} %deal.1), calls=%async_computation.1 | async-start | bytes 2752512 | tf_op jit(solution)/shard_map/all_to_all | solution.py:162
  9.9 0.9 fusion.15
  10.9 2.1 %collective-permute-start = (bf16[32,1280]{1,0:T(8,128)(2,1)S(1)}, bf16[32,1280]{1,0:T(8,128)(2,1)S(1)}, u32[]{:S(2)}, u32[]{:S(2)}) collective-permute-start(bf16[32,1280]{1,0:T(8,128)(2,1)S(1)} %get-tuple-element.5), channel_id=1, source_target_pairs={{0,1},{1,2},{2,3},{3,4},{4,5},{5,6},{6,7},{7,8},{8,9},{9,10},{10,1... | collective-permute-start | bytes 245768 | tf_op jit(solution)/shard_map/ppermute | solution.py:20
  12.9 3.5 %collective-permute-start.1 = (bf16[32,1280]{1,0:T(8,128)(2,1)S(1)}, bf16[32,1280]{1,0:T(8,128)(2,1)S(1)}, u32[]{:S(2)}, u32[]{:S(2)}) collective-permute-start(bf16[32,1280]{1,0:T(8,128)(2,1)S(1)} %get-tuple-element.4), channel_id=1, source_target_pairs={{1,0},{2,1},{3,2},{4,3},{5,4},{6,5},{7,6},{8,7},{9,8},{10,9},{11,1... | collective-permute-start | bytes 245768 | tf_op jit(solution)/shard_map/ppermute | solution.py:21
  16.5 0.2 convert_reduce_fusion
  16.7 0.1 fusion.14
  16.8 1.6 %convolution_convert_fusion.1 = bf16[512,1280]{1,0:T(8,128)(2,1)} fusion(bf16[256,1280]{1,0:T(8,128)(2,1)S(1)} %copy-done.1, s32[256]{0:T(256)S(1)} %add.71), kind=kOutput, calls=%fused_computation.3 | convolution fusion | flops 336330752 | bytes 1967104 | tf_op jit(solution)/shard_map/dot_general | solution.py:214
  18.4 23.4 %all-to-all-done.1.q_ref = bf16[16,336,128]{2,1,0:T(8,128)(2,1)S(1)} async-done(((bf16[16,336,128]{2,1,0:T(8,128)(2,1)}), bf16[16,336,128]{2,1,0:T(8,128)(2,1)S(1)}, u32[]{:S(2)}, u32[]{:S(2)}) %all-to-all-start.1) | async-done | bytes 1376288 | tf_op jit(solution)/shard_map/all_to_all | solution.py:162
  41.8 5.1 %all-to-all-start = ((bf16[16,32,1280]{2,1,0:T(8,128)(2,1)}), bf16[16,32,1280]{2,1,0:T(8,128)(2,1)S(1)}, u32[]{:S(2)}, u32[]{:S(2)}) async-start(bf16[16,32,1280]{2,1,0:T(8,128)(2,1)} %bitcast.30), calls=%async_computation | async-start | bytes 2621440 | tf_op jit(solution)/shard_map/all_to_all | solution.py:162
  46.9 0.1 fusion.8
  47.1 0.1 convolution_convert_fusion.2
  47.2 0.4 select_reduce_fusion.1
  47.8 0.8 select_reduce_fusion
  48.6 0.2 copy.21.doc_ref
  49.0 2.5 %copy-done = bf16[2048,1280]{1,0:T(8,128)(2,1)S(1)} copy-done((bf16[2048,1280]{1,0:T(8,128)(2,1)S(1)}, bf16[2048,1280]{1,0:T(8,128)(2,1)}, u32[]{:S(2)}) %copy-start) | copy-done | bytes 5242904
  51.5 10.1 %attend.1 = bf16[512,1280]{1,0:T(8,128)(2,1)S(1)} custom-call(bf16[16,336,128]{2,1,0:T(8,128)(2,1)S(1)} %all-to-all-done.1.q_ref, s32[512,1]{1,0:T(8,128)S(1)} %copy.21.doc_ref, bf16[2048,1280]{1,0:T(8,128)(2,1)S(1)} %copy-done, bf16[32,1280]{1,0:T(8,128)(2,1)S(1)} %collective-permute-done.before_ref, bf16[32,1280]{1,0:T(8,128)(2,1)S(1)} %collective-permute-done.1.after_ref, ...), custom_call_target="tpu_custom_call" | custom-call | flops 5368709120 | bytes 7864320 | tf_op jit(solution)/shard_map/attend/pallas_call | solution.py:105
  61.6 1.9 %convolution_convert_fusion = bf16[512,1280]{1,0:T(8,128)(2,1)} fusion(bf16[512,1280]{1,0:T(8,128)(2,1)S(1)} %attend.1, s32[512]{0:T(512)S(1)} %fusion.9, pred[512]{0:T(512)(128)(4,1)S(1)} %ge.13), kind=kOutput, calls=%fused_computation.2 | convolution fusion | flops 672268288 | bytes 2624000 | tf_op jit(solution)/shard_map/dot_general | solution.py:250
  63.5 13.7 %all-to-all-done = bf16[16,32,1280]{2,1,0:T(8,128)(2,1)S(1)} async-done(((bf16[16,32,1280]{2,1,0:T(8,128)(2,1)}), bf16[16,32,1280]{2,1,0:T(8,128)(2,1)S(1)}, u32[]{:S(2)}, u32[]{:S(2)}) %all-to-all-start) | async-done | bytes 1310752 | tf_op jit(solution)/shard_map/all_to_all | solution.py:162
  77.2 5.0 %all-to-all-start.2 = ((bf16[16,32,1280]{2,1,0:T(8,128)(2,1)}), bf16[16,32,1280]{2,1,0:T(8,128)(2,1)S(1)}, u32[]{:S(2)}, u32[]{:S(2)}) async-start(bf16[16,32,1280]{2,1,0:T(8,128)(2,1)} %bitcast.31), calls=%async_computation.2 | async-start | bytes 2621440 | tf_op jit(solution)/shard_map/all_to_all | solution.py:162
  82.2 1.6 %write_out.1 = bf16[512,1280]{1,0:T(8,128)(2,1)} custom-call(bf16[512,1280]{1,0:T(8,128)(2,1)S(1)} %bitcast.28), custom_call_target="tpu_custom_call" | custom-call | bytes 2621440 | tf_op jit(solution)/shard_map/write_out/pallas_call | solution.py:149
  83.9 0.1 select_reduce_fusion.2
  84.0 28.7 %all-to-all-done.2.x_ref = bf16[16,32,1280]{2,1,0:T(8,128)(2,1)S(1)} async-done(((bf16[16,32,1280]{2,1,0:T(8,128)(2,1)}), bf16[16,32,1280]{2,1,0:T(8,128)(2,1)S(1)}, u32[]{:S(2)}, u32[]{:S(2)}) %all-to-all-start.2) | async-done | bytes 1310752 | tf_op jit(solution)/shard_map/all_to_all | solution.py:162
  112.7 1.7 %place.1 = bf16[16,32,1280]{2,1,0:T(8,128)(2,1)} custom-call(s32[16]{0:T(128)S(1)} %broadcast_add_fusion.2.comes_ref, bf16[16,32,1280]{2,1,0:T(8,128)(2,1)S(1)} %all-to-all-done.2.x_ref), custom_call_target="tpu_custom_call" | custom-call | bytes 2621440 | tf_op jit(solution)/shard_map/place/pallas_call | solution.py:187
  (28 shorter events, 0.6 us)
Async XLA Ops:
  3.5 12.9 %copy-start.2 = (s32[32768]{0:T(1024)S(1)}, s32[32768]{0:T(1024)}, u32[]{:S(2)}) copy-start(s32[32768]{0:T(1024)} %param.7) | copy-start | bytes 393220
  3.5 12.9 %copy-start.3 = (s32[256,1]{0,1:T(1,128)S(1)}, s32[256,1]{0,1:T(1,128)}, u32[]{:S(2)}) copy-start(s32[256,1]{0,1:T(1,128)} %param.9) | copy-start | bytes 3076
  3.5 13.1 %copy-start.4 = (s32[256,1]{0,1:T(1,128)S(1)}, s32[256,1]{0,1:T(1,128)}, u32[]{:S(2)}) copy-start(s32[256,1]{0,1:T(1,128)} %param.11) | copy-start | bytes 3076
  3.5 13.3 %copy-start.1 = (bf16[256,1280]{1,0:T(8,128)(2,1)S(1)}, bf16[256,1280]{1,0:T(8,128)(2,1)}, u32[]{:S(2)}) copy-start(bf16[256,1280]{1,0:T(8,128)(2,1)} %rows_ref.1) | copy-start | bytes 1966084
  3.5 38.2 %all-to-all-start.1 = ((bf16[16,336,128]{2,1,0:T(8,128)(2,1)}), bf16[16,336,128]{2,1,0:T(8,128)(2,1)S(1)}, u32[]{:S(2)}, u32[]{:S(2)}) async-start(bf16[16,336,128]{2,1,0:T(8,128)(2,1)} %deal.1), calls=%async_computation.1 | async-start | bytes 2752512 | tf_op jit(solution)/shard_map/all_to_all | solution.py:162
  10.9 38.1 %collective-permute-start = (bf16[32,1280]{1,0:T(8,128)(2,1)S(1)}, bf16[32,1280]{1,0:T(8,128)(2,1)S(1)}, u32[]{:S(2)}, u32[]{:S(2)}) collective-permute-start(bf16[32,1280]{1,0:T(8,128)(2,1)S(1)} %get-tuple-element.5), channel_id=1, source_target_pairs={{0,1},{1,2},{2,3},{3,4},{4,5},{5,6},{6,7},{7,8},{8,9},{9,10},{10,1... | collective-permute-start | bytes 245768 | tf_op jit(solution)/shard_map/ppermute | solution.py:20
  12.9 36.0 %collective-permute-start.1 = (bf16[32,1280]{1,0:T(8,128)(2,1)S(1)}, bf16[32,1280]{1,0:T(8,128)(2,1)S(1)}, u32[]{:S(2)}, u32[]{:S(2)}) collective-permute-start(bf16[32,1280]{1,0:T(8,128)(2,1)S(1)} %get-tuple-element.4), channel_id=1, source_target_pairs={{1,0},{2,1},{3,2},{4,3},{5,4},{6,5},{7,6},{8,7},{9,8},{10,9},{11,1... | collective-permute-start | bytes 245768 | tf_op jit(solution)/shard_map/ppermute | solution.py:21
  41.8 35.5 %all-to-all-start = ((bf16[16,32,1280]{2,1,0:T(8,128)(2,1)}), bf16[16,32,1280]{2,1,0:T(8,128)(2,1)S(1)}, u32[]{:S(2)}, u32[]{:S(2)}) async-start(bf16[16,32,1280]{2,1,0:T(8,128)(2,1)} %bitcast.30), calls=%async_computation | async-start | bytes 2621440 | tf_op jit(solution)/shard_map/all_to_all | solution.py:162
  49.0 2.5 %copy-start = (bf16[2048,1280]{1,0:T(8,128)(2,1)S(1)}, bf16[2048,1280]{1,0:T(8,128)(2,1)}, u32[]{:S(2)}) copy-start(bf16[2048,1280]{1,0:T(8,128)(2,1)} %k_ref.1) | copy-start | bytes 15728644
  77.2 35.4 %all-to-all-start.2 = ((bf16[16,32,1280]{2,1,0:T(8,128)(2,1)}), bf16[16,32,1280]{2,1,0:T(8,128)(2,1)S(1)}, u32[]{:S(2)}, u32[]{:S(2)}) async-start(bf16[16,32,1280]{2,1,0:T(8,128)(2,1)} %bitcast.31), calls=%async_computation.2 | async-start | bytes 2621440 | tf_op jit(solution)/shard_map/all_to_all | solution.py:162

commit v9 on v8

--- a/solution.py
+++ b/solution.py
@@ -22,14 +22,14 @@
     return before, after
 
 
-def deal_kernel(cap, owner_ref, shard_ref, anchor_ref, rows_ref, o_ref):
-    members = o_ref.shape[0]
-    lines, n = owner_ref.shape[0], rows_ref.shape[0]
+def deal_kernel(cap, members, base_ref, owner_ref, shard_ref, anchor_ref, rows_ref, o_ref):
+    half, lines, (n, feature) = o_ref.shape[0], owner_ref.shape[0], rows_ref.shape
+    size = cap * feature // LANES
     owner, shard, anchor = owner_ref[...], shard_ref[...], anchor_ref[...]
     told = jnp.concatenate([owner, shard, anchor // LANES, anchor % LANES], axis=0)
     told = jnp.concatenate([told, jnp.zeros((TILE - 4 * lines, LANES), jnp.int32)], axis=0)
     told = told.astype(jnp.float32).astype(jnp.bfloat16)
-    owner = jnp.concatenate([owner[i : i + 1] for i in range(lines)], axis=1)
+    owner, shard = (jnp.concatenate([x[i : i + 1] for i in range(lines)], axis=1) for x in (owner, shard))
     label = lax.broadcasted_iota(jnp.int32, (members, n), 0)
     theirs = jnp.where(label == owner, 1.0, 0.0)
     sooner = lax.broadcasted_iota(jnp.int32, (n, n), 0) < lax.broadcasted_iota(jnp.int32, (n, n), 1)
@@ -37,13 +37,16 @@
         theirs.astype(jnp.bfloat16), jnp.where(sooner, 1.0, 0.0).astype(jnp.bfloat16), preferred_element_type=jnp.float32
     )
     rank = jnp.sum(theirs * before, axis=0, keepdims=True).astype(jnp.int32)
-    slot = lax.broadcasted_iota(jnp.int32, (members * cap, n), 0)
-    table = jnp.where(slot == owner * cap + rank, 1.0, 0.0).astype(jnp.bfloat16)
-    out = jnp.dot(table, rows_ref[...], preferred_element_type=jnp.float32).astype(jnp.bfloat16)
-    for d in range(members):
-        for t, r, c in tiles(cap, out.shape[1]):
-            o_ref[d, t : t + TILE] = out[d * cap + r : d * cap + r + TILE, c : c + LANES]
-        o_ref[d, cap * out.shape[1] // LANES :] = told
+    slot = lax.broadcasted_iota(jnp.int32, (half * cap, n), 0)
+    for k, target in enumerate((owner, shard)[: o_ref.shape[1] // size]):
+        place = (target - base_ref[0]) * cap + rank
+        table = jnp.where(slot == place, 1.0, 0.0).astype(jnp.bfloat16)
+        out = jnp.dot(table, rows_ref[...], preferred_element_type=jnp.float32).astype(jnp.bfloat16)
+        for d in range(half):
+            for t, r, c in tiles(cap, feature):
+                o_ref[d, k * size + t : k * size + t + TILE] = out[d * cap + r : d * cap + r + TILE, c : c + LANES]
+    for d in range(half):
+        o_ref[d, o_ref.shape[1] - TILE :] = told
 
 
 def tiles(rows, columns):
@@ -51,21 +54,56 @@
     return [(i * TILE, r, c) for i, (r, c) in enumerate(every)]
 
 
-def deal(images, owner, shard, anchor, members, cap):
+def deal(images, owner, shard, anchor, first, members, cap, regions):
     n, feature = images.shape
     lines = lambda a: a.reshape(n // LANES, LANES)
-    shape = (members, cap * feature // LANES + TILE, LANES)
-    return pl.pallas_call(
-        functools.partial(deal_kernel, cap),
-        in_specs=[pl.BlockSpec()] * 4,
+    half = members // 2
+    shape = (half, regions * cap * feature // LANES + TILE, LANES)
+    return pl.pallas_call(
+        functools.partial(deal_kernel, cap, members),
+        in_specs=[SMEM] + [pl.BlockSpec()] * 4,
         out_specs=pl.BlockSpec(),
         out_shape=jax.ShapeDtypeStruct(shape, jnp.bfloat16),
         compiler_params=pltpu.CompilerParams(vmem_limit_bytes=60 * 1024 * 1024),
         cost_estimate=pl.CostEstimate(
-            flops=2 * members * cap * n * feature, bytes_accessed=2 * (n + members * cap) * feature, transcendentals=0
+            flops=2 * regions * half * cap * n * feature, bytes_accessed=2 * (n + regions * half * cap) * feature, transcendentals=0
         ),
         name="deal",
-    )(lines(owner), lines(shard), lines(anchor), images)
+    )(first[None], lines(owner), lines(shard), lines(anchor), images)
+
+
+def merge_kernel(low_ref, near_ref, far_ref, o_ref):
+    cap, feature = far_ref.shape[1:]
+    size = cap * feature // LANES
+    s, half = pl.program_id(0), pl.num_programs(0) // 2
+    is_near = (s < half) == (low_ref[0] == 1)
+
+    @pl.when(is_near)
+    def _():
+        for t, r, c in tiles(cap, feature):
+            o_ref[0, r : r + TILE, c : c + LANES] = near_ref[0, size + t : size + t + TILE]
+
+    @pl.when(jnp.logical_not(is_near))
+    def _():
+        o_ref[...] = far_ref[...]
+
+
+def merge(near, far, low):
+    half, cap, feature = far.shape
+    return pl.pallas_call(
+        merge_kernel,
+        grid=(2 * half,),
+        in_specs=[
+            SMEM,
+            pl.BlockSpec((1, *near.shape[1:]), lambda i: (i % half, 0, 0)),
+            pl.BlockSpec((1, cap, feature), lambda i: (i % half, 0, 0)),
+        ],
+        out_specs=pl.BlockSpec((1, cap, feature), lambda i: (i, 0, 0)),
+        out_shape=jax.ShapeDtypeStruct((2 * half, cap, feature), far.dtype),
+        compiler_params=pltpu.CompilerParams(vmem_limit_bytes=8 * 1024 * 1024),
+        cost_estimate=pl.CostEstimate(flops=0, bytes_accessed=8 * half * cap * feature, transcendentals=0),
+        name="merge",
+    )(low.astype(jnp.int32)[None], near, far)
 
 
 def attend_kernel(temper, q_ref, doc_ref, k_ref, before_ref, after_ref, id_ref, id_before_ref, id_after_ref, o_ref, *scratch):
@@ -92,23 +130,22 @@
     ).astype(jnp.bfloat16)
 
 
-def attend(queries, docs, sentences, before, after, ids, id_before, id_after):
-    rows, (own, feature) = docs.shape[0], sentences.shape
+def attend(queries, cap, docs, known):
+    rows, (own, feature) = docs.shape[0], known[0].shape
     block = min(256, rows)
     whole = lambda a: pl.BlockSpec(a.shape, lambda i: (0, 0))
-    fixed = (sentences, before, after, ids, id_before, id_after)
     tiled = queries.ndim == 3
     queries_spec = pl.BlockSpec((block, feature), lambda i: (i, 0))
     if tiled:
-        buckets = block * queries.shape[0] // rows
-        queries_spec = pl.BlockSpec((buckets, *queries.shape[1:]), lambda i: (i, 0, 0))
+        region = cap * feature // LANES
+        queries_spec = pl.BlockSpec((block // cap, region, LANES), lambda i: (i, 0, 0))
     return pl.pallas_call(
         functools.partial(attend_kernel, feature**-0.5),
         grid=(rows // block,),
         in_specs=[
             queries_spec,
             pl.BlockSpec((block, 1), lambda i: (i, 0)),
-            *[whole(a) for a in fixed],
+            *[whole(a) for a in known],
         ],
         out_specs=pl.BlockSpec((block, feature), lambda i: (i, 0)),
         out_shape=jax.ShapeDtypeStruct((rows, feature), jnp.bfloat16),
@@ -118,7 +155,7 @@
             flops=4 * rows * own * feature, bytes_accessed=2 * (own + 2 * rows) * feature, transcendentals=rows * own
         ),
         name="attend",
-    )(queries, docs, *fixed)
+    )(queries, docs, *known)
 
 
 def every_device(row, arrived):
@@ -196,6 +233,10 @@
     )(comes, x).reshape(members * cap, feature)
 
 
+def one_hot_dot(table, rows):
+    return jnp.dot(table.astype(jnp.bfloat16), rows, preferred_element_type=jnp.float32).astype(jnp.bfloat16)
+
+
 def shards(sentences, sent_doc, images, image_owner, anchor, loader_shard):
     members = lax.axis_size("docs")
     me = lax.axis_index("docs")
@@ -203,52 +244,78 @@
     n = images.shape[0]
     cap = max(4, 2 * n // members)
     owner, shard = image_owner[:, 0], loader_shard[:, 0]
-
     spot = jnp.arange(n, dtype=jnp.int32)
-    earlier = (owner[:, None] == owner[None, :]) & (spot[None, :] < spot[:, None])
-    rank = jnp.sum(earlier.astype(jnp.int32), axis=1)
-    slot = jnp.arange(members * cap, dtype=jnp.int32)[:, None]
-
-    def buckets(targets):
-        table = (slot == (targets * cap + rank)[None, :]).astype(jnp.bfloat16)
-        out = jnp.dot(table, images, preferred_element_type=jnp.float32).astype(jnp.bfloat16)
-        return out.reshape(members, cap, feature)
-
-    whole_tiles = cap % TILE == 0 and feature % LANES == 0 and n % LANES == 0
-    if whole_tiles and 4 * n <= TILE * LANES and members <= 256 and own <= 256 * LANES:
-        queries = exchange(deal(images, owner, shard, anchor, members, cap))
-        told = queries[:, cap * feature // LANES :][:, : 4 * n // LANES].reshape(members, 4, n).astype(jnp.int32)
-        owner_of, shard_of, spot_of = told[:, 0], told[:, 1], told[:, 2] * LANES + told[:, 3]
-    else:
-        packed = (owner * members + shard) * own + anchor
-        every, arrived = every_device(packed, exchange(buckets(owner)))
-        queries = arrived.reshape(members * cap, feature)
-        owner_of, shard_of, spot_of = every // (own * members), every // own % members, every % own
-    loaded_images = write_out(exchange(buckets(shard)).reshape(members * cap, feature))
-    before, after = halo_of(sentences)
-
-    mine = owner_of == me
-    sooner = (spot[:, None] < spot[None, :]).astype(jnp.bfloat16)
-    ranks = jnp.dot(mine.astype(jnp.bfloat16), sooner, preferred_element_type=jnp.float32).astype(jnp.int32)
     slots = jnp.arange(cap, dtype=jnp.int32)
-    hit = mine[:, None, :] & (ranks[:, None, :] == slots[None, :, None])
-    spots = jnp.sum(jnp.where(hit, spot_of[:, None, :] + 1, 0), axis=2).reshape(members * cap) - 1
+
+    def by_shard(rows, owner, shard, start, count):
+        earlier = (owner[:, None] == owner[None, :]) & (spot[None, :] < spot[:, None])
+        rank = jnp.sum(earlier.astype(jnp.int32), axis=1)
+        slot = jnp.arange(count * cap, dtype=jnp.int32)[:, None]
+        return one_hot_dot(slot == ((shard - start) * cap + rank)[None, :], rows).reshape(count, cap, feature)
+
     ids = lax.dynamic_slice_in_dim(sent_doc, me * own, own)
-    here = spots[:, None] == jnp.arange(own, dtype=jnp.int32)[None, :]
-    docs = jnp.max(jnp.where(here, ids[None, :], -2), axis=1)
     padded = jnp.pad(sent_doc, (MOST_SENT, MOST_SENT), constant_values=-1)
     id_before = lax.dynamic_slice_in_dim(padded, me * own, MOST_SENT)
     id_after = lax.dynamic_slice_in_dim(padded, me * own + own + MOST_SENT, MOST_SENT)
-    aligned = attend(queries, docs[:, None], sentences, before, after, ids[None], id_before[None], id_after[None])
-
-    goes = jnp.max(jnp.where(mine, shard_of + 1, 0), axis=1) - 1
-    comes = jnp.max(jnp.where(shard_of == me, owner_of + 1, 0), axis=1) - 1
+    before, after = halo_of(sentences)
+    known = (sentences, before, after, ids[None], id_before[None], id_after[None])
+
+    def slots_of(owner_of, shard_of, spot_of):
+        mine = owner_of == me
+        sooner = (spot[:, None] < spot[None, :]).astype(jnp.bfloat16)
+        ranks = jnp.dot(mine.astype(jnp.bfloat16), sooner, preferred_element_type=jnp.float32).astype(jnp.int32)
+        hit = mine[:, None, :] & (ranks[:, None, :] == slots[None, :, None])
+        spots = jnp.sum(jnp.where(hit, spot_of[:, None, :] + 1, 0), axis=2).reshape(-1) - 1
+        here = spots[:, None] == jnp.arange(own, dtype=jnp.int32)[None, :]
+        docs = jnp.max(jnp.where(here, ids[None, :], -2), axis=1)
+        goes = jnp.max(jnp.where(mine, shard_of + 1, 0), axis=1) - 1
+        comes = jnp.max(jnp.where(shard_of == me, owner_of + 1, 0), axis=1) - 1
+        return docs[:, None], goes, comes
 
     row = jnp.arange(members * cap, dtype=jnp.int32)
-    puts = row[:, None] == (jnp.repeat(goes, cap) * cap + row % cap)[None, :]
-    puts = (puts & (jnp.repeat(goes, cap) >= 0)[None, :]).astype(jnp.bfloat16)
-    sent = jnp.dot(puts, aligned, preferred_element_type=jnp.float32).astype(jnp.bfloat16).reshape(members, cap, feature)
-    loaded_text = place(exchange(sent), comes)
+
+    def puts(goes):
+        block, slot = jnp.repeat(goes, cap), jnp.arange(goes.shape[0] * cap, dtype=jnp.int32) % cap
+        return (row[:, None] == (block * cap + slot)[None, :]) & (block >= 0)[None, :]
+
+    whole_tiles = cap % TILE == 0 and feature % LANES == 0 and n % LANES == 0 and members % 2 == 0
+    if whole_tiles and 4 * n <= TILE * LANES and members <= 256 and own <= 256 * LANES:
+        half = members // 2
+        first = me // half * half
+        halves = [list(range(half)), list(range(half, members))]
+        across = [(i, (i + half) % members) for i in range(members)]
+
+        def exchange_half(x):
+            return lax.all_to_all(x, "docs", split_axis=0, concat_axis=0, tiled=True, axis_index_groups=halves)
+
+        def told_by(x):
+            told = x[:, -TILE:][:, : 4 * n // LANES].reshape(half, 4, n).astype(jnp.int32)
+            return told[:, 0], told[:, 1], told[:, 2] * LANES + told[:, 3]
+
+        codes = jnp.stack([owner, shard, anchor])
+        mirrored, codes_mirror = lax.ppermute(images, "docs", across), lax.ppermute(codes, "docs", across)
+        near = exchange_half(deal(images, owner, shard, anchor, first, members, cap, 2))
+        docs, goes, comes = slots_of(*told_by(near))
+        aligned = attend(near, cap, docs, known)
+        sent, mirrored = lax.optimization_barrier((one_hot_dot(puts(goes), aligned), mirrored))
+
+        far = exchange_half(deal(mirrored, *codes_mirror, first, members, cap, 1))
+        far_images = exchange_half(by_shard(mirrored, codes_mirror[0], codes_mirror[1], first, half))
+        docs, goes, comes_far = slots_of(*told_by(far))
+        aligned = attend(far, cap, docs, known)
+        sent += jnp.dot(puts(goes).astype(jnp.bfloat16), aligned, preferred_element_type=jnp.float32)
+        sent, far_images = lax.optimization_barrier((sent.astype(jnp.bfloat16), far_images))
+        low = first == 0
+        comes = jnp.where(low, jnp.concatenate([comes, comes_far]), jnp.concatenate([comes_far, comes]))
+        loaded_images = merge(near, far_images, low).reshape(members * cap, feature)
+    else:
+        packed = (owner * members + shard) * own + anchor
+        every, queries = every_device(packed, exchange(by_shard(images, owner, owner, 0, members)))
+        loaded_images = write_out(exchange(by_shard(images, owner, shard, 0, members)).reshape(members * cap, feature))
+        docs, goes, comes = slots_of(every // (own * members), every // own % members, every % own)
+        aligned = attend(queries.reshape(members * cap, feature), cap, docs, known)
+        sent = one_hot_dot(puts(goes), aligned)
+    loaded_text = place(exchange(sent.reshape(members, cap, feature)), comes)
     return loaded_images, loaded_text
 
 

time: 115 us -> 124 us (1.078)
  waiting for transfers between devices: 65.8 us -> 55.7 us
  Pallas kernels: 16.4 us -> 22.5 us
  starting transfers between devices: 22 us -> 27.3 us
  local copies, waits for them, and re-layouts: 4.12 us -> 8 us
  matrix products: 3.68 us -> 5.72 us
    all_to_all x3 -> x1, waiting for transfers between devices: 65.8 us -> 24.9 us  [exchange(): return lax.all_to_all(x, 'docs', split_axis=0, concat_axis=0, tiled=True)]
    ppermute x0 -> x2, waiting for transfers between devices: none -> 23.9 us  [the longest x1 23.9 us: shards(): lax.ppermute(codes, 'docs', across)]
    all_to_all x0 -> x3, starting transfers between devices: none -> 13.3 us  [exchange_half(): lax.all_to_all(x, 'docs', split_axis=0, concat_axis=0, tiled=True, axis_i...]
    all_to_all x3 -> x1, starting transfers between devices: 16.5 us -> 6.66 us  [exchange(): return lax.all_to_all(x, 'docs', split_axis=0, concat_axis=0, tiled=True)]
    all_to_all x0 -> x3, waiting for transfers between devices: none -> 6.87 us  [exchange_half(): lax.all_to_all(x, 'docs', split_axis=0, concat_axis=0, tiled=True, axis_i...]
    pallas_call x2 -> x3, Pallas kernels: 4.52 us -> 10.6 us  [the longest x2 5.37 us: deal(): pl.pallas_call(functools.partial(deal_kernel, cap, members), in_specs=[SM...]
    unnamed x11 -> x20, local copies, waits for them, and re-layouts: 2.5 us -> 5.83 us
    ppermute x0 -> x2, starting transfers between devices: none -> 2.99 us  [the longest x1 2.59 us: shards(): lax.ppermute(images, 'docs', across)]
  transfers between devices with their start and end apart: 5 -> 8, of which waited for: 3 -> 3; matrix products, arithmetic and copies ran while one was open for 6% -> 9% of each run, Pallas kernels for 10% -> 13%
where the time goes in v9:
time: 124 us; the launch traced here: 123 us
  waiting for transfers between devices  55.7 us (45%)
  starting transfers between devices  27.3 us (22%)
  Pallas kernels  22.5 us (18%)
  local copies, waits for them, and re-layouts  8 us (6%)
  matrix products  5.72 us (5%)
  other arithmetic  2.65 us (2%)
    all_to_all x1, waiting for transfers between devices, exchange(): return lax.all_to_all(x, 'docs', split_axis=0, concat_axis=0, tiled=True)  24.9 us
    ppermute x1, waiting for transfers between devices, shards(): lax.ppermute(codes, 'docs', across)  23.9 us
    all_to_all x3, starting transfers between devices, exchange_half(): lax.all_to_all(x, 'docs', split_axis=0, concat_axis=0, tiled=True, axis_i...  13.3 us
    pallas_call x2, Pallas kernels, attend(): pl.pallas_call(functools.partial(attend_kernel, feature ** (-0.5)), grid=...  10.2 us
    all_to_all x3, waiting for transfers between devices, exchange_half(): lax.all_to_all(x, 'docs', split_axis=0, concat_axis=0, tiled=True, axis_i...  6.87 us
    all_to_all x1, starting transfers between devices, exchange(): return lax.all_to_all(x, 'docs', split_axis=0, concat_axis=0, tiled=True)  6.66 us
    unnamed x20, local copies, waits for them, and re-layouts  5.83 us
    pallas_call x2, Pallas kernels, deal(): pl.pallas_call(functools.partial(deal_kernel, cap, members), in_specs=[SM...  5.37 us
  transfers between devices with their start and end apart: 8, of which 3 were waited for; matrix products, arithmetic and copies ran while one was open for 9% of the time, Pallas kernels for 13%

profile of v9, /device:TPU:14, one launch (start us, length us, event | category | flops | bytes accessed | tf_op | source)
XLA Modules:
  0.0 123.1 jit_solution(7050424263457980827)
XLA Ops:
  0.7 2.9 %deal.2 = bf16[8,656,128]{2,1,0:T(8,128)(2,1)} custom-call(s32[1]{0:T(128)} %bitcast.1.base_ref, s32[2,128]{1,0:T(2,128)} %bitcast.55, s32[2,128]{1,0:T(2,128)} %bitcast.57, s32[2,128]{1,0:T(2,128)} %bitcast.59, bf16[256,1280]{1,0:T(8,128)(2,1)} %rows_ref.1), custom_call_target="tpu_custom_call" | custom-call | flops 335544320 | bytes 1966080 | tf_op jit(solution)/shard_map/deal/pallas_call | solution.py:62
  3.6 4.2 %all-to-all-start = ((bf16[8,656,128]{2,1,0:T(8,128)(2,1)}), bf16[8,656,128]{2,1,0:T(8,128)(2,1)S(1)}, u32[]{:S(2)}, u32[]{:S(2)}) async-start(bf16[8,656,128]{2,1,0:T(8,128)(2,1)} %deal.2), calls=%async_computation | async-start | bytes 2686976 | tf_op jit(solution)/shard_map/all_to_all | solution.py:289
  7.8 2.6 %collective-permute-start.2 = (bf16[256,1280]{1,0:T(8,128)(2,1)S(1)}, bf16[256,1280]{1,0:T(8,128)(2,1)S(1)}, u32[]{:S(2)}, u32[]{:S(2)}) collective-permute-start(bf16[256,1280]{1,0:T(8,128)(2,1)S(1)} %copy-done.4), channel_id=1, source_target_pairs={{0,8},{1,9},{2,10},{3,11},{4,12},{5,13},{6,14},{7,15},{8,0},{9,1},... | collective-permute-start | bytes 1966088 | tf_op jit(solution)/shard_map/ppermute | solution.py:296
  10.8 0.9 fusion.25
  11.8 1.9 %collective-permute-start.1 = (bf16[32,1280]{1,0:T(8,128)(2,1)S(1)}, bf16[32,1280]{1,0:T(8,128)(2,1)S(1)}, u32[]{:S(2)}, u32[]{:S(2)}) collective-permute-start(bf16[32,1280]{1,0:T(8,128)(2,1)S(1)} %get-tuple-element.14), channel_id=1, source_target_pairs={{1,0},{2,1},{3,2},{4,3},{5,4},{6,5},{7,6},{8,7},{9,8},{10,9},{11,1... | collective-permute-start | bytes 245768 | tf_op jit(solution)/shard_map/ppermute | solution.py:21
  13.7 2.4 %collective-permute-start = (bf16[32,1280]{1,0:T(8,128)(2,1)S(1)}, bf16[32,1280]{1,0:T(8,128)(2,1)S(1)}, u32[]{:S(2)}, u32[]{:S(2)}) collective-permute-start(bf16[32,1280]{1,0:T(8,128)(2,1)S(1)} %get-tuple-element.15), channel_id=1, source_target_pairs={{0,1},{1,2},{2,3},{3,4},{4,5},{5,6},{6,7},{7,8},{8,9},{9,10},{10,1... | collective-permute-start | bytes 245768 | tf_op jit(solution)/shard_map/ppermute | solution.py:20
  16.2 23.9 %collective-permute-done.3 = s32[3,256]{1,0:T(4,128)S(1)} collective-permute-done((s32[3,256]{1,0:T(4,128)S(1)}, s32[3,256]{1,0:T(4,128)S(1)}, u32[]{:S(2)}, u32[]{:S(2)}) %collective-permute-start.3) | collective-permute-done | bytes 3104 | tf_op jit(solution)/shard_map/ppermute | solution.py:296
  40.3 0.6 multiply_add_fusion
  42.6 2.5 %copy-done = bf16[2048,1280]{1,0:T(8,128)(2,1)S(1)} copy-done((bf16[2048,1280]{1,0:T(8,128)(2,1)S(1)}, bf16[2048,1280]{1,0:T(8,128)(2,1)}, u32[]{:S(2)}) %copy-start) | copy-done | bytes 5242904
  45.0 5.1 %attend.2 = bf16[256,1280]{1,0:T(8,128)(2,1)S(1)} custom-call(bf16[8,656,128]{2,1,0:T(8,128)(2,1)S(1)} %all-to-all-done.q_ref.near_ref, s32[256,1]{1,0:T(8,128)S(1)} %copy.32.doc_ref, bf16[2048,1280]{1,0:T(8,128)(2,1)S(1)} %copy-done, bf16[32,1280]{1,0:T(8,128)(2,1)S(1)} %collective-permute-done.before_ref, ...), custom_call_target="tpu_custom_call" | custom-call | flops 2684354560 | bytes 6553600 | tf_op jit(solution)/shard_map/attend/pallas_call | solution.py:142
  50.2 1.6 %convolution_convert_fusion = bf16[512,1280]{1,0:T(8,128)(2,1)} fusion(bf16[256,1280]{1,0:T(8,128)(2,1)S(1)} %attend.2, s32[256]{0:T(256)S(1)} %fusion.22, pred[256]{0:T(512)(128)(4,1)S(1)} %ge.23), kind=kOutput, calls=%fused_computation | convolution fusion | flops 336461824 | bytes 1967360 | tf_op jit(solution)/shard_map/dot_general | solution.py:237
  51.8 0.8 copy-done.3
  52.6 2.4 %deal.3 = bf16[8,336,128]{2,1,0:T(8,128)(2,1)} custom-call(s32[1]{0:T(128)} %bitcast.1.base_ref, s32[2,128]{1,0:T(2,128)} %bitcast.54, s32[2,128]{1,0:T(2,128)} %bitcast.66, s32[2,128]{1,0:T(2,128)} %bitcast.65, bf16[256,1280]{1,0:T(8,128)(2,1)} %copy-done.3), custom_call_target="tpu_custom_call" | custom-call | flops 167772160 | bytes 1310720 | tf_op jit(solution)/shard_map/deal/pallas_call | solution.py:62
  55.0 4.2 %all-to-all-start.1 = ((bf16[8,336,128]{2,1,0:T(8,128)(2,1)}), bf16[8,336,128]{2,1,0:T(8,128)(2,1)S(1)}, u32[]{:S(2)}, u32[]{:S(2)}) async-start(bf16[8,336,128]{2,1,0:T(8,128)(2,1)} %deal.3), calls=%async_computation.1 | async-start | bytes 1376256 | tf_op jit(solution)/shard_map/all_to_all | solution.py:289
  59.2 2.3 %convolution_convert_fusion.1 = bf16[256,1280]{1,0:T(8,128)(2,1)} fusion(bf16[256,1280]{1,0:T(8,128)(2,1)} %copy-done.3, s32[256]{0:T(256)S(1)} %bitcast.64), kind=kOutput, calls=%fused_computation.2 | convolution fusion | flops 168165376 | bytes 1311744 | tf_op jit(solution)/shard_map/dot_general | solution.py:237
  61.5 6.9 %all-to-all-done.1.q_ref = bf16[8,336,128]{2,1,0:T(8,128)(2,1)S(1)} async-done(((bf16[8,336,128]{2,1,0:T(8,128)(2,1)}), bf16[8,336,128]{2,1,0:T(8,128)(2,1)S(1)}, u32[]{:S(2)}, u32[]{:S(2)}) %all-to-all-start.1) | async-done | bytes 688160 | tf_op jit(solution)/shard_map/all_to_all | solution.py:289
  68.4 4.9 %all-to-all-start.2 = ((bf16[8,32,1280]{2,1,0:T(8,128)(2,1)}), bf16[8,32,1280]{2,1,0:T(8,128)(2,1)S(1)}, u32[]{:S(2)}, u32[]{:S(2)}) async-start(bf16[8,32,1280]{2,1,0:T(8,128)(2,1)} %bitcast.25), calls=%async_computation.2 | async-start | bytes 1310720 | tf_op jit(solution)/shard_map/all_to_all | solution.py:289
  74.9 2.5 %copy-done.1 = bf16[2048,1280]{1,0:T(8,128)(2,1)S(1)} copy-done((bf16[2048,1280]{1,0:T(8,128)(2,1)S(1)}, bf16[2048,1280]{1,0:T(8,128)(2,1)}, u32[]{:S(2)}) %copy-start.1) | copy-done | bytes 5242904
  77.4 5.1 %attend.3 = bf16[256,1280]{1,0:T(8,128)(2,1)S(1)} custom-call(bf16[8,336,128]{2,1,0:T(8,128)(2,1)S(1)} %all-to-all-done.1.q_ref, s32[256,1]{1,0:T(8,128)S(1)} %copy.37.doc_ref, bf16[2048,1280]{1,0:T(8,128)(2,1)S(1)} %copy-done.1, bf16[32,1280]{1,0:T(8,128)(2,1)S(1)} %collective-permute-done.before_ref, ...), custom_call_target="tpu_custom_call" | custom-call | flops 2684354560 | bytes 6553600 | tf_op jit(solution)/shard_map/attend/pallas_call | solution.py:142
  82.5 1.6 %add_convert_fusion = bf16[512,1280]{1,0:T(8,128)(2,1)} fusion(bf16[512,1280]{1,0:T(8,128)(2,1)S(1)} %copy-done.2, bf16[256,1280]{1,0:T(8,128)(2,1)S(1)} %attend.3, s32[256]{0:T(256)S(1)} %fusion.21, pred[256]{0:T(512)(128)(4,1)S(1)} %ge.25), kind=kOutput, calls=%fused_computation.1 | convolution fusion | flops 337772544 | bytes 3278080 | tf_op jit(solution)/shard_map/dot_general | solution.py:306
  84.1 6.7 %all-to-all-start.3 = ((bf16[16,32,1280]{2,1,0:T(8,128)(2,1)}), bf16[16,32,1280]{2,1,0:T(8,128)(2,1)S(1)}, u32[]{:S(2)}, u32[]{:S(2)}) async-start(bf16[16,32,1280]{2,1,0:T(8,128)(2,1)} %bitcast.50), calls=%async_computation.3 | async-start | bytes 2621440 | tf_op jit(solution)/shard_map/all_to_all | solution.py:199
  90.8 5.2 %merge.1 = bf16[16,32,1280]{2,1,0:T(8,128)(2,1)} custom-call(s32[1]{0:T(128)} %bitcast.low_ref, bf16[8,656,128]{2,1,0:T(8,128)(2,1)S(1)} %all-to-all-done.q_ref.near_ref, bf16[8,32,1280]{2,1,0:T(8,128)(2,1)S(1)} %all-to-all-done.2.far_ref), custom_call_target="tpu_custom_call" | custom-call | bytes 2621440 | tf_op jit(solution)/shard_map/merge/pallas_call | solution.py:93
  96.2 24.9 %all-to-all-done.3.x_ref = bf16[16,32,1280]{2,1,0:T(8,128)(2,1)S(1)} async-done(((bf16[16,32,1280]{2,1,0:T(8,128)(2,1)}), bf16[16,32,1280]{2,1,0:T(8,128)(2,1)S(1)}, u32[]{:S(2)}, u32[]{:S(2)}) %all-to-all-start.3) | async-done | bytes 1310752 | tf_op jit(solution)/shard_map/all_to_all | solution.py:199
  121.2 1.7 %place.1 = bf16[16,32,1280]{2,1,0:T(8,128)(2,1)} custom-call(s32[16]{0:T(128)S(1)} %broadcast_select_fusion.comes_ref, bf16[16,32,1280]{2,1,0:T(8,128)(2,1)S(1)} %all-to-all-done.3.x_ref), custom_call_target="tpu_custom_call" | custom-call | bytes 2621440 | tf_op jit(solution)/shard_map/place/pallas_call | solution.py:224
  (68 shorter events, 4.0 us)
Async XLA Ops:
  0.6 7.2 %copy-start.4 = (bf16[256,1280]{1,0:T(8,128)(2,1)S(1)}, bf16[256,1280]{1,0:T(8,128)(2,1)}, u32[]{:S(2)}) copy-start(bf16[256,1280]{1,0:T(8,128)(2,1)} %rows_ref.1) | copy-start | bytes 1966084
  0.7 9.8 %copy-start.7 = (s32[256,1]{0,1:T(1,128)S(1)}, s32[256,1]{0,1:T(1,128)}, u32[]{:S(2)}) copy-start(s32[256,1]{0,1:T(1,128)} %param.9) | copy-start | bytes 3076
  0.7 9.8 %copy-start.8 = (s32[256,1]{0,1:T(1,128)S(1)}, s32[256,1]{0,1:T(1,128)}, u32[]{:S(2)}) copy-start(s32[256,1]{0,1:T(1,128)} %param.11) | copy-start | bytes 3076
  0.7 9.8 %copy-start.9 = (s32[256]{0:T(256)S(1)}, s32[256]{0:T(256)}, u32[]{:S(2)}) copy-start(s32[256]{0:T(256)} %param.10) | copy-start | bytes 3076
  0.7 15.4 %copy-start.5 = (s32[32768]{0:T(1024)S(1)}, s32[32768]{0:T(1024)}, u32[]{:S(2)}) copy-start(s32[32768]{0:T(1024)} %param.7) | copy-start | bytes 393220
  3.6 37.3 %all-to-all-start = ((bf16[8,656,128]{2,1,0:T(8,128)(2,1)}), bf16[8,656,128]{2,1,0:T(8,128)(2,1)S(1)}, u32[]{:S(2)}, u32[]{:S(2)}) async-start(bf16[8,656,128]{2,1,0:T(8,128)(2,1)} %deal.2), calls=%async_computation | async-start | bytes 2686976 | tf_op jit(solution)/shard_map/all_to_all | solution.py:289
  7.8 43.9 %collective-permute-start.2 = (bf16[256,1280]{1,0:T(8,128)(2,1)S(1)}, bf16[256,1280]{1,0:T(8,128)(2,1)S(1)}, u32[]{:S(2)}, u32[]{:S(2)}) collective-permute-start(bf16[256,1280]{1,0:T(8,128)(2,1)S(1)} %copy-done.4), channel_id=1, source_target_pairs={{0,8},{1,9},{2,10},{3,11},{4,12},{5,13},{6,14},{7,15},{8,0},{9,1},... | collective-permute-start | bytes 1966088 | tf_op jit(solution)/shard_map/ppermute | solution.py:296
  10.4 29.7 %collective-permute-start.3 = (s32[3,256]{1,0:T(4,128)S(1)}, s32[3,256]{1,0:T(4,128)S(1)}, u32[]{:S(2)}, u32[]{:S(2)}) collective-permute-start(s32[3,256]{1,0:T(4,128)S(1)} %pad_add_fusion), channel_id=1, source_target_pairs={{0,8},{1,9},{2,10},{3,11},{4,12},{5,13},{6,14},{7,15},{8,0},{9,1},... | collective-permute-start | bytes 9224 | tf_op jit(solution)/shard_map/ppermute | solution.py:296
  11.8 30.8 %collective-permute-start.1 = (bf16[32,1280]{1,0:T(8,128)(2,1)S(1)}, bf16[32,1280]{1,0:T(8,128)(2,1)S(1)}, u32[]{:S(2)}, u32[]{:S(2)}) collective-permute-start(bf16[32,1280]{1,0:T(8,128)(2,1)S(1)} %get-tuple-element.14), channel_id=1, source_target_pairs={{1,0},{2,1},{3,2},{4,3},{5,4},{6,5},{7,6},{8,7},{9,8},{10,9},{11,1... | collective-permute-start | bytes 245768 | tf_op jit(solution)/shard_map/ppermute | solution.py:21
  13.7 28.8 %collective-permute-start = (bf16[32,1280]{1,0:T(8,128)(2,1)S(1)}, bf16[32,1280]{1,0:T(8,128)(2,1)S(1)}, u32[]{:S(2)}, u32[]{:S(2)}) collective-permute-start(bf16[32,1280]{1,0:T(8,128)(2,1)S(1)} %get-tuple-element.15), channel_id=1, source_target_pairs={{0,1},{1,2},{2,3},{3,4},{4,5},{5,6},{6,7},{7,8},{8,9},{9,10},{10,1... | collective-permute-start | bytes 245768 | tf_op jit(solution)/shard_map/ppermute | solution.py:20
  40.2 10.0 %copy-start.6 = (s32[1,256]{1,0:T(1,128)}, s32[1,256]{1,0:T(1,128)S(1)}, u32[]{:S(2)}) copy-start(s32[1,256]{1,0:T(1,128)S(1)} %unstack.12) | copy-start | bytes 3076
  42.6 2.5 %copy-start = (bf16[2048,1280]{1,0:T(8,128)(2,1)S(1)}, bf16[2048,1280]{1,0:T(8,128)(2,1)}, u32[]{:S(2)}) copy-start(bf16[2048,1280]{1,0:T(8,128)(2,1)} %k_ref.3) | copy-start | bytes 15728644
  51.8 0.8 copy-start.3
  55.0 13.3 %all-to-all-start.1 = ((bf16[8,336,128]{2,1,0:T(8,128)(2,1)}), bf16[8,336,128]{2,1,0:T(8,128)(2,1)S(1)}, u32[]{:S(2)}, u32[]{:S(2)}) async-start(bf16[8,336,128]{2,1,0:T(8,128)(2,1)} %deal.3), calls=%async_computation.1 | async-start | bytes 1376256 | tf_op jit(solution)/shard_map/all_to_all | solution.py:289
  68.4 15.7 %all-to-all-start.2 = ((bf16[8,32,1280]{2,1,0:T(8,128)(2,1)}), bf16[8,32,1280]{2,1,0:T(8,128)(2,1)S(1)}, u32[]{:S(2)}, u32[]{:S(2)}) async-start(bf16[8,32,1280]{2,1,0:T(8,128)(2,1)} %bitcast.25), calls=%async_computation.2 | async-start | bytes 1310720 | tf_op jit(solution)/shard_map/all_to_all | solution.py:289
  74.9 2.5 %copy-start.1 = (bf16[2048,1280]{1,0:T(8,128)(2,1)S(1)}, bf16[2048,1280]{1,0:T(8,128)(2,1)}, u32[]{:S(2)}) copy-start(bf16[2048,1280]{1,0:T(8,128)(2,1)} %k_ref.3) | copy-start | bytes 15728644
  77.4 5.1 %copy-start.2 = (bf16[512,1280]{1,0:T(8,128)(2,1)S(1)}, bf16[512,1280]{1,0:T(8,128)(2,1)}, u32[]{:S(2)}) copy-start(bf16[512,1280]{1,0:T(8,128)(2,1)} %convolution_convert_fusion) | copy-start | bytes 3932164
  84.1 37.1 %all-to-all-start.3 = ((bf16[16,32,1280]{2,1,0:T(8,128)(2,1)}), bf16[16,32,1280]{2,1,0:T(8,128)(2,1)S(1)}, u32[]{:S(2)}, u32[]{:S(2)}) async-start(bf16[16,32,1280]{2,1,0:T(8,128)(2,1)} %bitcast.50), calls=%async_computation.3 | async-start | bytes 2621440 | tf_op jit(solution)/shard_map/all_to_all | solution.py:199

commit v10 on v9

--- a/solution.py
+++ b/solution.py
@@ -297,7 +297,8 @@
         near = exchange_half(deal(images, owner, shard, anchor, first, members, cap, 2))
         docs, goes, comes = slots_of(*told_by(near))
         aligned = attend(near, cap, docs, known)
-        sent, mirrored = lax.optimization_barrier((one_hot_dot(puts(goes), aligned), mirrored))
+        sent = one_hot_dot(puts(goes), aligned)
+        sent, mirrored, codes_mirror = lax.optimization_barrier((sent, mirrored, codes_mirror))
 
         far = exchange_half(deal(mirrored, *codes_mirror, first, members, cap, 1))
         far_images = exchange_half(by_shard(mirrored, codes_mirror[0], codes_mirror[1], first, half))

time: 124 us -> 123 us (level)
  waiting for transfers between devices: 55.7 us -> 52.8 us
  starting transfers between devices: 27.3 us -> 29.5 us
    ppermute x1, waiting for transfers between devices: 23.9 us -> 0.01 us  [shards(): lax.ppermute(codes, 'docs', across)]
    all_to_all x3, waiting for transfers between devices: 6.87 us -> 27.8 us  [exchange_half(): lax.all_to_all(x, 'docs', split_axis=0, concat_axis=0, tiled=True, axis_i...]
    all_to_all x3, starting transfers between devices: 13.3 us -> 15 us  [exchange_half(): lax.all_to_all(x, 'docs', split_axis=0, concat_axis=0, tiled=True, axis_i...]
  transfers between devices with their start and end apart: 8 -> 8, of which waited for: 3 -> 3; matrix products, arithmetic and copies ran while one was open for 9% -> 8% of each run, Pallas kernels for 13% -> 13%
where the time goes in v10:
time: 123 us; the launch traced here: 121 us
  waiting for transfers between devices  52.8 us (43%)
  starting transfers between devices  29.5 us (24%)
  Pallas kernels  22.5 us (18%)
  local copies, waits for them, and re-layouts  7.22 us (6%)
  matrix products  5.72 us (5%)
  other arithmetic  2.64 us (2%)
    all_to_all x3, waiting for transfers between devices, exchange_half(): lax.all_to_all(x, 'docs', split_axis=0, concat_axis=0, tiled=True, axis_i...  27.8 us
    all_to_all x1, waiting for transfers between devices, exchange(): return lax.all_to_all(x, 'docs', split_axis=0, concat_axis=0, tiled=True)  24.9 us
    all_to_all x3, starting transfers between devices, exchange_half(): lax.all_to_all(x, 'docs', split_axis=0, concat_axis=0, tiled=True, axis_i...  15 us
    pallas_call x2, Pallas kernels, attend(): pl.pallas_call(functools.partial(attend_kernel, feature ** (-0.5)), grid=...  10.2 us
    all_to_all x1, starting transfers between devices, exchange(): return lax.all_to_all(x, 'docs', split_axis=0, concat_axis=0, tiled=True)  7.17 us
    pallas_call x2, Pallas kernels, deal(): pl.pallas_call(functools.partial(deal_kernel, cap, members), in_specs=[SM...  5.37 us
    pallas_call x1, Pallas kernels, merge(): pl.pallas_call(merge_kernel, grid=(2 * half,), in_specs=[SMEM, pl.BlockSp...  5.22 us
    unnamed x20, local copies, waits for them, and re-layouts  5.03 us
  transfers between devices with their start and end apart: 8, of which 3 were waited for; matrix products, arithmetic and copies ran while one was open for 8% of the time, Pallas kernels for 13%

profile of v10, /device:TPU:14, one launch (start us, length us, event | category | flops | bytes accessed | tf_op | source)
XLA Modules:
  0.0 121.5 jit_solution(18442387999137673973)
XLA Ops:
  0.7 2.9 %deal.2 = bf16[8,656,128]{2,1,0:T(8,128)(2,1)} custom-call(s32[1]{0:T(128)} %bitcast.1.base_ref, s32[2,128]{1,0:T(2,128)} %bitcast.55, s32[2,128]{1,0:T(2,128)} %bitcast.57, s32[2,128]{1,0:T(2,128)} %bitcast.59, bf16[256,1280]{1,0:T(8,128)(2,1)} %rows_ref.1), custom_call_target="tpu_custom_call" | custom-call | flops 335544320 | bytes 1966080 | tf_op jit(solution)/shard_map/deal/pallas_call | solution.py:62
  3.6 4.2 %all-to-all-start = ((bf16[8,656,128]{2,1,0:T(8,128)(2,1)}), bf16[8,656,128]{2,1,0:T(8,128)(2,1)S(1)}, u32[]{:S(2)}, u32[]{:S(2)}) async-start(bf16[8,656,128]{2,1,0:T(8,128)(2,1)} %deal.2), calls=%async_computation | async-start | bytes 2686976 | tf_op jit(solution)/shard_map/all_to_all | solution.py:289
  7.8 2.6 %collective-permute-start.2 = (bf16[256,1280]{1,0:T(8,128)(2,1)S(1)}, bf16[256,1280]{1,0:T(8,128)(2,1)S(1)}, u32[]{:S(2)}, u32[]{:S(2)}) collective-permute-start(bf16[256,1280]{1,0:T(8,128)(2,1)S(1)} %copy-done.4), channel_id=1, source_target_pairs={{0,8},{1,9},{2,10},{3,11},{4,12},{5,13},{6,14},{7,15},{8,0},{9,1},... | collective-permute-start | bytes 1966088 | tf_op jit(solution)/shard_map/ppermute | solution.py:296
  10.8 0.9 fusion.25
  11.8 1.9 %collective-permute-start.1 = (bf16[32,1280]{1,0:T(8,128)(2,1)S(1)}, bf16[32,1280]{1,0:T(8,128)(2,1)S(1)}, u32[]{:S(2)}, u32[]{:S(2)}) collective-permute-start(bf16[32,1280]{1,0:T(8,128)(2,1)S(1)} %get-tuple-element.16), channel_id=1, source_target_pairs={{1,0},{2,1},{3,2},{4,3},{5,4},{6,5},{7,6},{8,7},{9,8},{10,9},{11,1... | collective-permute-start | bytes 245768 | tf_op jit(solution)/shard_map/ppermute | solution.py:21
  13.7 2.4 %collective-permute-start = (bf16[32,1280]{1,0:T(8,128)(2,1)S(1)}, bf16[32,1280]{1,0:T(8,128)(2,1)S(1)}, u32[]{:S(2)}, u32[]{:S(2)}) collective-permute-start(bf16[32,1280]{1,0:T(8,128)(2,1)S(1)} %get-tuple-element.17), channel_id=1, source_target_pairs={{0,1},{1,2},{2,3},{3,4},{4,5},{5,6},{6,7},{7,8},{8,9},{9,10},{10,1... | collective-permute-start | bytes 245768 | tf_op jit(solution)/shard_map/ppermute | solution.py:20
  16.3 21.0 %all-to-all-done.q_ref.near_ref = bf16[8,656,128]{2,1,0:T(8,128)(2,1)S(1)} async-done(((bf16[8,656,128]{2,1,0:T(8,128)(2,1)}), bf16[8,656,128]{2,1,0:T(8,128)(2,1)S(1)}, u32[]{:S(2)}, u32[]{:S(2)}) %all-to-all-start) | async-done | bytes 1343520 | tf_op jit(solution)/shard_map/all_to_all | solution.py:289
  38.2 0.4 select_reduce_fusion.1
  38.8 2.5 %copy-done = bf16[2048,1280]{1,0:T(8,128)(2,1)S(1)} copy-done((bf16[2048,1280]{1,0:T(8,128)(2,1)S(1)}, bf16[2048,1280]{1,0:T(8,128)(2,1)}, u32[]{:S(2)}) %copy-start) | copy-done | bytes 5242904
  41.3 5.1 %attend.2 = bf16[256,1280]{1,0:T(8,128)(2,1)S(1)} custom-call(bf16[8,656,128]{2,1,0:T(8,128)(2,1)S(1)} %all-to-all-done.q_ref.near_ref, s32[256,1]{1,0:T(8,128)S(1)} %copy.32.doc_ref, bf16[2048,1280]{1,0:T(8,128)(2,1)S(1)} %copy-done, bf16[32,1280]{1,0:T(8,128)(2,1)S(1)} %collective-permute-done.before_ref, ...), custom_call_target="tpu_custom_call" | custom-call | flops 2684354560 | bytes 6553600 | tf_op jit(solution)/shard_map/attend/pallas_call | solution.py:142
  46.4 1.6 %convolution_convert_fusion = bf16[512,1280]{1,0:T(8,128)(2,1)} fusion(bf16[256,1280]{1,0:T(8,128)(2,1)S(1)} %attend.2, s32[256]{0:T(256)S(1)} %fusion.22, pred[256]{0:T(512)(128)(4,1)S(1)} %ge.23), kind=kOutput, calls=%fused_computation | convolution fusion | flops 336461824 | bytes 1967360 | tf_op jit(solution)/shard_map/dot_general | solution.py:237
  48.2 0.6 multiply_add_fusion
  48.8 2.4 %deal.3 = bf16[8,336,128]{2,1,0:T(8,128)(2,1)} custom-call(s32[1]{0:T(128)} %bitcast.1.base_ref, s32[2,128]{1,0:T(2,128)} %bitcast.54, s32[2,128]{1,0:T(2,128)} %bitcast.66, s32[2,128]{1,0:T(2,128)} %bitcast.65, bf16[256,1280]{1,0:T(8,128)(2,1)} %copy-done.3), custom_call_target="tpu_custom_call" | custom-call | flops 167772160 | bytes 1310720 | tf_op jit(solution)/shard_map/deal/pallas_call | solution.py:62
  51.3 5.9 %all-to-all-start.1 = ((bf16[8,336,128]{2,1,0:T(8,128)(2,1)}), bf16[8,336,128]{2,1,0:T(8,128)(2,1)S(1)}, u32[]{:S(2)}, u32[]{:S(2)}) async-start(bf16[8,336,128]{2,1,0:T(8,128)(2,1)} %deal.3), calls=%async_computation.1 | async-start | bytes 1376256 | tf_op jit(solution)/shard_map/all_to_all | solution.py:289
  57.1 2.3 %convolution_convert_fusion.1 = bf16[256,1280]{1,0:T(8,128)(2,1)} fusion(bf16[256,1280]{1,0:T(8,128)(2,1)} %copy-done.3, s32[256]{0:T(256)S(1)} %bitcast.64), kind=kOutput, calls=%fused_computation.2 | convolution fusion | flops 168165376 | bytes 1311744 | tf_op jit(solution)/shard_map/dot_general | solution.py:237
  59.4 6.9 %all-to-all-done.1.q_ref = bf16[8,336,128]{2,1,0:T(8,128)(2,1)S(1)} async-done(((bf16[8,336,128]{2,1,0:T(8,128)(2,1)}), bf16[8,336,128]{2,1,0:T(8,128)(2,1)S(1)}, u32[]{:S(2)}, u32[]{:S(2)}) %all-to-all-start.1) | async-done | bytes 688160 | tf_op jit(solution)/shard_map/all_to_all | solution.py:289
  66.3 4.9 %all-to-all-start.2 = ((bf16[8,32,1280]{2,1,0:T(8,128)(2,1)}), bf16[8,32,1280]{2,1,0:T(8,128)(2,1)S(1)}, u32[]{:S(2)}, u32[]{:S(2)}) async-start(bf16[8,32,1280]{2,1,0:T(8,128)(2,1)} %bitcast.25), calls=%async_computation.2 | async-start | bytes 1310720 | tf_op jit(solution)/shard_map/all_to_all | solution.py:289
  72.8 2.5 %copy-done.1 = bf16[2048,1280]{1,0:T(8,128)(2,1)S(1)} copy-done((bf16[2048,1280]{1,0:T(8,128)(2,1)S(1)}, bf16[2048,1280]{1,0:T(8,128)(2,1)}, u32[]{:S(2)}) %copy-start.1) | copy-done | bytes 5242904
  75.3 5.1 %attend.3 = bf16[256,1280]{1,0:T(8,128)(2,1)S(1)} custom-call(bf16[8,336,128]{2,1,0:T(8,128)(2,1)S(1)} %all-to-all-done.1.q_ref, s32[256,1]{1,0:T(8,128)S(1)} %copy.37.doc_ref, bf16[2048,1280]{1,0:T(8,128)(2,1)S(1)} %copy-done.1, bf16[32,1280]{1,0:T(8,128)(2,1)S(1)} %collective-permute-done.before_ref, ...), custom_call_target="tpu_custom_call" | custom-call | flops 2684354560 | bytes 6553600 | tf_op jit(solution)/shard_map/attend/pallas_call | solution.py:142
  80.4 1.6 %add_convert_fusion = bf16[512,1280]{1,0:T(8,128)(2,1)} fusion(bf16[512,1280]{1,0:T(8,128)(2,1)S(1)} %copy-done.2, bf16[256,1280]{1,0:T(8,128)(2,1)S(1)} %attend.3, s32[256]{0:T(256)S(1)} %fusion.21, pred[256]{0:T(512)(128)(4,1)S(1)} %ge.25), kind=kOutput, calls=%fused_computation.1 | convolution fusion | flops 337772544 | bytes 3278080 | tf_op jit(solution)/shard_map/dot_general | solution.py:307
  82.0 7.2 %all-to-all-start.3 = ((bf16[16,32,1280]{2,1,0:T(8,128)(2,1)}), bf16[16,32,1280]{2,1,0:T(8,128)(2,1)S(1)}, u32[]{:S(2)}, u32[]{:S(2)}) async-start(bf16[16,32,1280]{2,1,0:T(8,128)(2,1)} %bitcast.50), calls=%async_computation.3 | async-start | bytes 2621440 | tf_op jit(solution)/shard_map/all_to_all | solution.py:199
  89.2 5.2 %merge.1 = bf16[16,32,1280]{2,1,0:T(8,128)(2,1)} custom-call(s32[1]{0:T(128)} %bitcast.low_ref, bf16[8,656,128]{2,1,0:T(8,128)(2,1)S(1)} %all-to-all-done.q_ref.near_ref, bf16[8,32,1280]{2,1,0:T(8,128)(2,1)S(1)} %all-to-all-done.2.far_ref), custom_call_target="tpu_custom_call" | custom-call | bytes 2621440 | tf_op jit(solution)/shard_map/merge/pallas_call | solution.py:93
  94.6 24.9 %all-to-all-done.3.x_ref = bf16[16,32,1280]{2,1,0:T(8,128)(2,1)S(1)} async-done(((bf16[16,32,1280]{2,1,0:T(8,128)(2,1)}), bf16[16,32,1280]{2,1,0:T(8,128)(2,1)S(1)}, u32[]{:S(2)}, u32[]{:S(2)}) %all-to-all-start.3) | async-done | bytes 1310752 | tf_op jit(solution)/shard_map/all_to_all | solution.py:199
  119.6 1.7 %place.1 = bf16[16,32,1280]{2,1,0:T(8,128)(2,1)} custom-call(s32[16]{0:T(128)S(1)} %broadcast_select_fusion.comes_ref, bf16[16,32,1280]{2,1,0:T(8,128)(2,1)S(1)} %all-to-all-done.3.x_ref), custom_call_target="tpu_custom_call" | custom-call | bytes 2621440 | tf_op jit(solution)/shard_map/place/pallas_call | solution.py:224
  (68 shorter events, 3.7 us)
Async XLA Ops:
  0.6 7.2 %copy-start.4 = (bf16[256,1280]{1,0:T(8,128)(2,1)S(1)}, bf16[256,1280]{1,0:T(8,128)(2,1)}, u32[]{:S(2)}) copy-start(bf16[256,1280]{1,0:T(8,128)(2,1)} %rows_ref.1) | copy-start | bytes 1966084
  0.7 9.8 %copy-start.7 = (s32[256,1]{0,1:T(1,128)S(1)}, s32[256,1]{0,1:T(1,128)}, u32[]{:S(2)}) copy-start(s32[256,1]{0,1:T(1,128)} %param.9) | copy-start | bytes 3076
  0.7 9.8 %copy-start.8 = (s32[256,1]{0,1:T(1,128)S(1)}, s32[256,1]{0,1:T(1,128)}, u32[]{:S(2)}) copy-start(s32[256,1]{0,1:T(1,128)} %param.11) | copy-start | bytes 3076
  0.7 9.8 %copy-start.9 = (s32[256]{0:T(256)S(1)}, s32[256]{0:T(256)}, u32[]{:S(2)}) copy-start(s32[256]{0:T(256)} %param.10) | copy-start | bytes 3076
  0.7 15.4 %copy-start.5 = (s32[32768]{0:T(1024)S(1)}, s32[32768]{0:T(1024)}, u32[]{:S(2)}) copy-start(s32[32768]{0:T(1024)} %param.7) | copy-start | bytes 393220
  3.6 33.6 %all-to-all-start = ((bf16[8,656,128]{2,1,0:T(8,128)(2,1)}), bf16[8,656,128]{2,1,0:T(8,128)(2,1)S(1)}, u32[]{:S(2)}, u32[]{:S(2)}) async-start(bf16[8,656,128]{2,1,0:T(8,128)(2,1)} %deal.2), calls=%async_computation | async-start | bytes 2686976 | tf_op jit(solution)/shard_map/all_to_all | solution.py:289
  7.8 40.2 %collective-permute-start.2 = (bf16[256,1280]{1,0:T(8,128)(2,1)S(1)}, bf16[256,1280]{1,0:T(8,128)(2,1)S(1)}, u32[]{:S(2)}, u32[]{:S(2)}) collective-permute-start(bf16[256,1280]{1,0:T(8,128)(2,1)S(1)} %copy-done.4), channel_id=1, source_target_pairs={{0,8},{1,9},{2,10},{3,11},{4,12},{5,13},{6,14},{7,15},{8,0},{9,1},... | collective-permute-start | bytes 1966088 | tf_op jit(solution)/shard_map/ppermute | solution.py:296
  10.4 37.6 %collective-permute-start.3 = (s32[3,256]{1,0:T(4,128)S(1)}, s32[3,256]{1,0:T(4,128)S(1)}, u32[]{:S(2)}, u32[]{:S(2)}) collective-permute-start(s32[3,256]{1,0:T(4,128)S(1)} %pad_add_fusion), channel_id=1, source_target_pairs={{0,8},{1,9},{2,10},{3,11},{4,12},{5,13},{6,14},{7,15},{8,0},{9,1},... | collective-permute-start | bytes 9224 | tf_op jit(solution)/shard_map/ppermute | solution.py:296
  11.8 27.0 %collective-permute-start.1 = (bf16[32,1280]{1,0:T(8,128)(2,1)S(1)}, bf16[32,1280]{1,0:T(8,128)(2,1)S(1)}, u32[]{:S(2)}, u32[]{:S(2)}) collective-permute-start(bf16[32,1280]{1,0:T(8,128)(2,1)S(1)} %get-tuple-element.16), channel_id=1, source_target_pairs={{1,0},{2,1},{3,2},{4,3},{5,4},{6,5},{7,6},{8,7},{9,8},{10,9},{11,1... | collective-permute-start | bytes 245768 | tf_op jit(solution)/shard_map/ppermute | solution.py:21
  13.7 25.1 %collective-permute-start = (bf16[32,1280]{1,0:T(8,128)(2,1)S(1)}, bf16[32,1280]{1,0:T(8,128)(2,1)S(1)}, u32[]{:S(2)}, u32[]{:S(2)}) collective-permute-start(bf16[32,1280]{1,0:T(8,128)(2,1)S(1)} %get-tuple-element.17), channel_id=1, source_target_pairs={{0,1},{1,2},{2,3},{3,4},{4,5},{5,6},{6,7},{7,8},{8,9},{9,10},{10,1... | collective-permute-start | bytes 245768 | tf_op jit(solution)/shard_map/ppermute | solution.py:20
  38.8 2.5 %copy-start = (bf16[2048,1280]{1,0:T(8,128)(2,1)S(1)}, bf16[2048,1280]{1,0:T(8,128)(2,1)}, u32[]{:S(2)}) copy-start(bf16[2048,1280]{1,0:T(8,128)(2,1)} %k_ref.3) | copy-start | bytes 15728644
  48.0 0.8 copy-start.3
  48.0 0.8 copy-start.6
  51.3 15.0 %all-to-all-start.1 = ((bf16[8,336,128]{2,1,0:T(8,128)(2,1)}), bf16[8,336,128]{2,1,0:T(8,128)(2,1)S(1)}, u32[]{:S(2)}, u32[]{:S(2)}) async-start(bf16[8,336,128]{2,1,0:T(8,128)(2,1)} %deal.3), calls=%async_computation.1 | async-start | bytes 1376256 | tf_op jit(solution)/shard_map/all_to_all | solution.py:289
  66.3 15.7 %all-to-all-start.2 = ((bf16[8,32,1280]{2,1,0:T(8,128)(2,1)}), bf16[8,32,1280]{2,1,0:T(8,128)(2,1)S(1)}, u32[]{:S(2)}, u32[]{:S(2)}) async-start(bf16[8,32,1280]{2,1,0:T(8,128)(2,1)} %bitcast.25), calls=%async_computation.2 | async-start | bytes 1310720 | tf_op jit(solution)/shard_map/all_to_all | solution.py:289
  72.8 2.5 %copy-start.1 = (bf16[2048,1280]{1,0:T(8,128)(2,1)S(1)}, bf16[2048,1280]{1,0:T(8,128)(2,1)}, u32[]{:S(2)}) copy-start(bf16[2048,1280]{1,0:T(8,128)(2,1)} %k_ref.3) | copy-start | bytes 15728644
  75.3 5.1 %copy-start.2 = (bf16[512,1280]{1,0:T(8,128)(2,1)S(1)}, bf16[512,1280]{1,0:T(8,128)(2,1)}, u32[]{:S(2)}) copy-start(bf16[512,1280]{1,0:T(8,128)(2,1)} %convolution_convert_fusion) | copy-start | bytes 3932164
  82.0 37.6 %all-to-all-start.3 = ((bf16[16,32,1280]{2,1,0:T(8,128)(2,1)}), bf16[16,32,1280]{2,1,0:T(8,128)(2,1)S(1)}, u32[]{:S(2)}, u32[]{:S(2)}) async-start(bf16[16,32,1280]{2,1,0:T(8,128)(2,1)} %bitcast.50), calls=%async_computation.3 | async-start | bytes 2621440 | tf_op jit(solution)/shard_map/all_to_all | solution.py:199

commit v11 on v10

--- a/solution.py
+++ b/solution.py
@@ -73,31 +73,26 @@
 
 
 def merge_kernel(low_ref, near_ref, far_ref, o_ref):
-    cap, feature = far_ref.shape[1:]
+    cap, feature = o_ref.shape[1:]
     size = cap * feature // LANES
     s, half = pl.program_id(0), pl.num_programs(0) // 2
     is_near = (s < half) == (low_ref[0] == 1)
 
-    @pl.when(is_near)
-    def _():
+    def take(ref):
         for t, r, c in tiles(cap, feature):
-            o_ref[0, r : r + TILE, c : c + LANES] = near_ref[0, size + t : size + t + TILE]
-
-    @pl.when(jnp.logical_not(is_near))
-    def _():
-        o_ref[...] = far_ref[...]
-
-
-def merge(near, far, low):
-    half, cap, feature = far.shape
+            o_ref[0, r : r + TILE, c : c + LANES] = ref[0, size + t : size + t + TILE]
+
+    pl.when(is_near)(lambda: take(near_ref))
+    pl.when(jnp.logical_not(is_near))(lambda: take(far_ref))
+
+
+def merge(near, far, low, cap, feature):
+    half = near.shape[0]
+    spec = pl.BlockSpec((1, *near.shape[1:]), lambda i: (i % half, 0, 0))
     return pl.pallas_call(
         merge_kernel,
         grid=(2 * half,),
-        in_specs=[
-            SMEM,
-            pl.BlockSpec((1, *near.shape[1:]), lambda i: (i % half, 0, 0)),
-            pl.BlockSpec((1, cap, feature), lambda i: (i % half, 0, 0)),
-        ],
+        in_specs=[SMEM, spec, spec],
         out_specs=pl.BlockSpec((1, cap, feature), lambda i: (i, 0, 0)),
         out_shape=jax.ShapeDtypeStruct((2 * half, cap, feature), far.dtype),
         compiler_params=pltpu.CompilerParams(vmem_limit_bytes=8 * 1024 * 1024),
@@ -107,26 +102,36 @@
 
 
 def attend_kernel(temper, q_ref, doc_ref, k_ref, before_ref, after_ref, id_ref, id_before_ref, id_after_ref, o_ref, *scratch):
+    doc = doc_ref[...]
+    here = lambda: None
+    parts = [(before_ref, id_before_ref, here), (after_ref, id_after_ref, here)]
     if scratch:
-        rows, cap = scratch[0], o_ref.shape[0] // q_ref.shape[0]
+        rows, held, sems = scratch
+        length, cap = held.shape[0] // sems.shape[0], o_ref.shape[0] // q_ref.shape[0]
+        spans = [pl.ds(i * length, length) for i in range(sems.shape[0])]
+        copies = [pltpu.make_async_copy(k_ref.at[x], held.at[x], sems.at[i]) for i, x in enumerate(spans)]
+        for c in copies:
+            c.start()
         for d in range(q_ref.shape[0]):
             for t, r, c in tiles(cap, rows.shape[1]):
                 rows[d * cap + r : d * cap + r + TILE, c : c + LANES] = q_ref[d, t : t + TILE]
         q_ref = rows
+        parts += [(held.at[x], id_ref.at[:, x], c.wait) for x, c in zip(spans, copies)]
+    else:
+        parts.append((k_ref, id_ref, here))
     q = q_ref[...]
-    doc = doc_ref[...]
-    parts = ((k_ref, id_ref), (before_ref, id_before_ref), (after_ref, id_after_ref))
     scores = []
-    for rows, ids in parts:
+    for rows, ids, ready in parts:
+        ready()
         s = lax.dot_general(q, rows[...], (((1,), (1,)), ((), ())), preferred_element_type=jnp.float32) * temper
         scores.append(jnp.where(doc == ids[...], s, -1e30))
     peak = functools.reduce(jnp.maximum, [jnp.max(s, axis=1, keepdims=True) for s in scores])
-    raised = [jnp.where(doc == ids[...], jnp.exp(s - peak), 0.0) for s, (_, ids) in zip(scores, parts)]
+    raised = [jnp.where(doc == ids[...], jnp.exp(s - peak), 0.0) for s, (_, ids, _) in zip(scores, parts)]
     total = sum(jnp.sum(r, axis=1, keepdims=True) for r in raised)
     total = jnp.where(total > 0.0, total, 1.0)
     o_ref[...] = sum(
         jnp.dot((r / total).astype(jnp.bfloat16), rows[...], preferred_element_type=jnp.float32)
-        for r, (rows, _) in zip(raised, parts)
+        for r, (rows, _, _) in zip(raised, parts)
     ).astype(jnp.bfloat16)
 
 
@@ -135,6 +140,7 @@
     block = min(256, rows)
     whole = lambda a: pl.BlockSpec(a.shape, lambda i: (0, 0))
     tiled = queries.ndim == 3
+    block, chunks = rows if tiled else block, 4
     queries_spec = pl.BlockSpec((block, feature), lambda i: (i, 0))
     if tiled:
         region = cap * feature // LANES
@@ -145,12 +151,19 @@
         in_specs=[
             queries_spec,
             pl.BlockSpec((block, 1), lambda i: (i, 0)),
-            *[whole(a) for a in known],
+            HBM if tiled else whole(known[0]),
+            *[whole(a) for a in known[1:]],
         ],
         out_specs=pl.BlockSpec((block, feature), lambda i: (i, 0)),
         out_shape=jax.ShapeDtypeStruct((rows, feature), jnp.bfloat16),
-        scratch_shapes=[pltpu.VMEM((block, feature), jnp.bfloat16)] * tiled,
-        compiler_params=pltpu.CompilerParams(vmem_limit_bytes=40 * 1024 * 1024),
+        scratch_shapes=[
+            pltpu.VMEM((block, feature), jnp.bfloat16),
+            pltpu.VMEM((own, feature), jnp.bfloat16),
+            pltpu.SemaphoreType.DMA((chunks,)),
+        ]
+        if tiled
+        else [],
+        compiler_params=pltpu.CompilerParams(vmem_limit_bytes=(59 if tiled else 40) * 1024 * 1024),
         cost_estimate=pl.CostEstimate(
             flops=4 * rows * own * feature, bytes_accessed=2 * (own + 2 * rows) * feature, transcendentals=rows * own
         ),
@@ -279,7 +292,7 @@
         return (row[:, None] == (block * cap + slot)[None, :]) & (block >= 0)[None, :]
 
     whole_tiles = cap % TILE == 0 and feature % LANES == 0 and n % LANES == 0 and members % 2 == 0
-    if whole_tiles and 4 * n <= TILE * LANES and members <= 256 and own <= 256 * LANES:
+    if whole_tiles and 4 * n <= TILE * LANES and members <= 256 and own % (4 * TILE) == 0 and own <= 256 * LANES:
         half = members // 2
         first = me // half * half
         halves = [list(range(half)), list(range(half, members))]
@@ -295,20 +308,20 @@
         codes = jnp.stack([owner, shard, anchor])
         mirrored, codes_mirror = lax.ppermute(images, "docs", across), lax.ppermute(codes, "docs", across)
         near = exchange_half(deal(images, owner, shard, anchor, first, members, cap, 2))
+        near, mirrored, codes_mirror = lax.optimization_barrier((near, mirrored, codes_mirror))
         docs, goes, comes = slots_of(*told_by(near))
         aligned = attend(near, cap, docs, known)
         sent = one_hot_dot(puts(goes), aligned)
-        sent, mirrored, codes_mirror = lax.optimization_barrier((sent, mirrored, codes_mirror))
-
-        far = exchange_half(deal(mirrored, *codes_mirror, first, members, cap, 1))
-        far_images = exchange_half(by_shard(mirrored, codes_mirror[0], codes_mirror[1], first, half))
+
+        far = exchange_half(deal(mirrored, *codes_mirror, first, members, cap, 2))
+        sent, far = lax.optimization_barrier((sent, far))
         docs, goes, comes_far = slots_of(*told_by(far))
         aligned = attend(far, cap, docs, known)
         sent += jnp.dot(puts(goes).astype(jnp.bfloat16), aligned, preferred_element_type=jnp.float32)
-        sent, far_images = lax.optimization_barrier((sent.astype(jnp.bfloat16), far_images))
+        sent = sent.astype(jnp.bfloat16)
         low = first == 0
         comes = jnp.where(low, jnp.concatenate([comes, comes_far]), jnp.concatenate([comes_far, comes]))
-        loaded_images = merge(near, far_images, low).reshape(members * cap, feature)
+        loaded_images = merge(near, far, low, cap, feature).reshape(members * cap, feature)
     else:
         packed = (owner * members + shard) * own + anchor
         every, queries = every_device(packed, exchange(by_shard(images, owner, owner, 0, members)))

time: 123 us -> 119 us (0.967)
  Pallas kernels: 22.5 us -> 30.3 us
  starting transfers between devices: 29.5 us -> 22.5 us
  local copies, waits for them, and re-layouts: 7.22 us -> 5.52 us
    all_to_all x3 -> x2, waiting for transfers between devices: 27.8 us -> 3.3 us  [exchange_half(): lax.all_to_all(x, 'docs', split_axis=0, concat_axis=0, tiled=True, axis_i...]
    ppermute x1, waiting for transfers between devices: 0.01 us -> 23.4 us  [shards(): lax.ppermute(codes, 'docs', across)]
    all_to_all x3 -> x2, starting transfers between devices: 15 us -> 8.4 us  [exchange_half(): lax.all_to_all(x, 'docs', split_axis=0, concat_axis=0, tiled=True, axis_i...]
    pallas_call x2, Pallas kernels: 10.2 us -> 16.7 us  [attend(): pl.pallas_call(functools.partial(attend_kernel, feature ** (-0.5)), grid=...]
    unnamed x20 -> x30, local copies, waits for them, and re-layouts: 5.03 us -> 0.88 us
    dot_general x2 -> x1, matrix products: 3.84 us -> 1.61 us  [one_hot_dot(): jnp.dot(table.astype(jnp.bfloat16), rows, preferred_element_type=jnp.floa...]
    broadcast_in_dim x2, local copies, waits for them, and re-layouts: 0.28 us -> 1.61 us  [slots_of(): return (docs[:, None], goes, comes)]
  transfers between devices with their start and end apart: 8 -> 7, of which waited for: 3 -> 3; matrix products, arithmetic and copies ran while one was open for 8% -> 5% of each run, Pallas kernels for 13% -> 14%
where the time goes in v11:
time: 119 us; the launch traced here: 117 us
  waiting for transfers between devices  51.7 us (43%)
  Pallas kernels  30.3 us (25%)
  starting transfers between devices  22.5 us (19%)
  local copies, waits for them, and re-layouts  5.52 us (5%)
  matrix products  4.67 us (4%)
  other arithmetic  1.91 us (2%)
    all_to_all x1, waiting for transfers between devices, exchange(): return lax.all_to_all(x, 'docs', split_axis=0, concat_axis=0, tiled=True)  25 us
    ppermute x1, waiting for transfers between devices, shards(): lax.ppermute(codes, 'docs', across)  23.4 us
    pallas_call x2, Pallas kernels, attend(): pl.pallas_call(functools.partial(attend_kernel, feature ** (-0.5)), grid=...  16.7 us
    all_to_all x2, starting transfers between devices, exchange_half(): lax.all_to_all(x, 'docs', split_axis=0, concat_axis=0, tiled=True, axis_i...  8.4 us
    all_to_all x1, starting transfers between devices, exchange(): return lax.all_to_all(x, 'docs', split_axis=0, concat_axis=0, tiled=True)  6.82 us
    pallas_call x2, Pallas kernels, deal(): pl.pallas_call(functools.partial(deal_kernel, cap, members), in_specs=[SM...  5.81 us
    pallas_call x1, Pallas kernels, merge(): pl.pallas_call(merge_kernel, grid=(2 * half,), in_specs=[SMEM, spec, spec...  5.27 us
    all_to_all x2, waiting for transfers between devices, exchange_half(): lax.all_to_all(x, 'docs', split_axis=0, concat_axis=0, tiled=True, axis_i...  3.3 us
  transfers between devices with their start and end apart: 7, of which 3 were waited for; matrix products, arithmetic and copies ran while one was open for 5% of the time, Pallas kernels for 14%

profile of v11, /device:TPU:14, one launch (start us, length us, event | category | flops | bytes accessed | tf_op | source)
XLA Modules:
  0.0 117.5 jit_solution(10903969417133195656)
XLA Ops:
  0.7 3.0 %deal.2 = bf16[8,656,128]{2,1,0:T(8,128)(2,1)} custom-call(s32[1]{0:T(128)} %bitcast.1.base_ref, s32[2,128]{1,0:T(2,128)} %bitcast.52, s32[2,128]{1,0:T(2,128)} %bitcast.54, s32[2,128]{1,0:T(2,128)} %bitcast.56, bf16[256,1280]{1,0:T(8,128)(2,1)} %rows_ref.1), custom_call_target="tpu_custom_call" | custom-call | flops 335544320 | bytes 1966080 | tf_op jit(solution)/shard_map/deal/pallas_call | solution.py:62
  3.7 4.2 %all-to-all-start = ((bf16[8,656,128]{2,1,0:T(8,128)(2,1)}), bf16[8,656,128]{2,1,0:T(8,128)(2,1)S(1)}, u32[]{:S(2)}, u32[]{:S(2)}) async-start(bf16[8,656,128]{2,1,0:T(8,128)(2,1)} %deal.2), calls=%async_computation | async-start | bytes 2686976 | tf_op jit(solution)/shard_map/all_to_all | solution.py:302
  7.9 2.6 %collective-permute-start = (bf16[256,1280]{1,0:T(8,128)(2,1)S(1)}, bf16[256,1280]{1,0:T(8,128)(2,1)S(1)}, u32[]{:S(2)}, u32[]{:S(2)}) collective-permute-start(bf16[256,1280]{1,0:T(8,128)(2,1)S(1)} %copy-done.4), channel_id=1, source_target_pairs={{0,8},{1,9},{2,10},{3,11},{4,12},{5,13},{6,14},{7,15},{8,0},{9,1},... | collective-permute-start | bytes 1966088 | tf_op jit(solution)/shard_map/ppermute | solution.py:309
  10.9 0.9 fusion.19
  11.8 1.9 %collective-permute-start.3 = (bf16[32,1280]{1,0:T(8,128)(2,1)S(1)}, bf16[32,1280]{1,0:T(8,128)(2,1)S(1)}, u32[]{:S(2)}, u32[]{:S(2)}) collective-permute-start(bf16[32,1280]{1,0:T(8,128)(2,1)S(1)} %get-tuple-element.16), channel_id=1, source_target_pairs={{1,0},{2,1},{3,2},{4,3},{5,4},{6,5},{7,6},{8,7},{9,8},{10,9},{11,1... | collective-permute-start | bytes 245768 | tf_op jit(solution)/shard_map/ppermute | solution.py:21
  13.7 2.4 %collective-permute-start.2 = (bf16[32,1280]{1,0:T(8,128)(2,1)S(1)}, bf16[32,1280]{1,0:T(8,128)(2,1)S(1)}, u32[]{:S(2)}, u32[]{:S(2)}) collective-permute-start(bf16[32,1280]{1,0:T(8,128)(2,1)S(1)} %get-tuple-element.17), channel_id=1, source_target_pairs={{0,1},{1,2},{2,3},{3,4},{4,5},{5,6},{6,7},{7,8},{8,9},{9,10},{10,1... | collective-permute-start | bytes 245768 | tf_op jit(solution)/shard_map/ppermute | solution.py:20
  16.2 0.7 fusion.18
  16.8 23.4 %collective-permute-done.1 = s32[3,256]{1,0:T(4,128)S(1)} collective-permute-done((s32[3,256]{1,0:T(4,128)S(1)}, s32[3,256]{1,0:T(4,128)S(1)}, u32[]{:S(2)}, u32[]{:S(2)}) %collective-permute-start.1) | collective-permute-done | bytes 3104 | tf_op jit(solution)/shard_map/ppermute | solution.py:309
  40.2 0.6 fusion.21
  41.0 2.8 %deal.3 = bf16[8,656,128]{2,1,0:T(8,128)(2,1)} custom-call(s32[1]{0:T(128)} %bitcast.1.base_ref, s32[2,128]{1,0:T(2,128)} %bitcast.60, s32[2,128]{1,0:T(2,128)} %bitcast.59, s32[2,128]{1,0:T(2,128)} %bitcast.58, bf16[256,1280]{1,0:T(8,128)(2,1)} %copy-done.5), custom_call_target="tpu_custom_call" | custom-call | flops 335544320 | bytes 1966080 | tf_op jit(solution)/shard_map/deal/pallas_call | solution.py:62
  43.9 4.2 %all-to-all-start.1 = ((bf16[8,656,128]{2,1,0:T(8,128)(2,1)}), bf16[8,656,128]{2,1,0:T(8,128)(2,1)S(1)}, u32[]{:S(2)}, u32[]{:S(2)}) async-start(bf16[8,656,128]{2,1,0:T(8,128)(2,1)} %deal.3), calls=%async_computation.1 | async-start | bytes 2686976 | tf_op jit(solution)/shard_map/all_to_all | solution.py:302
  49.1 0.4 select_reduce_fusion.1
  49.5 0.8 copy.29.doc_ref
  50.3 0.6 copy-done.12
  51.0 8.3 %attend.2 = bf16[256,1280]{1,0:T(8,128)(2,1)} custom-call(bf16[8,656,128]{2,1,0:T(8,128)(2,1)} %copy-done, s32[256,1]{1,0:T(8,128)} %copy.29.doc_ref, bf16[2048,1280]{1,0:T(8,128)(2,1)} %k_ref.3, bf16[32,1280]{1,0:T(8,128)(2,1)} %copy-done.13, bf16[32,1280]{1,0:T(8,128)(2,1)} %copy-done.12, s32[1,2048]{1,0:T(1,128)} %bitcast.48, ...), custom_call_target="tpu_custom_call" | custom-call | flops 2684354560 | bytes 6553600 | tf_op jit(solution)/shard_map/attend/pallas_call | solution.py:148
  59.3 1.6 %convolution_convert_fusion = bf16[512,1280]{1,0:T(8,128)(2,1)S(1)} fusion(bf16[256,1280]{1,0:T(8,128)(2,1)} %attend.2, s32[256]{0:T(256)S(1)} %fusion.16, pred[256]{0:T(512)(128)(4,1)S(1)} %ge.23), kind=kOutput, calls=%fused_computation.2 | convolution fusion | flops 336461824 | bytes 1967360 | tf_op jit(solution)/shard_map/dot_general | solution.py:250
  60.9 3.3 %all-to-all-done.1.far_ref.q_ref = bf16[8,656,128]{2,1,0:T(8,128)(2,1)S(1)} async-done(((bf16[8,656,128]{2,1,0:T(8,128)(2,1)}), bf16[8,656,128]{2,1,0:T(8,128)(2,1)S(1)}, u32[]{:S(2)}, u32[]{:S(2)}) %all-to-all-start.1) | async-done | bytes 1343520 | tf_op jit(solution)/shard_map/all_to_all | solution.py:302
  65.7 0.8 copy.35.doc_ref
  66.5 8.4 %attend.3 = bf16[256,1280]{1,0:T(8,128)(2,1)} custom-call(bf16[8,656,128]{2,1,0:T(8,128)(2,1)} %copy-done.2, s32[256,1]{1,0:T(8,128)} %copy.35.doc_ref, bf16[2048,1280]{1,0:T(8,128)(2,1)} %k_ref.3, bf16[32,1280]{1,0:T(8,128)(2,1)} %copy-done.13, bf16[32,1280]{1,0:T(8,128)(2,1)} %copy-done.12, s32[1,2048]{1,0:T(1,128)} %bitcast.49, ...), custom_call_target="tpu_custom_call" | custom-call | flops 2684354560 | bytes 6553600 | tf_op jit(solution)/shard_map/attend/pallas_call | solution.py:148
  74.9 2.8 %fusion = bf16[512,1280]{1,0:T(8,128)(2,1)} fusion(bf16[256,1280]{1,0:T(8,128)(2,1)} %attend.3, bf16[512,1280]{1,0:T(8,128)(2,1)S(1)} %convolution_convert_fusion, s32[256]{0:T(256)S(1)} %fusion.15, pred[256]{0:T(512)(128)(4,1)S(1)} %ge.25), kind=kOutput, calls=%fused_computation.1 | convolution fusion | flops 337772544 | bytes 3278080 | tf_op jit(solution)/shard_map/dot_general | solution.py:320
  77.6 6.8 %all-to-all-start.2 = ((bf16[16,32,1280]{2,1,0:T(8,128)(2,1)}), bf16[16,32,1280]{2,1,0:T(8,128)(2,1)}, u32[]{:S(2)}, u32[]{:S(2)}) async-start(bf16[16,32,1280]{2,1,0:T(8,128)(2,1)} %bitcast.45), calls=%async_computation.2 | async-start | bytes 2621440 | tf_op jit(solution)/shard_map/all_to_all | solution.py:212
  84.5 5.3 %merge.1 = bf16[16,32,1280]{2,1,0:T(8,128)(2,1)} custom-call(s32[1]{0:T(128)} %bitcast.low_ref, bf16[8,656,128]{2,1,0:T(8,128)(2,1)S(1)} %copy-done.1, bf16[8,656,128]{2,1,0:T(8,128)(2,1)S(1)} %copy-done.3), custom_call_target="tpu_custom_call" | custom-call | bytes 2621440 | tf_op jit(solution)/shard_map/merge/pallas_call | solution.py:92
  90.0 25.0 %all-to-all-done.2.x_ref = bf16[16,32,1280]{2,1,0:T(8,128)(2,1)} async-done(((bf16[16,32,1280]{2,1,0:T(8,128)(2,1)}), bf16[16,32,1280]{2,1,0:T(8,128)(2,1)}, u32[]{:S(2)}, u32[]{:S(2)}) %all-to-all-start.2) | async-done | bytes 1310752 | tf_op jit(solution)/shard_map/all_to_all | solution.py:212
  115.0 2.5 %place.1 = bf16[16,32,1280]{2,1,0:T(8,128)(2,1)} custom-call(s32[16]{0:T(128)S(1)} %broadcast_select_fusion.comes_ref, bf16[16,32,1280]{2,1,0:T(8,128)(2,1)} %all-to-all-done.2.x_ref), custom_call_target="tpu_custom_call" | custom-call | bytes 2621440 | tf_op jit(solution)/shard_map/place/pallas_call | solution.py:237
  (71 shorter events, 3.3 us)
Async XLA Ops:
  0.6 7.2 %copy-start.4 = (bf16[256,1280]{1,0:T(8,128)(2,1)S(1)}, bf16[256,1280]{1,0:T(8,128)(2,1)}, u32[]{:S(2)}) copy-start(bf16[256,1280]{1,0:T(8,128)(2,1)} %rows_ref.1) | copy-start | bytes 1966084
  0.7 9.8 %copy-start.9 = (s32[256,1]{0,1:T(1,128)S(1)}, s32[256,1]{0,1:T(1,128)}, u32[]{:S(2)}) copy-start(s32[256,1]{0,1:T(1,128)} %param.9) | copy-start | bytes 3076
  0.7 9.8 %copy-start.10 = (s32[256,1]{0,1:T(1,128)S(1)}, s32[256,1]{0,1:T(1,128)}, u32[]{:S(2)}) copy-start(s32[256,1]{0,1:T(1,128)} %param.11) | copy-start | bytes 3076
  0.7 9.8 %copy-start.11 = (s32[256]{0:T(256)S(1)}, s32[256]{0:T(256)}, u32[]{:S(2)}) copy-start(s32[256]{0:T(256)} %param.10) | copy-start | bytes 3076
  0.7 15.5 %copy-start.6 = (s32[32768]{0:T(1024)S(1)}, s32[32768]{0:T(1024)}, u32[]{:S(2)}) copy-start(s32[32768]{0:T(1024)} %param.7) | copy-start | bytes 393220
  3.7 36.5 %all-to-all-start = ((bf16[8,656,128]{2,1,0:T(8,128)(2,1)}), bf16[8,656,128]{2,1,0:T(8,128)(2,1)S(1)}, u32[]{:S(2)}, u32[]{:S(2)}) async-start(bf16[8,656,128]{2,1,0:T(8,128)(2,1)} %deal.2), calls=%async_computation | async-start | bytes 2686976 | tf_op jit(solution)/shard_map/all_to_all | solution.py:302
  7.9 32.3 %collective-permute-start = (bf16[256,1280]{1,0:T(8,128)(2,1)S(1)}, bf16[256,1280]{1,0:T(8,128)(2,1)S(1)}, u32[]{:S(2)}, u32[]{:S(2)}) collective-permute-start(bf16[256,1280]{1,0:T(8,128)(2,1)S(1)} %copy-done.4), channel_id=1, source_target_pairs={{0,8},{1,9},{2,10},{3,11},{4,12},{5,13},{6,14},{7,15},{8,0},{9,1},... | collective-permute-start | bytes 1966088 | tf_op jit(solution)/shard_map/ppermute | solution.py:309
  10.5 29.7 %collective-permute-start.1 = (s32[3,256]{1,0:T(4,128)S(1)}, s32[3,256]{1,0:T(4,128)S(1)}, u32[]{:S(2)}, u32[]{:S(2)}) collective-permute-start(s32[3,256]{1,0:T(4,128)S(1)} %pad_add_fusion), channel_id=1, source_target_pairs={{0,8},{1,9},{2,10},{3,11},{4,12},{5,13},{6,14},{7,15},{8,0},{9,1},... | collective-permute-start | bytes 9224 | tf_op jit(solution)/shard_map/ppermute | solution.py:309
  11.8 38.5 %collective-permute-start.3 = (bf16[32,1280]{1,0:T(8,128)(2,1)S(1)}, bf16[32,1280]{1,0:T(8,128)(2,1)S(1)}, u32[]{:S(2)}, u32[]{:S(2)}) collective-permute-start(bf16[32,1280]{1,0:T(8,128)(2,1)S(1)} %get-tuple-element.16), channel_id=1, source_target_pairs={{1,0},{2,1},{3,2},{4,3},{5,4},{6,5},{7,6},{8,7},{9,8},{10,9},{11,1... | collective-permute-start | bytes 245768 | tf_op jit(solution)/shard_map/ppermute | solution.py:21
  13.7 36.6 %collective-permute-start.2 = (bf16[32,1280]{1,0:T(8,128)(2,1)S(1)}, bf16[32,1280]{1,0:T(8,128)(2,1)S(1)}, u32[]{:S(2)}, u32[]{:S(2)}) collective-permute-start(bf16[32,1280]{1,0:T(8,128)(2,1)S(1)} %get-tuple-element.17), channel_id=1, source_target_pairs={{0,1},{1,2},{2,3},{3,4},{4,5},{5,6},{6,7},{7,8},{8,9},{9,10},{10,1... | collective-permute-start | bytes 245768 | tf_op jit(solution)/shard_map/ppermute | solution.py:20
  16.8 32.2 %copy-start.7 = (s32[2048]{0:T(1024)}, s32[2048]{0:T(1024)S(1)}, u32[]{:S(2)}) copy-start(s32[2048]{0:T(1024)S(1)} %dynamic_slice.9) | copy-start | bytes 24580
  40.2 0.8 copy-start.5
  40.2 3.7 %copy-start = (bf16[8,656,128]{2,1,0:T(8,128)(2,1)}, bf16[8,656,128]{2,1,0:T(8,128)(2,1)S(1)}, u32[]{:S(2)}) copy-start(bf16[8,656,128]{2,1,0:T(8,128)(2,1)S(1)} %all-to-all-done.q_ref.near_ref) | copy-start | bytes 4030468
  43.9 20.4 %all-to-all-start.1 = ((bf16[8,656,128]{2,1,0:T(8,128)(2,1)}), bf16[8,656,128]{2,1,0:T(8,128)(2,1)S(1)}, u32[]{:S(2)}, u32[]{:S(2)}) async-start(bf16[8,656,128]{2,1,0:T(8,128)(2,1)} %deal.3), calls=%async_computation.1 | async-start | bytes 2686976 | tf_op jit(solution)/shard_map/all_to_all | solution.py:302
  50.3 0.6 copy-start.12
  50.3 0.7 copy-start.13
  59.3 5.9 %copy-start.8 = (s32[2048]{0:T(1024)S(1)}, s32[2048]{0:T(1024)}, u32[]{:S(2)}) copy-start(s32[2048]{0:T(1024)} %copy-done.7) | copy-start | bytes 24580
  64.2 2.3 %copy-start.2 = (bf16[8,656,128]{2,1,0:T(8,128)(2,1)}, bf16[8,656,128]{2,1,0:T(8,128)(2,1)S(1)}, u32[]{:S(2)}) copy-start(bf16[8,656,128]{2,1,0:T(8,128)(2,1)S(1)} %all-to-all-done.1.far_ref.q_ref) | copy-start | bytes 4030468
  74.9 9.6 %copy-start.3 = (bf16[8,656,128]{2,1,0:T(8,128)(2,1)S(1)}, bf16[8,656,128]{2,1,0:T(8,128)(2,1)}, u32[]{:S(2)}) copy-start(bf16[8,656,128]{2,1,0:T(8,128)(2,1)} %copy-done.2) | copy-start | bytes 4030468
  77.6 6.8 %copy-start.1 = (bf16[8,656,128]{2,1,0:T(8,128)(2,1)S(1)}, bf16[8,656,128]{2,1,0:T(8,128)(2,1)}, u32[]{:S(2)}) copy-start(bf16[8,656,128]{2,1,0:T(8,128)(2,1)} %copy-done) | copy-start | bytes 4030468
  77.6 37.3 %all-to-all-start.2 = ((bf16[16,32,1280]{2,1,0:T(8,128)(2,1)}), bf16[16,32,1280]{2,1,0:T(8,128)(2,1)}, u32[]{:S(2)}, u32[]{:S(2)}) async-start(bf16[16,32,1280]{2,1,0:T(8,128)(2,1)} %bitcast.45), calls=%async_computation.2 | async-start | bytes 2621440 | tf_op jit(solution)/shard_map/all_to_all | solution.py:212

commit v12 on v10

--- a/solution.py
+++ b/solution.py
@@ -73,31 +73,26 @@
 
 
 def merge_kernel(low_ref, near_ref, far_ref, o_ref):
-    cap, feature = far_ref.shape[1:]
+    cap, feature = o_ref.shape[1:]
     size = cap * feature // LANES
     s, half = pl.program_id(0), pl.num_programs(0) // 2
     is_near = (s < half) == (low_ref[0] == 1)
 
-    @pl.when(is_near)
-    def _():
+    def take(ref):
         for t, r, c in tiles(cap, feature):
-            o_ref[0, r : r + TILE, c : c + LANES] = near_ref[0, size + t : size + t + TILE]
-
-    @pl.when(jnp.logical_not(is_near))
-    def _():
-        o_ref[...] = far_ref[...]
-
-
-def merge(near, far, low):
-    half, cap, feature = far.shape
+            o_ref[0, r : r + TILE, c : c + LANES] = ref[0, size + t : size + t + TILE]
+
+    pl.when(is_near)(lambda: take(near_ref))
+    pl.when(jnp.logical_not(is_near))(lambda: take(far_ref))
+
+
+def merge(near, far, low, cap, feature):
+    half = near.shape[0]
+    spec = pl.BlockSpec((1, *near.shape[1:]), lambda i: (i % half, 0, 0))
     return pl.pallas_call(
         merge_kernel,
         grid=(2 * half,),
-        in_specs=[
-            SMEM,
-            pl.BlockSpec((1, *near.shape[1:]), lambda i: (i % half, 0, 0)),
-            pl.BlockSpec((1, cap, feature), lambda i: (i % half, 0, 0)),
-        ],
+        in_specs=[SMEM, spec, spec],
         out_specs=pl.BlockSpec((1, cap, feature), lambda i: (i, 0, 0)),
         out_shape=jax.ShapeDtypeStruct((2 * half, cap, feature), far.dtype),
         compiler_params=pltpu.CompilerParams(vmem_limit_bytes=8 * 1024 * 1024),
@@ -295,20 +290,21 @@
         codes = jnp.stack([owner, shard, anchor])
         mirrored, codes_mirror = lax.ppermute(images, "docs", across), lax.ppermute(codes, "docs", across)
         near = exchange_half(deal(images, owner, shard, anchor, first, members, cap, 2))
+        far = deal(mirrored, *codes_mirror, first, members, cap, 2)
+        near, far = lax.optimization_barrier((near, far))
         docs, goes, comes = slots_of(*told_by(near))
         aligned = attend(near, cap, docs, known)
         sent = one_hot_dot(puts(goes), aligned)
-        sent, mirrored, codes_mirror = lax.optimization_barrier((sent, mirrored, codes_mirror))
-
-        far = exchange_half(deal(mirrored, *codes_mirror, first, members, cap, 1))
-        far_images = exchange_half(by_shard(mirrored, codes_mirror[0], codes_mirror[1], first, half))
+
+        far = exchange_half(far)
+        sent, far = lax.optimization_barrier((sent, far))
         docs, goes, comes_far = slots_of(*told_by(far))
         aligned = attend(far, cap, docs, known)
         sent += jnp.dot(puts(goes).astype(jnp.bfloat16), aligned, preferred_element_type=jnp.float32)
-        sent, far_images = lax.optimization_barrier((sent.astype(jnp.bfloat16), far_images))
+        sent = sent.astype(jnp.bfloat16)
         low = first == 0
         comes = jnp.where(low, jnp.concatenate([comes, comes_far]), jnp.concatenate([comes_far, comes]))
-        loaded_images = merge(near, far_images, low).reshape(members * cap, feature)
+        loaded_images = merge(near, far, low, cap, feature).reshape(members * cap, feature)
     else:
         packed = (owner * members + shard) * own + anchor
         every, queries = every_device(packed, exchange(by_shard(images, owner, owner, 0, members)))

time: 123 us -> 116 us (0.943)
  starting transfers between devices: 29.5 us -> 22.4 us
  matrix products: 5.72 us -> 3.45 us
  waiting for transfers between devices: 52.8 us -> 54.3 us
  local copies, waits for them, and re-layouts: 7.22 us -> 8.56 us
  Pallas kernels: 22.5 us -> 23.8 us
    ppermute x1, waiting for transfers between devices: 0.01 us -> 23.9 us  [shards(): lax.ppermute(codes, 'docs', across)]
    all_to_all x3 -> x2, waiting for transfers between devices: 27.8 us -> 5.38 us  [exchange_half(): lax.all_to_all(x, 'docs', split_axis=0, concat_axis=0, tiled=True, axis_i...]
    all_to_all x3 -> x2, starting transfers between devices: 15 us -> 8.4 us  [exchange_half(): lax.all_to_all(x, 'docs', split_axis=0, concat_axis=0, tiled=True, axis_i...]
    dot_general x2 -> x1, matrix products: 3.84 us -> 1.57 us  [one_hot_dot(): jnp.dot(table.astype(jnp.bfloat16), rows, preferred_element_type=jnp.floa...]
  transfers between devices with their start and end apart: 8 -> 7, of which waited for: 3 -> 3; matrix products, arithmetic and copies ran while one was open for 8% -> 4% of each run, Pallas kernels for 13% -> 11%
where the time goes in v12:
time: 116 us; the launch traced here: 115 us
  waiting for transfers between devices  54.3 us (47%)
  Pallas kernels  23.8 us (21%)
  starting transfers between devices  22.4 us (19%)
  local copies, waits for them, and re-layouts  8.56 us (7%)
  matrix products  3.45 us (3%)
  other arithmetic  1.92 us (2%)
    all_to_all x1, waiting for transfers between devices, exchange(): return lax.all_to_all(x, 'docs', split_axis=0, concat_axis=0, tiled=True)  25 us
    ppermute x1, waiting for transfers between devices, shards(): lax.ppermute(codes, 'docs', across)  23.9 us
    pallas_call x2, Pallas kernels, attend(): pl.pallas_call(functools.partial(attend_kernel, feature ** (-0.5)), grid=...  10.2 us
    all_to_all x2, starting transfers between devices, exchange_half(): lax.all_to_all(x, 'docs', split_axis=0, concat_axis=0, tiled=True, axis_i...  8.4 us
    all_to_all x1, starting transfers between devices, exchange(): return lax.all_to_all(x, 'docs', split_axis=0, concat_axis=0, tiled=True)  6.67 us
    unnamed x20, local copies, waits for them, and re-layouts  5.83 us
    pallas_call x2, Pallas kernels, deal(): pl.pallas_call(functools.partial(deal_kernel, cap, members), in_specs=[SM...  5.8 us
    all_to_all x2, waiting for transfers between devices, exchange_half(): lax.all_to_all(x, 'docs', split_axis=0, concat_axis=0, tiled=True, axis_i...  5.38 us
  transfers between devices with their start and end apart: 7, of which 3 were waited for; matrix products, arithmetic and copies ran while one was open for 4% of the time, Pallas kernels for 11%

profile of v12, /device:TPU:14, one launch (start us, length us, event | category | flops | bytes accessed | tf_op | source)
XLA Modules:
  0.0 115.3 jit_solution(218534379736937755)
XLA Ops:
  0.7 2.9 %deal.2 = bf16[8,656,128]{2,1,0:T(8,128)(2,1)} custom-call(s32[1]{0:T(128)} %bitcast.1.base_ref, s32[2,128]{1,0:T(2,128)} %bitcast.52, s32[2,128]{1,0:T(2,128)} %bitcast.54, s32[2,128]{1,0:T(2,128)} %bitcast.56, bf16[256,1280]{1,0:T(8,128)(2,1)} %rows_ref.1), custom_call_target="tpu_custom_call" | custom-call | flops 335544320 | bytes 1966080 | tf_op jit(solution)/shard_map/deal/pallas_call | solution.py:62
  3.6 4.2 %all-to-all-start = ((bf16[8,656,128]{2,1,0:T(8,128)(2,1)}), bf16[8,656,128]{2,1,0:T(8,128)(2,1)S(1)}, u32[]{:S(2)}, u32[]{:S(2)}) async-start(bf16[8,656,128]{2,1,0:T(8,128)(2,1)} %deal.2), calls=%async_computation | async-start | bytes 2686976 | tf_op jit(solution)/shard_map/all_to_all | solution.py:284
  7.8 2.6 %collective-permute-start.1 = (bf16[256,1280]{1,0:T(8,128)(2,1)S(1)}, bf16[256,1280]{1,0:T(8,128)(2,1)S(1)}, u32[]{:S(2)}, u32[]{:S(2)}) collective-permute-start(bf16[256,1280]{1,0:T(8,128)(2,1)S(1)} %copy-done.3), channel_id=1, source_target_pairs={{0,8},{1,9},{2,10},{3,11},{4,12},{5,13},{6,14},{7,15},{8,0},{9,1},... | collective-permute-start | bytes 1966088 | tf_op jit(solution)/shard_map/ppermute | solution.py:291
  10.8 0.9 fusion.19
  11.8 1.9 %collective-permute-start.3 = (bf16[32,1280]{1,0:T(8,128)(2,1)S(1)}, bf16[32,1280]{1,0:T(8,128)(2,1)S(1)}, u32[]{:S(2)}, u32[]{:S(2)}) collective-permute-start(bf16[32,1280]{1,0:T(8,128)(2,1)S(1)} %get-tuple-element.14), channel_id=1, source_target_pairs={{1,0},{2,1},{3,2},{4,3},{5,4},{6,5},{7,6},{8,7},{9,8},{10,9},{11,1... | collective-permute-start | bytes 245768 | tf_op jit(solution)/shard_map/ppermute | solution.py:21
  13.7 2.4 %collective-permute-start.2 = (bf16[32,1280]{1,0:T(8,128)(2,1)S(1)}, bf16[32,1280]{1,0:T(8,128)(2,1)S(1)}, u32[]{:S(2)}, u32[]{:S(2)}) collective-permute-start(bf16[32,1280]{1,0:T(8,128)(2,1)S(1)} %get-tuple-element.15), channel_id=1, source_target_pairs={{0,1},{1,2},{2,3},{3,4},{4,5},{5,6},{6,7},{7,8},{8,9},{9,10},{10,1... | collective-permute-start | bytes 245768 | tf_op jit(solution)/shard_map/ppermute | solution.py:20
  16.2 23.9 %collective-permute-done = s32[3,256]{1,0:T(4,128)S(1)} collective-permute-done((s32[3,256]{1,0:T(4,128)S(1)}, s32[3,256]{1,0:T(4,128)S(1)}, u32[]{:S(2)}, u32[]{:S(2)}) %collective-permute-start) | collective-permute-done | bytes 3104 | tf_op jit(solution)/shard_map/ppermute | solution.py:291
  40.2 0.6 fusion.21
  40.8 0.8 copy-done.4
  41.6 2.9 %deal.3 = bf16[8,656,128]{2,1,0:T(8,128)(2,1)} custom-call(s32[1]{0:T(128)} %bitcast.1.base_ref, s32[2,128]{1,0:T(2,128)} %bitcast.60, s32[2,128]{1,0:T(2,128)} %bitcast.59, s32[2,128]{1,0:T(2,128)} %bitcast.58, bf16[256,1280]{1,0:T(8,128)(2,1)} %copy-done.4), custom_call_target="tpu_custom_call" | custom-call | flops 335544320 | bytes 1966080 | tf_op jit(solution)/shard_map/deal/pallas_call | solution.py:62
  44.5 4.2 %all-to-all-start.1 = ((bf16[8,656,128]{2,1,0:T(8,128)(2,1)}), bf16[8,656,128]{2,1,0:T(8,128)(2,1)S(1)}, u32[]{:S(2)}, u32[]{:S(2)}) async-start(bf16[8,656,128]{2,1,0:T(8,128)(2,1)} %deal.3), calls=%async_computation.1 | async-start | bytes 2686976 | tf_op jit(solution)/shard_map/all_to_all | solution.py:284
  49.7 0.4 select_reduce_fusion.1
  50.3 2.5 %copy-done = bf16[2048,1280]{1,0:T(8,128)(2,1)S(1)} copy-done((bf16[2048,1280]{1,0:T(8,128)(2,1)S(1)}, bf16[2048,1280]{1,0:T(8,128)(2,1)}, u32[]{:S(2)}) %copy-start) | copy-done | bytes 5242904
  52.8 5.1 %attend.2 = bf16[256,1280]{1,0:T(8,128)(2,1)S(1)} custom-call(bf16[8,656,128]{2,1,0:T(8,128)(2,1)S(1)} %all-to-all-done.q_ref.near_ref, s32[256,1]{1,0:T(8,128)S(1)} %copy.29.doc_ref, bf16[2048,1280]{1,0:T(8,128)(2,1)S(1)} %copy-done, bf16[32,1280]{1,0:T(8,128)(2,1)S(1)} %collective-permute-done.2.before_ref, ...), custom_call_target="tpu_custom_call" | custom-call | flops 2684354560 | bytes 6553600 | tf_op jit(solution)/shard_map/attend/pallas_call | solution.py:137
  57.9 1.6 %convolution_convert_fusion = bf16[512,1280]{1,0:T(8,128)(2,1)} fusion(bf16[256,1280]{1,0:T(8,128)(2,1)S(1)} %attend.2, s32[256]{0:T(256)S(1)} %fusion.16, pred[256]{0:T(512)(128)(4,1)S(1)} %ge.23), kind=kOutput, calls=%fused_computation.2 | convolution fusion | flops 336461824 | bytes 1967360 | tf_op jit(solution)/shard_map/dot_general | solution.py:232
  59.4 5.4 %all-to-all-done.1.far_ref.q_ref = bf16[8,656,128]{2,1,0:T(8,128)(2,1)S(1)} async-done(((bf16[8,656,128]{2,1,0:T(8,128)(2,1)}), bf16[8,656,128]{2,1,0:T(8,128)(2,1)S(1)}, u32[]{:S(2)}, u32[]{:S(2)}) %all-to-all-start.1) | async-done | bytes 1343520 | tf_op jit(solution)/shard_map/all_to_all | solution.py:284
  65.8 0.4 select_reduce_fusion
  66.4 2.5 %copy-done.1 = bf16[2048,1280]{1,0:T(8,128)(2,1)S(1)} copy-done((bf16[2048,1280]{1,0:T(8,128)(2,1)S(1)}, bf16[2048,1280]{1,0:T(8,128)(2,1)}, u32[]{:S(2)}) %copy-start.1) | copy-done | bytes 5242904
  68.9 5.1 %attend.3 = bf16[256,1280]{1,0:T(8,128)(2,1)S(1)} custom-call(bf16[8,656,128]{2,1,0:T(8,128)(2,1)S(1)} %all-to-all-done.1.far_ref.q_ref, s32[256,1]{1,0:T(8,128)S(1)} %copy.35.doc_ref, bf16[2048,1280]{1,0:T(8,128)(2,1)S(1)} %copy-done.1, bf16[32,1280]{1,0:T(8,128)(2,1)S(1)} %collective-permute-done.2.before_ref, ...), custom_call_target="tpu_custom_call" | custom-call | flops 2684354560 | bytes 6553600 | tf_op jit(solution)/shard_map/attend/pallas_call | solution.py:137
  74.0 1.6 %fusion = bf16[512,1280]{1,0:T(8,128)(2,1)} fusion(bf16[256,1280]{1,0:T(8,128)(2,1)S(1)} %attend.3, bf16[512,1280]{1,0:T(8,128)(2,1)S(1)} %copy-done.2, s32[256]{0:T(256)S(1)} %fusion.15, pred[256]{0:T(512)(128)(4,1)S(1)} %ge.25), kind=kOutput, calls=%fused_computation.1 | convolution fusion | flops 337772544 | bytes 3278080 | tf_op jit(solution)/shard_map/dot_general | solution.py:303
  75.6 6.7 %all-to-all-start.2 = ((bf16[16,32,1280]{2,1,0:T(8,128)(2,1)}), bf16[16,32,1280]{2,1,0:T(8,128)(2,1)}, u32[]{:S(2)}, u32[]{:S(2)}) async-start(bf16[16,32,1280]{2,1,0:T(8,128)(2,1)} %bitcast.47), calls=%async_computation.2 | async-start | bytes 2621440 | tf_op jit(solution)/shard_map/all_to_all | solution.py:194
  82.3 5.3 %merge.1 = bf16[16,32,1280]{2,1,0:T(8,128)(2,1)} custom-call(s32[1]{0:T(128)} %bitcast.low_ref, bf16[8,656,128]{2,1,0:T(8,128)(2,1)S(1)} %all-to-all-done.q_ref.near_ref, bf16[8,656,128]{2,1,0:T(8,128)(2,1)S(1)} %all-to-all-done.1.far_ref.q_ref), custom_call_target="tpu_custom_call" | custom-call | bytes 2621440 | tf_op jit(solution)/shard_map/merge/pallas_call | solution.py:92
  87.8 25.0 %all-to-all-done.2.x_ref = bf16[16,32,1280]{2,1,0:T(8,128)(2,1)} async-done(((bf16[16,32,1280]{2,1,0:T(8,128)(2,1)}), bf16[16,32,1280]{2,1,0:T(8,128)(2,1)}, u32[]{:S(2)}, u32[]{:S(2)}) %all-to-all-start.2) | async-done | bytes 1310752 | tf_op jit(solution)/shard_map/all_to_all | solution.py:194
  112.8 2.5 %place.1 = bf16[16,32,1280]{2,1,0:T(8,128)(2,1)} custom-call(s32[16]{0:T(128)S(1)} %broadcast_select_fusion.comes_ref, bf16[16,32,1280]{2,1,0:T(8,128)(2,1)} %all-to-all-done.2.x_ref), custom_call_target="tpu_custom_call" | custom-call | bytes 2621440 | tf_op jit(solution)/shard_map/place/pallas_call | solution.py:219
  (61 shorter events, 3.0 us)
Async XLA Ops:
  0.6 7.2 %copy-start.3 = (bf16[256,1280]{1,0:T(8,128)(2,1)S(1)}, bf16[256,1280]{1,0:T(8,128)(2,1)}, u32[]{:S(2)}) copy-start(bf16[256,1280]{1,0:T(8,128)(2,1)} %rows_ref.1) | copy-start | bytes 1966084
  0.7 9.8 %copy-start.6 = (s32[256,1]{0,1:T(1,128)S(1)}, s32[256,1]{0,1:T(1,128)}, u32[]{:S(2)}) copy-start(s32[256,1]{0,1:T(1,128)} %param.9) | copy-start | bytes 3076
  0.7 9.8 %copy-start.7 = (s32[256,1]{0,1:T(1,128)S(1)}, s32[256,1]{0,1:T(1,128)}, u32[]{:S(2)}) copy-start(s32[256,1]{0,1:T(1,128)} %param.11) | copy-start | bytes 3076
  0.7 9.8 %copy-start.8 = (s32[256]{0:T(256)S(1)}, s32[256]{0:T(256)}, u32[]{:S(2)}) copy-start(s32[256]{0:T(256)} %param.10) | copy-start | bytes 3076
  0.7 15.4 %copy-start.5 = (s32[32768]{0:T(1024)S(1)}, s32[32768]{0:T(1024)}, u32[]{:S(2)}) copy-start(s32[32768]{0:T(1024)} %param.7) | copy-start | bytes 393220
  3.6 40.8 %all-to-all-start = ((bf16[8,656,128]{2,1,0:T(8,128)(2,1)}), bf16[8,656,128]{2,1,0:T(8,128)(2,1)S(1)}, u32[]{:S(2)}, u32[]{:S(2)}) async-start(bf16[8,656,128]{2,1,0:T(8,128)(2,1)} %deal.2), calls=%async_computation | async-start | bytes 2686976 | tf_op jit(solution)/shard_map/all_to_all | solution.py:284
  7.8 32.9 %collective-permute-start.1 = (bf16[256,1280]{1,0:T(8,128)(2,1)S(1)}, bf16[256,1280]{1,0:T(8,128)(2,1)S(1)}, u32[]{:S(2)}, u32[]{:S(2)}) collective-permute-start(bf16[256,1280]{1,0:T(8,128)(2,1)S(1)} %copy-done.3), channel_id=1, source_target_pairs={{0,8},{1,9},{2,10},{3,11},{4,12},{5,13},{6,14},{7,15},{8,0},{9,1},... | collective-permute-start | bytes 1966088 | tf_op jit(solution)/shard_map/ppermute | solution.py:291
  10.4 29.7 %collective-permute-start = (s32[3,256]{1,0:T(4,128)S(1)}, s32[3,256]{1,0:T(4,128)S(1)}, u32[]{:S(2)}, u32[]{:S(2)}) collective-permute-start(s32[3,256]{1,0:T(4,128)S(1)} %pad_add_fusion), channel_id=1, source_target_pairs={{0,8},{1,9},{2,10},{3,11},{4,12},{5,13},{6,14},{7,15},{8,0},{9,1},... | collective-permute-start | bytes 9224 | tf_op jit(solution)/shard_map/ppermute | solution.py:291
  11.8 38.5 %collective-permute-start.3 = (bf16[32,1280]{1,0:T(8,128)(2,1)S(1)}, bf16[32,1280]{1,0:T(8,128)(2,1)S(1)}, u32[]{:S(2)}, u32[]{:S(2)}) collective-permute-start(bf16[32,1280]{1,0:T(8,128)(2,1)S(1)} %get-tuple-element.14), channel_id=1, source_target_pairs={{1,0},{2,1},{3,2},{4,3},{5,4},{6,5},{7,6},{8,7},{9,8},{10,9},{11,1... | collective-permute-start | bytes 245768 | tf_op jit(solution)/shard_map/ppermute | solution.py:21
  13.7 36.5 %collective-permute-start.2 = (bf16[32,1280]{1,0:T(8,128)(2,1)S(1)}, bf16[32,1280]{1,0:T(8,128)(2,1)S(1)}, u32[]{:S(2)}, u32[]{:S(2)}) collective-permute-start(bf16[32,1280]{1,0:T(8,128)(2,1)S(1)} %get-tuple-element.15), channel_id=1, source_target_pairs={{0,1},{1,2},{2,3},{3,4},{4,5},{5,6},{6,7},{7,8},{8,9},{9,10},{10,1... | collective-permute-start | bytes 245768 | tf_op jit(solution)/shard_map/ppermute | solution.py:20
  40.8 0.8 copy-start.4
  44.5 20.4 %all-to-all-start.1 = ((bf16[8,656,128]{2,1,0:T(8,128)(2,1)}), bf16[8,656,128]{2,1,0:T(8,128)(2,1)S(1)}, u32[]{:S(2)}, u32[]{:S(2)}) async-start(bf16[8,656,128]{2,1,0:T(8,128)(2,1)} %deal.3), calls=%async_computation.1 | async-start | bytes 2686976 | tf_op jit(solution)/shard_map/all_to_all | solution.py:284
  50.3 2.5 %copy-start = (bf16[2048,1280]{1,0:T(8,128)(2,1)S(1)}, bf16[2048,1280]{1,0:T(8,128)(2,1)}, u32[]{:S(2)}) copy-start(bf16[2048,1280]{1,0:T(8,128)(2,1)} %k_ref.3) | copy-start | bytes 15728644
  66.4 2.5 %copy-start.1 = (bf16[2048,1280]{1,0:T(8,128)(2,1)S(1)}, bf16[2048,1280]{1,0:T(8,128)(2,1)}, u32[]{:S(2)}) copy-start(bf16[2048,1280]{1,0:T(8,128)(2,1)} %k_ref.3) | copy-start | bytes 15728644
  68.9 5.1 %copy-start.2 = (bf16[512,1280]{1,0:T(8,128)(2,1)S(1)}, bf16[512,1280]{1,0:T(8,128)(2,1)}, u32[]{:S(2)}) copy-start(bf16[512,1280]{1,0:T(8,128)(2,1)} %convolution_convert_fusion) | copy-start | bytes 3932164
  75.6 37.2 %all-to-all-start.2 = ((bf16[16,32,1280]{2,1,0:T(8,128)(2,1)}), bf16[16,32,1280]{2,1,0:T(8,128)(2,1)}, u32[]{:S(2)}, u32[]{:S(2)}) async-start(bf16[16,32,1280]{2,1,0:T(8,128)(2,1)} %bitcast.47), calls=%async_computation.2 | async-start | bytes 2621440 | tf_op jit(solution)/shard_map/all_to_all | solution.py:194

commit v13 on v8

--- a/solution.py
+++ b/solution.py
@@ -22,9 +22,11 @@
     return before, after
 
 
-def deal_kernel(cap, owner_ref, shard_ref, anchor_ref, rows_ref, o_ref):
-    members = o_ref.shape[0]
-    lines, n = owner_ref.shape[0], rows_ref.shape[0]
+def deal_kernel(cap, owner_ref, shard_ref, anchor_ref, rows_ref, o_ref, rows, made, rows_sem, made_sem):
+    members, parts = o_ref.shape[0], made_sem.shape[0]
+    lines, (n, feature) = owner_ref.shape[0], rows_ref.shape
+    coming = pltpu.make_async_copy(rows_ref, rows, rows_sem)
+    coming.start()
     owner, shard, anchor = owner_ref[...], shard_ref[...], anchor_ref[...]
     told = jnp.concatenate([owner, shard, anchor // LANES, anchor % LANES], axis=0)
     told = jnp.concatenate([told, jnp.zeros((TILE - 4 * lines, LANES), jnp.int32)], axis=0)
@@ -37,13 +39,23 @@
         theirs.astype(jnp.bfloat16), jnp.where(sooner, 1.0, 0.0).astype(jnp.bfloat16), preferred_element_type=jnp.float32
     )
     rank = jnp.sum(theirs * before, axis=0, keepdims=True).astype(jnp.int32)
-    slot = lax.broadcasted_iota(jnp.int32, (members * cap, n), 0)
-    table = jnp.where(slot == owner * cap + rank, 1.0, 0.0).astype(jnp.bfloat16)
-    out = jnp.dot(table, rows_ref[...], preferred_element_type=jnp.float32).astype(jnp.bfloat16)
-    for d in range(members):
-        for t, r, c in tiles(cap, out.shape[1]):
-            o_ref[d, t : t + TILE] = out[d * cap + r : d * cap + r + TILE, c : c + LANES]
-        o_ref[d, cap * out.shape[1] // LANES :] = told
+    place = owner * cap + rank
+    each = members // parts
+    slot = lax.broadcasted_iota(jnp.int32, (each * cap, n), 0)
+    coming.wait()
+    leaving = []
+    for p in range(parts):
+        table = jnp.where(slot + p * each * cap == place, 1.0, 0.0).astype(jnp.bfloat16)
+        out = jnp.dot(table, rows[...], preferred_element_type=jnp.float32).astype(jnp.bfloat16)
+        for d in range(each):
+            for t, r, c in tiles(cap, feature):
+                made[p * each + d, t : t + TILE] = out[d * cap + r : d * cap + r + TILE, c : c + LANES]
+            made[p * each + d, cap * feature // LANES :] = told
+        part = pl.ds(p * each, each)
+        leaving.append(pltpu.make_async_copy(made.at[part], o_ref.at[part], made_sem.at[p]))
+        leaving[p].start()
+    for copy in leaving:
+        copy.wait()
 
 
 def tiles(rows, columns):
@@ -57,9 +69,15 @@
     shape = (members, cap * feature // LANES + TILE, LANES)
     return pl.pallas_call(
         functools.partial(deal_kernel, cap),
-        in_specs=[pl.BlockSpec()] * 4,
-        out_specs=pl.BlockSpec(),
+        in_specs=[VMEM] * 3 + [HBM],
+        out_specs=HBM,
         out_shape=jax.ShapeDtypeStruct(shape, jnp.bfloat16),
+        scratch_shapes=[
+            pltpu.VMEM((n, feature), jnp.bfloat16),
+            pltpu.VMEM(shape, jnp.bfloat16),
+            pltpu.SemaphoreType.DMA,
+            pltpu.SemaphoreType.DMA((4 if members % 4 == 0 else 1,)),
+        ],
         compiler_params=pltpu.CompilerParams(vmem_limit_bytes=60 * 1024 * 1024),
         cost_estimate=pl.CostEstimate(
             flops=2 * members * cap * n * feature, bytes_accessed=2 * (n + members * cap) * feature, transcendentals=0

time: 115 us -> 116 us (level)
  no operation moved by 1% of the time
where the time goes in v13:
time: 116 us; the launch traced here: 115 us
  waiting for transfers between devices  65.8 us (57%)
  starting transfers between devices  22 us (19%)
  Pallas kernels  16.7 us (14%)
  local copies, waits for them, and re-layouts  4.13 us (4%)
  matrix products  3.68 us (3%)
  other arithmetic  1.67 us (1%)
    all_to_all x3, waiting for transfers between devices, exchange(): return lax.all_to_all(x, 'docs', split_axis=0, concat_axis=0, tiled=True)  65.8 us
    all_to_all x3, starting transfers between devices, exchange(): return lax.all_to_all(x, 'docs', split_axis=0, concat_axis=0, tiled=True)  16.4 us
    pallas_call x1, Pallas kernels, attend(): pl.pallas_call(functools.partial(attend_kernel, feature ** (-0.5)), grid=...  10.1 us
    ppermute x1, starting transfers between devices, halo_of(): after = lax.ppermute(sentences[:MOST_SENT], 'docs', down)  3.51 us
    pallas_call x1, Pallas kernels, deal(): pl.pallas_call(functools.partial(deal_kernel, cap), in_specs=[VMEM] * 3 +...  3.22 us
    unnamed x11, local copies, waits for them, and re-layouts  2.51 us
  transfers between devices with their start and end apart: 5, of which 3 were waited for; matrix products, arithmetic and copies ran while one was open for 6% of the time, Pallas kernels for 10%

profile of v13, /device:TPU:14, one launch (start us, length us, event | category | flops | bytes accessed | tf_op | source)
XLA Modules:
  0.0 114.7 jit_solution(5945067881511837592)
XLA Ops:
  0.6 3.2 %deal.1 = bf16[16,336,128]{2,1,0:T(8,128)(2,1)} custom-call(s32[2,128]{1,0:T(2,128)} %bitcast.34, s32[2,128]{1,0:T(2,128)} %bitcast.37, s32[2,128]{1,0:T(2,128)} %bitcast.39, bf16[256,1280]{1,0:T(8,128)(2,1)} %rows_ref.1), custom_call_target="tpu_custom_call" | custom-call | flops 335544320 | bytes 1966080 | tf_op jit(solution)/shard_map/deal/pallas_call | solution.py:70
  3.9 6.4 %all-to-all-start.1 = ((bf16[16,336,128]{2,1,0:T(8,128)(2,1)}), bf16[16,336,128]{2,1,0:T(8,128)(2,1)S(1)}, u32[]{:S(2)}, u32[]{:S(2)}) async-start(bf16[16,336,128]{2,1,0:T(8,128)(2,1)} %deal.1), calls=%async_computation.1 | async-start | bytes 2752512 | tf_op jit(solution)/shard_map/all_to_all | solution.py:180
  10.3 0.9 fusion.15
  11.2 2.1 %collective-permute-start = (bf16[32,1280]{1,0:T(8,128)(2,1)S(1)}, bf16[32,1280]{1,0:T(8,128)(2,1)S(1)}, u32[]{:S(2)}, u32[]{:S(2)}) collective-permute-start(bf16[32,1280]{1,0:T(8,128)(2,1)S(1)} %get-tuple-element.5), channel_id=1, source_target_pairs={{0,1},{1,2},{2,3},{3,4},{4,5},{5,6},{6,7},{7,8},{8,9},{9,10},{10,1... | collective-permute-start | bytes 245768 | tf_op jit(solution)/shard_map/ppermute | solution.py:20
  13.3 3.5 %collective-permute-start.1 = (bf16[32,1280]{1,0:T(8,128)(2,1)S(1)}, bf16[32,1280]{1,0:T(8,128)(2,1)S(1)}, u32[]{:S(2)}, u32[]{:S(2)}) collective-permute-start(bf16[32,1280]{1,0:T(8,128)(2,1)S(1)} %get-tuple-element.4), channel_id=1, source_target_pairs={{1,0},{2,1},{3,2},{4,3},{5,4},{6,5},{7,6},{8,7},{9,8},{10,9},{11,1... | collective-permute-start | bytes 245768 | tf_op jit(solution)/shard_map/ppermute | solution.py:21
  16.8 0.2 convert_reduce_fusion
  17.1 0.1 fusion.14
  17.1 1.6 %convolution_convert_fusion.1 = bf16[512,1280]{1,0:T(8,128)(2,1)} fusion(bf16[256,1280]{1,0:T(8,128)(2,1)S(1)} %copy-done.1, s32[256]{0:T(256)S(1)} %add.71), kind=kOutput, calls=%fused_computation.3 | convolution fusion | flops 336330752 | bytes 1967104 | tf_op jit(solution)/shard_map/dot_general | solution.py:232
  18.7 23.4 %all-to-all-done.1.q_ref = bf16[16,336,128]{2,1,0:T(8,128)(2,1)S(1)} async-done(((bf16[16,336,128]{2,1,0:T(8,128)(2,1)}), bf16[16,336,128]{2,1,0:T(8,128)(2,1)S(1)}, u32[]{:S(2)}, u32[]{:S(2)}) %all-to-all-start.1) | async-done | bytes 1376288 | tf_op jit(solution)/shard_map/all_to_all | solution.py:180
  42.1 5.1 %all-to-all-start = ((bf16[16,32,1280]{2,1,0:T(8,128)(2,1)}), bf16[16,32,1280]{2,1,0:T(8,128)(2,1)S(1)}, u32[]{:S(2)}, u32[]{:S(2)}) async-start(bf16[16,32,1280]{2,1,0:T(8,128)(2,1)} %bitcast.30), calls=%async_computation | async-start | bytes 2621440 | tf_op jit(solution)/shard_map/all_to_all | solution.py:180
  47.3 0.1 fusion.8
  47.4 0.1 convolution_convert_fusion.2
  47.6 0.4 select_reduce_fusion.1
  48.2 0.8 select_reduce_fusion
  49.0 0.2 copy.21.doc_ref
  49.3 2.5 %copy-done = bf16[2048,1280]{1,0:T(8,128)(2,1)S(1)} copy-done((bf16[2048,1280]{1,0:T(8,128)(2,1)S(1)}, bf16[2048,1280]{1,0:T(8,128)(2,1)}, u32[]{:S(2)}) %copy-start) | copy-done | bytes 5242904
  51.8 10.1 %attend.1 = bf16[512,1280]{1,0:T(8,128)(2,1)S(1)} custom-call(bf16[16,336,128]{2,1,0:T(8,128)(2,1)S(1)} %all-to-all-done.1.q_ref, s32[512,1]{1,0:T(8,128)S(1)} %copy.21.doc_ref, bf16[2048,1280]{1,0:T(8,128)(2,1)S(1)} %copy-done, bf16[32,1280]{1,0:T(8,128)(2,1)S(1)} %collective-permute-done.before_ref, bf16[32,1280]{1,0:T(8,128)(2,1)S(1)} %collective-permute-done.1.after_ref, ...), custom_call_target="tpu_custom_call" | custom-call | flops 5368709120 | bytes 7864320 | tf_op jit(solution)/shard_map/attend/pallas_call | solution.py:123
  61.9 1.9 %convolution_convert_fusion = bf16[512,1280]{1,0:T(8,128)(2,1)} fusion(bf16[512,1280]{1,0:T(8,128)(2,1)S(1)} %attend.1, s32[512]{0:T(512)S(1)} %fusion.9, pred[512]{0:T(512)(128)(4,1)S(1)} %ge.13), kind=kOutput, calls=%fused_computation.2 | convolution fusion | flops 672268288 | bytes 2624000 | tf_op jit(solution)/shard_map/dot_general | solution.py:268
  63.9 13.7 %all-to-all-done = bf16[16,32,1280]{2,1,0:T(8,128)(2,1)S(1)} async-done(((bf16[16,32,1280]{2,1,0:T(8,128)(2,1)}), bf16[16,32,1280]{2,1,0:T(8,128)(2,1)S(1)}, u32[]{:S(2)}, u32[]{:S(2)}) %all-to-all-start) | async-done | bytes 1310752 | tf_op jit(solution)/shard_map/all_to_all | solution.py:180
  77.6 5.0 %all-to-all-start.2 = ((bf16[16,32,1280]{2,1,0:T(8,128)(2,1)}), bf16[16,32,1280]{2,1,0:T(8,128)(2,1)S(1)}, u32[]{:S(2)}, u32[]{:S(2)}) async-start(bf16[16,32,1280]{2,1,0:T(8,128)(2,1)} %bitcast.31), calls=%async_computation.2 | async-start | bytes 2621440 | tf_op jit(solution)/shard_map/all_to_all | solution.py:180
  82.6 1.6 %write_out.1 = bf16[512,1280]{1,0:T(8,128)(2,1)} custom-call(bf16[512,1280]{1,0:T(8,128)(2,1)S(1)} %bitcast.28), custom_call_target="tpu_custom_call" | custom-call | bytes 2621440 | tf_op jit(solution)/shard_map/write_out/pallas_call | solution.py:167
  84.2 0.1 select_reduce_fusion.2
  84.3 28.7 %all-to-all-done.2.x_ref = bf16[16,32,1280]{2,1,0:T(8,128)(2,1)S(1)} async-done(((bf16[16,32,1280]{2,1,0:T(8,128)(2,1)}), bf16[16,32,1280]{2,1,0:T(8,128)(2,1)S(1)}, u32[]{:S(2)}, u32[]{:S(2)}) %all-to-all-start.2) | async-done | bytes 1310752 | tf_op jit(solution)/shard_map/all_to_all | solution.py:180
  113.0 1.7 %place.1 = bf16[16,32,1280]{2,1,0:T(8,128)(2,1)} custom-call(s32[16]{0:T(128)S(1)} %broadcast_add_fusion.2.comes_ref, bf16[16,32,1280]{2,1,0:T(8,128)(2,1)S(1)} %all-to-all-done.2.x_ref), custom_call_target="tpu_custom_call" | custom-call | bytes 2621440 | tf_op jit(solution)/shard_map/place/pallas_call | solution.py:205
  (28 shorter events, 0.6 us)
Async XLA Ops:
  3.9 13.0 %copy-start.2 = (s32[32768]{0:T(1024)S(1)}, s32[32768]{0:T(1024)}, u32[]{:S(2)}) copy-start(s32[32768]{0:T(1024)} %param.7) | copy-start | bytes 393220
  3.9 13.0 %copy-start.3 = (s32[256,1]{0,1:T(1,128)S(1)}, s32[256,1]{0,1:T(1,128)}, u32[]{:S(2)}) copy-start(s32[256,1]{0,1:T(1,128)} %param.9) | copy-start | bytes 3076
  3.9 13.1 %copy-start.4 = (s32[256,1]{0,1:T(1,128)S(1)}, s32[256,1]{0,1:T(1,128)}, u32[]{:S(2)}) copy-start(s32[256,1]{0,1:T(1,128)} %param.11) | copy-start | bytes 3076
  3.9 13.3 %copy-start.1 = (bf16[256,1280]{1,0:T(8,128)(2,1)S(1)}, bf16[256,1280]{1,0:T(8,128)(2,1)}, u32[]{:S(2)}) copy-start(bf16[256,1280]{1,0:T(8,128)(2,1)} %rows_ref.1) | copy-start | bytes 1966084
  3.9 38.2 %all-to-all-start.1 = ((bf16[16,336,128]{2,1,0:T(8,128)(2,1)}), bf16[16,336,128]{2,1,0:T(8,128)(2,1)S(1)}, u32[]{:S(2)}, u32[]{:S(2)}) async-start(bf16[16,336,128]{2,1,0:T(8,128)(2,1)} %deal.1), calls=%async_computation.1 | async-start | bytes 2752512 | tf_op jit(solution)/shard_map/all_to_all | solution.py:180
  11.2 38.1 %collective-permute-start = (bf16[32,1280]{1,0:T(8,128)(2,1)S(1)}, bf16[32,1280]{1,0:T(8,128)(2,1)S(1)}, u32[]{:S(2)}, u32[]{:S(2)}) collective-permute-start(bf16[32,1280]{1,0:T(8,128)(2,1)S(1)} %get-tuple-element.5), channel_id=1, source_target_pairs={{0,1},{1,2},{2,3},{3,4},{4,5},{5,6},{6,7},{7,8},{8,9},{9,10},{10,1... | collective-permute-start | bytes 245768 | tf_op jit(solution)/shard_map/ppermute | solution.py:20
  13.3 36.0 %collective-permute-start.1 = (bf16[32,1280]{1,0:T(8,128)(2,1)S(1)}, bf16[32,1280]{1,0:T(8,128)(2,1)S(1)}, u32[]{:S(2)}, u32[]{:S(2)}) collective-permute-start(bf16[32,1280]{1,0:T(8,128)(2,1)S(1)} %get-tuple-element.4), channel_id=1, source_target_pairs={{1,0},{2,1},{3,2},{4,3},{5,4},{6,5},{7,6},{8,7},{9,8},{10,9},{11,1... | collective-permute-start | bytes 245768 | tf_op jit(solution)/shard_map/ppermute | solution.py:21
  42.1 35.5 %all-to-all-start = ((bf16[16,32,1280]{2,1,0:T(8,128)(2,1)}), bf16[16,32,1280]{2,1,0:T(8,128)(2,1)S(1)}, u32[]{:S(2)}, u32[]{:S(2)}) async-start(bf16[16,32,1280]{2,1,0:T(8,128)(2,1)} %bitcast.30), calls=%async_computation | async-start | bytes 2621440 | tf_op jit(solution)/shard_map/all_to_all | solution.py:180
  49.3 2.5 %copy-start = (bf16[2048,1280]{1,0:T(8,128)(2,1)S(1)}, bf16[2048,1280]{1,0:T(8,128)(2,1)}, u32[]{:S(2)}) copy-start(bf16[2048,1280]{1,0:T(8,128)(2,1)} %k_ref.1) | copy-start | bytes 15728644
  77.6 35.4 %all-to-all-start.2 = ((bf16[16,32,1280]{2,1,0:T(8,128)(2,1)}), bf16[16,32,1280]{2,1,0:T(8,128)(2,1)S(1)}, u32[]{:S(2)}, u32[]{:S(2)}) async-start(bf16[16,32,1280]{2,1,0:T(8,128)(2,1)} %bitcast.31), calls=%async_computation.2 | async-start | bytes 2621440 | tf_op jit(solution)/shard_map/all_to_all | solution.py:180

commit v14 on v13

--- a/solution.py
+++ b/solution.py
@@ -41,16 +41,16 @@
     rank = jnp.sum(theirs * before, axis=0, keepdims=True).astype(jnp.int32)
     place = owner * cap + rank
     each = members // parts
-    slot = lax.broadcasted_iota(jnp.int32, (each * cap, n), 0)
+    slot = lax.broadcasted_iota(jnp.int32, (members * cap, n), 0)
+    table = jnp.where(slot == place, 1.0, 0.0).astype(jnp.bfloat16)
     coming.wait()
+    out = jnp.dot(table, rows[...], preferred_element_type=jnp.float32).astype(jnp.bfloat16)
     leaving = []
     for p in range(parts):
-        table = jnp.where(slot + p * each * cap == place, 1.0, 0.0).astype(jnp.bfloat16)
-        out = jnp.dot(table, rows[...], preferred_element_type=jnp.float32).astype(jnp.bfloat16)
-        for d in range(each):
+        for d in range(p * each, (p + 1) * each):
             for t, r, c in tiles(cap, feature):
-                made[p * each + d, t : t + TILE] = out[d * cap + r : d * cap + r + TILE, c : c + LANES]
-            made[p * each + d, cap * feature // LANES :] = told
+                made[d, t : t + TILE] = out[d * cap + r : d * cap + r + TILE, c : c + LANES]
+            made[d, cap * feature // LANES :] = told
         part = pl.ds(p * each, each)
         leaving.append(pltpu.make_async_copy(made.at[part], o_ref.at[part], made_sem.at[p]))
         leaving[p].start()
@@ -182,15 +182,21 @@
 
 def place_kernel(comes_ref, x_ref, o_ref, zero, sem):
     zero[...] = jnp.zeros_like(zero)
-    members = x_ref.shape[0]
-    moves = [pltpu.make_async_copy(x_ref.at[jnp.maximum(comes_ref[d], 0)], o_ref.at[d], sem.at[d]) for d in range(members)]
-    clears = [pltpu.make_async_copy(zero, o_ref.at[d], sem.at[d]) for d in range(members)]
+    members, rows = x_ref.shape[0], zero.shape[0]
     for d in range(members):
-        pl.when(comes_ref[d] >= 0)(moves[d].start)
-        pl.when(comes_ref[d] < 0)(clears[d].start)
+        for i in range(x_ref.shape[1] // rows):
+            part = pl.ds(i * rows, rows)
+            move = pltpu.make_async_copy(x_ref.at[jnp.maximum(comes_ref[d], 0), part], o_ref.at[d, part], sem.at[d, i])
+            clear = pltpu.make_async_copy(zero, o_ref.at[d, part], sem.at[d, i])
+            pl.when(comes_ref[d] >= 0)(move.start)
+            pl.when(comes_ref[d] < 0)(clear.start)
     for d in range(members):
-        pl.when(comes_ref[d] >= 0)(moves[d].wait)
-        pl.when(comes_ref[d] < 0)(clears[d].wait)
+        for i in range(x_ref.shape[1] // rows):
+            part = pl.ds(i * rows, rows)
+            move = pltpu.make_async_copy(x_ref.at[jnp.maximum(comes_ref[d], 0), part], o_ref.at[d, part], sem.at[d, i])
+            clear = pltpu.make_async_copy(zero, o_ref.at[d, part], sem.at[d, i])
+            pl.when(comes_ref[d] >= 0)(move.wait)
+            pl.when(comes_ref[d] < 0)(clear.wait)
 
 
 def place(x, comes):
@@ -207,7 +213,7 @@
         in_specs=[SMEM, VMEM],
         out_specs=HBM,
         out_shape=jax.ShapeDtypeStruct(x.shape, x.dtype),
-        scratch_shapes=[pltpu.VMEM((cap, feature), x.dtype), pltpu.SemaphoreType.DMA((members,))],
+        scratch_shapes=[pltpu.VMEM((TILE, feature), x.dtype), pltpu.SemaphoreType.DMA((members, cap // TILE))],
         compiler_params=pltpu.CompilerParams(vmem_limit_bytes=8 * 1024 * 1024),
         cost_estimate=pl.CostEstimate(flops=0, bytes_accessed=4 * x.size, transcendentals=0),
         name="place",

time: 116 us -> 116 us (level)
  no operation moved by 1% of the time
where the time goes in v14:
time: 116 us; the launch traced here: 115 us
  waiting for transfers between devices  65.8 us (57%)
  starting transfers between devices  22 us (19%)
  Pallas kernels  17 us (15%)
  local copies, waits for them, and re-layouts  4.13 us (4%)
  matrix products  3.68 us (3%)
  other arithmetic  1.67 us (1%)
    all_to_all x3, waiting for transfers between devices, exchange(): return lax.all_to_all(x, 'docs', split_axis=0, concat_axis=0, tiled=True)  65.8 us
    all_to_all x3, starting transfers between devices, exchange(): return lax.all_to_all(x, 'docs', split_axis=0, concat_axis=0, tiled=True)  16.5 us
    pallas_call x1, Pallas kernels, attend(): pl.pallas_call(functools.partial(attend_kernel, feature ** (-0.5)), grid=...  10.1 us
    ppermute x1, starting transfers between devices, halo_of(): after = lax.ppermute(sentences[:MOST_SENT], 'docs', down)  3.51 us
    pallas_call x1, Pallas kernels, deal(): pl.pallas_call(functools.partial(deal_kernel, cap), in_specs=[VMEM] * 3 +...  3.37 us
    unnamed x11, local copies, waits for them, and re-layouts  2.51 us
  transfers between devices with their start and end apart: 5, of which 3 were waited for; matrix products, arithmetic and copies ran while one was open for 6% of the time, Pallas kernels for 10%

profile of v14, /device:TPU:14, one launch (start us, length us, event | category | flops | bytes accessed | tf_op | source)
XLA Modules:
  0.0 115.0 jit_solution(13728888916429344296)
XLA Ops:
  0.6 3.4 %deal.1 = bf16[16,336,128]{2,1,0:T(8,128)(2,1)} custom-call(s32[2,128]{1,0:T(2,128)} %bitcast.34, s32[2,128]{1,0:T(2,128)} %bitcast.37, s32[2,128]{1,0:T(2,128)} %bitcast.39, bf16[256,1280]{1,0:T(8,128)(2,1)} %rows_ref.1), custom_call_target="tpu_custom_call" | custom-call | flops 335544320 | bytes 1966080 | tf_op jit(solution)/shard_map/deal/pallas_call | solution.py:70
  4.1 6.4 %all-to-all-start.1 = ((bf16[16,336,128]{2,1,0:T(8,128)(2,1)}), bf16[16,336,128]{2,1,0:T(8,128)(2,1)S(1)}, u32[]{:S(2)}, u32[]{:S(2)}) async-start(bf16[16,336,128]{2,1,0:T(8,128)(2,1)} %deal.1), calls=%async_computation.1 | async-start | bytes 2752512 | tf_op jit(solution)/shard_map/all_to_all | solution.py:180
  10.4 0.9 fusion.15
  11.4 2.1 %collective-permute-start = (bf16[32,1280]{1,0:T(8,128)(2,1)S(1)}, bf16[32,1280]{1,0:T(8,128)(2,1)S(1)}, u32[]{:S(2)}, u32[]{:S(2)}) collective-permute-start(bf16[32,1280]{1,0:T(8,128)(2,1)S(1)} %get-tuple-element.5), channel_id=1, source_target_pairs={{0,1},{1,2},{2,3},{3,4},{4,5},{5,6},{6,7},{7,8},{8,9},{9,10},{10,1... | collective-permute-start | bytes 245768 | tf_op jit(solution)/shard_map/ppermute | solution.py:20
  13.4 3.5 %collective-permute-start.1 = (bf16[32,1280]{1,0:T(8,128)(2,1)S(1)}, bf16[32,1280]{1,0:T(8,128)(2,1)S(1)}, u32[]{:S(2)}, u32[]{:S(2)}) collective-permute-start(bf16[32,1280]{1,0:T(8,128)(2,1)S(1)} %get-tuple-element.4), channel_id=1, source_target_pairs={{1,0},{2,1},{3,2},{4,3},{5,4},{6,5},{7,6},{8,7},{9,8},{10,9},{11,1... | collective-permute-start | bytes 245768 | tf_op jit(solution)/shard_map/ppermute | solution.py:21
  17.0 0.2 convert_reduce_fusion
  17.2 0.1 fusion.14
  17.3 1.6 %convolution_convert_fusion.1 = bf16[512,1280]{1,0:T(8,128)(2,1)} fusion(bf16[256,1280]{1,0:T(8,128)(2,1)S(1)} %copy-done.1, s32[256]{0:T(256)S(1)} %add.71), kind=kOutput, calls=%fused_computation.3 | convolution fusion | flops 336330752 | bytes 1967104 | tf_op jit(solution)/shard_map/dot_general | solution.py:238
  18.9 23.4 %all-to-all-done.1.q_ref = bf16[16,336,128]{2,1,0:T(8,128)(2,1)S(1)} async-done(((bf16[16,336,128]{2,1,0:T(8,128)(2,1)}), bf16[16,336,128]{2,1,0:T(8,128)(2,1)S(1)}, u32[]{:S(2)}, u32[]{:S(2)}) %all-to-all-start.1) | async-done | bytes 1376288 | tf_op jit(solution)/shard_map/all_to_all | solution.py:180
  42.3 5.1 %all-to-all-start = ((bf16[16,32,1280]{2,1,0:T(8,128)(2,1)}), bf16[16,32,1280]{2,1,0:T(8,128)(2,1)S(1)}, u32[]{:S(2)}, u32[]{:S(2)}) async-start(bf16[16,32,1280]{2,1,0:T(8,128)(2,1)} %bitcast.30), calls=%async_computation | async-start | bytes 2621440 | tf_op jit(solution)/shard_map/all_to_all | solution.py:180
  47.5 0.1 fusion.8
  47.6 0.1 convolution_convert_fusion.2
  47.7 0.4 select_reduce_fusion.1
  48.4 0.8 select_reduce_fusion
  49.2 0.2 copy.21.doc_ref
  49.5 2.5 %copy-done = bf16[2048,1280]{1,0:T(8,128)(2,1)S(1)} copy-done((bf16[2048,1280]{1,0:T(8,128)(2,1)S(1)}, bf16[2048,1280]{1,0:T(8,128)(2,1)}, u32[]{:S(2)}) %copy-start) | copy-done | bytes 5242904
  52.0 10.1 %attend.1 = bf16[512,1280]{1,0:T(8,128)(2,1)S(1)} custom-call(bf16[16,336,128]{2,1,0:T(8,128)(2,1)S(1)} %all-to-all-done.1.q_ref, s32[512,1]{1,0:T(8,128)S(1)} %copy.21.doc_ref, bf16[2048,1280]{1,0:T(8,128)(2,1)S(1)} %copy-done, bf16[32,1280]{1,0:T(8,128)(2,1)S(1)} %collective-permute-done.before_ref, bf16[32,1280]{1,0:T(8,128)(2,1)S(1)} %collective-permute-done.1.after_ref, ...), custom_call_target="tpu_custom_call" | custom-call | flops 5368709120 | bytes 7864320 | tf_op jit(solution)/shard_map/attend/pallas_call | solution.py:123
  62.1 1.9 %convolution_convert_fusion = bf16[512,1280]{1,0:T(8,128)(2,1)} fusion(bf16[512,1280]{1,0:T(8,128)(2,1)S(1)} %attend.1, s32[512]{0:T(512)S(1)} %fusion.9, pred[512]{0:T(512)(128)(4,1)S(1)} %ge.13), kind=kOutput, calls=%fused_computation.2 | convolution fusion | flops 672268288 | bytes 2624000 | tf_op jit(solution)/shard_map/dot_general | solution.py:274
  64.0 13.7 %all-to-all-done = bf16[16,32,1280]{2,1,0:T(8,128)(2,1)S(1)} async-done(((bf16[16,32,1280]{2,1,0:T(8,128)(2,1)}), bf16[16,32,1280]{2,1,0:T(8,128)(2,1)S(1)}, u32[]{:S(2)}, u32[]{:S(2)}) %all-to-all-start) | async-done | bytes 1310752 | tf_op jit(solution)/shard_map/all_to_all | solution.py:180
  77.7 5.0 %all-to-all-start.2 = ((bf16[16,32,1280]{2,1,0:T(8,128)(2,1)}), bf16[16,32,1280]{2,1,0:T(8,128)(2,1)S(1)}, u32[]{:S(2)}, u32[]{:S(2)}) async-start(bf16[16,32,1280]{2,1,0:T(8,128)(2,1)} %bitcast.31), calls=%async_computation.2 | async-start | bytes 2621440 | tf_op jit(solution)/shard_map/all_to_all | solution.py:180
  82.8 1.6 %write_out.1 = bf16[512,1280]{1,0:T(8,128)(2,1)} custom-call(bf16[512,1280]{1,0:T(8,128)(2,1)S(1)} %bitcast.28), custom_call_target="tpu_custom_call" | custom-call | bytes 2621440 | tf_op jit(solution)/shard_map/write_out/pallas_call | solution.py:167
  84.4 0.1 select_reduce_fusion.2
  84.5 28.7 %all-to-all-done.2.x_ref = bf16[16,32,1280]{2,1,0:T(8,128)(2,1)S(1)} async-done(((bf16[16,32,1280]{2,1,0:T(8,128)(2,1)}), bf16[16,32,1280]{2,1,0:T(8,128)(2,1)S(1)}, u32[]{:S(2)}, u32[]{:S(2)}) %all-to-all-start.2) | async-done | bytes 1310752 | tf_op jit(solution)/shard_map/all_to_all | solution.py:180
  113.2 1.9 %place.1 = bf16[16,32,1280]{2,1,0:T(8,128)(2,1)} custom-call(s32[16]{0:T(128)S(1)} %broadcast_add_fusion.2.comes_ref, bf16[16,32,1280]{2,1,0:T(8,128)(2,1)S(1)} %all-to-all-done.2.x_ref), custom_call_target="tpu_custom_call" | custom-call | bytes 2621440 | tf_op jit(solution)/shard_map/place/pallas_call | solution.py:211
  (28 shorter events, 0.6 us)
Async XLA Ops:
  4.0 13.0 %copy-start.2 = (s32[32768]{0:T(1024)S(1)}, s32[32768]{0:T(1024)}, u32[]{:S(2)}) copy-start(s32[32768]{0:T(1024)} %param.7) | copy-start | bytes 393220
  4.0 13.0 %copy-start.3 = (s32[256,1]{0,1:T(1,128)S(1)}, s32[256,1]{0,1:T(1,128)}, u32[]{:S(2)}) copy-start(s32[256,1]{0,1:T(1,128)} %param.9) | copy-start | bytes 3076
  4.0 13.2 %copy-start.4 = (s32[256,1]{0,1:T(1,128)S(1)}, s32[256,1]{0,1:T(1,128)}, u32[]{:S(2)}) copy-start(s32[256,1]{0,1:T(1,128)} %param.11) | copy-start | bytes 3076
  4.0 13.3 %copy-start.1 = (bf16[256,1280]{1,0:T(8,128)(2,1)S(1)}, bf16[256,1280]{1,0:T(8,128)(2,1)}, u32[]{:S(2)}) copy-start(bf16[256,1280]{1,0:T(8,128)(2,1)} %rows_ref.1) | copy-start | bytes 1966084
  4.1 38.2 %all-to-all-start.1 = ((bf16[16,336,128]{2,1,0:T(8,128)(2,1)}), bf16[16,336,128]{2,1,0:T(8,128)(2,1)S(1)}, u32[]{:S(2)}, u32[]{:S(2)}) async-start(bf16[16,336,128]{2,1,0:T(8,128)(2,1)} %deal.1), calls=%async_computation.1 | async-start | bytes 2752512 | tf_op jit(solution)/shard_map/all_to_all | solution.py:180
  11.4 38.1 %collective-permute-start = (bf16[32,1280]{1,0:T(8,128)(2,1)S(1)}, bf16[32,1280]{1,0:T(8,128)(2,1)S(1)}, u32[]{:S(2)}, u32[]{:S(2)}) collective-permute-start(bf16[32,1280]{1,0:T(8,128)(2,1)S(1)} %get-tuple-element.5), channel_id=1, source_target_pairs={{0,1},{1,2},{2,3},{3,4},{4,5},{5,6},{6,7},{7,8},{8,9},{9,10},{10,1... | collective-permute-start | bytes 245768 | tf_op jit(solution)/shard_map/ppermute | solution.py:20
  13.4 36.0 %collective-permute-start.1 = (bf16[32,1280]{1,0:T(8,128)(2,1)S(1)}, bf16[32,1280]{1,0:T(8,128)(2,1)S(1)}, u32[]{:S(2)}, u32[]{:S(2)}) collective-permute-start(bf16[32,1280]{1,0:T(8,128)(2,1)S(1)} %get-tuple-element.4), channel_id=1, source_target_pairs={{1,0},{2,1},{3,2},{4,3},{5,4},{6,5},{7,6},{8,7},{9,8},{10,9},{11,1... | collective-permute-start | bytes 245768 | tf_op jit(solution)/shard_map/ppermute | solution.py:21
  42.3 35.5 %all-to-all-start = ((bf16[16,32,1280]{2,1,0:T(8,128)(2,1)}), bf16[16,32,1280]{2,1,0:T(8,128)(2,1)S(1)}, u32[]{:S(2)}, u32[]{:S(2)}) async-start(bf16[16,32,1280]{2,1,0:T(8,128)(2,1)} %bitcast.30), calls=%async_computation | async-start | bytes 2621440 | tf_op jit(solution)/shard_map/all_to_all | solution.py:180
  49.5 2.5 %copy-start = (bf16[2048,1280]{1,0:T(8,128)(2,1)S(1)}, bf16[2048,1280]{1,0:T(8,128)(2,1)}, u32[]{:S(2)}) copy-start(bf16[2048,1280]{1,0:T(8,128)(2,1)} %k_ref.1) | copy-start | bytes 15728644
  77.7 35.4 %all-to-all-start.2 = ((bf16[16,32,1280]{2,1,0:T(8,128)(2,1)}), bf16[16,32,1280]{2,1,0:T(8,128)(2,1)S(1)}, u32[]{:S(2)}, u32[]{:S(2)}) async-start(bf16[16,32,1280]{2,1,0:T(8,128)(2,1)} %bitcast.31), calls=%async_computation.2 | async-start | bytes 2621440 | tf_op jit(solution)/shard_map/all_to_all | solution.py:180

commit v15 on v8

--- a/solution.py
+++ b/solution.py
@@ -162,17 +162,18 @@
     return lax.all_to_all(x, "docs", split_axis=0, concat_axis=0, tiled=True)
 
 
-def place_kernel(comes_ref, x_ref, o_ref, zero, sem):
-    zero[...] = jnp.zeros_like(zero)
-    members = x_ref.shape[0]
-    moves = [pltpu.make_async_copy(x_ref.at[jnp.maximum(comes_ref[d], 0)], o_ref.at[d], sem.at[d]) for d in range(members)]
-    clears = [pltpu.make_async_copy(zero, o_ref.at[d], sem.at[d]) for d in range(members)]
-    for d in range(members):
-        pl.when(comes_ref[d] >= 0)(moves[d].start)
-        pl.when(comes_ref[d] < 0)(clears[d].start)
-    for d in range(members):
-        pl.when(comes_ref[d] >= 0)(moves[d].wait)
-        pl.when(comes_ref[d] < 0)(clears[d].wait)
+def place_kernel(comes_ref, x_ref, o_ref):
+    each = o_ref.shape[0]
+    for i in range(each):
+        block = comes_ref[pl.program_id(0) * each + i]
+
+        @pl.when(block >= 0)
+        def _():
+            o_ref[i] = x_ref[jnp.maximum(block, 0)]
+
+        @pl.when(block < 0)
+        def _():
+            o_ref[i] = jnp.zeros_like(o_ref[i])
 
 
 def place(x, comes):
@@ -184,12 +185,13 @@
         table = takes.astype(jnp.bfloat16)
         rows = x.reshape(members * cap, feature)
         return jnp.dot(table, rows, preferred_element_type=jnp.float32).astype(jnp.bfloat16)
+    steps = 4 if members % 4 == 0 else 1
     return pl.pallas_call(
         place_kernel,
+        grid=(steps,),
         in_specs=[SMEM, VMEM],
-        out_specs=HBM,
+        out_specs=pl.BlockSpec((members // steps, cap, feature), lambda i: (i, 0, 0)),
         out_shape=jax.ShapeDtypeStruct(x.shape, x.dtype),
-        scratch_shapes=[pltpu.VMEM((cap, feature), x.dtype), pltpu.SemaphoreType.DMA((members,))],
         compiler_params=pltpu.CompilerParams(vmem_limit_bytes=8 * 1024 * 1024),
         cost_estimate=pl.CostEstimate(flops=0, bytes_accessed=4 * x.size, transcendentals=0),
         name="place",

time: 115 us -> 116 us (level)
  no operation moved by 1% of the time
where the time goes in v15:
time: 116 us; the launch traced here: 115 us
  waiting for transfers between devices  65.8 us (57%)
  starting transfers between devices  22 us (19%)
  Pallas kernels  16.9 us (15%)
  local copies, waits for them, and re-layouts  4.12 us (4%)
  matrix products  3.68 us (3%)
  other arithmetic  1.67 us (1%)
    all_to_all x3, waiting for transfers between devices, exchange(): return lax.all_to_all(x, 'docs', split_axis=0, concat_axis=0, tiled=True)  65.8 us
    all_to_all x3, starting transfers between devices, exchange(): return lax.all_to_all(x, 'docs', split_axis=0, concat_axis=0, tiled=True)  16.5 us
    pallas_call x1, Pallas kernels, attend(): pl.pallas_call(functools.partial(attend_kernel, feature ** (-0.5)), grid=...  10.1 us
    ppermute x1, starting transfers between devices, halo_of(): after = lax.ppermute(sentences[:MOST_SENT], 'docs', down)  3.51 us
    pallas_call x1, Pallas kernels, deal(): pl.pallas_call(functools.partial(deal_kernel, cap), in_specs=[pl.BlockSpe...  2.9 us
    unnamed x11, local copies, waits for them, and re-layouts  2.5 us
  transfers between devices with their start and end apart: 5, of which 3 were waited for; matrix products, arithmetic and copies ran while one was open for 6% of the time, Pallas kernels for 10%

profile of v15, /device:TPU:14, one launch (start us, length us, event | category | flops | bytes accessed | tf_op | source)
XLA Modules:
  0.0 114.9 jit_solution(13281369889752060694)
XLA Ops:
  0.6 2.9 %deal.1 = bf16[16,336,128]{2,1,0:T(8,128)(2,1)} custom-call(s32[2,128]{1,0:T(2,128)} %bitcast.34, s32[2,128]{1,0:T(2,128)} %bitcast.37, s32[2,128]{1,0:T(2,128)} %bitcast.39, bf16[256,1280]{1,0:T(8,128)(2,1)} %rows_ref.1), custom_call_target="tpu_custom_call" | custom-call | flops 335544320 | bytes 1966080 | tf_op jit(solution)/shard_map/deal/pallas_call | solution.py:58
  3.5 6.4 %all-to-all-start.1 = ((bf16[16,336,128]{2,1,0:T(8,128)(2,1)}), bf16[16,336,128]{2,1,0:T(8,128)(2,1)S(1)}, u32[]{:S(2)}, u32[]{:S(2)}) async-start(bf16[16,336,128]{2,1,0:T(8,128)(2,1)} %deal.1), calls=%async_computation.1 | async-start | bytes 2752512 | tf_op jit(solution)/shard_map/all_to_all | solution.py:162
  9.9 0.9 fusion.15
  10.9 2.1 %collective-permute-start = (bf16[32,1280]{1,0:T(8,128)(2,1)S(1)}, bf16[32,1280]{1,0:T(8,128)(2,1)S(1)}, u32[]{:S(2)}, u32[]{:S(2)}) collective-permute-start(bf16[32,1280]{1,0:T(8,128)(2,1)S(1)} %get-tuple-element.5), channel_id=1, source_target_pairs={{0,1},{1,2},{2,3},{3,4},{4,5},{5,6},{6,7},{7,8},{8,9},{9,10},{10,1... | collective-permute-start | bytes 245768 | tf_op jit(solution)/shard_map/ppermute | solution.py:20
  12.9 3.5 %collective-permute-start.1 = (bf16[32,1280]{1,0:T(8,128)(2,1)S(1)}, bf16[32,1280]{1,0:T(8,128)(2,1)S(1)}, u32[]{:S(2)}, u32[]{:S(2)}) collective-permute-start(bf16[32,1280]{1,0:T(8,128)(2,1)S(1)} %get-tuple-element.4), channel_id=1, source_target_pairs={{1,0},{2,1},{3,2},{4,3},{5,4},{6,5},{7,6},{8,7},{9,8},{10,9},{11,1... | collective-permute-start | bytes 245768 | tf_op jit(solution)/shard_map/ppermute | solution.py:21
  16.5 0.2 convert_reduce_fusion
  16.7 0.1 fusion.14
  16.8 1.6 %convolution_convert_fusion.1 = bf16[512,1280]{1,0:T(8,128)(2,1)} fusion(bf16[256,1280]{1,0:T(8,128)(2,1)S(1)} %copy-done.1, s32[256]{0:T(256)S(1)} %add.71), kind=kOutput, calls=%fused_computation.3 | convolution fusion | flops 336330752 | bytes 1967104 | tf_op jit(solution)/shard_map/dot_general | solution.py:216
  18.4 23.4 %all-to-all-done.1.q_ref = bf16[16,336,128]{2,1,0:T(8,128)(2,1)S(1)} async-done(((bf16[16,336,128]{2,1,0:T(8,128)(2,1)}), bf16[16,336,128]{2,1,0:T(8,128)(2,1)S(1)}, u32[]{:S(2)}, u32[]{:S(2)}) %all-to-all-start.1) | async-done | bytes 1376288 | tf_op jit(solution)/shard_map/all_to_all | solution.py:162
  41.8 5.1 %all-to-all-start = ((bf16[16,32,1280]{2,1,0:T(8,128)(2,1)}), bf16[16,32,1280]{2,1,0:T(8,128)(2,1)S(1)}, u32[]{:S(2)}, u32[]{:S(2)}) async-start(bf16[16,32,1280]{2,1,0:T(8,128)(2,1)} %bitcast.30), calls=%async_computation | async-start | bytes 2621440 | tf_op jit(solution)/shard_map/all_to_all | solution.py:162
  46.9 0.1 fusion.8
  47.1 0.1 convolution_convert_fusion.2
  47.2 0.4 select_reduce_fusion.1
  47.8 0.8 select_reduce_fusion
  48.6 0.2 copy.21.doc_ref
  49.0 2.5 %copy-done = bf16[2048,1280]{1,0:T(8,128)(2,1)S(1)} copy-done((bf16[2048,1280]{1,0:T(8,128)(2,1)S(1)}, bf16[2048,1280]{1,0:T(8,128)(2,1)}, u32[]{:S(2)}) %copy-start) | copy-done | bytes 5242904
  51.5 10.1 %attend.1 = bf16[512,1280]{1,0:T(8,128)(2,1)S(1)} custom-call(bf16[16,336,128]{2,1,0:T(8,128)(2,1)S(1)} %all-to-all-done.1.q_ref, s32[512,1]{1,0:T(8,128)S(1)} %copy.21.doc_ref, bf16[2048,1280]{1,0:T(8,128)(2,1)S(1)} %copy-done, bf16[32,1280]{1,0:T(8,128)(2,1)S(1)} %collective-permute-done.before_ref, bf16[32,1280]{1,0:T(8,128)(2,1)S(1)} %collective-permute-done.1.after_ref, ...), custom_call_target="tpu_custom_call" | custom-call | flops 5368709120 | bytes 7864320 | tf_op jit(solution)/shard_map/attend/pallas_call | solution.py:105
  61.6 1.9 %convolution_convert_fusion = bf16[512,1280]{1,0:T(8,128)(2,1)} fusion(bf16[512,1280]{1,0:T(8,128)(2,1)S(1)} %attend.1, s32[512]{0:T(512)S(1)} %fusion.9, pred[512]{0:T(512)(128)(4,1)S(1)} %ge.13), kind=kOutput, calls=%fused_computation.2 | convolution fusion | flops 672268288 | bytes 2624000 | tf_op jit(solution)/shard_map/dot_general | solution.py:252
  63.5 13.7 %all-to-all-done = bf16[16,32,1280]{2,1,0:T(8,128)(2,1)S(1)} async-done(((bf16[16,32,1280]{2,1,0:T(8,128)(2,1)}), bf16[16,32,1280]{2,1,0:T(8,128)(2,1)S(1)}, u32[]{:S(2)}, u32[]{:S(2)}) %all-to-all-start) | async-done | bytes 1310752 | tf_op jit(solution)/shard_map/all_to_all | solution.py:162
  77.2 5.0 %all-to-all-start.2 = ((bf16[16,32,1280]{2,1,0:T(8,128)(2,1)}), bf16[16,32,1280]{2,1,0:T(8,128)(2,1)S(1)}, u32[]{:S(2)}, u32[]{:S(2)}) async-start(bf16[16,32,1280]{2,1,0:T(8,128)(2,1)} %bitcast.31), calls=%async_computation.2 | async-start | bytes 2621440 | tf_op jit(solution)/shard_map/all_to_all | solution.py:162
  82.2 1.6 %write_out.1 = bf16[512,1280]{1,0:T(8,128)(2,1)} custom-call(bf16[512,1280]{1,0:T(8,128)(2,1)S(1)} %bitcast.28), custom_call_target="tpu_custom_call" | custom-call | bytes 2621440 | tf_op jit(solution)/shard_map/write_out/pallas_call | solution.py:149
  83.9 0.1 select_reduce_fusion.2
  84.0 28.7 %all-to-all-done.2.x_ref = bf16[16,32,1280]{2,1,0:T(8,128)(2,1)S(1)} async-done(((bf16[16,32,1280]{2,1,0:T(8,128)(2,1)}), bf16[16,32,1280]{2,1,0:T(8,128)(2,1)S(1)}, u32[]{:S(2)}, u32[]{:S(2)}) %all-to-all-start.2) | async-done | bytes 1310752 | tf_op jit(solution)/shard_map/all_to_all | solution.py:162
  112.7 2.2 %place.1 = bf16[16,32,1280]{2,1,0:T(8,128)(2,1)} custom-call(s32[16]{0:T(128)S(1)} %broadcast_add_fusion.2.comes_ref, bf16[16,32,1280]{2,1,0:T(8,128)(2,1)S(1)} %all-to-all-done.2.x_ref), custom_call_target="tpu_custom_call" | custom-call | bytes 2621440 | tf_op jit(solution)/shard_map/place/pallas_call | solution.py:189
  (28 shorter events, 0.6 us)
Async XLA Ops:
  3.5 12.9 %copy-start.2 = (s32[32768]{0:T(1024)S(1)}, s32[32768]{0:T(1024)}, u32[]{:S(2)}) copy-start(s32[32768]{0:T(1024)} %param.7) | copy-start | bytes 393220
  3.5 12.9 %copy-start.3 = (s32[256,1]{0,1:T(1,128)S(1)}, s32[256,1]{0,1:T(1,128)}, u32[]{:S(2)}) copy-start(s32[256,1]{0,1:T(1,128)} %param.9) | copy-start | bytes 3076
  3.5 13.1 %copy-start.4 = (s32[256,1]{0,1:T(1,128)S(1)}, s32[256,1]{0,1:T(1,128)}, u32[]{:S(2)}) copy-start(s32[256,1]{0,1:T(1,128)} %param.11) | copy-start | bytes 3076
  3.5 13.3 %copy-start.1 = (bf16[256,1280]{1,0:T(8,128)(2,1)S(1)}, bf16[256,1280]{1,0:T(8,128)(2,1)}, u32[]{:S(2)}) copy-start(bf16[256,1280]{1,0:T(8,128)(2,1)} %rows_ref.1) | copy-start | bytes 1966084
  3.5 38.2 %all-to-all-start.1 = ((bf16[16,336,128]{2,1,0:T(8,128)(2,1)}), bf16[16,336,128]{2,1,0:T(8,128)(2,1)S(1)}, u32[]{:S(2)}, u32[]{:S(2)}) async-start(bf16[16,336,128]{2,1,0:T(8,128)(2,1)} %deal.1), calls=%async_computation.1 | async-start | bytes 2752512 | tf_op jit(solution)/shard_map/all_to_all | solution.py:162
  10.9 38.1 %collective-permute-start = (bf16[32,1280]{1,0:T(8,128)(2,1)S(1)}, bf16[32,1280]{1,0:T(8,128)(2,1)S(1)}, u32[]{:S(2)}, u32[]{:S(2)}) collective-permute-start(bf16[32,1280]{1,0:T(8,128)(2,1)S(1)} %get-tuple-element.5), channel_id=1, source_target_pairs={{0,1},{1,2},{2,3},{3,4},{4,5},{5,6},{6,7},{7,8},{8,9},{9,10},{10,1... | collective-permute-start | bytes 245768 | tf_op jit(solution)/shard_map/ppermute | solution.py:20
  12.9 36.0 %collective-permute-start.1 = (bf16[32,1280]{1,0:T(8,128)(2,1)S(1)}, bf16[32,1280]{1,0:T(8,128)(2,1)S(1)}, u32[]{:S(2)}, u32[]{:S(2)}) collective-permute-start(bf16[32,1280]{1,0:T(8,128)(2,1)S(1)} %get-tuple-element.4), channel_id=1, source_target_pairs={{1,0},{2,1},{3,2},{4,3},{5,4},{6,5},{7,6},{8,7},{9,8},{10,9},{11,1... | collective-permute-start | bytes 245768 | tf_op jit(solution)/shard_map/ppermute | solution.py:21
  41.8 35.5 %all-to-all-start = ((bf16[16,32,1280]{2,1,0:T(8,128)(2,1)}), bf16[16,32,1280]{2,1,0:T(8,128)(2,1)S(1)}, u32[]{:S(2)}, u32[]{:S(2)}) async-start(bf16[16,32,1280]{2,1,0:T(8,128)(2,1)} %bitcast.30), calls=%async_computation | async-start | bytes 2621440 | tf_op jit(solution)/shard_map/all_to_all | solution.py:162
  49.0 2.5 %copy-start = (bf16[2048,1280]{1,0:T(8,128)(2,1)S(1)}, bf16[2048,1280]{1,0:T(8,128)(2,1)}, u32[]{:S(2)}) copy-start(bf16[2048,1280]{1,0:T(8,128)(2,1)} %k_ref.1) | copy-start | bytes 15728644
  77.2 35.4 %all-to-all-start.2 = ((bf16[16,32,1280]{2,1,0:T(8,128)(2,1)}), bf16[16,32,1280]{2,1,0:T(8,128)(2,1)S(1)}, u32[]{:S(2)}, u32[]{:S(2)}) async-start(bf16[16,32,1280]{2,1,0:T(8,128)(2,1)} %bitcast.31), calls=%async_computation.2 | async-start | bytes 2621440 | tf_op jit(solution)/shard_map/all_to_all | solution.py:162

commit v16 on v8

--- a/solution.py
+++ b/solution.py
@@ -37,13 +37,16 @@
         theirs.astype(jnp.bfloat16), jnp.where(sooner, 1.0, 0.0).astype(jnp.bfloat16), preferred_element_type=jnp.float32
     )
     rank = jnp.sum(theirs * before, axis=0, keepdims=True).astype(jnp.int32)
-    slot = lax.broadcasted_iota(jnp.int32, (members * cap, n), 0)
-    table = jnp.where(slot == owner * cap + rank, 1.0, 0.0).astype(jnp.bfloat16)
-    out = jnp.dot(table, rows_ref[...], preferred_element_type=jnp.float32).astype(jnp.bfloat16)
-    for d in range(members):
-        for t, r, c in tiles(cap, out.shape[1]):
-            o_ref[d, t : t + TILE] = out[d * cap + r : d * cap + r + TILE, c : c + LANES]
-        o_ref[d, cap * out.shape[1] // LANES :] = told
+    each = members // (4 if members % 4 == 0 else 1)
+    slot = lax.broadcasted_iota(jnp.int32, (each * cap, n), 0)
+    place = owner * cap + rank
+    for start in range(0, members, each):
+        table = jnp.where(slot + start * cap == place, 1.0, 0.0).astype(jnp.bfloat16)
+        out = jnp.dot(table, rows_ref[...], preferred_element_type=jnp.float32).astype(jnp.bfloat16)
+        for d in range(each):
+            for t, r, c in tiles(cap, out.shape[1]):
+                o_ref[start + d, t : t + TILE] = out[d * cap + r : d * cap + r + TILE, c : c + LANES]
+            o_ref[start + d, cap * out.shape[1] // LANES :] = told
 
 
 def tiles(rows, columns):

time: 115 us -> 115 us (level)
  no operation moved by 1% of the time
where the time goes in v16:
time: 115 us; the launch traced here: 114 us
  waiting for transfers between devices  65.8 us (57%)
  starting transfers between devices  22 us (19%)
  Pallas kernels  16.4 us (14%)
  local copies, waits for them, and re-layouts  4.12 us (4%)
  matrix products  3.68 us (3%)
  other arithmetic  1.67 us (1%)
    all_to_all x3, waiting for transfers between devices, exchange(): return lax.all_to_all(x, 'docs', split_axis=0, concat_axis=0, tiled=True)  65.8 us
    all_to_all x3, starting transfers between devices, exchange(): return lax.all_to_all(x, 'docs', split_axis=0, concat_axis=0, tiled=True)  16.5 us
    pallas_call x1, Pallas kernels, attend(): pl.pallas_call(functools.partial(attend_kernel, feature ** (-0.5)), grid=...  10.1 us
    ppermute x1, starting transfers between devices, halo_of(): after = lax.ppermute(sentences[:MOST_SENT], 'docs', down)  3.51 us
    pallas_call x1, Pallas kernels, deal(): pl.pallas_call(functools.partial(deal_kernel, cap), in_specs=[pl.BlockSpe...  2.9 us
    unnamed x11, local copies, waits for them, and re-layouts  2.5 us
  transfers between devices with their start and end apart: 5, of which 3 were waited for; matrix products, arithmetic and copies ran while one was open for 6% of the time, Pallas kernels for 10%

profile of v16, /device:TPU:14, one launch (start us, length us, event | category | flops | bytes accessed | tf_op | source)
XLA Modules:
  0.0 114.4 jit_solution(4648994577722653243)
XLA Ops:
  0.6 2.9 %deal.1 = bf16[16,336,128]{2,1,0:T(8,128)(2,1)} custom-call(s32[2,128]{1,0:T(2,128)} %bitcast.34, s32[2,128]{1,0:T(2,128)} %bitcast.37, s32[2,128]{1,0:T(2,128)} %bitcast.39, bf16[256,1280]{1,0:T(8,128)(2,1)} %rows_ref.1), custom_call_target="tpu_custom_call" | custom-call | flops 335544320 | bytes 1966080 | tf_op jit(solution)/shard_map/deal/pallas_call | solution.py:61
  3.5 6.4 %all-to-all-start.1 = ((bf16[16,336,128]{2,1,0:T(8,128)(2,1)}), bf16[16,336,128]{2,1,0:T(8,128)(2,1)S(1)}, u32[]{:S(2)}, u32[]{:S(2)}) async-start(bf16[16,336,128]{2,1,0:T(8,128)(2,1)} %deal.1), calls=%async_computation.1 | async-start | bytes 2752512 | tf_op jit(solution)/shard_map/all_to_all | solution.py:165
  9.9 0.9 fusion.15
  10.9 2.1 %collective-permute-start = (bf16[32,1280]{1,0:T(8,128)(2,1)S(1)}, bf16[32,1280]{1,0:T(8,128)(2,1)S(1)}, u32[]{:S(2)}, u32[]{:S(2)}) collective-permute-start(bf16[32,1280]{1,0:T(8,128)(2,1)S(1)} %get-tuple-element.5), channel_id=1, source_target_pairs={{0,1},{1,2},{2,3},{3,4},{4,5},{5,6},{6,7},{7,8},{8,9},{9,10},{10,1... | collective-permute-start | bytes 245768 | tf_op jit(solution)/shard_map/ppermute | solution.py:20
  12.9 3.5 %collective-permute-start.1 = (bf16[32,1280]{1,0:T(8,128)(2,1)S(1)}, bf16[32,1280]{1,0:T(8,128)(2,1)S(1)}, u32[]{:S(2)}, u32[]{:S(2)}) collective-permute-start(bf16[32,1280]{1,0:T(8,128)(2,1)S(1)} %get-tuple-element.4), channel_id=1, source_target_pairs={{1,0},{2,1},{3,2},{4,3},{5,4},{6,5},{7,6},{8,7},{9,8},{10,9},{11,1... | collective-permute-start | bytes 245768 | tf_op jit(solution)/shard_map/ppermute | solution.py:21
  16.5 0.2 convert_reduce_fusion
  16.7 0.1 fusion.14
  16.8 1.6 %convolution_convert_fusion.1 = bf16[512,1280]{1,0:T(8,128)(2,1)} fusion(bf16[256,1280]{1,0:T(8,128)(2,1)S(1)} %copy-done.1, s32[256]{0:T(256)S(1)} %add.71), kind=kOutput, calls=%fused_computation.3 | convolution fusion | flops 336330752 | bytes 1967104 | tf_op jit(solution)/shard_map/dot_general | solution.py:217
  18.4 23.4 %all-to-all-done.1.q_ref = bf16[16,336,128]{2,1,0:T(8,128)(2,1)S(1)} async-done(((bf16[16,336,128]{2,1,0:T(8,128)(2,1)}), bf16[16,336,128]{2,1,0:T(8,128)(2,1)S(1)}, u32[]{:S(2)}, u32[]{:S(2)}) %all-to-all-start.1) | async-done | bytes 1376288 | tf_op jit(solution)/shard_map/all_to_all | solution.py:165
  41.8 5.1 %all-to-all-start = ((bf16[16,32,1280]{2,1,0:T(8,128)(2,1)}), bf16[16,32,1280]{2,1,0:T(8,128)(2,1)S(1)}, u32[]{:S(2)}, u32[]{:S(2)}) async-start(bf16[16,32,1280]{2,1,0:T(8,128)(2,1)} %bitcast.30), calls=%async_computation | async-start | bytes 2621440 | tf_op jit(solution)/shard_map/all_to_all | solution.py:165
  46.9 0.1 fusion.8
  47.1 0.1 convolution_convert_fusion.2
  47.2 0.4 select_reduce_fusion.1
  47.8 0.8 select_reduce_fusion
  48.6 0.2 copy.21.doc_ref
  49.0 2.5 %copy-done = bf16[2048,1280]{1,0:T(8,128)(2,1)S(1)} copy-done((bf16[2048,1280]{1,0:T(8,128)(2,1)S(1)}, bf16[2048,1280]{1,0:T(8,128)(2,1)}, u32[]{:S(2)}) %copy-start) | copy-done | bytes 5242904
  51.5 10.1 %attend.1 = bf16[512,1280]{1,0:T(8,128)(2,1)S(1)} custom-call(bf16[16,336,128]{2,1,0:T(8,128)(2,1)S(1)} %all-to-all-done.1.q_ref, s32[512,1]{1,0:T(8,128)S(1)} %copy.21.doc_ref, bf16[2048,1280]{1,0:T(8,128)(2,1)S(1)} %copy-done, bf16[32,1280]{1,0:T(8,128)(2,1)S(1)} %collective-permute-done.before_ref, bf16[32,1280]{1,0:T(8,128)(2,1)S(1)} %collective-permute-done.1.after_ref, ...), custom_call_target="tpu_custom_call" | custom-call | flops 5368709120 | bytes 7864320 | tf_op jit(solution)/shard_map/attend/pallas_call | solution.py:108
  61.6 1.9 %convolution_convert_fusion = bf16[512,1280]{1,0:T(8,128)(2,1)} fusion(bf16[512,1280]{1,0:T(8,128)(2,1)S(1)} %attend.1, s32[512]{0:T(512)S(1)} %fusion.9, pred[512]{0:T(512)(128)(4,1)S(1)} %ge.13), kind=kOutput, calls=%fused_computation.2 | convolution fusion | flops 672268288 | bytes 2624000 | tf_op jit(solution)/shard_map/dot_general | solution.py:253
  63.5 13.7 %all-to-all-done = bf16[16,32,1280]{2,1,0:T(8,128)(2,1)S(1)} async-done(((bf16[16,32,1280]{2,1,0:T(8,128)(2,1)}), bf16[16,32,1280]{2,1,0:T(8,128)(2,1)S(1)}, u32[]{:S(2)}, u32[]{:S(2)}) %all-to-all-start) | async-done | bytes 1310752 | tf_op jit(solution)/shard_map/all_to_all | solution.py:165
  77.2 5.0 %all-to-all-start.2 = ((bf16[16,32,1280]{2,1,0:T(8,128)(2,1)}), bf16[16,32,1280]{2,1,0:T(8,128)(2,1)S(1)}, u32[]{:S(2)}, u32[]{:S(2)}) async-start(bf16[16,32,1280]{2,1,0:T(8,128)(2,1)} %bitcast.31), calls=%async_computation.2 | async-start | bytes 2621440 | tf_op jit(solution)/shard_map/all_to_all | solution.py:165
  82.3 1.6 %write_out.1 = bf16[512,1280]{1,0:T(8,128)(2,1)} custom-call(bf16[512,1280]{1,0:T(8,128)(2,1)S(1)} %bitcast.28), custom_call_target="tpu_custom_call" | custom-call | bytes 2621440 | tf_op jit(solution)/shard_map/write_out/pallas_call | solution.py:152
  83.9 0.1 select_reduce_fusion.2
  84.0 28.7 %all-to-all-done.2.x_ref = bf16[16,32,1280]{2,1,0:T(8,128)(2,1)S(1)} async-done(((bf16[16,32,1280]{2,1,0:T(8,128)(2,1)}), bf16[16,32,1280]{2,1,0:T(8,128)(2,1)S(1)}, u32[]{:S(2)}, u32[]{:S(2)}) %all-to-all-start.2) | async-done | bytes 1310752 | tf_op jit(solution)/shard_map/all_to_all | solution.py:165
  112.7 1.7 %place.1 = bf16[16,32,1280]{2,1,0:T(8,128)(2,1)} custom-call(s32[16]{0:T(128)S(1)} %broadcast_add_fusion.2.comes_ref, bf16[16,32,1280]{2,1,0:T(8,128)(2,1)S(1)} %all-to-all-done.2.x_ref), custom_call_target="tpu_custom_call" | custom-call | bytes 2621440 | tf_op jit(solution)/shard_map/place/pallas_call | solution.py:190
  (28 shorter events, 0.6 us)
Async XLA Ops:
  3.5 12.9 %copy-start.2 = (s32[32768]{0:T(1024)S(1)}, s32[32768]{0:T(1024)}, u32[]{:S(2)}) copy-start(s32[32768]{0:T(1024)} %param.7) | copy-start | bytes 393220
  3.5 12.9 %copy-start.3 = (s32[256,1]{0,1:T(1,128)S(1)}, s32[256,1]{0,1:T(1,128)}, u32[]{:S(2)}) copy-start(s32[256,1]{0,1:T(1,128)} %param.9) | copy-start | bytes 3076
  3.5 13.1 %copy-start.4 = (s32[256,1]{0,1:T(1,128)S(1)}, s32[256,1]{0,1:T(1,128)}, u32[]{:S(2)}) copy-start(s32[256,1]{0,1:T(1,128)} %param.11) | copy-start | bytes 3076
  3.5 13.3 %copy-start.1 = (bf16[256,1280]{1,0:T(8,128)(2,1)S(1)}, bf16[256,1280]{1,0:T(8,128)(2,1)}, u32[]{:S(2)}) copy-start(bf16[256,1280]{1,0:T(8,128)(2,1)} %rows_ref.1) | copy-start | bytes 1966084
  3.5 38.2 %all-to-all-start.1 = ((bf16[16,336,128]{2,1,0:T(8,128)(2,1)}), bf16[16,336,128]{2,1,0:T(8,128)(2,1)S(1)}, u32[]{:S(2)}, u32[]{:S(2)}) async-start(bf16[16,336,128]{2,1,0:T(8,128)(2,1)} %deal.1), calls=%async_computation.1 | async-start | bytes 2752512 | tf_op jit(solution)/shard_map/all_to_all | solution.py:165
  10.9 38.1 %collective-permute-start = (bf16[32,1280]{1,0:T(8,128)(2,1)S(1)}, bf16[32,1280]{1,0:T(8,128)(2,1)S(1)}, u32[]{:S(2)}, u32[]{:S(2)}) collective-permute-start(bf16[32,1280]{1,0:T(8,128)(2,1)S(1)} %get-tuple-element.5), channel_id=1, source_target_pairs={{0,1},{1,2},{2,3},{3,4},{4,5},{5,6},{6,7},{7,8},{8,9},{9,10},{10,1... | collective-permute-start | bytes 245768 | tf_op jit(solution)/shard_map/ppermute | solution.py:20
  12.9 36.0 %collective-permute-start.1 = (bf16[32,1280]{1,0:T(8,128)(2,1)S(1)}, bf16[32,1280]{1,0:T(8,128)(2,1)S(1)}, u32[]{:S(2)}, u32[]{:S(2)}) collective-permute-start(bf16[32,1280]{1,0:T(8,128)(2,1)S(1)} %get-tuple-element.4), channel_id=1, source_target_pairs={{1,0},{2,1},{3,2},{4,3},{5,4},{6,5},{7,6},{8,7},{9,8},{10,9},{11,1... | collective-permute-start | bytes 245768 | tf_op jit(solution)/shard_map/ppermute | solution.py:21
  41.8 35.5 %all-to-all-start = ((bf16[16,32,1280]{2,1,0:T(8,128)(2,1)}), bf16[16,32,1280]{2,1,0:T(8,128)(2,1)S(1)}, u32[]{:S(2)}, u32[]{:S(2)}) async-start(bf16[16,32,1280]{2,1,0:T(8,128)(2,1)} %bitcast.30), calls=%async_computation | async-start | bytes 2621440 | tf_op jit(solution)/shard_map/all_to_all | solution.py:165
  49.0 2.5 %copy-start = (bf16[2048,1280]{1,0:T(8,128)(2,1)S(1)}, bf16[2048,1280]{1,0:T(8,128)(2,1)}, u32[]{:S(2)}) copy-start(bf16[2048,1280]{1,0:T(8,128)(2,1)} %k_ref.1) | copy-start | bytes 15728644
  77.2 35.4 %all-to-all-start.2 = ((bf16[16,32,1280]{2,1,0:T(8,128)(2,1)}), bf16[16,32,1280]{2,1,0:T(8,128)(2,1)S(1)}, u32[]{:S(2)}, u32[]{:S(2)}) async-start(bf16[16,32,1280]{2,1,0:T(8,128)(2,1)} %bitcast.31), calls=%async_computation.2 | async-start | bytes 2621440 | tf_op jit(solution)/shard_map/all_to_all | solution.py:165
